TPU v7x, 32 devices: a whole 2x2x4 slice. The times are simulated.
32 devices in a mesh: grp: 2 (over x), blk: 16 (over z, y, core).
Axes of the slice: x: 2, y: 2, z: 4, core: 2. Of those that a mesh axis runs over, the one named last changes fastest.
Arguments:
- queries: bfloat16 [32, 64, 128], P(('grp', 'blk')), may hold values from -120 to 120
- prefix_kv: bfloat16 [2, 2, 16384, 128], P(None, 'grp', 'blk'), may hold values from -6 to 6
- suffix_kv: bfloat16 [32, 256, 2, 4, 128], P(('grp', 'blk')), may hold values from -8 to 8
- new_kv: bfloat16 [32, 2, 4, 128], P(('grp', 'blk')), may hold values from -5 to 5
- suffix_len: int32 [32], P(('grp', 'blk')), may hold values from 1 to 256, as said below
Outputs:
- attended: bfloat16 [32, 64, 128], P(('grp', 'blk'))
Inputs may be any that keep to these rules, and one draw needn't show every extreme that they name: `suffix_len`: some request has all 256 positions live in every draw.
All inputs are finite; a program needn't handle non-finite values.
Results may differ from a plain program's by a relative error of at most 0.0044.
Values may be sent and summed in bfloat16 or wider, within the bound.
No kernel may reach another device: no remote copies, remote signals or barrier semaphores. Data moves between devices by JAX's collectives and lax.ppermute only.
A program may use at most 64 MiB of HBM per device.

v0:
```python
import jax
import jax.numpy as jnp
from jax import lax
from jax.sharding import PartitionSpec as P

H = 64
KVH = 4
HD = 128
SL = 256


def combine(first, second):
    best_score = jnp.maximum(first[2], second[2])
    early = jnp.exp(first[2] - best_score)
    later = jnp.exp(second[2] - best_score)
    numerator = first[0] * early[..., None] + second[0] * later[..., None]
    denominator = first[1] * early + second[1] * later
    return (numerator, denominator, best_score)


def piece_partial(running, rows_per_head, segment_key_rows, segment_value_rows):
    scores = jnp.einsum(
        "cou,fju->fcoj", rows_per_head, segment_key_rows, preferred_element_type=jnp.float32
    ) * HD ** (-0.5)
    block_best = jnp.max(scores, -1)
    softmax_weight = jnp.exp(scores - block_best[..., None]).astype(jnp.bfloat16)
    block_den = jnp.sum(softmax_weight.astype(jnp.float32), -1)
    block_num = jnp.einsum(
        "zhsx,zxv->zhsv", softmax_weight, segment_value_rows, preferred_element_type=jnp.float32
    )
    best_score = jnp.maximum(running[2], jnp.max(block_best, 0))
    early = jnp.exp(running[2] - best_score)
    later = jnp.exp(block_best - best_score[None])
    numerator = running[0] * early[..., None] + jnp.sum(block_num * later[..., None], 0)
    denominator = running[1] * early + jnp.sum(block_den * later, 0)
    return (numerator, denominator, best_score)


def suffix_partial(own_queries, suffix_kv, new_kv, suffix_len):
    reciprocal_scale = HD ** (-0.5)
    scores = (
        jnp.einsum(
            "rgpd,rsgd->grps", own_queries, suffix_kv[:, :, 0], preferred_element_type=jnp.float32
        )
        * reciprocal_scale
    )
    inside = jnp.arange(suffix_kv.shape[1], dtype=jnp.int32)[None, :] < suffix_len[:, None]
    scores = jnp.where(inside[None, :, None, :], scores, -jnp.inf)
    own_score = (
        jnp.einsum("rgpd,rgd->grp", own_queries, new_kv[:, 0], preferred_element_type=jnp.float32)
        * reciprocal_scale
    )
    best_score = jnp.maximum(jnp.max(scores, -1), own_score)
    softmax_weight = jnp.exp(scores - best_score[..., None]).astype(jnp.bfloat16)
    own_weight = jnp.exp(own_score - best_score).astype(jnp.bfloat16).astype(jnp.float32)
    denominator = jnp.sum(softmax_weight.astype(jnp.float32), -1) + own_weight
    numerator = jnp.einsum(
        "grps,rsgd->grpd", softmax_weight, suffix_kv[:, :, 1], preferred_element_type=jnp.float32
    )
    new_values = jnp.swapaxes(new_kv[:, 1], 0, 1).astype(jnp.float32)
    numerator = numerator + own_weight[..., None] * new_values[:, :, None, :]
    return (numerator, denominator, best_score)


def local(queries, prefix_kv, suffix_kv, new_kv, suffix_len):
    local_rows = queries.shape[0]
    sharing = H // KVH
    members = lax.axis_size("blk")
    per_head = members // KVH
    position = lax.axis_index("blk")
    my_head = position // per_head
    own_queries = queries.reshape(local_rows, KVH, sharing, HD)
    outgoing = jnp.repeat(jnp.transpose(own_queries, (1, 0, 2, 3)), per_head, axis=0)
    arrived = lax.all_to_all(outgoing, "blk", split_axis=0, concat_axis=0, tiled=True)
    group_rows = members * local_rows
    rows_per_head = arrived.reshape(group_rows, sharing, HD)
    replica = lax.all_gather(prefix_kv, "grp", axis=1, tiled=True)
    blocks = replica.shape[2] // SL

    def absorb(running, slice_index):
        keys = lax.dynamic_index_in_dim(replica[0], slice_index, 0, keepdims=False).reshape(
            blocks, SL, HD
        )
        values = lax.dynamic_index_in_dim(replica[1], slice_index, 0, keepdims=False).reshape(
            blocks, SL, HD
        )
        return (piece_partial(running, rows_per_head, keys, values), None)

    initial = (
        jnp.zeros((group_rows, sharing, HD), jnp.float32),
        jnp.zeros((group_rows, sharing), jnp.float32),
        jnp.full((group_rows, sharing), -jnp.inf, jnp.float32),
    )
    running, unused = lax.scan(absorb, initial, jnp.arange(lax.axis_size("grp"), dtype=jnp.int32))
    numerator, denominator, best_score = running
    is_mine = (jnp.arange(KVH, dtype=jnp.int32) == my_head)[:, None, None]
    placed_best = jnp.where(is_mine, best_score[None], -jnp.inf)
    group_best = lax.pmax(placed_best, "blk")
    head_best = lax.dynamic_index_in_dim(group_best, my_head, 0, keepdims=False)
    factor = jnp.exp(best_score - head_best)
    placed_num = jnp.where(is_mine[..., None], (numerator * factor[..., None])[None], 0.0)
    placed_den = jnp.where(is_mine, (denominator * factor)[None], 0.0)
    shared = (
        lax.psum_scatter(placed_num, "blk", scatter_dimension=1, tiled=True),
        lax.psum_scatter(placed_den, "blk", scatter_dimension=1, tiled=True),
    )
    local_peak_score = lax.dynamic_slice_in_dim(group_best, position * local_rows, local_rows, 1)
    prefix_part = (shared[0], shared[1], local_peak_score)
    total = combine(prefix_part, suffix_partial(own_queries, suffix_kv, new_kv, suffix_len))
    result = total[0] / total[1][..., None]
    return jnp.transpose(result, (1, 0, 2, 3)).reshape(local_rows, H, HD).astype(jnp.bfloat16)


def solution(mesh):
    in_specs = (
        P(("grp", "blk"), None, None),
        P(None, "grp", "blk", None),
        P(("grp", "blk"), None, None, None, None),
        P(("grp", "blk"), None, None, None),
        P(("grp", "blk")),
    )
    out_specs = P(("grp", "blk"), None, None)
    return jax.shard_map(local, mesh=mesh, in_specs=in_specs, out_specs=out_specs, check_vma=False)
```

profile of v0, /device:TPU:0, one launch (start us, length us, event | category | flops | bytes accessed | tf_op | source)
XLA Modules:
  0.0 180.7 jit_solution(17355831582274992026)
XLA Ops:
  6.5 1.4 broadcast_in_dim.99
  7.9 7.4 %all-to-all-start = ((bf16[16,1,16,128]{3,2,1,0:T(8,128)(2,1)}), bf16[16,1,16,128]{3,2,1,0:T(8,128)(2,1)S(1)}, u32[]{:S(2)}, u32[]{:S(2)}) async-start(bf16[16,1,16,128]{3,2,1,0:T(8,128)(2,1)} %bitcast.1), calls=%async_computation | async-start | bytes 131072 | tf_op jit(solution)/shard_map/all_to_all | solution.py:74
  15.4 0.7 all-gather.2.cloned.1.call-update
  16.8 0.7 copy-done.2
  17.5 0.2 fusion.24
  17.6 0.5 copy-done.1
  18.2 0.3 fusion.25
  18.4 0.1 fusion.15
  18.6 0.7 copy-done.3
  19.2 0.6 dynamic-slice.2
  19.8 2.4 %all-to-all-done = bf16[16,1,16,128]{3,2,1,0:T(8,128)(2,1)S(1)} async-done(((bf16[16,1,16,128]{3,2,1,0:T(8,128)(2,1)}), bf16[16,1,16,128]{3,2,1,0:T(8,128)(2,1)S(1)}, u32[]{:S(2)}, u32[]{:S(2)}) %all-to-all-start) | async-done | bytes 65568 | tf_op jit(solution)/shard_map/all_to_all | solution.py:74
  22.2 18.1 %all-gather.2.cloned.1.call-done = bf16[2,2,1024,128]{3,2,1,0:T(8,128)(2,1)} async-done(((bf16[2,1,1024,128]{3,2,1,0:T(8,128)(2,1)}), bf16[2,2,1024,128]{3,2,1,0:T(8,128)(2,1)}) %all-gather.2.cloned.1.call-update) | async-done | bytes 1048592 | tf_op jit(solution)/shard_map/all_gather | solution.py:77
  40.4 11.0 %while.15 = (s32[]{:T(128)}, f32[16,16,128]{2,1,0:T(8,128)S(1)}, f32[16,16]{1,0:T(8,128)S(1)}, f32[16,16]{1,0:T(8,128)S(1)}, bf16[2,2,1024,128]{3,2,1,0:T(8,128)...) while((s32[]{:T(128)}, f32[16,16,128]{2,1,0:T(8,128)S(1)}, ...), condition=%wide.region_6.7_spmd.clone, body=%wide.region_0.6_spmd.clone.sunk | while | flops 136907008 | bytes 7453859 | solution.py:94
  40.4 0.7 dynamic_slice.39
  43.1 1.3 fusion.39
  44.4 0.4 fusion.40
  44.8 0.4 convert_reduce_fusion.3
  45.3 0.4 fusion.41
  45.7 0.1 fusion.43
  45.9 0.7 dynamic_slice.39
  48.6 1.3 fusion.39
  49.9 0.4 fusion.40
  50.3 0.4 convert_reduce_fusion.3
  50.8 0.4 fusion.41
  51.2 0.1 fusion.43
  51.4 61.2 %pmax.7 = f32[4,16,16]{2,0,1:T(4,128)S(1)} all-reduce(f32[4,16,16]{2,0,1:T(4,128)S(1)} %broadcast_select_fusion.2), channel_id=1, replica_groups=mesh['grp'=2,'blk'=16] {'blk'}, use_global_device_ids=true, to_apply=%region_7.8 | all-reduce | flops 1024 | bytes 8192 | tf_op jit(solution)/shard_map/pmax | solution.py:98
  112.6 0.1 broadcast_multiply_fusion
  112.7 0.9 broadcast_select_fusion
  113.8 57.7 %all-reduce = f32[4,16,16]{2,0,1:T(4,128)S(1)} all-reduce(f32[4,16,16]{2,0,1:T(4,128)S(1)} %broadcast_select_fusion.1), channel_id=3, replica_groups=mesh['grp'=2,'blk'=16] {'blk'}, use_global_device_ids=true, to_apply=%region_10.11.clone | all-reduce | flops 1024 | bytes 8192
  171.5 0.2 convert_reduce_fusion.1
  171.7 0.6 fusion.14
  172.3 1.6 fusion.10
  (31 shorter events, 0.5 us)
Async XLA Ops:
  6.5 10.9 %copy-start = (bf16[1,256,2,4,128]{4,3,2,1,0:T(4,128)(2,1)S(1)}, bf16[1,256,2,4,128]{4,3,2,1,0:T(4,128)(2,1)}, u32[]{:S(2)}) copy-start(bf16[1,256,2,4,128]{4,3,2,1,0:T(4,128)(2,1)} %param.9) | copy-start | bytes 1572868
  7.9 14.3 %all-to-all-start = ((bf16[16,1,16,128]{3,2,1,0:T(8,128)(2,1)}), bf16[16,1,16,128]{3,2,1,0:T(8,128)(2,1)S(1)}, u32[]{:S(2)}, u32[]{:S(2)}) async-start(bf16[16,1,16,128]{3,2,1,0:T(8,128)(2,1)} %bitcast.1), calls=%async_computation | async-start | bytes 131072 | tf_op jit(solution)/shard_map/all_to_all | solution.py:74
  15.3 25.0 %all-gather.2.cloned.1.call-start = ((), (), s32[]{:S(2)}) async-start(), calls=%async_computation.2 | async-start | bytes 1572864 | tf_op jit(solution)/shard_map/all_gather | solution.py:77
  16.1 156.2 %reduce-scatter.2.cloned.1.call-start = ((), (), s32[]{:S(2)}) async-start(), calls=%async_computation.3 | async-start | bytes 557056 | tf_op jit(solution)/shard_map/reduce_scatter | solution.py:104
  16.8 0.7 copy-start.2
  17.5 0.7 copy-start.1
  18.6 0.7 copy-start.3
Sparse Core Ops, SparseCore 0:
  17.7 22.6 all-gather.1
  113.8 52.1 reduce-scatter.1
where the time goes:
time: 181 us
  blocking collectives  119 us (66%)
  waiting for transfers between devices  21.3 us (12%)
  between operations  14.1 us (8%)
  local copies, waits for them, and re-layouts  7.99 us (4%)
  starting transfers between devices  7.46 us (4%)
  loops' own time  4.32 us (2%)
  matrix products  3.51 us (2%)
  other arithmetic  3.09 us (2%)
    pmax x1, blocking collectives, local(): group_best = lax.pmax(placed_best, 'blk')  61.2 us
    unnamed x1, blocking collectives  57.7 us
    all_gather x1, waiting for transfers between devices, local(): replica = lax.all_gather(prefix_kv, 'grp', axis=1, tiled=True)  18.1 us
    all_to_all x1, starting transfers between devices, local(): lax.all_to_all(outgoing, 'blk', split_axis=0, concat_axis=0, tiled=True)  7.39 us
    another operation x1, loops' own time, local(): lax.scan(absorb, initial, jnp.arange(lax.axis_size('grp'), dtype=jnp.int32))  4.32 us
  transfers between devices with their start and end apart: 3, of which 2 were waited for; matrix products, arithmetic and copies ran while one was open for 1% of the time, Pallas kernels for 0%

commit v1 on v0

v1 whole, which is shorter than its diff:
```python
import functools
import math

import jax
import jax.numpy as jnp
from jax import lax
from jax.experimental import pallas as pl
from jax.experimental.pallas import tpu as pltpu
from jax.sharding import PartitionSpec as P

H = 64
KVH = 4
HD = 128
SHARE = H // KVH
SCALE2 = HD ** (-0.5) * math.log2(math.e)
VMEM = pl.BlockSpec(memory_space=pltpu.VMEM)
ROWS = 128
NT = (((1,), (1,)), ((), ()))


def dot_nt(a, b):
    return lax.dot_general(a, b, NT, preferred_element_type=jnp.float32)


def dot(a, b):
    return jnp.dot(a, b, preferred_element_type=jnp.float32)


def log2(x):
    return jnp.log(x) * math.log2(math.e)


def split3(x):
    hi = x.astype(jnp.bfloat16).astype(jnp.float32)
    rest = x - hi
    mid = rest.astype(jnp.bfloat16).astype(jnp.float32)
    low = (rest - mid).astype(jnp.bfloat16).astype(jnp.float32)
    return hi, mid, low


def prefix_kernel(q_ref, kv_ref, out_ref):
    per_step = ROWS // SHARE
    requests = q_ref.shape[0]
    lane = lax.broadcasted_iota(jnp.int32, (ROWS, HD), 1)

    def step(at):
        keys = kv_ref[0]
        values = kv_ref[1]
        extended = jnp.concatenate([values, jnp.ones_like(values)], axis=1)
        rows = q_ref[pl.ds(at, per_step)].reshape(ROWS, HD)
        scores = dot_nt(rows, keys)
        best = jnp.max(scores, axis=1, keepdims=True)
        weight = jnp.exp2((scores - best) * SCALE2).astype(jnp.bfloat16)
        both = dot(weight, extended)
        total = both[:, HD:]
        result = both[:, :HD] / total
        hi, mid, low = split3(best * SCALE2 + log2(total))
        stats = jnp.where(lane == 0, hi, jnp.where(lane == 1, mid, jnp.where(lane == 2, low, 0.0)))
        out_ref[pl.ds(at, per_step), :SHARE] = result.astype(jnp.bfloat16).reshape(per_step, SHARE, HD)
        out_ref[pl.ds(at, per_step), SHARE:] = stats.astype(jnp.bfloat16).reshape(per_step, SHARE, HD)

    unrolled = 4 if requests % (4 * per_step) == 0 else 1

    def steps(index, unused):
        for inner in range(unrolled):
            step((index * unrolled + inner) * per_step)
        return unused

    trips = requests // (per_step * unrolled)
    if trips == 1:
        steps(0, 0)
    else:
        lax.fori_loop(0, trips, steps, 0)


def suffix_kernel(len_ref, q_ref, cache_ref, new_ref, out_ref, lse_ref):
    q = q_ref[0]
    rows = cache_ref.shape[1]
    live = len_ref[0]

    def masked(scores, limit):
        at = lax.broadcasted_iota(jnp.int32, scores.shape, 1)
        head = lax.broadcasted_iota(jnp.int32, scores.shape, 0) // SHARE
        own = (at % (2 * KVH) == head) & (at < limit * (2 * KVH))
        return jnp.where(own, scores, -jnp.inf)

    cache = cache_ref[0]
    new = new_ref[0]
    scores = masked(dot_nt(q, cache), live)
    new_scores = masked(dot_nt(q, new), 1)
    best = jnp.maximum(jnp.max(scores, axis=1, keepdims=True), jnp.max(new_scores, axis=1, keepdims=True))
    weight = jnp.exp2((scores - best) * SCALE2).astype(jnp.bfloat16).astype(jnp.float32)
    new_weight = jnp.exp2((new_scores - best) * SCALE2).astype(jnp.bfloat16).astype(jnp.float32)
    total = jnp.sum(weight, axis=1, keepdims=True) + jnp.sum(new_weight, axis=1, keepdims=True)
    moved = pltpu.roll(weight, KVH, 1).astype(jnp.bfloat16)
    new_moved = jnp.concatenate([new_weight[:, KVH:], new_weight[:, :KVH]], axis=1).astype(jnp.bfloat16)
    numerator = dot(moved, cache) + dot(new_moved, new)
    out_ref[...] = numerator / total
    lse_ref[...] = jnp.broadcast_to(best * SCALE2 + log2(total), lse_ref.shape)


def merge_kernel(groups, per_head, part_ref, suffix_ref, lse_ref, out_ref):
    sources = part_ref.shape[0]
    stats = part_ref[:, SHARE:].reshape(sources * SHARE, HD)
    part_lse = dot(stats, jnp.ones((HD, HD), jnp.bfloat16)).reshape(sources, SHARE, HD)
    for head in range(KVH):
        span = slice(head * SHARE, (head + 1) * SHARE)
        own = [(g * KVH + head) * per_head + i for g in range(groups) for i in range(per_head)]
        own_lse = lse_ref[span]
        best = own_lse
        for source in own:
            best = jnp.maximum(best, part_lse[source])
        total = jnp.exp2(own_lse - best)
        numerator = total * suffix_ref[span]
        for source in own:
            factor = jnp.exp2(part_lse[source] - best)
            total = total + factor
            numerator = numerator + factor * part_ref[source, :SHARE].astype(jnp.float32)
        out_ref[0, span] = (numerator / total).astype(jnp.bfloat16)


def local(queries, prefix_kv, suffix_kv, new_kv, suffix_len):
    groups = lax.axis_size("grp")
    members = lax.axis_size("blk")
    per_head = members // KVH
    devices = groups * members
    span = prefix_kv.shape[2]
    own = queries.reshape(1, KVH, 1, SHARE, HD)
    outgoing = jnp.broadcast_to(own, (groups, KVH, per_head, SHARE, HD)).reshape(devices, SHARE, HD)
    arrived = lax.all_to_all(outgoing, ("grp", "blk"), split_axis=0, concat_axis=0, tiled=True)

    suffix, suffix_lse = pl.pallas_call(
        suffix_kernel,
        out_shape=[jax.ShapeDtypeStruct((H, HD), jnp.float32)] * 2,
        in_specs=[pl.BlockSpec(memory_space=pltpu.SMEM), VMEM, VMEM, VMEM],
        out_specs=[VMEM, VMEM],
        name="suffix",
        cost_estimate=pl.CostEstimate(flops=70_000_000, bytes_accessed=600_000, transcendentals=140_000),
    )(suffix_len, queries, suffix_kv.reshape(1, -1, HD), new_kv.reshape(1, -1, HD))

    partial = pl.pallas_call(
        prefix_kernel,
        out_shape=jax.ShapeDtypeStruct((devices, 2 * SHARE, HD), jnp.bfloat16),
        in_specs=[VMEM, VMEM],
        out_specs=VMEM,
        name="prefix",
        compiler_params=pltpu.CompilerParams(vmem_limit_bytes=48 * 1024 * 1024),
        cost_estimate=pl.CostEstimate(
            flops=6 * devices * SHARE * span * HD, bytes_accessed=800_000, transcendentals=devices * SHARE * span
        ),
    )(arrived, prefix_kv.reshape(2, span, HD))

    returned = lax.all_to_all(partial, ("grp", "blk"), split_axis=0, concat_axis=0, tiled=True)
    return pl.pallas_call(
        functools.partial(merge_kernel, groups, per_head),
        out_shape=jax.ShapeDtypeStruct((1, H, HD), jnp.bfloat16),
        in_specs=[VMEM, VMEM, VMEM],
        out_specs=VMEM,
        name="merge",
        compiler_params=pltpu.CompilerParams(vmem_limit_bytes=48 * 1024 * 1024),
    )(returned, suffix, suffix_lse)


def solution(mesh):
    in_specs = (
        P(("grp", "blk"), None, None),
        P(None, "grp", "blk", None),
        P(("grp", "blk"), None, None, None, None),
        P(("grp", "blk"), None, None, None),
        P(("grp", "blk")),
    )
    out_specs = P(("grp", "blk"), None, None)
    return jax.shard_map(local, mesh=mesh, in_specs=in_specs, out_specs=out_specs, check_vma=False)
```

time: 181 us -> 34.5 us (0.19)
  blocking collectives: 119 us -> 15.3 us
  waiting for transfers between devices: 21.3 us -> 7.28 us
  between operations: 14.1 us -> 0.66 us
  Pallas kernels: 0 us -> 4.92 us
  starting transfers between devices: 7.46 us -> 2.58 us
  local copies, waits for them, and re-layouts: 7.99 us -> 3.29 us
  loops' own time: 4.32 us -> 0 us
  matrix products: 3.51 us -> 0 us
  other arithmetic: 3.09 us -> 0 us
    pmax x1 -> x0, blocking collectives: 61.2 us -> none  [local(): group_best = lax.pmax(placed_best, 'blk')]
    unnamed x1 -> x0, blocking collectives: 57.7 us -> none
    all_gather x1 -> x0, waiting for transfers between devices: 18.1 us -> none  [local(): replica = lax.all_gather(prefix_kv, 'grp', axis=1, tiled=True)]
    all_to_all x0 -> x1, blocking collectives: none -> 15.3 us  [local(): lax.all_to_all(outgoing, ('grp', 'blk'), split_axis=0, concat_axis=0, til...]
    pallas_call x0 -> x3, Pallas kernels: none -> 4.92 us  [the longest x1 2.35 us: local(): pl.pallas_call(suffix_kernel, out_shape=[jax.ShapeDtypeStruct((H, HD), jn...]
    all_to_all x1, waiting for transfers between devices: 2.44 us -> 7.28 us  [local(): lax.all_to_all(partial, ('grp', 'blk'), split_axis=0, concat_axis=0, tile...]
    all_to_all x1, starting transfers between devices: 7.39 us -> 2.58 us  [local(): lax.all_to_all(partial, ('grp', 'blk'), split_axis=0, concat_axis=0, tile...]
    another operation x1 -> x0, loops' own time: 4.32 us -> none  [local(): lax.scan(absorb, initial, jnp.arange(lax.axis_size('grp'), dtype=jnp.int32))]
  transfers between devices with their start and end apart: 3 -> 1, of which waited for: 2 -> 1; matrix products, arithmetic and copies ran while one was open for 1% -> 0% of each run, Pallas kernels for 0% -> 7%
where the time goes in v1:
time: 34.5 us; the launch traced here: 34.1 us
  blocking collectives  15.3 us (44%)
  waiting for transfers between devices  7.28 us (21%)
  Pallas kernels  4.92 us (14%)
  local copies, waits for them, and re-layouts  3.29 us (10%)
  starting transfers between devices  2.58 us (7%)
  between operations  0.66 us (2%)
    all_to_all x1, blocking collectives, local(): lax.all_to_all(outgoing, ('grp', 'blk'), split_axis=0, concat_axis=0, til...  15.3 us
    all_to_all x1, waiting for transfers between devices, local(): lax.all_to_all(partial, ('grp', 'blk'), split_axis=0, concat_axis=0, tile...  7.28 us
    all_to_all x1, starting transfers between devices, local(): lax.all_to_all(partial, ('grp', 'blk'), split_axis=0, concat_axis=0, tile...  2.58 us
    unnamed x6, local copies, waits for them, and re-layouts  2.56 us
    pallas_call x1, Pallas kernels, local(): pl.pallas_call(suffix_kernel, out_shape=[jax.ShapeDtypeStruct((H, HD), jn...  2.35 us
    pallas_call x1, Pallas kernels, local(): pl.pallas_call(prefix_kernel, out_shape=jax.ShapeDtypeStruct((devices, 2...  1.74 us
    pallas_call x1, Pallas kernels, local(): pl.pallas_call(functools.partial(merge_kernel, groups, per_head), out_sha...  0.83 us
    broadcast_in_dim x1, local copies, waits for them, and re-layouts, local(): jnp.broadcast_to(own, (groups, KVH, per_head, SHARE, HD))  0.73 us
  transfers between devices with their start and end apart: 1, of which 1 were waited for; matrix products, arithmetic and copies ran while one was open for 0% of the time, Pallas kernels for 7%

profile of v1, /device:TPU:0, one launch (start us, length us, event | category | flops | bytes accessed | tf_op | source)
XLA Modules:
  0.0 34.1 jit_solution(6091381077557524131)
XLA Ops:
  0.0 0.7 %broadcast_in_dim.8 = bf16[2,4,4,16,128]{4,3,2,1,0:T(8,128)(2,1)S(1)} broadcast(bf16[4,16,128]{2,1,0:T(8,128)(2,1)} %bitcast.8), dimensions={1,3,4} | broadcast | bytes 147456 | tf_op jit(solution)/shard_map/broadcast_in_dim | solution.py:129
  0.7 15.3 %all_to_all.10.q_ref = bf16[32,16,128]{2,1,0:T(8,128)(2,1)S(1)} all-to-all(bf16[32,16,128]{2,1,0:T(8,128)(2,1)S(1)} %bitcast.7), channel_id=1, replica_groups=mesh['grp'=2,'blk'=16] {'grp','blk'}, dimensions={0} | all-to-all | bytes 262144 | tf_op jit(solution)/shard_map/all_to_all | solution.py:130
  16.1 0.0 copy-start.2
  16.1 1.0 %copy-done.2 = bf16[2,1,1024,128]{3,2,1,0:T(8,128)(2,1)S(1)} copy-done((bf16[2,1,1024,128]{3,2,1,0:T(8,128)(2,1)S(1)}, bf16[2,1,1024,128]{3,2,1,0:T(8,128)(2,1)}, u32[]{:S(2)}) %copy-start.2) | copy-done | bytes 524312
  17.1 1.7 %prefix.1 = bf16[32,32,128]{2,1,0:T(8,128)(2,1)} custom-call(bf16[32,16,128]{2,1,0:T(8,128)(2,1)S(1)} %all_to_all.10.q_ref, bf16[2,1024,128]{2,1,0:T(8,128)(2,1)S(1)} %bitcast.5), custom_call_target="tpu_custom_call" | custom-call | flops 402653184 | bytes 800000 | tf_op jit(solution)/shard_map/prefix/pallas_call | solution.py:141
  18.9 2.6 %all-to-all-start.1 = ((bf16[32,32,128]{2,1,0:T(8,128)(2,1)}), bf16[32,32,128]{2,1,0:T(8,128)(2,1)S(1)}, u32[]{:S(2)}, u32[]{:S(2)}) async-start(bf16[32,32,128]{2,1,0:T(8,128)(2,1)} %prefix.1), calls=%async_computation.1 | async-start | bytes 524288 | tf_op jit(solution)/shard_map/all_to_all | solution.py:153
  22.1 2.4 %suffix.1 = (f32[64,128]{1,0:T(8,128)}, f32[64,128]{1,0:T(8,128)}) custom-call(s32[1]{0:T(128)S(6)} %copy.6.len_ref, bf16[1,64,128]{2,1,0:T(8,128)(2,1)} %q_ref.1, bf16[1,2048,128]{2,1,0:T(8,128)(2,1)} %bitcast.6, bf16[1,8,128]{2,1,0:T(8,128)(2,1)} %bitcast.9), custom_call_target="tpu_custom_call" | custom-call | flops 70000000 | bytes 600000 | tf_op jit(solution)/shard_map/suffix/pallas_call | solution.py:132
  24.4 7.3 %all-to-all-done.1.part_ref = bf16[32,32,128]{2,1,0:T(8,128)(2,1)S(1)} async-done(((bf16[32,32,128]{2,1,0:T(8,128)(2,1)}), bf16[32,32,128]{2,1,0:T(8,128)(2,1)S(1)}, u32[]{:S(2)}, u32[]{:S(2)}) %all-to-all-start.1) | async-done | bytes 262176 | tf_op jit(solution)/shard_map/all_to_all | solution.py:153
  31.7 0.0 copy-start
  31.7 0.8 %copy-done = f32[64,128]{1,0:T(8,128)S(1)} copy-done((f32[64,128]{1,0:T(8,128)S(1)}, f32[64,128]{1,0:T(8,128)}, u32[]{:S(2)}) %copy-start) | copy-done | bytes 32792
  32.5 0.0 copy-start.1
  32.5 0.8 %copy-done.1 = f32[64,128]{1,0:T(8,128)S(1)} copy-done((f32[64,128]{1,0:T(8,128)S(1)}, f32[64,128]{1,0:T(8,128)}, u32[]{:S(2)}) %copy-start.1) | copy-done | bytes 32792
  33.2 0.8 %merge.1 = bf16[1,64,128]{2,1,0:T(8,128)(2,1)} custom-call(bf16[32,32,128]{2,1,0:T(8,128)(2,1)S(1)} %all-to-all-done.1.part_ref, f32[64,128]{1,0:T(8,128)S(1)} %copy-done, f32[64,128]{1,0:T(8,128)S(1)} %copy-done.1), custom_call_target="tpu_custom_call" | custom-call | tf_op jit(solution)/shard_map/merge/pallas_call | solution.py:154
Async XLA Ops:
  16.1 1.0 %copy-start.2 = (bf16[2,1,1024,128]{3,2,1,0:T(8,128)(2,1)S(1)}, bf16[2,1,1024,128]{3,2,1,0:T(8,128)(2,1)}, u32[]{:S(2)}) copy-start(bf16[2,1,1024,128]{3,2,1,0:T(8,128)(2,1)} %param.6) | copy-start | bytes 1572868
  18.9 12.9 %all-to-all-start.1 = ((bf16[32,32,128]{2,1,0:T(8,128)(2,1)}), bf16[32,32,128]{2,1,0:T(8,128)(2,1)S(1)}, u32[]{:S(2)}, u32[]{:S(2)}) async-start(bf16[32,32,128]{2,1,0:T(8,128)(2,1)} %prefix.1), calls=%async_computation.1 | async-start | bytes 524288 | tf_op jit(solution)/shard_map/all_to_all | solution.py:153
  31.7 0.8 %copy-start = (f32[64,128]{1,0:T(8,128)S(1)}, f32[64,128]{1,0:T(8,128)}, u32[]{:S(2)}) copy-start(f32[64,128]{1,0:T(8,128)} %get-tuple-element.7.suffix_ref) | copy-start | bytes 98308
  32.5 0.8 %copy-start.1 = (f32[64,128]{1,0:T(8,128)S(1)}, f32[64,128]{1,0:T(8,128)}, u32[]{:S(2)}) copy-start(f32[64,128]{1,0:T(8,128)} %get-tuple-element.8.lse_ref) | copy-start | bytes 98308

commit v2 on v1

--- a/solution.py
+++ b/solution.py
@@ -15,6 +15,8 @@
 SCALE2 = HD ** (-0.5) * math.log2(math.e)
 VMEM = pl.BlockSpec(memory_space=pltpu.VMEM)
 ROWS = 128
+CORES = 2
+LIMIT = 24 * 1024 * 1024
 NT = (((1,), (1,)), ((), ()))
 
 
@@ -38,20 +40,22 @@
     return hi, mid, low
 
 
-def prefix_kernel(q_ref, kv_ref, out_ref):
+def prefix_kernel(q_ref, kv_ref, other_ref, out_ref):
     per_step = ROWS // SHARE
     requests = q_ref.shape[0]
     lane = lax.broadcasted_iota(jnp.int32, (ROWS, HD), 1)
 
+    def extended(ref):
+        return jnp.concatenate([ref[1], jnp.ones_like(ref[1])], axis=1)
+
     def step(at):
-        keys = kv_ref[0]
-        values = kv_ref[1]
-        extended = jnp.concatenate([values, jnp.ones_like(values)], axis=1)
         rows = q_ref[pl.ds(at, per_step)].reshape(ROWS, HD)
-        scores = dot_nt(rows, keys)
-        best = jnp.max(scores, axis=1, keepdims=True)
+        scores = dot_nt(rows, kv_ref[0])
+        other_scores = dot_nt(rows, other_ref[0])
+        best = jnp.max(jnp.maximum(scores, other_scores), axis=1, keepdims=True)
         weight = jnp.exp2((scores - best) * SCALE2).astype(jnp.bfloat16)
-        both = dot(weight, extended)
+        other_weight = jnp.exp2((other_scores - best) * SCALE2).astype(jnp.bfloat16)
+        both = dot(weight, extended(kv_ref)) + dot(other_weight, extended(other_ref))
         total = both[:, HD:]
         result = both[:, :HD] / total
         hi, mid, low = split3(best * SCALE2 + log2(total))
@@ -59,7 +63,7 @@
         out_ref[pl.ds(at, per_step), :SHARE] = result.astype(jnp.bfloat16).reshape(per_step, SHARE, HD)
         out_ref[pl.ds(at, per_step), SHARE:] = stats.astype(jnp.bfloat16).reshape(per_step, SHARE, HD)
 
-    unrolled = 4 if requests % (4 * per_step) == 0 else 1
+    unrolled = 2 if requests % (2 * per_step) == 0 else 1
 
     def steps(index, unused):
         for inner in range(unrolled):
@@ -122,12 +126,20 @@
 def local(queries, prefix_kv, suffix_kv, new_kv, suffix_len):
     groups = lax.axis_size("grp")
     members = lax.axis_size("blk")
-    per_head = members // KVH
-    devices = groups * members
+    pairs = members // CORES
+    per_head = pairs // KVH
+    partners = groups * pairs
     span = prefix_kv.shape[2]
+    everyone = ("grp", "blk")
+    lanes = [[chip * CORES + core for chip in range(partners)] for core in range(CORES)]
+
+    other = lax.ppermute(prefix_kv, "blk", [(i, i ^ 1) for i in range(members)])
     own = queries.reshape(1, KVH, 1, SHARE, HD)
-    outgoing = jnp.broadcast_to(own, (groups, KVH, per_head, SHARE, HD)).reshape(devices, SHARE, HD)
-    arrived = lax.all_to_all(outgoing, ("grp", "blk"), split_axis=0, concat_axis=0, tiled=True)
+    outgoing = jnp.broadcast_to(own, (groups, KVH, per_head, SHARE, HD)).reshape(partners, SHARE, HD)
+    exchange = functools.partial(
+        lax.all_to_all, axis_name=everyone, split_axis=0, concat_axis=0, axis_index_groups=lanes, tiled=True
+    )
+    arrived = exchange(outgoing)
 
     suffix, suffix_lse = pl.pallas_call(
         suffix_kernel,
@@ -135,29 +147,32 @@
         in_specs=[pl.BlockSpec(memory_space=pltpu.SMEM), VMEM, VMEM, VMEM],
         out_specs=[VMEM, VMEM],
         name="suffix",
+        compiler_params=pltpu.CompilerParams(vmem_limit_bytes=LIMIT),
         cost_estimate=pl.CostEstimate(flops=70_000_000, bytes_accessed=600_000, transcendentals=140_000),
     )(suffix_len, queries, suffix_kv.reshape(1, -1, HD), new_kv.reshape(1, -1, HD))
 
     partial = pl.pallas_call(
         prefix_kernel,
-        out_shape=jax.ShapeDtypeStruct((devices, 2 * SHARE, HD), jnp.bfloat16),
-        in_specs=[VMEM, VMEM],
+        out_shape=jax.ShapeDtypeStruct((partners, 2 * SHARE, HD), jnp.bfloat16),
+        in_specs=[VMEM, VMEM, VMEM],
         out_specs=VMEM,
         name="prefix",
-        compiler_params=pltpu.CompilerParams(vmem_limit_bytes=48 * 1024 * 1024),
+        compiler_params=pltpu.CompilerParams(vmem_limit_bytes=LIMIT),
         cost_estimate=pl.CostEstimate(
-            flops=6 * devices * SHARE * span * HD, bytes_accessed=800_000, transcendentals=devices * SHARE * span
+            flops=12 * partners * SHARE * span * HD,
+            bytes_accessed=1_600_000,
+            transcendentals=2 * partners * SHARE * span,
         ),
-    )(arrived, prefix_kv.reshape(2, span, HD))
+    )(arrived, prefix_kv.reshape(2, span, HD), other.reshape(2, span, HD))
 
-    returned = lax.all_to_all(partial, ("grp", "blk"), split_axis=0, concat_axis=0, tiled=True)
+    returned = exchange(partial)
     return pl.pallas_call(
         functools.partial(merge_kernel, groups, per_head),
         out_shape=jax.ShapeDtypeStruct((1, H, HD), jnp.bfloat16),
         in_specs=[VMEM, VMEM, VMEM],
         out_specs=VMEM,
         name="merge",
-        compiler_params=pltpu.CompilerParams(vmem_limit_bytes=48 * 1024 * 1024),
+        compiler_params=pltpu.CompilerParams(vmem_limit_bytes=LIMIT),
     )(returned, suffix, suffix_lse)
 
 

time: 34.5 us -> 31.9 us (0.925)
  Pallas kernels: 4.92 us -> 3.31 us
  waiting for transfers between devices: 7.28 us -> 5.73 us
  starting transfers between devices: 2.58 us -> 4.09 us
  local copies, waits for them, and re-layouts: 3.29 us -> 2.43 us
    pallas_call x1, Pallas kernels: 2.35 us -> 0.7 us  [local(): pl.pallas_call(suffix_kernel, out_shape=[jax.ShapeDtypeStruct((H, HD), jn...]
    all_to_all x1, waiting for transfers between devices: 7.28 us -> 5.73 us  [local(): returned = exchange(partial)]
    all_to_all x1, starting transfers between devices: 2.58 us -> 3.64 us  [local(): returned = exchange(partial)]
    unnamed x6 -> x8, local copies, waits for them, and re-layouts: 2.56 us -> 1.71 us
    ppermute x0 -> x1, starting transfers between devices: none -> 0.45 us  [local(): other = lax.ppermute(prefix_kv, 'blk', [(i, i ^ 1) for i in range(members)])]
  transfers between devices with their start and end apart: 1 -> 2, of which waited for: 1 -> 1; matrix products, arithmetic and copies ran while one was open for 0% -> 2% of each run, Pallas kernels for 7% -> 2%
where the time goes in v2:
time: 31.9 us; the launch traced here: 31.5 us
  blocking collectives  15.2 us (48%)
  waiting for transfers between devices  5.73 us (18%)
  starting transfers between devices  4.09 us (13%)
  Pallas kernels  3.31 us (10%)
  local copies, waits for them, and re-layouts  2.43 us (8%)
  between operations  0.69 us (2%)
    all_to_all x1, blocking collectives, local(): arrived = exchange(outgoing)  15.2 us
    all_to_all x1, waiting for transfers between devices, local(): returned = exchange(partial)  5.73 us
    all_to_all x1, starting transfers between devices, local(): returned = exchange(partial)  3.64 us
    pallas_call x1, Pallas kernels, local(): pl.pallas_call(prefix_kernel, out_shape=jax.ShapeDtypeStruct((partners, 2...  1.83 us
    unnamed x8, local copies, waits for them, and re-layouts  1.71 us
    pallas_call x1, Pallas kernels, local(): pl.pallas_call(functools.partial(merge_kernel, groups, per_head), out_sha...  0.79 us
    broadcast_in_dim x1, local copies, waits for them, and re-layouts, local(): jnp.broadcast_to(own, (groups, KVH, per_head, SHARE, HD))  0.73 us
    pallas_call x1, Pallas kernels, local(): pl.pallas_call(suffix_kernel, out_shape=[jax.ShapeDtypeStruct((H, HD), jn...  0.7 us
  transfers between devices with their start and end apart: 2, of which 1 were waited for; matrix products, arithmetic and copies ran while one was open for 2% of the time, Pallas kernels for 2%

profile of v2, /device:TPU:0, one launch (start us, length us, event | category | flops | bytes accessed | tf_op | source)
XLA Modules:
  0.0 31.5 jit_solution(13498226037934863616)
XLA Ops:
  0.0 0.5 %collective-permute-start = (bf16[2,1,1024,128]{3,2,0,1:T(8,128)(2,1)}, bf16[2,1,1024,128]{3,2,0,1:T(8,128)(2,1)S(1)}, u32[]{:S(2)}, u32[]{:S(2)}) collective-permute-start(bf16[2,1,1024,128]{3,2,0,1:T(8,128)(2,1)} %bitcast.10), channel_id=1, source_target_pairs={{0,1},{1,0},{2,3},{3,2},{4,5},{5,4},{6,7},{7,6},{8,9},{9,8},{10,11... | collective-permute-start | bytes 1572872 | tf_op jit(solution)/shard_map/ppermute | solution.py:136
  0.5 0.7 %broadcast_in_dim.8 = bf16[2,4,2,16,128]{4,3,2,1,0:T(8,128)(2,1)S(1)} broadcast(bf16[4,16,128]{2,1,0:T(8,128)(2,1)} %bitcast.8), dimensions={1,3,4} | broadcast | bytes 81920 | tf_op jit(solution)/shard_map/broadcast_in_dim | solution.py:138
  1.2 15.2 %all_to_all.10.q_ref = bf16[16,16,128]{2,1,0:T(8,128)(2,1)S(1)} all-to-all(bf16[16,16,128]{2,1,0:T(8,128)(2,1)S(1)} %bitcast.13), channel_id=1, replica_groups={{0,2,4,6,8,10,12,14,16,18,20,22,24,26,28,30},{1,3,5,7,9,11,13,15,17,19,..., dimensions={0} | all-to-all | bytes 131072 | tf_op jit(solution)/shard_map/all_to_all | solution.py:142
  16.4 0.0 collective-permute-done
  16.4 0.0 copy-start.3
  16.4 1.0 %copy-done.3 = bf16[2,1,1024,128]{3,2,1,0:T(8,128)(2,1)S(1)} copy-done((bf16[2,1,1024,128]{3,2,1,0:T(8,128)(2,1)S(1)}, bf16[2,1,1024,128]{3,2,1,0:T(8,128)(2,1)}, u32[]{:S(2)}) %copy-start.3) | copy-done | bytes 524312
  17.4 0.0 copy-start
  17.4 1.8 %prefix.1 = bf16[16,32,128]{2,1,0:T(8,128)(2,1)} custom-call(bf16[16,16,128]{2,1,0:T(8,128)(2,1)S(1)} %all_to_all.10.q_ref, bf16[2,1024,128]{2,1,0:T(8,128)(2,1)S(1)} %bitcast.11, bf16[2,1024,128]{2,1,0:T(8,128)(2,1)S(1)} %bitcast.12), custom_call_target="tpu_custom_call" | custom-call | flops 402653184 | bytes 1600000 | tf_op jit(solution)/shard_map/prefix/pallas_call | solution.py:154
  19.3 0.0 copy-start.1
  19.3 3.6 %all-to-all-start.1 = ((bf16[16,32,128]{2,1,0:T(8,128)(2,1)}), bf16[16,32,128]{2,1,0:T(8,128)(2,1)S(1)}, u32[]{:S(2)}, u32[]{:S(2)}) async-start(bf16[16,32,128]{2,1,0:T(8,128)(2,1)} %prefix.1), calls=%async_computation.1 | async-start | bytes 262144 | tf_op jit(solution)/shard_map/all_to_all | solution.py:168
  23.6 0.0 copy-start.2
  23.6 0.0 copy-done
  23.6 0.0 copy-done.1
  23.6 0.7 %copy-done.2 = bf16[1,2,4,128]{3,2,1,0:T(4,128)(2,1)S(1)} copy-done((bf16[1,2,4,128]{3,2,1,0:T(4,128)(2,1)S(1)}, bf16[1,2,4,128]{3,2,1,0:T(4,128)(2,1)}, u32[]{:S(2)}) %copy-start.2) | copy-done | bytes 2072
  24.2 0.7 %suffix.1 = (f32[64,128]{1,0:T(8,128)S(1)}, f32[64,128]{1,0:T(8,128)S(1)}) custom-call(s32[1]{0:T(128)S(6)} %copy.7.len_ref, bf16[1,64,128]{2,1,0:T(8,128)(2,1)S(1)} %copy-done.1, bf16[1,2048,128]{2,1,0:T(8,128)(2,1)S(1)} %bitcast.7, bf16[1,8,128]{2,1,0:T(8,128)(2,1)S(1)} %bitcast.9), custom_call_target="tpu_custom_call" | custom-call | flops 70000000 | bytes 600000 | tf_op jit(solution)/shard_map/suffix/pallas_call | solution.py:144
  24.9 5.7 %all-to-all-done.1.part_ref = bf16[16,32,128]{2,1,0:T(8,128)(2,1)S(1)} async-done(((bf16[16,32,128]{2,1,0:T(8,128)(2,1)}), bf16[16,32,128]{2,1,0:T(8,128)(2,1)S(1)}, u32[]{:S(2)}, u32[]{:S(2)}) %all-to-all-start.1) | async-done | bytes 131104 | tf_op jit(solution)/shard_map/all_to_all | solution.py:168
  30.7 0.8 %merge.1 = bf16[1,64,128]{2,1,0:T(8,128)(2,1)} custom-call(bf16[16,32,128]{2,1,0:T(8,128)(2,1)S(1)} %all-to-all-done.1.part_ref, f32[64,128]{1,0:T(8,128)S(1)} %get-tuple-element.7.suffix_ref, f32[64,128]{1,0:T(8,128)S(1)} %get-tuple-element.8.lse_ref), custom_call_target="tpu_custom_call" | custom-call | tf_op jit(solution)/shard_map/merge/pallas_call | solution.py:169
Async XLA Ops:
  0.0 16.4 %collective-permute-start = (bf16[2,1,1024,128]{3,2,0,1:T(8,128)(2,1)}, bf16[2,1,1024,128]{3,2,0,1:T(8,128)(2,1)S(1)}, u32[]{:S(2)}, u32[]{:S(2)}) collective-permute-start(bf16[2,1,1024,128]{3,2,0,1:T(8,128)(2,1)} %bitcast.10), channel_id=1, source_target_pairs={{0,1},{1,0},{2,3},{3,2},{4,5},{5,4},{6,7},{7,6},{8,9},{9,8},{10,11... | collective-permute-start | bytes 1572872 | tf_op jit(solution)/shard_map/ppermute | solution.py:136
  16.4 1.0 %copy-start.3 = (bf16[2,1,1024,128]{3,2,1,0:T(8,128)(2,1)S(1)}, bf16[2,1,1024,128]{3,2,1,0:T(8,128)(2,1)}, u32[]{:S(2)}) copy-start(bf16[2,1,1024,128]{3,2,1,0:T(8,128)(2,1)} %param.6) | copy-start | bytes 1572868
  17.4 6.1 %copy-start = (bf16[1,256,2,4,128]{4,3,2,1,0:T(4,128)(2,1)S(1)}, bf16[1,256,2,4,128]{4,3,2,1,0:T(4,128)(2,1)}, u32[]{:S(2)}) copy-start(bf16[1,256,2,4,128]{4,3,2,1,0:T(4,128)(2,1)} %param.7) | copy-start | bytes 1572868
  19.3 4.3 %copy-start.1 = (bf16[1,64,128]{2,1,0:T(8,128)(2,1)S(1)}, bf16[1,64,128]{2,1,0:T(8,128)(2,1)}, u32[]{:S(2)}) copy-start(bf16[1,64,128]{2,1,0:T(8,128)(2,1)} %q_ref.1) | copy-start | bytes 49156
  19.3 11.4 %all-to-all-start.1 = ((bf16[16,32,128]{2,1,0:T(8,128)(2,1)}), bf16[16,32,128]{2,1,0:T(8,128)(2,1)S(1)}, u32[]{:S(2)}, u32[]{:S(2)}) async-start(bf16[16,32,128]{2,1,0:T(8,128)(2,1)} %prefix.1), calls=%async_computation.1 | async-start | bytes 262144 | tf_op jit(solution)/shard_map/all_to_all | solution.py:168
  23.6 0.7 %copy-start.2 = (bf16[1,2,4,128]{3,2,1,0:T(4,128)(2,1)S(1)}, bf16[1,2,4,128]{3,2,1,0:T(4,128)(2,1)}, u32[]{:S(2)}) copy-start(bf16[1,2,4,128]{3,2,1,0:T(4,128)(2,1)} %param.8) | copy-start | bytes 6148

commit v3 on v2

v3 whole, which is shorter than its diff:
```python
import functools
import math

import jax
import jax.numpy as jnp
from jax import lax
from jax.experimental import pallas as pl
from jax.experimental.pallas import tpu as pltpu
from jax.sharding import PartitionSpec as P

H = 64
KVH = 4
HD = 128
SHARE = H // KVH
SCALE2 = HD ** (-0.5) * math.log2(math.e)
VMEM = pl.BlockSpec(memory_space=pltpu.VMEM)
ROWS = 128
CORES = 2
HALF = SHARE // CORES
LIMIT = 24 * 1024 * 1024
NT = (((1,), (1,)), ((), ()))


def dot_nt(a, b):
    return lax.dot_general(a, b, NT, preferred_element_type=jnp.float32)


def dot(a, b):
    return jnp.dot(a, b, preferred_element_type=jnp.float32)


def log2(x):
    return jnp.log(x) * math.log2(math.e)


def split3(x):
    hi = x.astype(jnp.bfloat16).astype(jnp.float32)
    rest = x - hi
    mid = rest.astype(jnp.bfloat16).astype(jnp.float32)
    low = (rest - mid).astype(jnp.bfloat16).astype(jnp.float32)
    return hi, mid, low


def prefix_kernel(q_ref, kv_ref, other_ref, out_ref):
    per_step = ROWS // HALF
    lane = lax.broadcasted_iota(jnp.int32, (ROWS, HD), 1)

    def extended(ref):
        return jnp.concatenate([ref[1], jnp.ones_like(ref[1])], axis=1)

    def step(at):
        rows = q_ref[pl.ds(at * HALF, ROWS)]
        scores = dot_nt(rows, kv_ref[0])
        other_scores = dot_nt(rows, other_ref[0])
        best = jnp.max(jnp.maximum(scores, other_scores), axis=1, keepdims=True)
        weight = jnp.exp2((scores - best) * SCALE2).astype(jnp.bfloat16)
        other_weight = jnp.exp2((other_scores - best) * SCALE2).astype(jnp.bfloat16)
        both = dot(weight, extended(kv_ref)) + dot(other_weight, extended(other_ref))
        total = both[:, HD:]
        result = both[:, :HD] / total
        hi, mid, low = split3(best * SCALE2 + log2(total))
        stats = jnp.where(lane == 0, hi, jnp.where(lane == 1, mid, jnp.where(lane == 2, low, 0.0)))
        shape = (per_step, HALF, HD)
        message = jnp.concatenate([result.reshape(shape), stats.reshape(shape)], axis=1)
        out_ref[pl.ds(at * 2 * HALF, 2 * ROWS)] = message.reshape(2 * ROWS, HD).astype(jnp.bfloat16)

    trips = q_ref.shape[0] // ROWS
    if trips <= 4:
        for trip in range(trips):
            step(trip * per_step)
    else:

        def body(trip, unused):
            step(pl.multiple_of(trip * per_step, per_step))
            return unused

        lax.fori_loop(0, trips, body, 0)


def owned(shape, limit):
    at = lax.broadcasted_iota(jnp.int32, shape, 1)
    head = lax.broadcasted_iota(jnp.int32, shape, 0) // SHARE
    return (at % (2 * KVH) == head) & (at < limit * (2 * KVH))


def suffix_kernel(len_ref, q_ref, cache_ref, new_ref, out_ref, best_ref, total_ref):
    q = q_ref[0]
    cache = cache_ref[0]
    raw = dot_nt(q, cache)
    scores = jnp.where(owned(raw.shape, len_ref[0]), raw, -jnp.inf)
    new_raw = dot_nt(q, new_ref[0])
    new_scores = jnp.where(owned(new_raw.shape, 1), new_raw, -jnp.inf)
    best = jnp.maximum(jnp.max(scores, axis=1, keepdims=True), jnp.max(new_scores, axis=1, keepdims=True))
    weight = jnp.exp2((scores - best) * SCALE2).astype(jnp.bfloat16).astype(jnp.float32)
    moved = pltpu.roll(weight, KVH, 1).astype(jnp.bfloat16)
    out_ref[...] = dot(moved, cache)
    best_ref[...] = jnp.broadcast_to(best, best_ref.shape)
    total_ref[...] = jnp.broadcast_to(jnp.sum(weight, axis=1, keepdims=True), total_ref.shape)


def fresh_kernel(q_ref, new_ref, num_ref, best_ref, total_ref, out_ref, lse_ref):
    new = new_ref[0]
    raw = dot_nt(q_ref[0], new)
    best = best_ref[...]
    scores = jnp.where(owned(raw.shape, 1), raw, -jnp.inf)
    weight = jnp.exp2((scores - best[:, : raw.shape[1]]) * SCALE2).astype(jnp.bfloat16).astype(jnp.float32)
    moved = jnp.concatenate([weight[:, KVH:], weight[:, :KVH]], axis=1).astype(jnp.bfloat16)
    total = total_ref[...] + jnp.sum(weight, axis=1, keepdims=True)
    out_ref[...] = (num_ref[...] + dot(moved, new)) / total
    lse_ref[...] = best * SCALE2 + log2(total)


def fan_kernel(served, q_ref, out_ref):
    q = q_ref[0].astype(jnp.float32)
    out_ref[...] = jnp.concatenate([q[its * HALF : (its + 1) * HALF] for its in served], axis=0).astype(jnp.bfloat16)


def merge_kernel(served, part_ref, suffix_ref, lse_ref, out_ref):
    sums = dot(part_ref[...], jnp.ones((HD, HD), jnp.bfloat16)).reshape(len(served), 2 * HALF, HD)
    rows = part_ref[...].astype(jnp.float32).reshape(len(served), 2 * HALF, HD)
    blocks = []
    for block in range(H // HALF):
        span = slice(block * HALF, (block + 1) * HALF)
        own = [slot for slot, its in enumerate(served) if its == block]
        own_lse = lse_ref[span]
        best = own_lse
        for slot in own:
            best = jnp.maximum(best, sums[slot, HALF:])
        total = jnp.exp2(own_lse - best)
        numerator = total * suffix_ref[span]
        for slot in own:
            factor = jnp.exp2(sums[slot, HALF:] - best)
            total = total + factor
            numerator = numerator + factor * rows[slot, :HALF]
        blocks.append(numerator / total)
    out_ref[0] = jnp.concatenate(blocks, axis=0).astype(jnp.bfloat16)


def call(kernel, name, outs, operands, specs=None, **cost):
    return pl.pallas_call(
        kernel,
        out_shape=outs,
        in_specs=specs or [VMEM] * len(operands),
        out_specs=jax.tree.map(lambda _: VMEM, outs),
        name=name,
        compiler_params=pltpu.CompilerParams(vmem_limit_bytes=LIMIT),
        cost_estimate=pl.CostEstimate(**cost) if cost else None,
    )(*operands)


def local(queries, prefix_kv, suffix_kv, new_kv, suffix_len):
    groups = lax.axis_size("grp")
    members = lax.axis_size("blk")
    per_head = members // KVH
    devices = groups * members
    span = prefix_kv.shape[2]
    order = list(reversed(range(devices)))
    served = [device % members // per_head * CORES + device % CORES for device in order]

    def one(rows, dtype=jnp.float32):
        return jax.ShapeDtypeStruct((rows, HD), dtype)

    def exchange(array):
        return lax.all_to_all(array, ("grp", "blk"), 0, 0, axis_index_groups=[order], tiled=True)

    other = lax.ppermute(prefix_kv, "blk", [(i, i ^ 1) for i in range(members)])
    outgoing = call(functools.partial(fan_kernel, served), "fan", one(devices * HALF, jnp.bfloat16), (queries,))
    arrived = exchange(outgoing.reshape(devices, HALF, HD)).reshape(devices * HALF, HD)

    new = new_kv.reshape(1, -1, HD)
    suffix = call(
        suffix_kernel,
        "suffix",
        [one(H)] * 3,
        (suffix_len, queries, suffix_kv.reshape(1, -1, HD), new),
        [pl.BlockSpec(memory_space=pltpu.SMEM), VMEM, VMEM, VMEM],
        flops=70_000_000,
        bytes_accessed=600_000,
        transcendentals=140_000,
    )
    arrived, suffix = lax.optimization_barrier((arrived, suffix))
    partial = call(
        prefix_kernel,
        "prefix",
        one(devices * 2 * HALF, jnp.bfloat16),
        (arrived, prefix_kv.reshape(2, span, HD), other.reshape(2, span, HD)),
        flops=12 * devices * HALF * span * HD,
        bytes_accessed=1_600_000,
        transcendentals=2 * devices * HALF * span,
    )
    partial, suffix = lax.optimization_barrier((partial, suffix))
    returned = exchange(partial.reshape(devices, 2 * HALF, HD)).reshape(-1, HD)
    fresh = call(fresh_kernel, "fresh", [one(H)] * 2, (queries, new, *suffix), flops=1_000_000, bytes_accessed=200_000, transcendentals=10_000)
    return call(
        functools.partial(merge_kernel, served),
        "merge",
        jax.ShapeDtypeStruct((1, H, HD), jnp.bfloat16),
        (returned, *fresh),
    )


def solution(mesh):
    in_specs = (
        P(("grp", "blk"), None, None),
        P(None, "grp", "blk", None),
        P(("grp", "blk"), None, None, None, None),
        P(("grp", "blk"), None, None, None),
        P(("grp", "blk")),
    )
    out_specs = P(("grp", "blk"), None, None)
    return jax.shard_map(local, mesh=mesh, in_specs=in_specs, out_specs=out_specs, check_vma=False)
```

time: 31.9 us -> 29.7 us (0.931)
  blocking collectives: 15.2 us -> 0 us
  waiting for transfers between devices: 5.73 us -> 11.9 us
  starting transfers between devices: 4.09 us -> 9.98 us
  Pallas kernels: 3.31 us -> 4.29 us
    all_to_all x1 -> x0, blocking collectives: 15.2 us -> none  [local(): arrived = exchange(outgoing)]
    all_to_all x1 -> x2, waiting for transfers between devices: 5.73 us -> 11.9 us  [exchange(): lax.all_to_all(array, ('grp', 'blk'), 0, 0, axis_index_groups=[order], ti...]
    all_to_all x1 -> x2, starting transfers between devices: 3.64 us -> 9.53 us  [exchange(): lax.all_to_all(array, ('grp', 'blk'), 0, 0, axis_index_groups=[order], ti...]
    pallas_call x3 -> x5, Pallas kernels: 3.31 us -> 4.29 us  [call(): pl.pallas_call(kernel, out_shape=outs, in_specs=specs or [VMEM] * len(ope...]
    broadcast_in_dim x1 -> x0, local copies, waits for them, and re-layouts: 0.73 us -> none  [local(): jnp.broadcast_to(own, (groups, KVH, per_head, SHARE, HD))]
    unnamed x8 -> x10, local copies, waits for them, and re-layouts: 1.71 us -> 2.43 us
  transfers between devices with their start and end apart: 2 -> 3, of which waited for: 1 -> 2; matrix products, arithmetic and copies ran while one was open for 2% -> 0% of each run, Pallas kernels for 2% -> 6%
where the time goes in v3:
time: 29.7 us; the launch traced here: 29.3 us
  waiting for transfers between devices  11.9 us (40%)
  starting transfers between devices  9.98 us (34%)
  Pallas kernels  4.29 us (14%)
  local copies, waits for them, and re-layouts  2.43 us (8%)
  between operations  0.69 us (2%)
    all_to_all x2, waiting for transfers between devices, exchange(): lax.all_to_all(array, ('grp', 'blk'), 0, 0, axis_index_groups=[order], ti...  11.9 us
    all_to_all x2, starting transfers between devices, exchange(): lax.all_to_all(array, ('grp', 'blk'), 0, 0, axis_index_groups=[order], ti...  9.53 us
    pallas_call x5, Pallas kernels, call(): pl.pallas_call(kernel, out_shape=outs, in_specs=specs or [VMEM] * len(ope...  4.29 us
    unnamed x10, local copies, waits for them, and re-layouts  2.43 us
  transfers between devices with their start and end apart: 3, of which 2 were waited for; matrix products, arithmetic and copies ran while one was open for 0% of the time, Pallas kernels for 6%

profile of v3, /device:TPU:0, one launch (start us, length us, event | category | flops | bytes accessed | tf_op | source)
XLA Modules:
  0.0 29.3 jit_solution(14252886482569152005)
XLA Ops:
  0.0 0.5 %collective-permute-start = (bf16[2,1,1024,128]{3,2,0,1:T(8,128)(2,1)}, bf16[2,1,1024,128]{3,2,0,1:T(8,128)(2,1)S(1)}, u32[]{:S(2)}, u32[]{:S(2)}) collective-permute-start(bf16[2,1,1024,128]{3,2,0,1:T(8,128)(2,1)} %bitcast.14), channel_id=1, source_target_pairs={{0,1},{1,0},{2,3},{3,2},{4,5},{5,4},{6,7},{7,6},{8,9},{9,8},{10,11... | collective-permute-start | bytes 1572872 | tf_op jit(solution)/shard_map/ppermute | solution.py:166
  0.5 0.0 copy-start.1
  0.5 0.7 %copy-done.1 = bf16[1,64,128]{2,1,0:T(8,128)(2,1)S(1)} copy-done((bf16[1,64,128]{2,1,0:T(8,128)(2,1)S(1)}, bf16[1,64,128]{2,1,0:T(8,128)(2,1)}, u32[]{:S(2)}) %copy-start.1) | copy-done | bytes 16408
  1.2 0.6 %fan.1 = bf16[256,128]{1,0:T(8,128)(2,1)} custom-call(bf16[1,64,128]{2,1,0:T(8,128)(2,1)S(1)} %copy-done.1), custom_call_target="tpu_custom_call" | custom-call | tf_op jit(solution)/shard_map/fan/pallas_call | solution.py:140
  1.8 0.0 copy-start.2
  1.8 7.0 %all-to-all-start = ((bf16[32,8,128]{2,1,0:T(8,128)(2,1)}), bf16[32,8,128]{2,1,0:T(8,128)(2,1)S(1)}, u32[]{:S(2)}, u32[]{:S(2)}) async-start(bf16[32,8,128]{2,1,0:T(8,128)(2,1)} %bitcast), calls=%async_computation | async-start | bytes 131072 | tf_op jit(solution)/shard_map/all_to_all | solution.py:164
  9.4 0.0 copy-start.3
  9.4 0.0 copy-done.2
  9.4 0.7 %copy-done.3 = bf16[1,2,4,128]{3,2,1,0:T(4,128)(2,1)S(1)} copy-done((bf16[1,2,4,128]{3,2,1,0:T(4,128)(2,1)S(1)}, bf16[1,2,4,128]{3,2,1,0:T(4,128)(2,1)}, u32[]{:S(2)}) %copy-start.3) | copy-done | bytes 2072
  10.1 0.0 copy-start
  10.1 1.0 %copy-done = bf16[1,256,2,4,128]{4,3,2,1,0:T(4,128)(2,1)S(1)} copy-done((bf16[1,256,2,4,128]{4,3,2,1,0:T(4,128)(2,1)S(1)}, bf16[1,256,2,4,128]{4,3,2,1,0:T(4,128)(2,1)}, u32[]{:S(2)}) %copy-start) | copy-done | bytes 524312
  11.1 0.0 copy-start.4
  11.1 0.7 %suffix.1 = (f32[64,128]{1,0:T(8,128)S(1)}, f32[64,128]{1,0:T(8,128)S(1)}, f32[64,128]{1,0:T(8,128)S(1)}) custom-call(s32[1]{0:T(128)S(6)} %copy.7.len_ref, bf16[1,64,128]{2,1,0:T(8,128)(2,1)S(1)} %copy-done.2, bf16[1,2048,128]{2,1,0:T(8,128)(2,1)S(1)} %bitcast.9, bf16[1,8,128]{2,1,0:T(8,128)(2,1)S(1)} %bitcast.12), custom_call_target="tpu_custom_call" | custom-call | flops 70000000 | bytes 600000 | tf_op jit(solution)/shard_map/suffix/pallas_call | solution.py:140
  11.8 4.3 %all-to-all-done = bf16[32,8,128]{2,1,0:T(8,128)(2,1)S(1)} async-done(((bf16[32,8,128]{2,1,0:T(8,128)(2,1)}), bf16[32,8,128]{2,1,0:T(8,128)(2,1)S(1)}, u32[]{:S(2)}, u32[]{:S(2)}) %all-to-all-start) | async-done | bytes 65568 | tf_op jit(solution)/shard_map/all_to_all | solution.py:164
  16.1 0.0 collective-permute-done
  16.1 0.0 copy-done.4
  16.1 1.8 %prefix.1 = bf16[512,128]{1,0:T(8,128)(2,1)} custom-call(bf16[256,128]{1,0:T(8,128)(2,1)S(1)} %bitcast.11, bf16[2,1024,128]{2,1,0:T(8,128)(2,1)S(1)} %bitcast.15, bf16[2,1024,128]{2,1,0:T(8,128)(2,1)S(1)} %bitcast.16), custom_call_target="tpu_custom_call" | custom-call | flops 402653184 | bytes 1600000 | tf_op jit(solution)/shard_map/prefix/pallas_call | solution.py:140
  18.0 2.6 %all-to-all-start.1 = ((bf16[32,16,128]{2,1,0:T(8,128)(2,1)}), bf16[32,16,128]{2,1,0:T(8,128)(2,1)S(1)}, u32[]{:S(2)}, u32[]{:S(2)}) async-start(bf16[32,16,128]{2,1,0:T(8,128)(2,1)} %bitcast.7), calls=%async_computation.1 | async-start | bytes 262144 | tf_op jit(solution)/shard_map/all_to_all | solution.py:164
  20.5 0.3 %fresh.1 = (f32[64,128]{1,0:T(8,128)S(1)}, f32[64,128]{1,0:T(8,128)S(1)}) custom-call(bf16[1,64,128]{2,1,0:T(8,128)(2,1)S(1)} %copy-done.2, bf16[1,8,128]{2,1,0:T(8,128)(2,1)S(1)} %bitcast.13, f32[64,128]{1,0:T(8,128)S(1)} %get-tuple-element.26.num_ref, f32[64,128]{1,0:T(8,128)S(1)} %get-tuple-element.27.best_ref, f32[64,128]{1,0:T(8,128)S(1)} %get-tuple-element.28.total_ref), custom_call_target="tpu_custom_call" | custom-call | flops 1000000 | bytes 200000 | tf_op jit(solution)/shard_map/fresh/pallas_call | solution.py:140
  20.9 7.7 %all-to-all-done.1 = bf16[32,16,128]{2,1,0:T(8,128)(2,1)S(1)} async-done(((bf16[32,16,128]{2,1,0:T(8,128)(2,1)}), bf16[32,16,128]{2,1,0:T(8,128)(2,1)S(1)}, u32[]{:S(2)}, u32[]{:S(2)}) %all-to-all-start.1) | async-done | bytes 131104 | tf_op jit(solution)/shard_map/all_to_all | solution.py:164
  28.5 0.8 %merge.1 = bf16[1,64,128]{2,1,0:T(8,128)(2,1)} custom-call(bf16[512,128]{1,0:T(8,128)(2,1)S(1)} %bitcast.10, f32[64,128]{1,0:T(8,128)S(1)} %get-tuple-element.29.suffix_ref, f32[64,128]{1,0:T(8,128)S(1)} %get-tuple-element.30.lse_ref), custom_call_target="tpu_custom_call" | custom-call | tf_op jit(solution)/shard_map/merge/pallas_call | solution.py:140
Async XLA Ops:
  0.0 16.1 %collective-permute-start = (bf16[2,1,1024,128]{3,2,0,1:T(8,128)(2,1)}, bf16[2,1,1024,128]{3,2,0,1:T(8,128)(2,1)S(1)}, u32[]{:S(2)}, u32[]{:S(2)}) collective-permute-start(bf16[2,1,1024,128]{3,2,0,1:T(8,128)(2,1)} %bitcast.14), channel_id=1, source_target_pairs={{0,1},{1,0},{2,3},{3,2},{4,5},{5,4},{6,7},{7,6},{8,9},{9,8},{10,11... | collective-permute-start | bytes 1572872 | tf_op jit(solution)/shard_map/ppermute | solution.py:166
  0.5 0.7 %copy-start.1 = (bf16[1,64,128]{2,1,0:T(8,128)(2,1)S(1)}, bf16[1,64,128]{2,1,0:T(8,128)(2,1)}, u32[]{:S(2)}) copy-start(bf16[1,64,128]{2,1,0:T(8,128)(2,1)} %q_ref.5) | copy-start | bytes 49156
  1.8 7.6 %copy-start.2 = (bf16[1,64,128]{2,1,0:T(8,128)(2,1)S(1)}, bf16[1,64,128]{2,1,0:T(8,128)(2,1)}, u32[]{:S(2)}) copy-start(bf16[1,64,128]{2,1,0:T(8,128)(2,1)} %q_ref.5) | copy-start | bytes 49156
  1.8 14.3 %all-to-all-start = ((bf16[32,8,128]{2,1,0:T(8,128)(2,1)}), bf16[32,8,128]{2,1,0:T(8,128)(2,1)S(1)}, u32[]{:S(2)}, u32[]{:S(2)}) async-start(bf16[32,8,128]{2,1,0:T(8,128)(2,1)} %bitcast), calls=%async_computation | async-start | bytes 131072 | tf_op jit(solution)/shard_map/all_to_all | solution.py:164
  9.4 0.7 %copy-start.3 = (bf16[1,2,4,128]{3,2,1,0:T(4,128)(2,1)S(1)}, bf16[1,2,4,128]{3,2,1,0:T(4,128)(2,1)}, u32[]{:S(2)}) copy-start(bf16[1,2,4,128]{3,2,1,0:T(4,128)(2,1)} %param.8) | copy-start | bytes 6148
  10.1 1.0 %copy-start = (bf16[1,256,2,4,128]{4,3,2,1,0:T(4,128)(2,1)S(1)}, bf16[1,256,2,4,128]{4,3,2,1,0:T(4,128)(2,1)}, u32[]{:S(2)}) copy-start(bf16[1,256,2,4,128]{4,3,2,1,0:T(4,128)(2,1)} %param.7) | copy-start | bytes 1572868
  11.1 5.0 %copy-start.4 = (bf16[2,1,1024,128]{3,2,1,0:T(8,128)(2,1)S(1)}, bf16[2,1,1024,128]{3,2,1,0:T(8,128)(2,1)}, u32[]{:S(2)}) copy-start(bf16[2,1,1024,128]{3,2,1,0:T(8,128)(2,1)} %param.6) | copy-start | bytes 1572868
  18.0 10.6 %all-to-all-start.1 = ((bf16[32,16,128]{2,1,0:T(8,128)(2,1)}), bf16[32,16,128]{2,1,0:T(8,128)(2,1)S(1)}, u32[]{:S(2)}, u32[]{:S(2)}) async-start(bf16[32,16,128]{2,1,0:T(8,128)(2,1)} %bitcast.7), calls=%async_computation.1 | async-start | bytes 262144 | tf_op jit(solution)/shard_map/all_to_all | solution.py:164

commit v4 on v3

--- a/solution.py
+++ b/solution.py
@@ -83,36 +83,34 @@
     return (at % (2 * KVH) == head) & (at < limit * (2 * KVH))
 
 
-def suffix_kernel(len_ref, q_ref, cache_ref, new_ref, out_ref, best_ref, total_ref):
+def suffix_kernel(len_ref, q_ref, cache_ref, new_ref, out_ref, lse_ref):
     q = q_ref[0]
     cache = cache_ref[0]
+    new = new_ref[0]
     raw = dot_nt(q, cache)
     scores = jnp.where(owned(raw.shape, len_ref[0]), raw, -jnp.inf)
-    new_raw = dot_nt(q, new_ref[0])
+    new_raw = dot_nt(q, new)
     new_scores = jnp.where(owned(new_raw.shape, 1), new_raw, -jnp.inf)
     best = jnp.maximum(jnp.max(scores, axis=1, keepdims=True), jnp.max(new_scores, axis=1, keepdims=True))
     weight = jnp.exp2((scores - best) * SCALE2).astype(jnp.bfloat16).astype(jnp.float32)
+    new_weight = jnp.exp2((new_scores - best) * SCALE2).astype(jnp.bfloat16).astype(jnp.float32)
+    total = jnp.sum(weight, axis=1, keepdims=True) + jnp.sum(new_weight, axis=1, keepdims=True)
     moved = pltpu.roll(weight, KVH, 1).astype(jnp.bfloat16)
-    out_ref[...] = dot(moved, cache)
-    best_ref[...] = jnp.broadcast_to(best, best_ref.shape)
-    total_ref[...] = jnp.broadcast_to(jnp.sum(weight, axis=1, keepdims=True), total_ref.shape)
-
-
-def fresh_kernel(q_ref, new_ref, num_ref, best_ref, total_ref, out_ref, lse_ref):
-    new = new_ref[0]
-    raw = dot_nt(q_ref[0], new)
-    best = best_ref[...]
-    scores = jnp.where(owned(raw.shape, 1), raw, -jnp.inf)
-    weight = jnp.exp2((scores - best[:, : raw.shape[1]]) * SCALE2).astype(jnp.bfloat16).astype(jnp.float32)
-    moved = jnp.concatenate([weight[:, KVH:], weight[:, :KVH]], axis=1).astype(jnp.bfloat16)
-    total = total_ref[...] + jnp.sum(weight, axis=1, keepdims=True)
-    out_ref[...] = (num_ref[...] + dot(moved, new)) / total
-    lse_ref[...] = best * SCALE2 + log2(total)
-
-
-def fan_kernel(served, q_ref, out_ref):
-    q = q_ref[0].astype(jnp.float32)
-    out_ref[...] = jnp.concatenate([q[its * HALF : (its + 1) * HALF] for its in served], axis=0).astype(jnp.bfloat16)
+    new_moved = jnp.concatenate([new_weight[:, KVH:], new_weight[:, :KVH]], axis=1).astype(jnp.bfloat16)
+    out_ref[...] = (dot(moved, cache) + dot(new_moved, new)) / total
+    lse_ref[...] = jnp.broadcast_to(best * SCALE2 + log2(total), lse_ref.shape)
+
+
+def fan_kernel(q_ref, out_ref, sems):
+    copies = [
+        pltpu.make_async_copy(q_ref, out_ref.at[group, :, chip], sems.at[group, chip])
+        for group in range(out_ref.shape[0])
+        for chip in range(out_ref.shape[2])
+    ]
+    for copy in copies:
+        copy.start()
+    for copy in copies:
+        copy.wait()
 
 
 def merge_kernel(served, part_ref, suffix_ref, lse_ref, out_ref):
@@ -154,24 +152,31 @@
     per_head = members // KVH
     devices = groups * members
     span = prefix_kv.shape[2]
-    order = list(reversed(range(devices)))
-    served = [device % members // per_head * CORES + device % CORES for device in order]
+    chips = per_head // CORES
+    served = [device % members // per_head * CORES + device % CORES for device in range(devices)]
 
     def one(rows, dtype=jnp.float32):
         return jax.ShapeDtypeStruct((rows, HD), dtype)
 
     def exchange(array):
-        return lax.all_to_all(array, ("grp", "blk"), 0, 0, axis_index_groups=[order], tiled=True)
+        return lax.all_to_all(array, ("grp", "blk"), 0, 0, tiled=True)
 
     other = lax.ppermute(prefix_kv, "blk", [(i, i ^ 1) for i in range(members)])
-    outgoing = call(functools.partial(fan_kernel, served), "fan", one(devices * HALF, jnp.bfloat16), (queries,))
+    outgoing = pl.pallas_call(
+        fan_kernel,
+        out_shape=jax.ShapeDtypeStruct((groups, KVH, chips, SHARE, HD), jnp.bfloat16),
+        in_specs=[pl.BlockSpec(memory_space=pl.ANY)],
+        out_specs=pl.BlockSpec(memory_space=pl.ANY),
+        scratch_shapes=[pltpu.SemaphoreType.DMA((groups, chips))],
+        name="fan",
+    )(queries.reshape(KVH, SHARE, HD))
     arrived = exchange(outgoing.reshape(devices, HALF, HD)).reshape(devices * HALF, HD)
 
     new = new_kv.reshape(1, -1, HD)
     suffix = call(
         suffix_kernel,
         "suffix",
-        [one(H)] * 3,
+        [one(H)] * 2,
         (suffix_len, queries, suffix_kv.reshape(1, -1, HD), new),
         [pl.BlockSpec(memory_space=pltpu.SMEM), VMEM, VMEM, VMEM],
         flops=70_000_000,
@@ -188,14 +193,12 @@
         bytes_accessed=1_600_000,
         transcendentals=2 * devices * HALF * span,
     )
-    partial, suffix = lax.optimization_barrier((partial, suffix))
     returned = exchange(partial.reshape(devices, 2 * HALF, HD)).reshape(-1, HD)
-    fresh = call(fresh_kernel, "fresh", [one(H)] * 2, (queries, new, *suffix), flops=1_000_000, bytes_accessed=200_000, transcendentals=10_000)
     return call(
         functools.partial(merge_kernel, served),
         "merge",
         jax.ShapeDtypeStruct((1, H, HD), jnp.bfloat16),
-        (returned, *fresh),
+        (returned, *suffix),
     )
 
 

time: 29.7 us -> 30.2 us (1.017)
  blocking collectives: 0 us -> 9.93 us
  waiting for transfers between devices: 11.9 us -> 4.33 us
  starting transfers between devices: 9.98 us -> 7.42 us
  Pallas kernels: 4.29 us -> 5.79 us
  local copies, waits for them, and re-layouts: 2.43 us -> 1.72 us
    all_to_all x0 -> x1, blocking collectives: none -> 9.93 us  [exchange(): return lax.all_to_all(array, ('grp', 'blk'), 0, 0, tiled=True)]
    all_to_all x2 -> x1, waiting for transfers between devices: 11.9 us -> 4.33 us  [exchange(): return lax.all_to_all(array, ('grp', 'blk'), 0, 0, tiled=True)]
    pallas_call x0 -> x1, Pallas kernels: none -> 3.12 us  [local(): pl.pallas_call(fan_kernel, out_shape=jax.ShapeDtypeStruct((groups, KVH, c...]
    all_to_all x2 -> x1, starting transfers between devices: 9.53 us -> 6.97 us  [exchange(): return lax.all_to_all(array, ('grp', 'blk'), 0, 0, tiled=True)]
    pallas_call x5 -> x3, Pallas kernels: 4.29 us -> 2.67 us  [call(): pl.pallas_call(kernel, out_shape=outs, in_specs=specs or [VMEM] * len(ope...]
    unnamed x10 -> x8, local copies, waits for them, and re-layouts: 2.43 us -> 1.72 us
  transfers between devices with their start and end apart: 3 -> 2, of which waited for: 2 -> 1; matrix products, arithmetic and copies ran while one was open for 0% -> 0% of each run, Pallas kernels for 6% -> 13%
where the time goes in v4:
time: 30.2 us; the launch traced here: 29.9 us
  blocking collectives  9.93 us (33%)
  starting transfers between devices  7.42 us (25%)
  Pallas kernels  5.79 us (19%)
  waiting for transfers between devices  4.33 us (14%)
  local copies, waits for them, and re-layouts  1.72 us (6%)
  between operations  0.71 us (2%)
    all_to_all x1, blocking collectives, exchange(): return lax.all_to_all(array, ('grp', 'blk'), 0, 0, tiled=True)  9.93 us
    all_to_all x1, starting transfers between devices, exchange(): return lax.all_to_all(array, ('grp', 'blk'), 0, 0, tiled=True)  6.97 us
    all_to_all x1, waiting for transfers between devices, exchange(): return lax.all_to_all(array, ('grp', 'blk'), 0, 0, tiled=True)  4.33 us
    pallas_call x1, Pallas kernels, local(): pl.pallas_call(fan_kernel, out_shape=jax.ShapeDtypeStruct((groups, KVH, c...  3.12 us
    pallas_call x3, Pallas kernels, call(): pl.pallas_call(kernel, out_shape=outs, in_specs=specs or [VMEM] * len(ope...  2.67 us
    unnamed x8, local copies, waits for them, and re-layouts  1.72 us
  transfers between devices with their start and end apart: 2, of which 1 were waited for; matrix products, arithmetic and copies ran while one was open for 0% of the time, Pallas kernels for 13%

profile of v4, /device:TPU:0, one launch (start us, length us, event | category | flops | bytes accessed | tf_op | source)
XLA Modules:
  0.0 29.9 jit_solution(5467271834655272643)
XLA Ops:
  0.0 0.5 %collective-permute-start = (bf16[2,1,1024,128]{3,2,0,1:T(8,128)(2,1)}, bf16[2,1,1024,128]{3,2,0,1:T(8,128)(2,1)S(1)}, u32[]{:S(2)}, u32[]{:S(2)}) collective-permute-start(bf16[2,1,1024,128]{3,2,0,1:T(8,128)(2,1)} %bitcast.16), channel_id=1, source_target_pairs={{0,1},{1,0},{2,3},{3,2},{4,5},{5,4},{6,7},{7,6},{8,9},{9,8},{10,11... | collective-permute-start | bytes 1572872 | tf_op jit(solution)/shard_map/ppermute | solution.py:164
  0.5 3.1 %fan.1 = bf16[2,4,2,16,128]{4,3,2,1,0:T(8,128)(2,1)} custom-call(bf16[4,16,128]{2,1,0:T(8,128)(2,1)} %bitcast.13), custom_call_target="tpu_custom_call" | custom-call | tf_op jit(solution)/shard_map/fan/pallas_call | solution.py:165
  3.6 0.0 copy-start.1
  3.6 7.0 %all-to-all-start = ((bf16[32,8,128]{2,1,0:T(8,128)(2,1)}), bf16[32,8,128]{2,1,0:T(8,128)(2,1)S(1)}, u32[]{:S(2)}, u32[]{:S(2)}) async-start(bf16[32,8,128]{2,1,0:T(8,128)(2,1)} %bitcast.19), calls=%async_computation | async-start | bytes 131072 | tf_op jit(solution)/shard_map/all_to_all | solution.py:162
  11.2 0.0 copy-start.2
  11.2 0.0 copy-done.1
  11.2 0.7 %copy-done.2 = bf16[1,2,4,128]{3,2,1,0:T(4,128)(2,1)S(1)} copy-done((bf16[1,2,4,128]{3,2,1,0:T(4,128)(2,1)S(1)}, bf16[1,2,4,128]{3,2,1,0:T(4,128)(2,1)}, u32[]{:S(2)}) %copy-start.2) | copy-done | bytes 2072
  11.9 0.0 copy-start
  11.9 1.0 %copy-done = bf16[1,256,2,4,128]{4,3,2,1,0:T(4,128)(2,1)S(1)} copy-done((bf16[1,256,2,4,128]{4,3,2,1,0:T(4,128)(2,1)S(1)}, bf16[1,256,2,4,128]{4,3,2,1,0:T(4,128)(2,1)}, u32[]{:S(2)}) %copy-start) | copy-done | bytes 524312
  12.9 0.0 copy-start.3
  12.9 0.7 %suffix.1 = (f32[64,128]{1,0:T(8,128)S(1)}, f32[64,128]{1,0:T(8,128)S(1)}) custom-call(s32[1]{0:T(128)S(6)} %copy.7.len_ref, bf16[1,64,128]{2,1,0:T(8,128)(2,1)S(1)} %copy-done.1, bf16[1,2048,128]{2,1,0:T(8,128)(2,1)S(1)} %bitcast.10, bf16[1,8,128]{2,1,0:T(8,128)(2,1)S(1)} %bitcast.15), custom_call_target="tpu_custom_call" | custom-call | flops 70000000 | bytes 600000 | tf_op jit(solution)/shard_map/suffix/pallas_call | solution.py:138
  13.6 4.3 %all-to-all-done = bf16[32,8,128]{2,1,0:T(8,128)(2,1)S(1)} async-done(((bf16[32,8,128]{2,1,0:T(8,128)(2,1)}), bf16[32,8,128]{2,1,0:T(8,128)(2,1)S(1)}, u32[]{:S(2)}, u32[]{:S(2)}) %all-to-all-start) | async-done | bytes 65568 | tf_op jit(solution)/shard_map/all_to_all | solution.py:162
  18.0 0.0 collective-permute-done
  18.0 0.0 copy-done.3
  18.0 1.2 %prefix.1 = bf16[512,128]{1,0:T(8,128)(2,1)S(1)} custom-call(bf16[256,128]{1,0:T(8,128)(2,1)S(1)} %bitcast.14, bf16[2,1024,128]{2,1,0:T(8,128)(2,1)S(1)} %bitcast.17, bf16[2,1024,128]{2,1,0:T(8,128)(2,1)S(1)} %bitcast.18), custom_call_target="tpu_custom_call" | custom-call | flops 402653184 | bytes 1600000 | tf_op jit(solution)/shard_map/prefix/pallas_call | solution.py:138
  19.2 9.9 %all_to_all.10 = bf16[32,16,128]{2,1,0:T(8,128)(2,1)S(1)} all-to-all(bf16[32,16,128]{2,1,0:T(8,128)(2,1)S(1)} %bitcast.12), channel_id=1, replica_groups=mesh['grp'=2,'blk'=16] {'grp','blk'}, dimensions={0} | all-to-all | bytes 262144 | tf_op jit(solution)/shard_map/all_to_all | solution.py:162
  29.1 0.8 %merge.1 = bf16[1,64,128]{2,1,0:T(8,128)(2,1)} custom-call(bf16[512,128]{1,0:T(8,128)(2,1)S(1)} %bitcast.11, f32[64,128]{1,0:T(8,128)S(1)} %get-tuple-element.13.suffix_ref, f32[64,128]{1,0:T(8,128)S(1)} %get-tuple-element.14.lse_ref), custom_call_target="tpu_custom_call" | custom-call | tf_op jit(solution)/shard_map/merge/pallas_call | solution.py:138
Async XLA Ops:
  0.0 18.0 %collective-permute-start = (bf16[2,1,1024,128]{3,2,0,1:T(8,128)(2,1)}, bf16[2,1,1024,128]{3,2,0,1:T(8,128)(2,1)S(1)}, u32[]{:S(2)}, u32[]{:S(2)}) collective-permute-start(bf16[2,1,1024,128]{3,2,0,1:T(8,128)(2,1)} %bitcast.16), channel_id=1, source_target_pairs={{0,1},{1,0},{2,3},{3,2},{4,5},{5,4},{6,7},{7,6},{8,9},{9,8},{10,11... | collective-permute-start | bytes 1572872 | tf_op jit(solution)/shard_map/ppermute | solution.py:164
  3.6 7.6 %copy-start.1 = (bf16[1,64,128]{2,1,0:T(8,128)(2,1)S(1)}, bf16[1,64,128]{2,1,0:T(8,128)(2,1)}, u32[]{:S(2)}) copy-start(bf16[1,64,128]{2,1,0:T(8,128)(2,1)} %q_ref.1) | copy-start | bytes 49156
  3.6 14.4 %all-to-all-start = ((bf16[32,8,128]{2,1,0:T(8,128)(2,1)}), bf16[32,8,128]{2,1,0:T(8,128)(2,1)S(1)}, u32[]{:S(2)}, u32[]{:S(2)}) async-start(bf16[32,8,128]{2,1,0:T(8,128)(2,1)} %bitcast.19), calls=%async_computation | async-start | bytes 131072 | tf_op jit(solution)/shard_map/all_to_all | solution.py:162
  11.2 0.7 %copy-start.2 = (bf16[1,2,4,128]{3,2,1,0:T(4,128)(2,1)S(1)}, bf16[1,2,4,128]{3,2,1,0:T(4,128)(2,1)}, u32[]{:S(2)}) copy-start(bf16[1,2,4,128]{3,2,1,0:T(4,128)(2,1)} %param.8) | copy-start | bytes 6148
  11.9 1.0 %copy-start = (bf16[1,256,2,4,128]{4,3,2,1,0:T(4,128)(2,1)S(1)}, bf16[1,256,2,4,128]{4,3,2,1,0:T(4,128)(2,1)}, u32[]{:S(2)}) copy-start(bf16[1,256,2,4,128]{4,3,2,1,0:T(4,128)(2,1)} %param.7) | copy-start | bytes 1572868
  12.9 5.0 %copy-start.3 = (bf16[2,1,1024,128]{3,2,1,0:T(8,128)(2,1)S(1)}, bf16[2,1,1024,128]{3,2,1,0:T(8,128)(2,1)}, u32[]{:S(2)}) copy-start(bf16[2,1,1024,128]{3,2,1,0:T(8,128)(2,1)} %param.6) | copy-start | bytes 1572868

commit v5 on v4

v5 whole, which is shorter than its diff:
```python
import functools
import math

import jax
import jax.numpy as jnp
from jax import lax
from jax.experimental import pallas as pl
from jax.experimental.pallas import tpu as pltpu
from jax.sharding import PartitionSpec as P

H = 64
KVH = 4
HD = 128
SHARE = H // KVH
SCALE2 = HD ** (-0.5) * math.log2(math.e)
VMEM = pl.BlockSpec(memory_space=pltpu.VMEM)
HBM = pl.BlockSpec(memory_space=pltpu.HBM)
ROWS = 128
CORES = 2
HALF = SHARE // CORES
LIMIT = 24 * 1024 * 1024
NT = (((1,), (1,)), ((), ()))


def dot_nt(a, b):
    return lax.dot_general(a, b, NT, preferred_element_type=jnp.float32)


def dot(a, b):
    return jnp.dot(a, b, preferred_element_type=jnp.float32)


def log2(x):
    return jnp.log(x) * math.log2(math.e)


def split3(x):
    hi = x.astype(jnp.bfloat16).astype(jnp.float32)
    rest = x - hi
    mid = rest.astype(jnp.bfloat16).astype(jnp.float32)
    low = (rest - mid).astype(jnp.bfloat16).astype(jnp.float32)
    return hi, mid, low


def load_kernel(q_ref, kv_ref, cache_ref, new_ref, len_ref, fan_ref, q_out, kv_out, cache_out, new_out, live_ref, len_vmem, sems):
    pairs = [(q_ref, q_out), (len_ref, len_vmem), (new_ref, new_out), (kv_ref, kv_out), (cache_ref, cache_out)]
    copies = [pltpu.make_async_copy(source, target, sems.at[i]) for i, (source, target) in enumerate(pairs)]
    for copy in copies:
        copy.start()
    copies[0].wait()
    q = q_out[...].reshape(KVH, SHARE, HD)
    for group in range(fan_ref.shape[0]):
        for chip in range(fan_ref.shape[2]):
            fan_ref[group, :, chip] = q
    for copy in copies[1:]:
        copy.wait()
    live_ref[...] = jnp.broadcast_to(len_vmem[...], live_ref.shape)


def prefix_step(rows, kv_ref, other_ref):
    def extended(ref):
        return jnp.concatenate([ref[1], jnp.ones_like(ref[1])], axis=1)

    scores = dot_nt(rows, kv_ref[0])
    other_scores = dot_nt(rows, other_ref[0])
    best = jnp.max(jnp.maximum(scores, other_scores), axis=1, keepdims=True)
    weight = jnp.exp2((scores - best) * SCALE2).astype(jnp.bfloat16)
    other_weight = jnp.exp2((other_scores - best) * SCALE2).astype(jnp.bfloat16)
    both = dot(weight, extended(kv_ref)) + dot(other_weight, extended(other_ref))
    total = both[:, HD:]
    result = both[:, :HD] / total
    hi, mid, low = split3(best * SCALE2 + log2(total))
    lane = lax.broadcasted_iota(jnp.int32, (ROWS, HD), 1)
    stats = jnp.where(lane == 0, hi, jnp.where(lane == 1, mid, jnp.where(lane == 2, low, 0.0)))
    shape = (ROWS // HALF, HALF, HD)
    message = jnp.concatenate([result.reshape(shape), stats.reshape(shape)], axis=1)
    return message.reshape(2 * ROWS, HD).astype(jnp.bfloat16)


def suffix_part(q, cache, new, live):
    def owned(shape, limit):
        at = lax.broadcasted_iota(jnp.int32, shape, 1)
        head = lax.broadcasted_iota(jnp.int32, shape, 0) // SHARE
        return (at % (2 * KVH) == head) & (at < limit)

    raw = dot_nt(q, cache)
    limit = jnp.concatenate([live[:1] * (2 * KVH)] * (raw.shape[1] // HD), axis=1)
    scores = jnp.where(owned(raw.shape, limit), raw, -jnp.inf)
    new_raw = dot_nt(q, new)
    new_scores = jnp.where(owned(new_raw.shape, 2 * KVH), new_raw, -jnp.inf)
    best = jnp.maximum(jnp.max(scores, axis=1, keepdims=True), jnp.max(new_scores, axis=1, keepdims=True))
    weight = jnp.exp2((scores - best) * SCALE2).astype(jnp.bfloat16).astype(jnp.float32)
    new_weight = jnp.exp2((new_scores - best) * SCALE2).astype(jnp.bfloat16).astype(jnp.float32)
    total = jnp.sum(weight, axis=1, keepdims=True) + jnp.sum(new_weight, axis=1, keepdims=True)
    moved = pltpu.roll(weight, KVH, 1).astype(jnp.bfloat16)
    new_moved = jnp.concatenate([new_weight[:, KVH:], new_weight[:, :KVH]], axis=1).astype(jnp.bfloat16)
    return (dot(moved, cache) + dot(new_moved, new)) / total, best * SCALE2 + log2(total)


def attend_kernel(arrived_ref, kv_ref, other_ref, q_ref, cache_ref, new_ref, live_ref, out_ref, suffix_ref, lse_ref):
    trips = arrived_ref.shape[0] // ROWS

    def step(trip):
        out_ref[pl.ds(trip * 2 * ROWS, 2 * ROWS)] = prefix_step(arrived_ref[pl.ds(trip * ROWS, ROWS)], kv_ref, other_ref)

    if trips <= 4:
        for trip in range(trips):
            step(trip)
    else:

        def body(trip, unused):
            step(trip)
            return unused

        lax.fori_loop(0, trips, body, 0)
    suffix, lse = suffix_part(q_ref[...], cache_ref[...], new_ref[...], live_ref[...])
    suffix_ref[...] = suffix
    lse_ref[...] = jnp.broadcast_to(lse, lse_ref.shape)


def merge_kernel(served, part_ref, suffix_ref, lse_ref, out_ref):
    sums = dot(part_ref[...], jnp.ones((HD, HD), jnp.bfloat16)).reshape(len(served), 2 * HALF, HD)
    rows = part_ref[...].astype(jnp.float32).reshape(len(served), 2 * HALF, HD)
    blocks = []
    for block in range(H // HALF):
        span = slice(block * HALF, (block + 1) * HALF)
        own = [slot for slot, its in enumerate(served) if its == block]
        own_lse = lse_ref[span]
        best = own_lse
        for slot in own:
            best = jnp.maximum(best, sums[slot, HALF:])
        total = jnp.exp2(own_lse - best)
        numerator = total * suffix_ref[span]
        for slot in own:
            factor = jnp.exp2(sums[slot, HALF:] - best)
            total = total + factor
            numerator = numerator + factor * rows[slot, :HALF]
        blocks.append(numerator / total)
    out_ref[0] = jnp.concatenate(blocks, axis=0).astype(jnp.bfloat16)


def call(kernel, name, outs, operands, space=VMEM, scratch=(), **cost):
    if space is HBM:
        operands = [pltpu.with_memory_space_constraint(x, pltpu.HBM) if x.size > 1 else x for x in operands]
    return pl.pallas_call(
        kernel,
        out_shape=outs,
        in_specs=[space] * len(operands),
        out_specs=jax.tree.map(lambda _: VMEM, outs),
        scratch_shapes=scratch,
        name=name,
        compiler_params=pltpu.CompilerParams(vmem_limit_bytes=LIMIT),
        cost_estimate=pl.CostEstimate(**cost) if cost else None,
    )(*operands)


def local(queries, prefix_kv, suffix_kv, new_kv, suffix_len):
    groups = lax.axis_size("grp")
    members = lax.axis_size("blk")
    per_head = members // KVH
    devices = groups * members
    span = prefix_kv.shape[2]
    cache_rows = suffix_kv.shape[1] * 2 * KVH
    chips = per_head // CORES
    served = [device % members // per_head * CORES + device % CORES for device in range(devices)]

    def half(*shape):
        return jax.ShapeDtypeStruct((*shape, HD), jnp.bfloat16)

    def full(*shape):
        return jax.ShapeDtypeStruct((*shape, HD), jnp.float32)

    def exchange(array):
        array = array.reshape(devices, -1, HD)
        return lax.all_to_all(array, ("grp", "blk"), 0, 0, tiled=True).reshape(-1, HD)

    other = lax.ppermute(prefix_kv, "blk", [(i, i ^ 1) for i in range(members)])
    outgoing, q, kv, cache, new, live = call(
        load_kernel,
        "load",
        [
            half(groups, KVH, chips, SHARE),
            half(H),
            half(2, span),
            half(cache_rows),
            half(2 * KVH),
            jax.ShapeDtypeStruct((8, HD), jnp.int32),
        ],
        (
            queries.reshape(H, HD),
            prefix_kv.reshape(2, span, HD),
            suffix_kv.reshape(cache_rows, HD),
            new_kv.reshape(2 * KVH, HD),
            suffix_len.reshape(1, 1),
        ),
        HBM,
        [pltpu.VMEM((1, 1), jnp.int32), pltpu.SemaphoreType.DMA((5,))],
    )
    arrived = exchange(outgoing)
    partial, suffix, lse = call(
        attend_kernel,
        "attend",
        [half(devices * 2 * HALF), full(H), full(H)],
        (arrived, kv, other.reshape(2, span, HD), q, cache, new, live),
        flops=12 * devices * HALF * span * HD,
        bytes_accessed=1_600_000,
        transcendentals=2 * devices * HALF * span,
    )
    returned = exchange(partial)
    return call(
        functools.partial(merge_kernel, served),
        "merge",
        jax.ShapeDtypeStruct((1, H, HD), jnp.bfloat16),
        (returned, suffix, lse),
    )


def solution(mesh):
    in_specs = (
        P(("grp", "blk"), None, None),
        P(None, "grp", "blk", None),
        P(("grp", "blk"), None, None, None, None),
        P(("grp", "blk"), None, None, None),
        P(("grp", "blk")),
    )
    out_specs = P(("grp", "blk"), None, None)
    return jax.shard_map(local, mesh=mesh, in_specs=in_specs, out_specs=out_specs, check_vma=False)
```

time: 30.2 us -> 29 us (0.960)
  blocking collectives: 9.93 us -> 24.1 us
  starting transfers between devices: 7.42 us -> 0.45 us
  waiting for transfers between devices: 4.33 us -> 0.01 us
  Pallas kernels: 5.79 us -> 3.51 us
  local copies, waits for them, and re-layouts: 1.72 us -> 0 us
    all_to_all x1 -> x2, blocking collectives: 9.93 us -> 24.1 us  [exchange(): lax.all_to_all(array, ('grp', 'blk'), 0, 0, tiled=True).reshape(-1, HD)]
    all_to_all x1 -> x0, starting transfers between devices: 6.97 us -> none  [exchange(): return lax.all_to_all(array, ('grp', 'blk'), 0, 0, tiled=True)]
    all_to_all x1 -> x0, waiting for transfers between devices: 4.33 us -> none  [exchange(): return lax.all_to_all(array, ('grp', 'blk'), 0, 0, tiled=True)]
    pallas_call x4 -> x3, Pallas kernels: 5.79 us -> 3.51 us  [call(): pl.pallas_call(kernel, out_shape=outs, in_specs=[space] * len(operands),...]
    unnamed x8 -> x0, local copies, waits for them, and re-layouts: 1.72 us -> none
  transfers between devices with their start and end apart: 2 -> 1, of which waited for: 1 -> 0; matrix products, arithmetic and copies ran while one was open for 0% -> 0% of each run, Pallas kernels for 13% -> 5%
where the time goes in v5:
time: 29 us; the launch traced here: 28.7 us
  blocking collectives  24.1 us (83%)
  Pallas kernels  3.51 us (12%)
  between operations  0.67 us (2%)
  starting transfers between devices  0.45 us (2%)
    all_to_all x2, blocking collectives, exchange(): lax.all_to_all(array, ('grp', 'blk'), 0, 0, tiled=True).reshape(-1, HD)  24.1 us
    pallas_call x3, Pallas kernels, call(): pl.pallas_call(kernel, out_shape=outs, in_specs=[space] * len(operands),...  3.51 us
  transfers between devices with their start and end apart: 1, of which 0 were waited for; matrix products, arithmetic and copies ran while one was open for 0% of the time, Pallas kernels for 5%

profile of v5, /device:TPU:0, one launch (start us, length us, event | category | flops | bytes accessed | tf_op | source)
XLA Modules:
  0.0 28.7 jit_solution(12705052716770824551)
XLA Ops:
  0.0 0.5 %collective-permute-start = (bf16[2,1,1024,128]{3,2,0,1:T(8,128)(2,1)}, bf16[2,1,1024,128]{3,2,0,1:T(8,128)(2,1)S(1)}, u32[]{:S(2)}, u32[]{:S(2)}) collective-permute-start(bf16[2,1,1024,128]{3,2,0,1:T(8,128)(2,1)} %bitcast.18), channel_id=1, source_target_pairs={{0,1},{1,0},{2,3},{3,2},{4,5},{5,4},{6,7},{7,6},{8,9},{9,8},{10,11... | collective-permute-start | bytes 1572872 | tf_op jit(solution)/shard_map/ppermute | solution.py:177
  1.1 1.3 %load.1 = (bf16[2,4,2,16,128]{4,3,2,1,0:T(8,128)(2,1)S(1)}, bf16[64,128]{1,0:T(8,128)(2,1)S(1)}, bf16[2,1024,128]{2,1,0:T(8,128)(2,1)S(1)}, bf16[2048,128]{1,0:T...) custom-call(bf16[64,128]{1,0:T(8,128)(2,1)} %bitcast.20, bf16[2,1024,128]{2,1,0:T(8,128)(2,1)} %bitcast.19, ...), custom_call_target="tpu_custom_call" | custom-call | tf_op jit(solution)/shard_map/load/pallas_call | solution.py:145
  2.5 14.2 %all_to_all.10 = bf16[32,8,128]{2,1,0:T(8,128)(2,1)S(1)} all-to-all(bf16[32,8,128]{2,1,0:T(8,128)(2,1)S(1)} %bitcast.16), channel_id=1, replica_groups=mesh['grp'=2,'blk'=16] {'grp','blk'}, dimensions={0} | all-to-all | bytes 131072 | tf_op jit(solution)/shard_map/all_to_all | solution.py:175
  16.6 0.0 collective-permute-done
  16.6 1.4 %attend.1 = (bf16[512,128]{1,0:T(8,128)(2,1)S(1)}, f32[64,128]{1,0:T(8,128)S(1)}, f32[64,128]{1,0:T(8,128)S(1)}) custom-call(bf16[256,128]{1,0:T(8,128)(2,1)S(1)} %bitcast.14, bf16[2,1024,128]{2,1,0:T(8,128)(2,1)S(1)} %get-tuple-element.15.kv_ref, bf16[2,1024,128]{2,1,0:T(8,128)(2,1)S(1)} %bitcast.12, bf16[64,128]{1,0:T(8,128)(2,1)S(1)} %get-tuple-element.16.q_ref, ...), custom_call_target="tpu_custom_call" | custom-call | flops 402653184 | bytes 1600000 | tf_op jit(solution)/shard_map/attend/pallas_call | solution.py:145
  18.0 9.9 %all_to_all.11 = bf16[32,16,128]{2,1,0:T(8,128)(2,1)S(1)} all-to-all(bf16[32,16,128]{2,1,0:T(8,128)(2,1)S(1)} %bitcast.15), channel_id=1, replica_groups=mesh['grp'=2,'blk'=16] {'grp','blk'}, dimensions={0} | all-to-all | bytes 262144 | tf_op jit(solution)/shard_map/all_to_all | solution.py:175
  27.9 0.8 %merge.1 = bf16[1,64,128]{2,1,0:T(8,128)(2,1)} custom-call(bf16[512,128]{1,0:T(8,128)(2,1)S(1)} %bitcast.13, f32[64,128]{1,0:T(8,128)S(1)} %get-tuple-element.21.suffix_ref, f32[64,128]{1,0:T(8,128)S(1)} %get-tuple-element.22.lse_ref), custom_call_target="tpu_custom_call" | custom-call | tf_op jit(solution)/shard_map/merge/pallas_call | solution.py:145
Async XLA Ops:
  0.0 16.6 %collective-permute-start = (bf16[2,1,1024,128]{3,2,0,1:T(8,128)(2,1)}, bf16[2,1,1024,128]{3,2,0,1:T(8,128)(2,1)S(1)}, u32[]{:S(2)}, u32[]{:S(2)}) collective-permute-start(bf16[2,1,1024,128]{3,2,0,1:T(8,128)(2,1)} %bitcast.18), channel_id=1, source_target_pairs={{0,1},{1,0},{2,3},{3,2},{4,5},{5,4},{6,7},{7,6},{8,9},{9,8},{10,11... | collective-permute-start | bytes 1572872 | tf_op jit(solution)/shard_map/ppermute | solution.py:177

commit v6 on v4

--- a/solution.py
+++ b/solution.py
@@ -101,9 +101,12 @@
     lse_ref[...] = jnp.broadcast_to(best * SCALE2 + log2(total), lse_ref.shape)
 
 
-def fan_kernel(q_ref, out_ref, sems):
+def fan_kernel(q_ref, out_ref, q_vmem, sem, sems):
+    load = pltpu.make_async_copy(q_ref, q_vmem, sem)
+    load.start()
+    load.wait()
     copies = [
-        pltpu.make_async_copy(q_ref, out_ref.at[group, :, chip], sems.at[group, chip])
+        pltpu.make_async_copy(q_vmem, out_ref.at[group, :, chip], sems.at[group, chip])
         for group in range(out_ref.shape[0])
         for chip in range(out_ref.shape[2])
     ]
@@ -167,9 +170,13 @@
         out_shape=jax.ShapeDtypeStruct((groups, KVH, chips, SHARE, HD), jnp.bfloat16),
         in_specs=[pl.BlockSpec(memory_space=pl.ANY)],
         out_specs=pl.BlockSpec(memory_space=pl.ANY),
-        scratch_shapes=[pltpu.SemaphoreType.DMA((groups, chips))],
+        scratch_shapes=[
+            pltpu.VMEM((KVH, SHARE, HD), jnp.bfloat16),
+            pltpu.SemaphoreType.DMA,
+            pltpu.SemaphoreType.DMA((groups, chips)),
+        ],
         name="fan",
-    )(queries.reshape(KVH, SHARE, HD))
+    )(pltpu.with_memory_space_constraint(queries.reshape(KVH, SHARE, HD), pltpu.HBM))
     arrived = exchange(outgoing.reshape(devices, HALF, HD)).reshape(devices * HALF, HD)
 
     new = new_kv.reshape(1, -1, HD)

time: 30.2 us -> 28.5 us (0.944)
  Pallas kernels: 5.79 us -> 4.05 us
    pallas_call x1, Pallas kernels: 3.12 us -> 1.38 us  [local(): pl.pallas_call(fan_kernel, out_shape=jax.ShapeDtypeStruct((groups, KVH, c...]
  transfers between devices with their start and end apart: 2 -> 2, of which waited for: 1 -> 1; matrix products, arithmetic and copies ran while one was open for 0% -> 0% of each run, Pallas kernels for 13% -> 7%
where the time goes in v6:
time: 28.5 us; the launch traced here: 28.2 us
  blocking collectives  9.93 us (35%)
  starting transfers between devices  7.42 us (26%)
  waiting for transfers between devices  4.33 us (15%)
  Pallas kernels  4.05 us (14%)
  local copies, waits for them, and re-layouts  1.72 us (6%)
  between operations  0.71 us (2%)
    all_to_all x1, blocking collectives, exchange(): return lax.all_to_all(array, ('grp', 'blk'), 0, 0, tiled=True)  9.93 us
    all_to_all x1, starting transfers between devices, exchange(): return lax.all_to_all(array, ('grp', 'blk'), 0, 0, tiled=True)  6.97 us
    all_to_all x1, waiting for transfers between devices, exchange(): return lax.all_to_all(array, ('grp', 'blk'), 0, 0, tiled=True)  4.33 us
    pallas_call x3, Pallas kernels, call(): pl.pallas_call(kernel, out_shape=outs, in_specs=specs or [VMEM] * len(ope...  2.67 us
    unnamed x8, local copies, waits for them, and re-layouts  1.72 us
    pallas_call x1, Pallas kernels, local(): pl.pallas_call(fan_kernel, out_shape=jax.ShapeDtypeStruct((groups, KVH, c...  1.38 us
  transfers between devices with their start and end apart: 2, of which 1 were waited for; matrix products, arithmetic and copies ran while one was open for 0% of the time, Pallas kernels for 7%

profile of v6, /device:TPU:0, one launch (start us, length us, event | category | flops | bytes accessed | tf_op | source)
XLA Modules:
  0.0 28.2 jit_solution(9062204976872348347)
XLA Ops:
  0.0 0.5 %collective-permute-start = (bf16[2,1,1024,128]{3,2,0,1:T(8,128)(2,1)}, bf16[2,1,1024,128]{3,2,0,1:T(8,128)(2,1)S(1)}, u32[]{:S(2)}, u32[]{:S(2)}) collective-permute-start(bf16[2,1,1024,128]{3,2,0,1:T(8,128)(2,1)} %bitcast.16), channel_id=1, source_target_pairs={{0,1},{1,0},{2,3},{3,2},{4,5},{5,4},{6,7},{7,6},{8,9},{9,8},{10,11... | collective-permute-start | bytes 1572872 | tf_op jit(solution)/shard_map/ppermute | solution.py:167
  0.5 1.4 %fan.1 = bf16[2,4,2,16,128]{4,3,2,1,0:T(8,128)(2,1)} custom-call(bf16[4,16,128]{2,1,0:T(8,128)(2,1)} %bitcast.13), custom_call_target="tpu_custom_call" | custom-call | tf_op jit(solution)/shard_map/fan/pallas_call | solution.py:168
  1.8 0.0 copy-start.1
  1.9 7.0 %all-to-all-start = ((bf16[32,8,128]{2,1,0:T(8,128)(2,1)}), bf16[32,8,128]{2,1,0:T(8,128)(2,1)S(1)}, u32[]{:S(2)}, u32[]{:S(2)}) async-start(bf16[32,8,128]{2,1,0:T(8,128)(2,1)} %bitcast.19), calls=%async_computation | async-start | bytes 131072 | tf_op jit(solution)/shard_map/all_to_all | solution.py:165
  9.5 0.0 copy-start.2
  9.5 0.0 copy-done.1
  9.5 0.7 %copy-done.2 = bf16[1,2,4,128]{3,2,1,0:T(4,128)(2,1)S(1)} copy-done((bf16[1,2,4,128]{3,2,1,0:T(4,128)(2,1)S(1)}, bf16[1,2,4,128]{3,2,1,0:T(4,128)(2,1)}, u32[]{:S(2)}) %copy-start.2) | copy-done | bytes 2072
  10.2 0.0 copy-start
  10.2 1.0 %copy-done = bf16[1,256,2,4,128]{4,3,2,1,0:T(4,128)(2,1)S(1)} copy-done((bf16[1,256,2,4,128]{4,3,2,1,0:T(4,128)(2,1)S(1)}, bf16[1,256,2,4,128]{4,3,2,1,0:T(4,128)(2,1)}, u32[]{:S(2)}) %copy-start) | copy-done | bytes 524312
  11.2 0.0 copy-start.3
  11.2 0.7 %suffix.1 = (f32[64,128]{1,0:T(8,128)S(1)}, f32[64,128]{1,0:T(8,128)S(1)}) custom-call(s32[1]{0:T(128)S(6)} %copy.7.len_ref, bf16[1,64,128]{2,1,0:T(8,128)(2,1)S(1)} %copy-done.1, bf16[1,2048,128]{2,1,0:T(8,128)(2,1)S(1)} %bitcast.10, bf16[1,8,128]{2,1,0:T(8,128)(2,1)S(1)} %bitcast.15), custom_call_target="tpu_custom_call" | custom-call | flops 70000000 | bytes 600000 | tf_op jit(solution)/shard_map/suffix/pallas_call | solution.py:141
  11.9 4.3 %all-to-all-done = bf16[32,8,128]{2,1,0:T(8,128)(2,1)S(1)} async-done(((bf16[32,8,128]{2,1,0:T(8,128)(2,1)}), bf16[32,8,128]{2,1,0:T(8,128)(2,1)S(1)}, u32[]{:S(2)}, u32[]{:S(2)}) %all-to-all-start) | async-done | bytes 65568 | tf_op jit(solution)/shard_map/all_to_all | solution.py:165
  16.2 0.0 collective-permute-done
  16.2 0.0 copy-done.3
  16.2 1.2 %prefix.1 = bf16[512,128]{1,0:T(8,128)(2,1)S(1)} custom-call(bf16[256,128]{1,0:T(8,128)(2,1)S(1)} %bitcast.14, bf16[2,1024,128]{2,1,0:T(8,128)(2,1)S(1)} %bitcast.17, bf16[2,1024,128]{2,1,0:T(8,128)(2,1)S(1)} %bitcast.18), custom_call_target="tpu_custom_call" | custom-call | flops 402653184 | bytes 1600000 | tf_op jit(solution)/shard_map/prefix/pallas_call | solution.py:141
  17.4 9.9 %all_to_all.10 = bf16[32,16,128]{2,1,0:T(8,128)(2,1)S(1)} all-to-all(bf16[32,16,128]{2,1,0:T(8,128)(2,1)S(1)} %bitcast.12), channel_id=1, replica_groups=mesh['grp'=2,'blk'=16] {'grp','blk'}, dimensions={0} | all-to-all | bytes 262144 | tf_op jit(solution)/shard_map/all_to_all | solution.py:165
  27.4 0.8 %merge.1 = bf16[1,64,128]{2,1,0:T(8,128)(2,1)} custom-call(bf16[512,128]{1,0:T(8,128)(2,1)S(1)} %bitcast.11, f32[64,128]{1,0:T(8,128)S(1)} %get-tuple-element.13.suffix_ref, f32[64,128]{1,0:T(8,128)S(1)} %get-tuple-element.14.lse_ref), custom_call_target="tpu_custom_call" | custom-call | tf_op jit(solution)/shard_map/merge/pallas_call | solution.py:141
Async XLA Ops:
  0.0 16.2 %collective-permute-start = (bf16[2,1,1024,128]{3,2,0,1:T(8,128)(2,1)}, bf16[2,1,1024,128]{3,2,0,1:T(8,128)(2,1)S(1)}, u32[]{:S(2)}, u32[]{:S(2)}) collective-permute-start(bf16[2,1,1024,128]{3,2,0,1:T(8,128)(2,1)} %bitcast.16), channel_id=1, source_target_pairs={{0,1},{1,0},{2,3},{3,2},{4,5},{5,4},{6,7},{7,6},{8,9},{9,8},{10,11... | collective-permute-start | bytes 1572872 | tf_op jit(solution)/shard_map/ppermute | solution.py:167
  1.8 7.6 %copy-start.1 = (bf16[1,64,128]{2,1,0:T(8,128)(2,1)S(1)}, bf16[1,64,128]{2,1,0:T(8,128)(2,1)}, u32[]{:S(2)}) copy-start(bf16[1,64,128]{2,1,0:T(8,128)(2,1)} %q_ref.1) | copy-start | bytes 49156
  1.9 14.4 %all-to-all-start = ((bf16[32,8,128]{2,1,0:T(8,128)(2,1)}), bf16[32,8,128]{2,1,0:T(8,128)(2,1)S(1)}, u32[]{:S(2)}, u32[]{:S(2)}) async-start(bf16[32,8,128]{2,1,0:T(8,128)(2,1)} %bitcast.19), calls=%async_computation | async-start | bytes 131072 | tf_op jit(solution)/shard_map/all_to_all | solution.py:165
  9.5 0.7 %copy-start.2 = (bf16[1,2,4,128]{3,2,1,0:T(4,128)(2,1)S(1)}, bf16[1,2,4,128]{3,2,1,0:T(4,128)(2,1)}, u32[]{:S(2)}) copy-start(bf16[1,2,4,128]{3,2,1,0:T(4,128)(2,1)} %param.8) | copy-start | bytes 6148
  10.2 1.0 %copy-start = (bf16[1,256,2,4,128]{4,3,2,1,0:T(4,128)(2,1)S(1)}, bf16[1,256,2,4,128]{4,3,2,1,0:T(4,128)(2,1)}, u32[]{:S(2)}) copy-start(bf16[1,256,2,4,128]{4,3,2,1,0:T(4,128)(2,1)} %param.7) | copy-start | bytes 1572868
  11.2 5.0 %copy-start.3 = (bf16[2,1,1024,128]{3,2,1,0:T(8,128)(2,1)S(1)}, bf16[2,1,1024,128]{3,2,1,0:T(8,128)(2,1)}, u32[]{:S(2)}) copy-start(bf16[2,1,1024,128]{3,2,1,0:T(8,128)(2,1)} %param.6) | copy-start | bytes 1572868

commit v7 on v6

--- a/solution.py
+++ b/solution.py
@@ -14,7 +14,7 @@
 SHARE = H // KVH
 SCALE2 = HD ** (-0.5) * math.log2(math.e)
 VMEM = pl.BlockSpec(memory_space=pltpu.VMEM)
-ROWS = 128
+ROWS = 256
 CORES = 2
 HALF = SHARE // CORES
 LIMIT = 24 * 1024 * 1024
@@ -101,19 +101,13 @@
     lse_ref[...] = jnp.broadcast_to(best * SCALE2 + log2(total), lse_ref.shape)
 
 
-def fan_kernel(q_ref, out_ref, q_vmem, sem, sems):
+def fan_kernel(q_ref, out_ref, q_vmem, sem):
     load = pltpu.make_async_copy(q_ref, q_vmem, sem)
     load.start()
     load.wait()
-    copies = [
-        pltpu.make_async_copy(q_vmem, out_ref.at[group, :, chip], sems.at[group, chip])
-        for group in range(out_ref.shape[0])
-        for chip in range(out_ref.shape[2])
-    ]
-    for copy in copies:
-        copy.start()
-    for copy in copies:
-        copy.wait()
+    for group in range(out_ref.shape[0]):
+        for chip in range(out_ref.shape[2]):
+            out_ref[group, :, chip] = q_vmem[...]
 
 
 def merge_kernel(served, part_ref, suffix_ref, lse_ref, out_ref):
@@ -167,15 +161,12 @@
     other = lax.ppermute(prefix_kv, "blk", [(i, i ^ 1) for i in range(members)])
     outgoing = pl.pallas_call(
         fan_kernel,
-        out_shape=jax.ShapeDtypeStruct((groups, KVH, chips, SHARE, HD), jnp.bfloat16),
-        in_specs=[pl.BlockSpec(memory_space=pl.ANY)],
-        out_specs=pl.BlockSpec(memory_space=pl.ANY),
-        scratch_shapes=[
-            pltpu.VMEM((KVH, SHARE, HD), jnp.bfloat16),
-            pltpu.SemaphoreType.DMA,
-            pltpu.SemaphoreType.DMA((groups, chips)),
-        ],
+        out_shape=pltpu.VMEM((groups, KVH, chips, SHARE, HD), jnp.bfloat16),
+        in_specs=[pl.BlockSpec(memory_space=pltpu.HBM)],
+        out_specs=VMEM,
+        scratch_shapes=[pltpu.VMEM((KVH, SHARE, HD), jnp.bfloat16), pltpu.SemaphoreType.DMA],
         name="fan",
+        compiler_params=pltpu.CompilerParams(vmem_limit_bytes=LIMIT),
     )(pltpu.with_memory_space_constraint(queries.reshape(KVH, SHARE, HD), pltpu.HBM))
     arrived = exchange(outgoing.reshape(devices, HALF, HD)).reshape(devices * HALF, HD)
 

time: 28.5 us -> 28.7 us (level)
  no operation moved by 1% of the time
where the time goes in v7:
time: 28.7 us; the launch traced here: 28.3 us
  blocking collectives  9.93 us (35%)
  starting transfers between devices  7.42 us (26%)
  waiting for transfers between devices  4.33 us (15%)
  Pallas kernels  4.24 us (15%)
  local copies, waits for them, and re-layouts  1.72 us (6%)
  between operations  0.7 us (2%)
    all_to_all x1, blocking collectives, exchange(): return lax.all_to_all(array, ('grp', 'blk'), 0, 0, tiled=True)  9.93 us
    all_to_all x1, starting transfers between devices, exchange(): return lax.all_to_all(array, ('grp', 'blk'), 0, 0, tiled=True)  6.97 us
    all_to_all x1, waiting for transfers between devices, exchange(): return lax.all_to_all(array, ('grp', 'blk'), 0, 0, tiled=True)  4.33 us
    pallas_call x3, Pallas kernels, call(): pl.pallas_call(kernel, out_shape=outs, in_specs=specs or [VMEM] * len(ope...  2.88 us
    unnamed x8, local copies, waits for them, and re-layouts  1.72 us
    pallas_call x1, Pallas kernels, local(): pl.pallas_call(fan_kernel, out_shape=pltpu.VMEM((groups, KVH, chips, SHAR...  1.35 us
  transfers between devices with their start and end apart: 2, of which 1 were waited for; matrix products, arithmetic and copies ran while one was open for 0% of the time, Pallas kernels for 7%

profile of v7, /device:TPU:0, one launch (start us, length us, event | category | flops | bytes accessed | tf_op | source)
XLA Modules:
  0.0 28.3 jit_solution(2480567076709238809)
XLA Ops:
  0.0 0.5 %collective-permute-start = (bf16[2,1,1024,128]{3,2,0,1:T(8,128)(2,1)}, bf16[2,1,1024,128]{3,2,0,1:T(8,128)(2,1)S(1)}, u32[]{:S(2)}, u32[]{:S(2)}) collective-permute-start(bf16[2,1,1024,128]{3,2,0,1:T(8,128)(2,1)} %bitcast.16), channel_id=1, source_target_pairs={{0,1},{1,0},{2,3},{3,2},{4,5},{5,4},{6,7},{7,6},{8,9},{9,8},{10,11... | collective-permute-start | bytes 1572872 | tf_op jit(solution)/shard_map/ppermute | solution.py:161
  0.5 1.4 %fan.1 = bf16[2,4,2,16,128]{4,3,2,1,0:T(8,128)(2,1)} custom-call(bf16[4,16,128]{2,1,0:T(8,128)(2,1)} %bitcast.13), custom_call_target="tpu_custom_call" | custom-call | tf_op jit(solution)/shard_map/fan/pallas_call | solution.py:162
  1.8 0.0 copy-start.1
  1.8 7.0 %all-to-all-start = ((bf16[32,8,128]{2,1,0:T(8,128)(2,1)}), bf16[32,8,128]{2,1,0:T(8,128)(2,1)S(1)}, u32[]{:S(2)}, u32[]{:S(2)}) async-start(bf16[32,8,128]{2,1,0:T(8,128)(2,1)} %bitcast.1), calls=%async_computation | async-start | bytes 131072 | tf_op jit(solution)/shard_map/all_to_all | solution.py:159
  9.4 0.0 copy-start.2
  9.5 0.0 copy-done.1
  9.5 0.7 %copy-done.2 = bf16[1,2,4,128]{3,2,1,0:T(4,128)(2,1)S(1)} copy-done((bf16[1,2,4,128]{3,2,1,0:T(4,128)(2,1)S(1)}, bf16[1,2,4,128]{3,2,1,0:T(4,128)(2,1)}, u32[]{:S(2)}) %copy-start.2) | copy-done | bytes 2072
  10.1 0.0 copy-start
  10.1 1.0 %copy-done = bf16[1,256,2,4,128]{4,3,2,1,0:T(4,128)(2,1)S(1)} copy-done((bf16[1,256,2,4,128]{4,3,2,1,0:T(4,128)(2,1)S(1)}, bf16[1,256,2,4,128]{4,3,2,1,0:T(4,128)(2,1)}, u32[]{:S(2)}) %copy-start) | copy-done | bytes 524312
  11.2 0.0 copy-start.3
  11.2 0.7 %suffix.1 = (f32[64,128]{1,0:T(8,128)S(1)}, f32[64,128]{1,0:T(8,128)S(1)}) custom-call(s32[1]{0:T(128)S(6)} %copy.7.len_ref, bf16[1,64,128]{2,1,0:T(8,128)(2,1)S(1)} %copy-done.1, bf16[1,2048,128]{2,1,0:T(8,128)(2,1)S(1)} %bitcast.10, bf16[1,8,128]{2,1,0:T(8,128)(2,1)S(1)} %bitcast.15), custom_call_target="tpu_custom_call" | custom-call | flops 70000000 | bytes 600000 | tf_op jit(solution)/shard_map/suffix/pallas_call | solution.py:135
  11.9 4.3 %all-to-all-done = bf16[32,8,128]{2,1,0:T(8,128)(2,1)S(1)} async-done(((bf16[32,8,128]{2,1,0:T(8,128)(2,1)}), bf16[32,8,128]{2,1,0:T(8,128)(2,1)S(1)}, u32[]{:S(2)}, u32[]{:S(2)}) %all-to-all-start) | async-done | bytes 65568 | tf_op jit(solution)/shard_map/all_to_all | solution.py:159
  16.2 0.0 collective-permute-done
  16.2 0.0 copy-done.3
  16.2 1.4 %prefix.1 = bf16[512,128]{1,0:T(8,128)(2,1)S(1)} custom-call(bf16[256,128]{1,0:T(8,128)(2,1)S(1)} %bitcast.14, bf16[2,1024,128]{2,1,0:T(8,128)(2,1)S(1)} %bitcast.17, bf16[2,1024,128]{2,1,0:T(8,128)(2,1)S(1)} %bitcast.18), custom_call_target="tpu_custom_call" | custom-call | flops 402653184 | bytes 1600000 | tf_op jit(solution)/shard_map/prefix/pallas_call | solution.py:135
  17.6 9.9 %all_to_all.10 = bf16[32,16,128]{2,1,0:T(8,128)(2,1)S(1)} all-to-all(bf16[32,16,128]{2,1,0:T(8,128)(2,1)S(1)} %bitcast.12), channel_id=1, replica_groups=mesh['grp'=2,'blk'=16] {'grp','blk'}, dimensions={0} | all-to-all | bytes 262144 | tf_op jit(solution)/shard_map/all_to_all | solution.py:159
  27.5 0.8 %merge.1 = bf16[1,64,128]{2,1,0:T(8,128)(2,1)} custom-call(bf16[512,128]{1,0:T(8,128)(2,1)S(1)} %bitcast.11, f32[64,128]{1,0:T(8,128)S(1)} %get-tuple-element.13.suffix_ref, f32[64,128]{1,0:T(8,128)S(1)} %get-tuple-element.14.lse_ref), custom_call_target="tpu_custom_call" | custom-call | tf_op jit(solution)/shard_map/merge/pallas_call | solution.py:135
Async XLA Ops:
  0.0 16.2 %collective-permute-start = (bf16[2,1,1024,128]{3,2,0,1:T(8,128)(2,1)}, bf16[2,1,1024,128]{3,2,0,1:T(8,128)(2,1)S(1)}, u32[]{:S(2)}, u32[]{:S(2)}) collective-permute-start(bf16[2,1,1024,128]{3,2,0,1:T(8,128)(2,1)} %bitcast.16), channel_id=1, source_target_pairs={{0,1},{1,0},{2,3},{3,2},{4,5},{5,4},{6,7},{7,6},{8,9},{9,8},{10,11... | collective-permute-start | bytes 1572872 | tf_op jit(solution)/shard_map/ppermute | solution.py:161
  1.8 7.6 %copy-start.1 = (bf16[1,64,128]{2,1,0:T(8,128)(2,1)S(1)}, bf16[1,64,128]{2,1,0:T(8,128)(2,1)}, u32[]{:S(2)}) copy-start(bf16[1,64,128]{2,1,0:T(8,128)(2,1)} %q_ref.1) | copy-start | bytes 49156
  1.8 14.4 %all-to-all-start = ((bf16[32,8,128]{2,1,0:T(8,128)(2,1)}), bf16[32,8,128]{2,1,0:T(8,128)(2,1)S(1)}, u32[]{:S(2)}, u32[]{:S(2)}) async-start(bf16[32,8,128]{2,1,0:T(8,128)(2,1)} %bitcast.1), calls=%async_computation | async-start | bytes 131072 | tf_op jit(solution)/shard_map/all_to_all | solution.py:159
  9.4 0.7 %copy-start.2 = (bf16[1,2,4,128]{3,2,1,0:T(4,128)(2,1)S(1)}, bf16[1,2,4,128]{3,2,1,0:T(4,128)(2,1)}, u32[]{:S(2)}) copy-start(bf16[1,2,4,128]{3,2,1,0:T(4,128)(2,1)} %param.8) | copy-start | bytes 6148
  10.1 1.0 %copy-start = (bf16[1,256,2,4,128]{4,3,2,1,0:T(4,128)(2,1)S(1)}, bf16[1,256,2,4,128]{4,3,2,1,0:T(4,128)(2,1)}, u32[]{:S(2)}) copy-start(bf16[1,256,2,4,128]{4,3,2,1,0:T(4,128)(2,1)} %param.7) | copy-start | bytes 1572868
  11.2 5.0 %copy-start.3 = (bf16[2,1,1024,128]{3,2,1,0:T(8,128)(2,1)S(1)}, bf16[2,1,1024,128]{3,2,1,0:T(8,128)(2,1)}, u32[]{:S(2)}) copy-start(bf16[2,1,1024,128]{3,2,1,0:T(8,128)(2,1)} %param.6) | copy-start | bytes 1572868

commit v8 on v6

--- a/solution.py
+++ b/solution.py
@@ -14,7 +14,8 @@
 SHARE = H // KVH
 SCALE2 = HD ** (-0.5) * math.log2(math.e)
 VMEM = pl.BlockSpec(memory_space=pltpu.VMEM)
-ROWS = 128
+ROWS = 256
+CHUNK = 512
 CORES = 2
 HALF = SHARE // CORES
 LIMIT = 24 * 1024 * 1024
@@ -41,37 +42,44 @@
     return hi, mid, low
 
 
-def prefix_kernel(q_ref, kv_ref, other_ref, out_ref):
-    per_step = ROWS // HALF
+def prefix_kernel(q_ref, keys_ref, other_keys_ref, kv_ref, other_ref, out_ref):
     lane = lax.broadcasted_iota(jnp.int32, (ROWS, HD), 1)
-
-    def extended(ref):
-        return jnp.concatenate([ref[1], jnp.ones_like(ref[1])], axis=1)
-
-    def step(at):
-        rows = q_ref[pl.ds(at * HALF, ROWS)]
-        scores = dot_nt(rows, kv_ref[0])
-        other_scores = dot_nt(rows, other_ref[0])
-        best = jnp.max(jnp.maximum(scores, other_scores), axis=1, keepdims=True)
-        weight = jnp.exp2((scores - best) * SCALE2).astype(jnp.bfloat16)
-        other_weight = jnp.exp2((other_scores - best) * SCALE2).astype(jnp.bfloat16)
-        both = dot(weight, extended(kv_ref)) + dot(other_weight, extended(other_ref))
+    shape = (ROWS // HALF, HALF, HD)
+    pairs = [(other_keys_ref, other_ref), (keys_ref, kv_ref)]
+    chunks = [(keys, ref, at) for keys, ref in pairs for at in range(0, ref.shape[1], CHUNK)]
+
+    def block(at):
+        rows = q_ref[pl.ds(at, ROWS)]
+
+        def score(keys, ref, first):
+            return dot(rows, keys[:, first : first + CHUNK])
+
+        parts = []
+        ahead = score(*chunks[0])
+        for index, (keys, ref, first) in enumerate(chunks):
+            scores = ahead
+            if index + 1 < len(chunks):
+                ahead = score(*chunks[index + 1])
+            best = jnp.max(scores, axis=1, keepdims=True)
+            weight = jnp.exp2((scores - best) * SCALE2).astype(jnp.bfloat16)
+            values = ref[1, first : first + CHUNK]
+            parts.append((best, dot(weight, jnp.concatenate([values, jnp.ones_like(values)], axis=1))))
+        best = functools.reduce(jnp.maximum, [part[0] for part in parts])
+        both = sum(jnp.exp2((its - best) * SCALE2) * sums for its, sums in parts)
         total = both[:, HD:]
         result = both[:, :HD] / total
         hi, mid, low = split3(best * SCALE2 + log2(total))
         stats = jnp.where(lane == 0, hi, jnp.where(lane == 1, mid, jnp.where(lane == 2, low, 0.0)))
-        shape = (per_step, HALF, HD)
         message = jnp.concatenate([result.reshape(shape), stats.reshape(shape)], axis=1)
-        out_ref[pl.ds(at * 2 * HALF, 2 * ROWS)] = message.reshape(2 * ROWS, HD).astype(jnp.bfloat16)
+        out_ref[pl.ds(at * 2, 2 * ROWS)] = message.reshape(2 * ROWS, HD).astype(jnp.bfloat16)
 
     trips = q_ref.shape[0] // ROWS
-    if trips <= 4:
-        for trip in range(trips):
-            step(trip * per_step)
+    if trips == 1:
+        block(0)
     else:
 
         def body(trip, unused):
-            step(pl.multiple_of(trip * per_step, per_step))
+            block(pl.multiple_of(trip * ROWS, ROWS))
             return unused
 
         lax.fori_loop(0, trips, body, 0)
@@ -83,10 +91,20 @@
     return (at % (2 * KVH) == head) & (at < limit * (2 * KVH))
 
 
-def suffix_kernel(len_ref, q_ref, cache_ref, new_ref, out_ref, lse_ref):
-    q = q_ref[0]
-    cache = cache_ref[0]
-    new = new_ref[0]
+def aside_kernel(
+    len_ref, q_hbm, cache_hbm, new_hbm, kv_hbm, other_ref, out_ref, lse_ref, keys_ref, other_keys_ref, kv_ref, q_ref, cache_ref, new_ref, sems
+):
+    pairs = [(kv_hbm, kv_ref), (cache_hbm, cache_ref), (q_hbm, q_ref), (new_hbm, new_ref)]
+    copies = [pltpu.make_async_copy(source, target, sems.at[i]) for i, (source, target) in enumerate(pairs)]
+    for copy in copies:
+        copy.start()
+    other_keys_ref[...] = other_ref[0].T
+    for copy in copies:
+        copy.wait()
+    keys_ref[...] = kv_ref[0].T
+    q = q_ref[...]
+    cache = cache_ref[...]
+    new = new_ref[...]
     raw = dot_nt(q, cache)
     scores = jnp.where(owned(raw.shape, len_ref[0]), raw, -jnp.inf)
     new_raw = dot_nt(q, new)
@@ -155,11 +173,15 @@
     per_head = members // KVH
     devices = groups * members
     span = prefix_kv.shape[2]
+    cache_rows = suffix_kv.shape[1] * 2 * KVH
     chips = per_head // CORES
     served = [device % members // per_head * CORES + device % CORES for device in range(devices)]
 
-    def one(rows, dtype=jnp.float32):
-        return jax.ShapeDtypeStruct((rows, HD), dtype)
+    def one(rows):
+        return jax.ShapeDtypeStruct((rows, HD), jnp.float32)
+
+    def half(*shape):
+        return jax.ShapeDtypeStruct((*shape, HD), jnp.bfloat16)
 
     def exchange(array):
         return lax.all_to_all(array, ("grp", "blk"), 0, 0, tiled=True)
@@ -179,23 +201,38 @@
     )(pltpu.with_memory_space_constraint(queries.reshape(KVH, SHARE, HD), pltpu.HBM))
     arrived = exchange(outgoing.reshape(devices, HALF, HD)).reshape(devices * HALF, HD)
 
-    new = new_kv.reshape(1, -1, HD)
-    suffix = call(
-        suffix_kernel,
-        "suffix",
-        [one(H)] * 2,
-        (suffix_len, queries, suffix_kv.reshape(1, -1, HD), new),
-        [pl.BlockSpec(memory_space=pltpu.SMEM), VMEM, VMEM, VMEM],
-        flops=70_000_000,
-        bytes_accessed=600_000,
-        transcendentals=140_000,
-    )
-    arrived, suffix = lax.optimization_barrier((arrived, suffix))
+    other = other.reshape(2, span, HD)
+    bound = [
+        pltpu.with_memory_space_constraint(array, pltpu.HBM)
+        for array in (
+            queries.reshape(H, HD),
+            suffix_kv.reshape(cache_rows, HD),
+            new_kv.reshape(2 * KVH, HD),
+            prefix_kv.reshape(2, span, HD),
+        )
+    ]
+    aside = pl.pallas_call(
+        aside_kernel,
+        out_shape=[one(H), one(H), *[jax.ShapeDtypeStruct((HD, span), jnp.bfloat16)] * 2, half(2, span)],
+        in_specs=[pl.BlockSpec(memory_space=pltpu.SMEM), *[pl.BlockSpec(memory_space=pltpu.HBM)] * 4, VMEM],
+        out_specs=[VMEM] * 5,
+        scratch_shapes=[
+            pltpu.VMEM((H, HD), jnp.bfloat16),
+            pltpu.VMEM((cache_rows, HD), jnp.bfloat16),
+            pltpu.VMEM((2 * KVH, HD), jnp.bfloat16),
+            pltpu.SemaphoreType.DMA((4,)),
+        ],
+        name="aside",
+        compiler_params=pltpu.CompilerParams(vmem_limit_bytes=LIMIT),
+        cost_estimate=pl.CostEstimate(flops=70_000_000, bytes_accessed=1_200_000, transcendentals=140_000),
+    )(suffix_len, *bound, other)
+    arrived, aside = lax.optimization_barrier((arrived, aside))
+    suffix, suffix_lse, keys, other_keys, kv = aside
     partial = call(
         prefix_kernel,
         "prefix",
-        one(devices * 2 * HALF, jnp.bfloat16),
-        (arrived, prefix_kv.reshape(2, span, HD), other.reshape(2, span, HD)),
+        half(devices * 2 * HALF),
+        (arrived, keys, other_keys, kv, other),
         flops=12 * devices * HALF * span * HD,
         bytes_accessed=1_600_000,
         transcendentals=2 * devices * HALF * span,
@@ -205,7 +242,7 @@
         functools.partial(merge_kernel, served),
         "merge",
         jax.ShapeDtypeStruct((1, H, HD), jnp.bfloat16),
-        (returned, *suffix),
+        (returned, suffix, suffix_lse),
     )
 
 

time: 28.5 us -> 28.2 us (0.989)
  local copies, waits for them, and re-layouts: 1.72 us -> 0 us
  Pallas kernels: 4.05 us -> 5.08 us
  waiting for transfers between devices: 4.33 us -> 4.8 us
    pallas_call x0 -> x1, Pallas kernels: none -> 1.95 us  [local(): pl.pallas_call(aside_kernel, out_shape=[one(H), one(H), *[jax.ShapeDtypeS...]
    unnamed x8 -> x0, local copies, waits for them, and re-layouts: 1.72 us -> none
    pallas_call x3 -> x2, Pallas kernels: 2.67 us -> 1.76 us  [call(): pl.pallas_call(kernel, out_shape=outs, in_specs=specs or [VMEM] * len(ope...]
    all_to_all x1, waiting for transfers between devices: 4.33 us -> 4.8 us  [exchange(): return lax.all_to_all(array, ('grp', 'blk'), 0, 0, tiled=True)]
  transfers between devices with their start and end apart: 2 -> 2, of which waited for: 1 -> 1; matrix products, arithmetic and copies ran while one was open for 0% -> 0% of each run, Pallas kernels for 7% -> 12%
where the time goes in v8:
time: 28.2 us; the launch traced here: 27.9 us
  blocking collectives  9.93 us (35%)
  starting transfers between devices  7.42 us (26%)
  Pallas kernels  5.08 us (18%)
  waiting for transfers between devices  4.8 us (17%)
  between operations  0.69 us (2%)
    all_to_all x1, blocking collectives, exchange(): return lax.all_to_all(array, ('grp', 'blk'), 0, 0, tiled=True)  9.93 us
    all_to_all x1, starting transfers between devices, exchange(): return lax.all_to_all(array, ('grp', 'blk'), 0, 0, tiled=True)  6.97 us
    all_to_all x1, waiting for transfers between devices, exchange(): return lax.all_to_all(array, ('grp', 'blk'), 0, 0, tiled=True)  4.8 us
    pallas_call x1, Pallas kernels, local(): pl.pallas_call(aside_kernel, out_shape=[one(H), one(H), *[jax.ShapeDtypeS...  1.95 us
    pallas_call x2, Pallas kernels, call(): pl.pallas_call(kernel, out_shape=outs, in_specs=specs or [VMEM] * len(ope...  1.76 us
    pallas_call x1, Pallas kernels, local(): pl.pallas_call(fan_kernel, out_shape=jax.ShapeDtypeStruct((groups, KVH, c...  1.38 us
  transfers between devices with their start and end apart: 2, of which 1 were waited for; matrix products, arithmetic and copies ran while one was open for 0% of the time, Pallas kernels for 12%

profile of v8, /device:TPU:0, one launch (start us, length us, event | category | flops | bytes accessed | tf_op | source)
XLA Modules:
  0.0 27.9 jit_solution(13066591915483795775)
XLA Ops:
  0.0 0.5 %collective-permute-start = (bf16[2,1,1024,128]{3,2,0,1:T(8,128)(2,1)}, bf16[2,1,1024,128]{3,2,0,1:T(8,128)(2,1)S(1)}, u32[]{:S(2)}, u32[]{:S(2)}) collective-permute-start(bf16[2,1,1024,128]{3,2,0,1:T(8,128)(2,1)} %bitcast.17), channel_id=1, source_target_pairs={{0,1},{1,0},{2,3},{3,2},{4,5},{5,4},{6,7},{7,6},{8,9},{9,8},{10,11... | collective-permute-start | bytes 1572872 | tf_op jit(solution)/shard_map/ppermute | solution.py:189
  0.5 1.4 %fan.1 = bf16[2,4,2,16,128]{4,3,2,1,0:T(8,128)(2,1)} custom-call(bf16[4,16,128]{2,1,0:T(8,128)(2,1)} %bitcast.20), custom_call_target="tpu_custom_call" | custom-call | tf_op jit(solution)/shard_map/fan/pallas_call | solution.py:190
  1.8 7.0 %all-to-all-start = ((bf16[32,8,128]{2,1,0:T(8,128)(2,1)}), bf16[32,8,128]{2,1,0:T(8,128)(2,1)S(1)}, u32[]{:S(2)}, u32[]{:S(2)}) async-start(bf16[32,8,128]{2,1,0:T(8,128)(2,1)} %bitcast.19), calls=%async_computation | async-start | bytes 131072 | tf_op jit(solution)/shard_map/all_to_all | solution.py:187
  9.5 0.0 collective-permute-done
  9.5 1.9 %aside.1 = (f32[64,128]{1,0:T(8,128)S(1)}, f32[64,128]{1,0:T(8,128)S(1)}, bf16[128,1024]{1,0:T(8,128)(2,1)S(1)}, bf16[128,1024]{1,0:T(8,128)(2,1)S(1)}, bf16[2,1024,128]{2,1,0:T(8,128)(2,1)S(1)}) custom-call(s32[1]{0:T(128)S(6)} %copy.7.len_ref, bf16[64,128]{1,0:T(8,128)(2,1)} %bitcast.21, bf16[2048,128]{1,0:T(8,128)(2,1)} %bitcast.16, ...), custom_call_target="tpu_custom_call" | custom-call | flops 70000000 | bytes 1200000 | tf_op jit(solution)/shard_map/aside/pallas_call | solution.py:214
  11.4 4.8 %all-to-all-done = bf16[32,8,128]{2,1,0:T(8,128)(2,1)S(1)} async-done(((bf16[32,8,128]{2,1,0:T(8,128)(2,1)}), bf16[32,8,128]{2,1,0:T(8,128)(2,1)S(1)}, u32[]{:S(2)}, u32[]{:S(2)}) %all-to-all-start) | async-done | bytes 65568 | tf_op jit(solution)/shard_map/all_to_all | solution.py:187
  16.2 1.0 %prefix.1 = bf16[512,128]{1,0:T(8,128)(2,1)S(1)} custom-call(bf16[256,128]{1,0:T(8,128)(2,1)S(1)} %bitcast.15, bf16[128,1024]{1,0:T(8,128)(2,1)S(1)} %get-tuple-element.22.keys_ref, bf16[128,1024]{1,0:T(8,128)(2,1)S(1)} %get-tuple-element.23.other_keys_ref, bf16[2,1024,128]{2,1,0:T(8,128)(2,1)S(1)} %get-tuple-element.24.kv_ref, ...), custom_call_target="tpu_custom_call" | custom-call | flops 402653184 | bytes 1600000 | tf_op jit(solution)/shard_map/prefix/pallas_call | solution.py:159
  17.2 9.9 %all_to_all.10 = bf16[32,16,128]{2,1,0:T(8,128)(2,1)S(1)} all-to-all(bf16[32,16,128]{2,1,0:T(8,128)(2,1)S(1)} %bitcast.13), channel_id=1, replica_groups=mesh['grp'=2,'blk'=16] {'grp','blk'}, dimensions={0} | all-to-all | bytes 262144 | tf_op jit(solution)/shard_map/all_to_all | solution.py:187
  27.1 0.8 %merge.1 = bf16[1,64,128]{2,1,0:T(8,128)(2,1)} custom-call(bf16[512,128]{1,0:T(8,128)(2,1)S(1)} %bitcast.14, f32[64,128]{1,0:T(8,128)S(1)} %get-tuple-element.25.suffix_ref, f32[64,128]{1,0:T(8,128)S(1)} %get-tuple-element.26.lse_ref), custom_call_target="tpu_custom_call" | custom-call | tf_op jit(solution)/shard_map/merge/pallas_call | solution.py:159
Async XLA Ops:
  0.0 9.5 %collective-permute-start = (bf16[2,1,1024,128]{3,2,0,1:T(8,128)(2,1)}, bf16[2,1,1024,128]{3,2,0,1:T(8,128)(2,1)S(1)}, u32[]{:S(2)}, u32[]{:S(2)}) collective-permute-start(bf16[2,1,1024,128]{3,2,0,1:T(8,128)(2,1)} %bitcast.17), channel_id=1, source_target_pairs={{0,1},{1,0},{2,3},{3,2},{4,5},{5,4},{6,7},{7,6},{8,9},{9,8},{10,11... | collective-permute-start | bytes 1572872 | tf_op jit(solution)/shard_map/ppermute | solution.py:189
  1.8 14.4 %all-to-all-start = ((bf16[32,8,128]{2,1,0:T(8,128)(2,1)}), bf16[32,8,128]{2,1,0:T(8,128)(2,1)S(1)}, u32[]{:S(2)}, u32[]{:S(2)}) async-start(bf16[32,8,128]{2,1,0:T(8,128)(2,1)} %bitcast.19), calls=%async_computation | async-start | bytes 131072 | tf_op jit(solution)/shard_map/all_to_all | solution.py:187

commit v9 on v8

--- a/solution.py
+++ b/solution.py
@@ -42,21 +42,20 @@
     return hi, mid, low
 
 
-def prefix_kernel(q_ref, keys_ref, other_keys_ref, kv_ref, other_ref, out_ref):
+def prefix_part(q_ref, kv_ref, other_ref, out_ref):
     lane = lax.broadcasted_iota(jnp.int32, (ROWS, HD), 1)
     shape = (ROWS // HALF, HALF, HD)
-    pairs = [(other_keys_ref, other_ref), (keys_ref, kv_ref)]
-    chunks = [(keys, ref, at) for keys, ref in pairs for at in range(0, ref.shape[1], CHUNK)]
+    chunks = [(ref, at) for ref in (other_ref, kv_ref) for at in range(0, ref.shape[1], CHUNK)]
 
     def block(at):
         rows = q_ref[pl.ds(at, ROWS)]
 
-        def score(keys, ref, first):
-            return dot(rows, keys[:, first : first + CHUNK])
+        def score(ref, first):
+            return dot_nt(rows, ref[0, first : first + CHUNK])
 
         parts = []
         ahead = score(*chunks[0])
-        for index, (keys, ref, first) in enumerate(chunks):
+        for index, (ref, first) in enumerate(chunks):
             scores = ahead
             if index + 1 < len(chunks):
                 ahead = score(*chunks[index + 1])
@@ -91,22 +90,9 @@
     return (at % (2 * KVH) == head) & (at < limit * (2 * KVH))
 
 
-def aside_kernel(
-    len_ref, q_hbm, cache_hbm, new_hbm, kv_hbm, other_ref, out_ref, lse_ref, keys_ref, other_keys_ref, kv_ref, q_ref, cache_ref, new_ref, sems
-):
-    pairs = [(kv_hbm, kv_ref), (cache_hbm, cache_ref), (q_hbm, q_ref), (new_hbm, new_ref)]
-    copies = [pltpu.make_async_copy(source, target, sems.at[i]) for i, (source, target) in enumerate(pairs)]
-    for copy in copies:
-        copy.start()
-    other_keys_ref[...] = other_ref[0].T
-    for copy in copies:
-        copy.wait()
-    keys_ref[...] = kv_ref[0].T
-    q = q_ref[...]
-    cache = cache_ref[...]
-    new = new_ref[...]
+def suffix_part(q, cache, new, live, out_ref, lse_ref):
     raw = dot_nt(q, cache)
-    scores = jnp.where(owned(raw.shape, len_ref[0]), raw, -jnp.inf)
+    scores = jnp.where(owned(raw.shape, live), raw, -jnp.inf)
     new_raw = dot_nt(q, new)
     new_scores = jnp.where(owned(new_raw.shape, 1), new_raw, -jnp.inf)
     best = jnp.maximum(jnp.max(scores, axis=1, keepdims=True), jnp.max(new_scores, axis=1, keepdims=True))
@@ -119,19 +105,17 @@
     lse_ref[...] = jnp.broadcast_to(best * SCALE2 + log2(total), lse_ref.shape)
 
 
-def fan_kernel(q_ref, out_ref, q_vmem, sem, sems):
-    load = pltpu.make_async_copy(q_ref, q_vmem, sem)
-    load.start()
-    load.wait()
-    copies = [
-        pltpu.make_async_copy(q_vmem, out_ref.at[group, :, chip], sems.at[group, chip])
-        for group in range(out_ref.shape[0])
-        for chip in range(out_ref.shape[2])
-    ]
+def attend_kernel(
+    arrived_ref, kv_ref, other_ref, q_hbm, cache_hbm, new_hbm, len_hbm, out_ref, suffix_ref, lse_ref, q_ref, cache_ref, new_ref, len_ref, sems
+):
+    pairs = [(cache_hbm, cache_ref), (q_hbm, q_ref), (new_hbm, new_ref), (len_hbm, len_ref)]
+    copies = [pltpu.make_async_copy(source, target, sems.at[i]) for i, (source, target) in enumerate(pairs)]
     for copy in copies:
         copy.start()
+    prefix_part(arrived_ref, kv_ref, other_ref, out_ref)
     for copy in copies:
         copy.wait()
+    suffix_part(q_ref[...], cache_ref[...], new_ref[...], len_ref[...], suffix_ref, lse_ref)
 
 
 def merge_kernel(served, part_ref, suffix_ref, lse_ref, out_ref):
@@ -177,72 +161,54 @@
     chips = per_head // CORES
     served = [device % members // per_head * CORES + device % CORES for device in range(devices)]
 
-    def one(rows):
-        return jax.ShapeDtypeStruct((rows, HD), jnp.float32)
-
     def half(*shape):
         return jax.ShapeDtypeStruct((*shape, HD), jnp.bfloat16)
 
+    def full(*shape):
+        return jax.ShapeDtypeStruct((*shape, HD), jnp.float32)
+
     def exchange(array):
-        return lax.all_to_all(array, ("grp", "blk"), 0, 0, tiled=True)
-
-    other = lax.ppermute(prefix_kv, "blk", [(i, i ^ 1) for i in range(members)])
-    outgoing = pl.pallas_call(
-        fan_kernel,
-        out_shape=jax.ShapeDtypeStruct((groups, KVH, chips, SHARE, HD), jnp.bfloat16),
-        in_specs=[pl.BlockSpec(memory_space=pl.ANY)],
-        out_specs=pl.BlockSpec(memory_space=pl.ANY),
-        scratch_shapes=[
-            pltpu.VMEM((KVH, SHARE, HD), jnp.bfloat16),
-            pltpu.SemaphoreType.DMA,
-            pltpu.SemaphoreType.DMA((groups, chips)),
-        ],
-        name="fan",
-    )(pltpu.with_memory_space_constraint(queries.reshape(KVH, SHARE, HD), pltpu.HBM))
-    arrived = exchange(outgoing.reshape(devices, HALF, HD)).reshape(devices * HALF, HD)
-
-    other = other.reshape(2, span, HD)
+        array = array.reshape(devices, -1, HD)
+        return lax.all_to_all(array, ("grp", "blk"), 0, 0, tiled=True).reshape(-1, HD)
+
+    def fetch(array, step=0):
+        return lax.ppermute(array, "blk", [(i, i ^ step) for i in range(members)])
+
+    other = fetch(prefix_kv, 1).reshape(2, span, HD)
+    kv = fetch(prefix_kv).reshape(2, span, HD)
+    live = fetch(suffix_len).reshape(1, 1)
+    outgoing = queries.reshape(1, KVH, 1, SHARE, HD)
+    arrived = exchange(jnp.broadcast_to(outgoing, (groups, KVH, chips, SHARE, HD)))
     bound = [
         pltpu.with_memory_space_constraint(array, pltpu.HBM)
-        for array in (
-            queries.reshape(H, HD),
-            suffix_kv.reshape(cache_rows, HD),
-            new_kv.reshape(2 * KVH, HD),
-            prefix_kv.reshape(2, span, HD),
-        )
+        for array in (queries.reshape(H, HD), suffix_kv.reshape(cache_rows, HD), new_kv.reshape(2 * KVH, HD), live)
     ]
-    aside = pl.pallas_call(
-        aside_kernel,
-        out_shape=[one(H), one(H), *[jax.ShapeDtypeStruct((HD, span), jnp.bfloat16)] * 2, half(2, span)],
-        in_specs=[pl.BlockSpec(memory_space=pltpu.SMEM), *[pl.BlockSpec(memory_space=pltpu.HBM)] * 4, VMEM],
-        out_specs=[VMEM] * 5,
+    partial, suffix, lse = pl.pallas_call(
+        attend_kernel,
+        out_shape=[half(devices * 2 * HALF), full(H), full(H)],
+        in_specs=[VMEM] * 3 + [pl.BlockSpec(memory_space=pltpu.HBM)] * 4,
+        out_specs=[VMEM] * 3,
         scratch_shapes=[
             pltpu.VMEM((H, HD), jnp.bfloat16),
             pltpu.VMEM((cache_rows, HD), jnp.bfloat16),
             pltpu.VMEM((2 * KVH, HD), jnp.bfloat16),
+            pltpu.VMEM((1, 1), jnp.int32),
             pltpu.SemaphoreType.DMA((4,)),
         ],
-        name="aside",
+        name="attend",
         compiler_params=pltpu.CompilerParams(vmem_limit_bytes=LIMIT),
-        cost_estimate=pl.CostEstimate(flops=70_000_000, bytes_accessed=1_200_000, transcendentals=140_000),
-    )(suffix_len, *bound, other)
-    arrived, aside = lax.optimization_barrier((arrived, aside))
-    suffix, suffix_lse, keys, other_keys, kv = aside
-    partial = call(
-        prefix_kernel,
-        "prefix",
-        half(devices * 2 * HALF),
-        (arrived, keys, other_keys, kv, other),
-        flops=12 * devices * HALF * span * HD,
-        bytes_accessed=1_600_000,
-        transcendentals=2 * devices * HALF * span,
-    )
-    returned = exchange(partial.reshape(devices, 2 * HALF, HD)).reshape(-1, HD)
+        cost_estimate=pl.CostEstimate(
+            flops=12 * devices * HALF * span * HD,
+            bytes_accessed=1_600_000,
+            transcendentals=2 * devices * HALF * span,
+        ),
+    )(arrived, kv, other, *bound)
+    returned = exchange(partial)
     return call(
         functools.partial(merge_kernel, served),
         "merge",
         jax.ShapeDtypeStruct((1, H, HD), jnp.bfloat16),
-        (returned, suffix, suffix_lse),
+        (returned, suffix, lse),
     )
 
 

time: 28.2 us -> 30.7 us (1.089)
  starting transfers between devices: 7.42 us -> 9.67 us
  Pallas kernels: 5.08 us -> 3.22 us
  waiting for transfers between devices: 4.8 us -> 6.19 us
  local copies, waits for them, and re-layouts: 0 us -> 1.34 us
  between operations: 0.69 us -> 0.02 us
    ppermute x1 -> x3, starting transfers between devices: 0.45 us -> 2.72 us  [fetch(): return lax.ppermute(array, 'blk', [(i, i ^ step) for i in range(members)])]
    all_to_all x1, waiting for transfers between devices: 4.8 us -> 6.18 us  [exchange(): lax.all_to_all(array, ('grp', 'blk'), 0, 0, tiled=True).reshape(-1, HD)]
    broadcast_in_dim x0 -> x1, local copies, waits for them, and re-layouts: none -> 1.34 us  [local(): jnp.broadcast_to(outgoing, (groups, KVH, chips, SHARE, HD))]
    pallas_call x2 -> x1, Pallas kernels: 1.76 us -> 0.8 us  [call(): pl.pallas_call(kernel, out_shape=outs, in_specs=specs or [VMEM] * len(ope...]
    pallas_call x2 -> x1, Pallas kernels: 3.32 us -> 2.41 us  [local(): pl.pallas_call(attend_kernel, out_shape=[half(devices * 2 * HALF), full(H...]
  transfers between devices with their start and end apart: 2 -> 4, of which waited for: 1 -> 1; matrix products, arithmetic and copies ran while one was open for 0% -> 4% of each run, Pallas kernels for 12% -> 0%
where the time goes in v9:
time: 30.7 us; the launch traced here: 30.4 us
  blocking collectives  9.93 us (32%)
  starting transfers between devices  9.67 us (31%)
  waiting for transfers between devices  6.19 us (20%)
  Pallas kernels  3.22 us (10%)
  local copies, waits for them, and re-layouts  1.34 us (4%)
    all_to_all x1, blocking collectives, exchange(): lax.all_to_all(array, ('grp', 'blk'), 0, 0, tiled=True).reshape(-1, HD)  9.93 us
    all_to_all x1, starting transfers between devices, exchange(): lax.all_to_all(array, ('grp', 'blk'), 0, 0, tiled=True).reshape(-1, HD)  6.96 us
    all_to_all x1, waiting for transfers between devices, exchange(): lax.all_to_all(array, ('grp', 'blk'), 0, 0, tiled=True).reshape(-1, HD)  6.18 us
    ppermute x3, starting transfers between devices, fetch(): return lax.ppermute(array, 'blk', [(i, i ^ step) for i in range(members)])  2.72 us
    pallas_call x1, Pallas kernels, local(): pl.pallas_call(attend_kernel, out_shape=[half(devices * 2 * HALF), full(H...  2.41 us
    broadcast_in_dim x1, local copies, waits for them, and re-layouts, local(): jnp.broadcast_to(outgoing, (groups, KVH, chips, SHARE, HD))  1.34 us
    pallas_call x1, Pallas kernels, call(): pl.pallas_call(kernel, out_shape=outs, in_specs=specs or [VMEM] * len(ope...  0.8 us
  transfers between devices with their start and end apart: 4, of which 1 were waited for; matrix products, arithmetic and copies ran while one was open for 4% of the time, Pallas kernels for 0%

profile of v9, /device:TPU:0, one launch (start us, length us, event | category | flops | bytes accessed | tf_op | source)
XLA Modules:
  0.0 30.4 jit_solution(7821957797614790801)
XLA Ops:
  0.0 0.5 %collective-permute-start.1 = (bf16[2,1,1024,128]{3,2,0,1:T(8,128)(2,1)}, bf16[2,1,1024,128]{3,2,0,1:T(8,128)(2,1)S(1)}, u32[]{:S(2)}, u32[]{:S(2)}) collective-permute-start(bf16[2,1,1024,128]{3,2,0,1:T(8,128)(2,1)} %bitcast.21), channel_id=1, source_target_pairs={{0,1},{1,0},{2,3},{3,2},{4,5},{5,4},{6,7},{7,6},{8,9},{9,8},{10,11... | collective-permute-start | bytes 1572872 | tf_op jit(solution)/shard_map/ppermute | solution.py:175
  0.5 1.0 %collective-permute-start = (bf16[2,1,1024,128]{3,2,0,1:T(8,128)(2,1)}, bf16[2,1,1024,128]{3,2,0,1:T(8,128)(2,1)S(1)}, u32[]{:S(2)}, u32[]{:S(2)}) collective-permute-start(bf16[2,1,1024,128]{3,2,0,1:T(8,128)(2,1)} %bitcast.22), channel_id=1, source_target_pairs={{0,0},{1,1},{2,2},{3,3},{4,4},{5,5},{6,6},{7,7},{8,8},{9,9},{10,10... | collective-permute-start | bytes 1572872 | tf_op jit(solution)/shard_map/ppermute | solution.py:175
  1.5 1.3 %broadcast_in_dim.8 = bf16[2,4,2,16,128]{4,3,2,1,0:T(8,128)(2,1)} broadcast(bf16[4,16,128]{2,1,0:T(8,128)(2,1)} %bitcast.18), dimensions={1,3,4} | broadcast | bytes 81920 | tf_op jit(solution)/shard_map/broadcast_in_dim | solution.py:181
  2.8 7.0 %all-to-all-start = ((bf16[32,8,128]{2,1,0:T(8,128)(2,1)}), bf16[32,8,128]{2,1,0:T(8,128)(2,1)S(1)}, u32[]{:S(2)}, u32[]{:S(2)}) async-start(bf16[32,8,128]{2,1,0:T(8,128)(2,1)} %bitcast.1), calls=%async_computation | async-start | bytes 131072 | tf_op jit(solution)/shard_map/all_to_all | solution.py:172
  9.8 1.2 %collective-permute-start.2 = (s32[1]{0:T(128)}, s32[1]{0:T(128)}, u32[]{:S(2)}, u32[]{:S(2)}) collective-permute-start(s32[1]{0:T(128)} %param.9), channel_id=1, source_target_pairs={{0,0},{1,1},{2,2},{3,3},{4,4},{5,5},{6,6},{7,7},{8,8},{9,9},{10,10... | collective-permute-start | bytes 20 | tf_op jit(solution)/shard_map/ppermute | solution.py:175
  11.0 0.0 collective-permute-done.2
  11.0 6.2 %all-to-all-done = bf16[32,8,128]{2,1,0:T(8,128)(2,1)S(1)} async-done(((bf16[32,8,128]{2,1,0:T(8,128)(2,1)}), bf16[32,8,128]{2,1,0:T(8,128)(2,1)S(1)}, u32[]{:S(2)}, u32[]{:S(2)}) %all-to-all-start) | async-done | bytes 65568 | tf_op jit(solution)/shard_map/all_to_all | solution.py:172
  17.2 0.0 collective-permute-done.1
  17.2 0.0 collective-permute-done
  17.2 2.4 %attend.1 = (bf16[512,128]{1,0:T(8,128)(2,1)S(1)}, f32[64,128]{1,0:T(8,128)S(1)}, f32[64,128]{1,0:T(8,128)S(1)}) custom-call(bf16[256,128]{1,0:T(8,128)(2,1)S(1)} %bitcast.15, bf16[2,1024,128]{2,1,0:T(8,128)(2,1)S(1)} %bitcast.13, bf16[2,1024,128]{2,1,0:T(8,128)(2,1)S(1)} %bitcast.12, bf16[64,128]{1,0:T(8,128)(2,1)} %bitcast.19, bf16[2048,128]{1,0:T(8,128)(2,1)} %bitcast.17, ...), custom_call_target="tpu_custom_call" | custom-call | flops 402653184 | bytes 1600000 | tf_op jit(solution)/shard_map/attend/pallas_call | solution.py:186
  19.6 9.9 %all_to_all.10 = bf16[32,16,128]{2,1,0:T(8,128)(2,1)S(1)} all-to-all(bf16[32,16,128]{2,1,0:T(8,128)(2,1)S(1)} %bitcast.16), channel_id=1, replica_groups=mesh['grp'=2,'blk'=16] {'grp','blk'}, dimensions={0} | all-to-all | bytes 262144 | tf_op jit(solution)/shard_map/all_to_all | solution.py:172
  29.6 0.8 %merge.1 = bf16[1,64,128]{2,1,0:T(8,128)(2,1)} custom-call(bf16[512,128]{1,0:T(8,128)(2,1)S(1)} %bitcast.14, f32[64,128]{1,0:T(8,128)S(1)} %get-tuple-element.9.suffix_ref, f32[64,128]{1,0:T(8,128)S(1)} %get-tuple-element.10.lse_ref), custom_call_target="tpu_custom_call" | custom-call | tf_op jit(solution)/shard_map/merge/pallas_call | solution.py:143
Async XLA Ops:
  0.0 17.2 %collective-permute-start.1 = (bf16[2,1,1024,128]{3,2,0,1:T(8,128)(2,1)}, bf16[2,1,1024,128]{3,2,0,1:T(8,128)(2,1)S(1)}, u32[]{:S(2)}, u32[]{:S(2)}) collective-permute-start(bf16[2,1,1024,128]{3,2,0,1:T(8,128)(2,1)} %bitcast.21), channel_id=1, source_target_pairs={{0,1},{1,0},{2,3},{3,2},{4,5},{5,4},{6,7},{7,6},{8,9},{9,8},{10,11... | collective-permute-start | bytes 1572872 | tf_op jit(solution)/shard_map/ppermute | solution.py:175
  0.5 16.8 %collective-permute-start = (bf16[2,1,1024,128]{3,2,0,1:T(8,128)(2,1)}, bf16[2,1,1024,128]{3,2,0,1:T(8,128)(2,1)S(1)}, u32[]{:S(2)}, u32[]{:S(2)}) collective-permute-start(bf16[2,1,1024,128]{3,2,0,1:T(8,128)(2,1)} %bitcast.22), channel_id=1, source_target_pairs={{0,0},{1,1},{2,2},{3,3},{4,4},{5,5},{6,6},{7,7},{8,8},{9,9},{10,10... | collective-permute-start | bytes 1572872 | tf_op jit(solution)/shard_map/ppermute | solution.py:175
  2.8 14.4 %all-to-all-start = ((bf16[32,8,128]{2,1,0:T(8,128)(2,1)}), bf16[32,8,128]{2,1,0:T(8,128)(2,1)S(1)}, u32[]{:S(2)}, u32[]{:S(2)}) async-start(bf16[32,8,128]{2,1,0:T(8,128)(2,1)} %bitcast.1), calls=%async_computation | async-start | bytes 131072 | tf_op jit(solution)/shard_map/all_to_all | solution.py:172
  9.8 1.2 %collective-permute-start.2 = (s32[1]{0:T(128)}, s32[1]{0:T(128)}, u32[]{:S(2)}, u32[]{:S(2)}) collective-permute-start(s32[1]{0:T(128)} %param.9), channel_id=1, source_target_pairs={{0,0},{1,1},{2,2},{3,3},{4,4},{5,5},{6,6},{7,7},{8,8},{9,9},{10,10... | collective-permute-start | bytes 20 | tf_op jit(solution)/shard_map/ppermute | solution.py:175

commit v10 on v8

--- a/solution.py
+++ b/solution.py
@@ -18,6 +18,8 @@
 CHUNK = 512
 CORES = 2
 HALF = SHARE // CORES
+MESSAGE = HALF + 2
+LANES = HD // HALF
 LIMIT = 24 * 1024 * 1024
 NT = (((1,), (1,)), ((), ()))
 
@@ -34,29 +36,35 @@
     return jnp.log(x) * math.log2(math.e)
 
 
-def split3(x):
+def pack_stats(x):
     hi = x.astype(jnp.bfloat16).astype(jnp.float32)
     rest = x - hi
     mid = rest.astype(jnp.bfloat16).astype(jnp.float32)
-    low = (rest - mid).astype(jnp.bfloat16).astype(jnp.float32)
-    return hi, mid, low
-
-
-def prefix_kernel(q_ref, keys_ref, other_keys_ref, kv_ref, other_ref, out_ref):
-    lane = lax.broadcasted_iota(jnp.int32, (ROWS, HD), 1)
-    shape = (ROWS // HALF, HALF, HD)
-    pairs = [(other_keys_ref, other_ref), (keys_ref, kv_ref)]
-    chunks = [(keys, ref, at) for keys, ref in pairs for at in range(0, ref.shape[1], CHUNK)]
-
-    def block(at):
-        rows = q_ref[pl.ds(at, ROWS)]
-
-        def score(keys, ref, first):
-            return dot(rows, keys[:, first : first + CHUNK])
+    low = rest - mid
+    row = lax.broadcasted_iota(jnp.int32, x.shape, 1)
+    lane = lax.broadcasted_iota(jnp.int32, x.shape, 2) - row * LANES
+    return jnp.sum(jnp.where(lane == 0, hi, jnp.where(lane == 1, mid, jnp.where(lane == 2, low, 0.0))), axis=1)
+
+
+def unpack_stats(rows):
+    shape = (HALF, HD)
+    mine = lax.broadcasted_iota(jnp.int32, shape, 1) // LANES == lax.broadcasted_iota(jnp.int32, shape, 0)
+    pieces = [jnp.where(mine, jnp.broadcast_to(row, shape), 0.0) for row in rows]
+    return dot(jnp.concatenate(pieces, axis=0).astype(jnp.bfloat16), jnp.ones((HD, HD), jnp.bfloat16))
+
+
+def prefix_kernel(q_ref, kv_ref, other_ref, out_ref):
+    chunks = [(ref, at) for ref in (other_ref, kv_ref) for at in range(0, ref.shape[1], CHUNK)]
+
+    def block(trip):
+        rows = q_ref[pl.ds(trip * ROWS, ROWS)]
+
+        def score(ref, first):
+            return dot_nt(rows, ref[0, first : first + CHUNK])
 
         parts = []
         ahead = score(*chunks[0])
-        for index, (keys, ref, first) in enumerate(chunks):
+        for index, (ref, first) in enumerate(chunks):
             scores = ahead
             if index + 1 < len(chunks):
                 ahead = score(*chunks[index + 1])
@@ -68,10 +76,13 @@
         both = sum(jnp.exp2((its - best) * SCALE2) * sums for its, sums in parts)
         total = both[:, HD:]
         result = both[:, :HD] / total
-        hi, mid, low = split3(best * SCALE2 + log2(total))
-        stats = jnp.where(lane == 0, hi, jnp.where(lane == 1, mid, jnp.where(lane == 2, low, 0.0)))
-        message = jnp.concatenate([result.reshape(shape), stats.reshape(shape)], axis=1)
-        out_ref[pl.ds(at * 2, 2 * ROWS)] = message.reshape(2 * ROWS, HD).astype(jnp.bfloat16)
+        slots = ROWS // HALF
+        stats = pack_stats((best * SCALE2 + log2(total)).reshape(slots, HALF, HD))
+        empty = jnp.zeros((1, HD), jnp.float32)
+        pieces = []
+        for slot in range(slots):
+            pieces += [result[slot * HALF : (slot + 1) * HALF], stats[slot : slot + 1], empty]
+        out_ref[pl.ds(trip * slots * MESSAGE, slots * MESSAGE)] = jnp.concatenate(pieces, axis=0).astype(jnp.bfloat16)
 
     trips = q_ref.shape[0] // ROWS
     if trips == 1:
@@ -79,7 +90,7 @@
     else:
 
         def body(trip, unused):
-            block(pl.multiple_of(trip * ROWS, ROWS))
+            block(trip)
             return unused
 
         lax.fori_loop(0, trips, body, 0)
@@ -91,17 +102,13 @@
     return (at % (2 * KVH) == head) & (at < limit * (2 * KVH))
 
 
-def aside_kernel(
-    len_ref, q_hbm, cache_hbm, new_hbm, kv_hbm, other_ref, out_ref, lse_ref, keys_ref, other_keys_ref, kv_ref, q_ref, cache_ref, new_ref, sems
-):
-    pairs = [(kv_hbm, kv_ref), (cache_hbm, cache_ref), (q_hbm, q_ref), (new_hbm, new_ref)]
+def aside_kernel(len_ref, new_ref, q_hbm, cache_hbm, kv_hbm, out_ref, lse_ref, kv_ref, q_ref, cache_ref, sems):
+    pairs = [(q_hbm, q_ref), (cache_hbm, cache_ref), (kv_hbm, kv_ref)]
     copies = [pltpu.make_async_copy(source, target, sems.at[i]) for i, (source, target) in enumerate(pairs)]
     for copy in copies:
         copy.start()
-    other_keys_ref[...] = other_ref[0].T
-    for copy in copies:
-        copy.wait()
-    keys_ref[...] = kv_ref[0].T
+    copies[0].wait()
+    copies[1].wait()
     q = q_ref[...]
     cache = cache_ref[...]
     new = new_ref[...]
@@ -117,6 +124,7 @@
     new_moved = jnp.concatenate([new_weight[:, KVH:], new_weight[:, :KVH]], axis=1).astype(jnp.bfloat16)
     out_ref[...] = (dot(moved, cache) + dot(new_moved, new)) / total
     lse_ref[...] = jnp.broadcast_to(best * SCALE2 + log2(total), lse_ref.shape)
+    copies[2].wait()
 
 
 def fan_kernel(q_ref, out_ref, q_vmem, sem, sems):
@@ -135,8 +143,10 @@
 
 
 def merge_kernel(served, part_ref, suffix_ref, lse_ref, out_ref):
-    sums = dot(part_ref[...], jnp.ones((HD, HD), jnp.bfloat16)).reshape(len(served), 2 * HALF, HD)
-    rows = part_ref[...].astype(jnp.float32).reshape(len(served), 2 * HALF, HD)
+    part = part_ref[...].astype(jnp.float32)
+    starts = range(0, len(served) * MESSAGE, MESSAGE)
+    rows = [part[at : at + HALF] for at in starts]
+    sums = unpack_stats([part[at + HALF : at + HALF + 1] for at in starts]).reshape(len(served), HALF, HD)
     blocks = []
     for block in range(H // HALF):
         span = slice(block * HALF, (block + 1) * HALF)
@@ -144,13 +154,13 @@
         own_lse = lse_ref[span]
         best = own_lse
         for slot in own:
-            best = jnp.maximum(best, sums[slot, HALF:])
+            best = jnp.maximum(best, sums[slot])
         total = jnp.exp2(own_lse - best)
         numerator = total * suffix_ref[span]
         for slot in own:
-            factor = jnp.exp2(sums[slot, HALF:] - best)
+            factor = jnp.exp2(sums[slot] - best)
             total = total + factor
-            numerator = numerator + factor * rows[slot, :HALF]
+            numerator = numerator + factor * rows[slot]
         blocks.append(numerator / total)
     out_ref[0] = jnp.concatenate(blocks, axis=0).astype(jnp.bfloat16)
 
@@ -204,40 +214,34 @@
     other = other.reshape(2, span, HD)
     bound = [
         pltpu.with_memory_space_constraint(array, pltpu.HBM)
-        for array in (
-            queries.reshape(H, HD),
-            suffix_kv.reshape(cache_rows, HD),
-            new_kv.reshape(2 * KVH, HD),
-            prefix_kv.reshape(2, span, HD),
-        )
+        for array in (queries.reshape(H, HD), suffix_kv.reshape(cache_rows, HD), prefix_kv.reshape(2, span, HD))
     ]
     aside = pl.pallas_call(
         aside_kernel,
-        out_shape=[one(H), one(H), *[jax.ShapeDtypeStruct((HD, span), jnp.bfloat16)] * 2, half(2, span)],
-        in_specs=[pl.BlockSpec(memory_space=pltpu.SMEM), *[pl.BlockSpec(memory_space=pltpu.HBM)] * 4, VMEM],
-        out_specs=[VMEM] * 5,
+        out_shape=[one(H), one(H), half(2, span)],
+        in_specs=[pl.BlockSpec(memory_space=pltpu.SMEM), VMEM, *[pl.BlockSpec(memory_space=pltpu.HBM)] * 3],
+        out_specs=[VMEM] * 3,
         scratch_shapes=[
             pltpu.VMEM((H, HD), jnp.bfloat16),
             pltpu.VMEM((cache_rows, HD), jnp.bfloat16),
-            pltpu.VMEM((2 * KVH, HD), jnp.bfloat16),
-            pltpu.SemaphoreType.DMA((4,)),
+            pltpu.SemaphoreType.DMA((3,)),
         ],
         name="aside",
         compiler_params=pltpu.CompilerParams(vmem_limit_bytes=LIMIT),
         cost_estimate=pl.CostEstimate(flops=70_000_000, bytes_accessed=1_200_000, transcendentals=140_000),
-    )(suffix_len, *bound, other)
+    )(suffix_len, new_kv.reshape(2 * KVH, HD), *bound)
     arrived, aside = lax.optimization_barrier((arrived, aside))
-    suffix, suffix_lse, keys, other_keys, kv = aside
+    suffix, suffix_lse, kv = aside
     partial = call(
         prefix_kernel,
         "prefix",
-        half(devices * 2 * HALF),
-        (arrived, keys, other_keys, kv, other),
+        half(devices * MESSAGE),
+        (arrived, kv, other),
         flops=12 * devices * HALF * span * HD,
         bytes_accessed=1_600_000,
         transcendentals=2 * devices * HALF * span,
     )
-    returned = exchange(partial.reshape(devices, 2 * HALF, HD)).reshape(-1, HD)
+    returned = exchange(partial.reshape(devices, MESSAGE // 2, 2, HD)).reshape(-1, HD)
     return call(
         functools.partial(merge_kernel, served),
         "merge",

time: 28.2 us -> 27.8 us (0.986)
  local copies, waits for them, and re-layouts: 0 us -> 0.68 us
  blocking collectives: 9.93 us -> 9.3 us
  waiting for transfers between devices: 4.8 us -> 4.28 us
    unnamed x0 -> x2, local copies, waits for them, and re-layouts: none -> 0.68 us
    all_to_all x1, blocking collectives: 9.93 us -> 9.3 us  [exchange(): return lax.all_to_all(array, ('grp', 'blk'), 0, 0, tiled=True)]
    all_to_all x1, waiting for transfers between devices: 4.8 us -> 4.28 us  [exchange(): return lax.all_to_all(array, ('grp', 'blk'), 0, 0, tiled=True)]
where the time goes in v10:
time: 27.8 us; the launch traced here: 27.3 us
  blocking collectives  9.3 us (33%)
  starting transfers between devices  7.42 us (27%)
  Pallas kernels  4.97 us (18%)
  waiting for transfers between devices  4.28 us (15%)
  between operations  0.69 us (2%)
  local copies, waits for them, and re-layouts  0.68 us (2%)
    all_to_all x1, blocking collectives, exchange(): return lax.all_to_all(array, ('grp', 'blk'), 0, 0, tiled=True)  9.3 us
    all_to_all x1, starting transfers between devices, exchange(): return lax.all_to_all(array, ('grp', 'blk'), 0, 0, tiled=True)  6.97 us
    all_to_all x1, waiting for transfers between devices, exchange(): return lax.all_to_all(array, ('grp', 'blk'), 0, 0, tiled=True)  4.28 us
    pallas_call x2, Pallas kernels, call(): pl.pallas_call(kernel, out_shape=outs, in_specs=specs or [VMEM] * len(ope...  1.8 us
    pallas_call x1, Pallas kernels, local(): pl.pallas_call(aside_kernel, out_shape=[one(H), one(H), half(2, span)], i...  1.79 us
    pallas_call x1, Pallas kernels, local(): pl.pallas_call(fan_kernel, out_shape=jax.ShapeDtypeStruct((groups, KVH, c...  1.38 us
    unnamed x2, local copies, waits for them, and re-layouts  0.68 us
  transfers between devices with their start and end apart: 2, of which 1 were waited for; matrix products, arithmetic and copies ran while one was open for 0% of the time, Pallas kernels for 12%

profile of v10, /device:TPU:0, one launch (start us, length us, event | category | flops | bytes accessed | tf_op | source)
XLA Modules:
  0.0 27.3 jit_solution(6627441561465936331)
XLA Ops:
  0.0 0.5 %collective-permute-start = (bf16[2,1,1024,128]{3,2,0,1:T(8,128)(2,1)}, bf16[2,1,1024,128]{3,2,0,1:T(8,128)(2,1)S(1)}, u32[]{:S(2)}, u32[]{:S(2)}) collective-permute-start(bf16[2,1,1024,128]{3,2,0,1:T(8,128)(2,1)} %bitcast.17), channel_id=1, source_target_pairs={{0,1},{1,0},{2,3},{3,2},{4,5},{5,4},{6,7},{7,6},{8,9},{9,8},{10,11... | collective-permute-start | bytes 1572872 | tf_op jit(solution)/shard_map/ppermute | solution.py:199
  0.5 1.4 %fan.1 = bf16[2,4,2,16,128]{4,3,2,1,0:T(8,128)(2,1)} custom-call(bf16[4,16,128]{2,1,0:T(8,128)(2,1)} %bitcast.20), custom_call_target="tpu_custom_call" | custom-call | tf_op jit(solution)/shard_map/fan/pallas_call | solution.py:200
  1.8 7.0 %all-to-all-start = ((bf16[32,8,128]{2,1,0:T(8,128)(2,1)}), bf16[32,8,128]{2,1,0:T(8,128)(2,1)S(1)}, u32[]{:S(2)}, u32[]{:S(2)}) async-start(bf16[32,8,128]{2,1,0:T(8,128)(2,1)} %bitcast.19), calls=%async_computation | async-start | bytes 131072 | tf_op jit(solution)/shard_map/all_to_all | solution.py:197
  9.5 0.0 copy-start
  9.5 0.7 %copy-done = bf16[1,2,4,128]{3,2,1,0:T(4,128)(2,1)S(1)} copy-done((bf16[1,2,4,128]{3,2,1,0:T(4,128)(2,1)S(1)}, bf16[1,2,4,128]{3,2,1,0:T(4,128)(2,1)}, u32[]{:S(2)}) %copy-start) | copy-done | bytes 2072
  10.1 1.8 %aside.1 = (f32[64,128]{1,0:T(8,128)S(1)}, f32[64,128]{1,0:T(8,128)S(1)}, bf16[2,1024,128]{2,1,0:T(8,128)(2,1)S(1)}) custom-call(s32[1]{0:T(128)S(6)} %copy.7.len_ref, bf16[8,128]{1,0:T(8,128)(2,1)S(1)} %bitcast.14, bf16[64,128]{1,0:T(8,128)(2,1)} %bitcast.21, bf16[2048,128]{1,0:T(8,128)(2,1)} %bitcast.16, bf16[2,1024,128]{2,1,0:T(8,128)(2,1)} %bitcast.18), custom_call_target="tpu_custom_call" | custom-call | flops 70000000 | bytes 1200000 | tf_op jit(solution)/shard_map/aside/pallas_call | solution.py:219
  11.9 4.3 %all-to-all-done = bf16[32,8,128]{2,1,0:T(8,128)(2,1)S(1)} async-done(((bf16[32,8,128]{2,1,0:T(8,128)(2,1)}), bf16[32,8,128]{2,1,0:T(8,128)(2,1)S(1)}, u32[]{:S(2)}, u32[]{:S(2)}) %all-to-all-start) | async-done | bytes 65568 | tf_op jit(solution)/shard_map/all_to_all | solution.py:197
  16.2 0.0 collective-permute-done
  16.2 1.0 %prefix.1 = bf16[320,128]{1,0:T(8,128)(2,1)S(1)} custom-call(bf16[256,128]{1,0:T(8,128)(2,1)S(1)} %bitcast.13, bf16[2,1024,128]{2,1,0:T(8,128)(2,1)S(1)} %get-tuple-element.16.kv_ref, bf16[2,1024,128]{2,1,0:T(8,128)(2,1)S(1)} %bitcast.15), custom_call_target="tpu_custom_call" | custom-call | flops 402653184 | bytes 1600000 | tf_op jit(solution)/shard_map/prefix/pallas_call | solution.py:169
  17.2 9.3 %all_to_all.10 = bf16[32,5,2,128]{3,2,1,0:T(2,128)(2,1)S(1)} all-to-all(bf16[32,5,2,128]{3,2,1,0:T(2,128)(2,1)S(1)} %bitcast.12), channel_id=1, replica_groups=mesh['grp'=2,'blk'=16] {'grp','blk'}, dimensions={0} | all-to-all | bytes 163840 | tf_op jit(solution)/shard_map/all_to_all | solution.py:197
  26.5 0.8 %merge.1 = bf16[1,64,128]{2,1,0:T(8,128)(2,1)} custom-call(bf16[320,128]{1,0:T(8,128)(2,1)S(1)} %bitcast.11, f32[64,128]{1,0:T(8,128)S(1)} %get-tuple-element.17.suffix_ref, f32[64,128]{1,0:T(8,128)S(1)} %get-tuple-element.18.lse_ref), custom_call_target="tpu_custom_call" | custom-call | tf_op jit(solution)/shard_map/merge/pallas_call | solution.py:169
Async XLA Ops:
  0.0 16.2 %collective-permute-start = (bf16[2,1,1024,128]{3,2,0,1:T(8,128)(2,1)}, bf16[2,1,1024,128]{3,2,0,1:T(8,128)(2,1)S(1)}, u32[]{:S(2)}, u32[]{:S(2)}) collective-permute-start(bf16[2,1,1024,128]{3,2,0,1:T(8,128)(2,1)} %bitcast.17), channel_id=1, source_target_pairs={{0,1},{1,0},{2,3},{3,2},{4,5},{5,4},{6,7},{7,6},{8,9},{9,8},{10,11... | collective-permute-start | bytes 1572872 | tf_op jit(solution)/shard_map/ppermute | solution.py:199
  1.8 14.4 %all-to-all-start = ((bf16[32,8,128]{2,1,0:T(8,128)(2,1)}), bf16[32,8,128]{2,1,0:T(8,128)(2,1)S(1)}, u32[]{:S(2)}, u32[]{:S(2)}) async-start(bf16[32,8,128]{2,1,0:T(8,128)(2,1)} %bitcast.19), calls=%async_computation | async-start | bytes 131072 | tf_op jit(solution)/shard_map/all_to_all | solution.py:197
  9.5 0.7 %copy-start = (bf16[1,2,4,128]{3,2,1,0:T(4,128)(2,1)S(1)}, bf16[1,2,4,128]{3,2,1,0:T(4,128)(2,1)}, u32[]{:S(2)}) copy-start(bf16[1,2,4,128]{3,2,1,0:T(4,128)(2,1)} %param.8) | copy-start | bytes 6148

commit v11 on v10

--- a/solution.py
+++ b/solution.py
@@ -102,14 +102,8 @@
     return (at % (2 * KVH) == head) & (at < limit * (2 * KVH))
 
 
-def aside_kernel(len_ref, new_ref, q_hbm, cache_hbm, kv_hbm, out_ref, lse_ref, kv_ref, q_ref, cache_ref, sems):
-    pairs = [(q_hbm, q_ref), (cache_hbm, cache_ref), (kv_hbm, kv_ref)]
-    copies = [pltpu.make_async_copy(source, target, sems.at[i]) for i, (source, target) in enumerate(pairs)]
-    for copy in copies:
-        copy.start()
-    copies[0].wait()
-    copies[1].wait()
-    q = q_ref[...]
+def suffix_kernel(len_ref, new_ref, q_ref, cache_ref, out_ref, lse_ref):
+    q = q_ref[...].reshape(H, HD)
     cache = cache_ref[...]
     new = new_ref[...]
     raw = dot_nt(q, cache)
@@ -124,21 +118,22 @@
     new_moved = jnp.concatenate([new_weight[:, KVH:], new_weight[:, :KVH]], axis=1).astype(jnp.bfloat16)
     out_ref[...] = (dot(moved, cache) + dot(new_moved, new)) / total
     lse_ref[...] = jnp.broadcast_to(best * SCALE2 + log2(total), lse_ref.shape)
-    copies[2].wait()
-
-
-def fan_kernel(q_ref, out_ref, q_vmem, sem, sems):
-    load = pltpu.make_async_copy(q_ref, q_vmem, sem)
-    load.start()
-    load.wait()
+
+
+def fan_kernel(q_hbm, kv_hbm, cache_hbm, out_ref, q_ref, kv_ref, cache_ref, sems, fan_sems):
+    pairs = [(q_hbm, q_ref), (cache_hbm, cache_ref), (kv_hbm, kv_ref)]
+    loads = [pltpu.make_async_copy(source, target, sems.at[i]) for i, (source, target) in enumerate(pairs)]
+    for load in loads:
+        load.start()
+    loads[0].wait()
     copies = [
-        pltpu.make_async_copy(q_vmem, out_ref.at[group, :, chip], sems.at[group, chip])
+        pltpu.make_async_copy(q_ref, out_ref.at[group, :, chip], fan_sems.at[group, chip])
         for group in range(out_ref.shape[0])
         for chip in range(out_ref.shape[2])
     ]
     for copy in copies:
         copy.start()
-    for copy in copies:
+    for copy in copies + loads[1:]:
         copy.wait()
 
 
@@ -196,42 +191,36 @@
     def exchange(array):
         return lax.all_to_all(array, ("grp", "blk"), 0, 0, tiled=True)
 
-    other = lax.ppermute(prefix_kv, "blk", [(i, i ^ 1) for i in range(members)])
-    outgoing = pl.pallas_call(
-        fan_kernel,
-        out_shape=jax.ShapeDtypeStruct((groups, KVH, chips, SHARE, HD), jnp.bfloat16),
-        in_specs=[pl.BlockSpec(memory_space=pl.ANY)],
-        out_specs=pl.BlockSpec(memory_space=pl.ANY),
-        scratch_shapes=[
-            pltpu.VMEM((KVH, SHARE, HD), jnp.bfloat16),
-            pltpu.SemaphoreType.DMA,
-            pltpu.SemaphoreType.DMA((groups, chips)),
-        ],
-        name="fan",
-    )(pltpu.with_memory_space_constraint(queries.reshape(KVH, SHARE, HD), pltpu.HBM))
-    arrived = exchange(outgoing.reshape(devices, HALF, HD)).reshape(devices * HALF, HD)
-
-    other = other.reshape(2, span, HD)
+    other = lax.ppermute(prefix_kv, "blk", [(i, i ^ 1) for i in range(members)]).reshape(2, span, HD)
     bound = [
         pltpu.with_memory_space_constraint(array, pltpu.HBM)
-        for array in (queries.reshape(H, HD), suffix_kv.reshape(cache_rows, HD), prefix_kv.reshape(2, span, HD))
+        for array in (
+            queries.reshape(KVH, SHARE, HD),
+            prefix_kv.reshape(2, span, HD),
+            suffix_kv.reshape(cache_rows, HD),
+        )
     ]
-    aside = pl.pallas_call(
-        aside_kernel,
-        out_shape=[one(H), one(H), half(2, span)],
-        in_specs=[pl.BlockSpec(memory_space=pltpu.SMEM), VMEM, *[pl.BlockSpec(memory_space=pltpu.HBM)] * 3],
-        out_specs=[VMEM] * 3,
-        scratch_shapes=[
-            pltpu.VMEM((H, HD), jnp.bfloat16),
-            pltpu.VMEM((cache_rows, HD), jnp.bfloat16),
-            pltpu.SemaphoreType.DMA((3,)),
-        ],
-        name="aside",
+    outgoing, q, kv, cache = pl.pallas_call(
+        fan_kernel,
+        out_shape=[half(groups, KVH, chips, SHARE), half(KVH, SHARE), half(2, span), half(cache_rows)],
+        in_specs=[pl.BlockSpec(memory_space=pltpu.HBM)] * 3,
+        out_specs=[pl.BlockSpec(memory_space=pl.ANY), VMEM, VMEM, VMEM],
+        scratch_shapes=[pltpu.SemaphoreType.DMA((3,)), pltpu.SemaphoreType.DMA((groups, chips))],
+        name="fan",
         compiler_params=pltpu.CompilerParams(vmem_limit_bytes=LIMIT),
-        cost_estimate=pl.CostEstimate(flops=70_000_000, bytes_accessed=1_200_000, transcendentals=140_000),
-    )(suffix_len, new_kv.reshape(2 * KVH, HD), *bound)
-    arrived, aside = lax.optimization_barrier((arrived, aside))
-    suffix, suffix_lse, kv = aside
+    )(*bound)
+    arrived = exchange(outgoing.reshape(devices, HALF, HD)).reshape(devices * HALF, HD)
+    suffix = call(
+        suffix_kernel,
+        "suffix",
+        [one(H)] * 2,
+        (suffix_len, new_kv.reshape(2 * KVH, HD), q, cache),
+        [pl.BlockSpec(memory_space=pltpu.SMEM), VMEM, VMEM, VMEM],
+        flops=70_000_000,
+        bytes_accessed=600_000,
+        transcendentals=140_000,
+    )
+    arrived, suffix = lax.optimization_barrier((arrived, suffix))
     partial = call(
         prefix_kernel,
         "prefix",
@@ -246,7 +235,7 @@
         functools.partial(merge_kernel, served),
         "merge",
         jax.ShapeDtypeStruct((1, H, HD), jnp.bfloat16),
-        (returned, suffix, suffix_lse),
+        (returned, *suffix),
     )
 
 

time: 27.8 us -> 27.7 us (level)
  waiting for transfers between devices: 4.28 us -> 5.38 us
  Pallas kernels: 4.97 us -> 3.89 us
    pallas_call x2 -> x1, Pallas kernels: 3.16 us -> 1.4 us  [local(): pl.pallas_call(fan_kernel, out_shape=[half(groups, KVH, chips, SHARE), ha...]
    all_to_all x1, waiting for transfers between devices: 4.28 us -> 5.38 us  [exchange(): return lax.all_to_all(array, ('grp', 'blk'), 0, 0, tiled=True)]
    pallas_call x2 -> x3, Pallas kernels: 1.8 us -> 2.5 us  [call(): pl.pallas_call(kernel, out_shape=outs, in_specs=specs or [VMEM] * len(ope...]
  transfers between devices with their start and end apart: 2 -> 2, of which waited for: 1 -> 1; matrix products, arithmetic and copies ran while one was open for 0% -> 0% of each run, Pallas kernels for 12% -> 8%
where the time goes in v11:
time: 27.7 us; the launch traced here: 27.4 us
  blocking collectives  9.3 us (34%)
  starting transfers between devices  7.42 us (27%)
  waiting for transfers between devices  5.38 us (19%)
  Pallas kernels  3.89 us (14%)
  between operations  0.69 us (2%)
  local copies, waits for them, and re-layouts  0.68 us (2%)
    all_to_all x1, blocking collectives, exchange(): return lax.all_to_all(array, ('grp', 'blk'), 0, 0, tiled=True)  9.3 us
    all_to_all x1, starting transfers between devices, exchange(): return lax.all_to_all(array, ('grp', 'blk'), 0, 0, tiled=True)  6.97 us
    all_to_all x1, waiting for transfers between devices, exchange(): return lax.all_to_all(array, ('grp', 'blk'), 0, 0, tiled=True)  5.38 us
    pallas_call x3, Pallas kernels, call(): pl.pallas_call(kernel, out_shape=outs, in_specs=specs or [VMEM] * len(ope...  2.5 us
    pallas_call x1, Pallas kernels, local(): pl.pallas_call(fan_kernel, out_shape=[half(groups, KVH, chips, SHARE), ha...  1.4 us
    unnamed x2, local copies, waits for them, and re-layouts  0.68 us
  transfers between devices with their start and end apart: 2, of which 1 were waited for; matrix products, arithmetic and copies ran while one was open for 0% of the time, Pallas kernels for 8%

profile of v11, /device:TPU:0, one launch (start us, length us, event | category | flops | bytes accessed | tf_op | source)
XLA Modules:
  0.0 27.4 jit_solution(9086931606178361454)
XLA Ops:
  0.0 0.5 %collective-permute-start = (bf16[2,1,1024,128]{3,2,0,1:T(8,128)(2,1)}, bf16[2,1,1024,128]{3,2,0,1:T(8,128)(2,1)S(1)}, u32[]{:S(2)}, u32[]{:S(2)}) collective-permute-start(bf16[2,1,1024,128]{3,2,0,1:T(8,128)(2,1)} %bitcast.16), channel_id=1, source_target_pairs={{0,1},{1,0},{2,3},{3,2},{4,5},{5,4},{6,7},{7,6},{8,9},{9,8},{10,11... | collective-permute-start | bytes 1572872 | tf_op jit(solution)/shard_map/ppermute | solution.py:194
  0.5 1.4 %fan.1 = (bf16[2,4,2,16,128]{4,3,2,1,0:T(8,128)(2,1)}, bf16[4,16,128]{2,1,0:T(8,128)(2,1)S(1)}, bf16[2,1024,128]{2,1,0:T(8,128)(2,1)S(1)}, bf16[2048,128]{1,0:T(8,128)(2,1)S(1)}) custom-call(bf16[4,16,128]{2,1,0:T(8,128)(2,1)} %bitcast.18, bf16[2,1024,128]{2,1,0:T(8,128)(2,1)} %bitcast.17, bf16[2048,128]{1,0:T(8,128)(2,1)} %bitcast.15), custom_call_target="tpu_custom_call" | custom-call | tf_op jit(solution)/shard_map/fan/pallas_call | solution.py:203
  1.9 7.0 %all-to-all-start = ((bf16[32,8,128]{2,1,0:T(8,128)(2,1)}), bf16[32,8,128]{2,1,0:T(8,128)(2,1)S(1)}, u32[]{:S(2)}, u32[]{:S(2)}) async-start(bf16[32,8,128]{2,1,0:T(8,128)(2,1)} %bitcast.3), calls=%async_computation | async-start | bytes 131072 | tf_op jit(solution)/shard_map/all_to_all | solution.py:192
  9.5 0.0 copy-start
  9.5 0.7 %copy-done = bf16[1,2,4,128]{3,2,1,0:T(4,128)(2,1)S(1)} copy-done((bf16[1,2,4,128]{3,2,1,0:T(4,128)(2,1)S(1)}, bf16[1,2,4,128]{3,2,1,0:T(4,128)(2,1)}, u32[]{:S(2)}) %copy-start) | copy-done | bytes 2072
  10.2 0.7 %suffix.1 = (f32[64,128]{1,0:T(8,128)S(1)}, f32[64,128]{1,0:T(8,128)S(1)}) custom-call(s32[1]{0:T(128)S(6)} %copy.7.len_ref, bf16[8,128]{1,0:T(8,128)(2,1)S(1)} %bitcast.13, bf16[4,16,128]{2,1,0:T(8,128)(2,1)S(1)} %get-tuple-element.15.q_ref, bf16[2048,128]{1,0:T(8,128)(2,1)S(1)} %get-tuple-element.16.cache_ref), custom_call_target="tpu_custom_call" | custom-call | flops 70000000 | bytes 600000 | tf_op jit(solution)/shard_map/suffix/pallas_call | solution.py:164
  10.9 5.4 %all-to-all-done = bf16[32,8,128]{2,1,0:T(8,128)(2,1)S(1)} async-done(((bf16[32,8,128]{2,1,0:T(8,128)(2,1)}), bf16[32,8,128]{2,1,0:T(8,128)(2,1)S(1)}, u32[]{:S(2)}, u32[]{:S(2)}) %all-to-all-start) | async-done | bytes 65568 | tf_op jit(solution)/shard_map/all_to_all | solution.py:192
  16.2 0.0 collective-permute-done
  16.2 1.0 %prefix.1 = bf16[320,128]{1,0:T(8,128)(2,1)S(1)} custom-call(bf16[256,128]{1,0:T(8,128)(2,1)S(1)} %bitcast.12, bf16[2,1024,128]{2,1,0:T(8,128)(2,1)S(1)} %get-tuple-element.20.kv_ref, bf16[2,1024,128]{2,1,0:T(8,128)(2,1)S(1)} %bitcast.14), custom_call_target="tpu_custom_call" | custom-call | flops 402653184 | bytes 1600000 | tf_op jit(solution)/shard_map/prefix/pallas_call | solution.py:164
  17.3 9.3 %all_to_all.10 = bf16[32,5,2,128]{3,2,1,0:T(2,128)(2,1)S(1)} all-to-all(bf16[32,5,2,128]{3,2,1,0:T(2,128)(2,1)S(1)} %bitcast.11), channel_id=1, replica_groups=mesh['grp'=2,'blk'=16] {'grp','blk'}, dimensions={0} | all-to-all | bytes 163840 | tf_op jit(solution)/shard_map/all_to_all | solution.py:192
  26.6 0.8 %merge.1 = bf16[1,64,128]{2,1,0:T(8,128)(2,1)} custom-call(bf16[320,128]{1,0:T(8,128)(2,1)S(1)} %bitcast.10, f32[64,128]{1,0:T(8,128)S(1)} %get-tuple-element.21.suffix_ref, f32[64,128]{1,0:T(8,128)S(1)} %get-tuple-element.22.lse_ref), custom_call_target="tpu_custom_call" | custom-call | tf_op jit(solution)/shard_map/merge/pallas_call | solution.py:164
Async XLA Ops:
  0.0 16.2 %collective-permute-start = (bf16[2,1,1024,128]{3,2,0,1:T(8,128)(2,1)}, bf16[2,1,1024,128]{3,2,0,1:T(8,128)(2,1)S(1)}, u32[]{:S(2)}, u32[]{:S(2)}) collective-permute-start(bf16[2,1,1024,128]{3,2,0,1:T(8,128)(2,1)} %bitcast.16), channel_id=1, source_target_pairs={{0,1},{1,0},{2,3},{3,2},{4,5},{5,4},{6,7},{7,6},{8,9},{9,8},{10,11... | collective-permute-start | bytes 1572872 | tf_op jit(solution)/shard_map/ppermute | solution.py:194
  1.9 14.4 %all-to-all-start = ((bf16[32,8,128]{2,1,0:T(8,128)(2,1)}), bf16[32,8,128]{2,1,0:T(8,128)(2,1)S(1)}, u32[]{:S(2)}, u32[]{:S(2)}) async-start(bf16[32,8,128]{2,1,0:T(8,128)(2,1)} %bitcast.3), calls=%async_computation | async-start | bytes 131072 | tf_op jit(solution)/shard_map/all_to_all | solution.py:192
  9.5 0.7 %copy-start = (bf16[1,2,4,128]{3,2,1,0:T(4,128)(2,1)S(1)}, bf16[1,2,4,128]{3,2,1,0:T(4,128)(2,1)}, u32[]{:S(2)}) copy-start(bf16[1,2,4,128]{3,2,1,0:T(4,128)(2,1)} %param.8) | copy-start | bytes 6148

commit v12 on v11

--- a/solution.py
+++ b/solution.py
@@ -15,7 +15,7 @@
 SCALE2 = HD ** (-0.5) * math.log2(math.e)
 VMEM = pl.BlockSpec(memory_space=pltpu.VMEM)
 ROWS = 256
-CHUNK = 512
+CHUNK = 1024
 CORES = 2
 HALF = SHARE // CORES
 MESSAGE = HALF + 2
@@ -36,14 +36,19 @@
     return jnp.log(x) * math.log2(math.e)
 
 
-def pack_stats(x):
+def compact(x):
+    x = x.reshape(-1, HALF, HD)
+    mine = lax.broadcasted_iota(jnp.int32, x.shape, 2) // LANES == lax.broadcasted_iota(jnp.int32, x.shape, 1)
+    return jnp.sum(jnp.where(mine, x, 0.0), axis=1)
+
+
+def pieces_of(x):
     hi = x.astype(jnp.bfloat16).astype(jnp.float32)
     rest = x - hi
     mid = rest.astype(jnp.bfloat16).astype(jnp.float32)
     low = rest - mid
-    row = lax.broadcasted_iota(jnp.int32, x.shape, 1)
-    lane = lax.broadcasted_iota(jnp.int32, x.shape, 2) - row * LANES
-    return jnp.sum(jnp.where(lane == 0, hi, jnp.where(lane == 1, mid, jnp.where(lane == 2, low, 0.0))), axis=1)
+    lane = lax.broadcasted_iota(jnp.int32, x.shape, 1) % LANES
+    return jnp.where(lane == 0, hi, jnp.where(lane == 1, mid, jnp.where(lane == 2, low, 0.0)))
 
 
 def unpack_stats(rows):
@@ -77,7 +82,8 @@
         total = both[:, HD:]
         result = both[:, :HD] / total
         slots = ROWS // HALF
-        stats = pack_stats((best * SCALE2 + log2(total)).reshape(slots, HALF, HD))
+        best = jnp.broadcast_to(best, total.shape)
+        stats = pieces_of(compact(best) * SCALE2 + log2(compact(total)))
         empty = jnp.zeros((1, HD), jnp.float32)
         pieces = []
         for slot in range(slots):

time: 27.7 us -> 27.7 us (level)
  no operation moved by 1% of the time
where the time goes in v12:
time: 27.7 us; the launch traced here: 27.4 us
  blocking collectives  9.3 us (34%)
  starting transfers between devices  7.42 us (27%)
  waiting for transfers between devices  5.38 us (19%)
  Pallas kernels  3.93 us (14%)
  between operations  0.69 us (2%)
  local copies, waits for them, and re-layouts  0.68 us (2%)
    all_to_all x1, blocking collectives, exchange(): return lax.all_to_all(array, ('grp', 'blk'), 0, 0, tiled=True)  9.3 us
    all_to_all x1, starting transfers between devices, exchange(): return lax.all_to_all(array, ('grp', 'blk'), 0, 0, tiled=True)  6.97 us
    all_to_all x1, waiting for transfers between devices, exchange(): return lax.all_to_all(array, ('grp', 'blk'), 0, 0, tiled=True)  5.38 us
    pallas_call x3, Pallas kernels, call(): pl.pallas_call(kernel, out_shape=outs, in_specs=specs or [VMEM] * len(ope...  2.54 us
    pallas_call x1, Pallas kernels, local(): pl.pallas_call(fan_kernel, out_shape=[half(groups, KVH, chips, SHARE), ha...  1.4 us
    unnamed x2, local copies, waits for them, and re-layouts  0.68 us
  transfers between devices with their start and end apart: 2, of which 1 were waited for; matrix products, arithmetic and copies ran while one was open for 0% of the time, Pallas kernels for 8%

profile of v12, /device:TPU:0, one launch (start us, length us, event | category | flops | bytes accessed | tf_op | source)
XLA Modules:
  0.0 27.4 jit_solution(547817764348121113)
XLA Ops:
  0.0 0.5 %collective-permute-start = (bf16[2,1,1024,128]{3,2,0,1:T(8,128)(2,1)}, bf16[2,1,1024,128]{3,2,0,1:T(8,128)(2,1)S(1)}, u32[]{:S(2)}, u32[]{:S(2)}) collective-permute-start(bf16[2,1,1024,128]{3,2,0,1:T(8,128)(2,1)} %bitcast.16), channel_id=1, source_target_pairs={{0,1},{1,0},{2,3},{3,2},{4,5},{5,4},{6,7},{7,6},{8,9},{9,8},{10,11... | collective-permute-start | bytes 1572872 | tf_op jit(solution)/shard_map/ppermute | solution.py:200
  0.5 1.4 %fan.1 = (bf16[2,4,2,16,128]{4,3,2,1,0:T(8,128)(2,1)}, bf16[4,16,128]{2,1,0:T(8,128)(2,1)S(1)}, bf16[2,1024,128]{2,1,0:T(8,128)(2,1)S(1)}, bf16[2048,128]{1,0:T(8,128)(2,1)S(1)}) custom-call(bf16[4,16,128]{2,1,0:T(8,128)(2,1)} %bitcast.18, bf16[2,1024,128]{2,1,0:T(8,128)(2,1)} %bitcast.17, bf16[2048,128]{1,0:T(8,128)(2,1)} %bitcast.15), custom_call_target="tpu_custom_call" | custom-call | tf_op jit(solution)/shard_map/fan/pallas_call | solution.py:209
  1.9 7.0 %all-to-all-start = ((bf16[32,8,128]{2,1,0:T(8,128)(2,1)}), bf16[32,8,128]{2,1,0:T(8,128)(2,1)S(1)}, u32[]{:S(2)}, u32[]{:S(2)}) async-start(bf16[32,8,128]{2,1,0:T(8,128)(2,1)} %bitcast.3), calls=%async_computation | async-start | bytes 131072 | tf_op jit(solution)/shard_map/all_to_all | solution.py:198
  9.5 0.0 copy-start
  9.5 0.7 %copy-done = bf16[1,2,4,128]{3,2,1,0:T(4,128)(2,1)S(1)} copy-done((bf16[1,2,4,128]{3,2,1,0:T(4,128)(2,1)S(1)}, bf16[1,2,4,128]{3,2,1,0:T(4,128)(2,1)}, u32[]{:S(2)}) %copy-start) | copy-done | bytes 2072
  10.2 0.7 %suffix.1 = (f32[64,128]{1,0:T(8,128)S(1)}, f32[64,128]{1,0:T(8,128)S(1)}) custom-call(s32[1]{0:T(128)S(6)} %copy.7.len_ref, bf16[8,128]{1,0:T(8,128)(2,1)S(1)} %bitcast.13, bf16[4,16,128]{2,1,0:T(8,128)(2,1)S(1)} %get-tuple-element.15.q_ref, bf16[2048,128]{1,0:T(8,128)(2,1)S(1)} %get-tuple-element.16.cache_ref), custom_call_target="tpu_custom_call" | custom-call | flops 70000000 | bytes 600000 | tf_op jit(solution)/shard_map/suffix/pallas_call | solution.py:170
  10.9 5.4 %all-to-all-done = bf16[32,8,128]{2,1,0:T(8,128)(2,1)S(1)} async-done(((bf16[32,8,128]{2,1,0:T(8,128)(2,1)}), bf16[32,8,128]{2,1,0:T(8,128)(2,1)S(1)}, u32[]{:S(2)}, u32[]{:S(2)}) %all-to-all-start) | async-done | bytes 65568 | tf_op jit(solution)/shard_map/all_to_all | solution.py:198
  16.2 0.0 collective-permute-done
  16.2 1.1 %prefix.1 = bf16[320,128]{1,0:T(8,128)(2,1)S(1)} custom-call(bf16[256,128]{1,0:T(8,128)(2,1)S(1)} %bitcast.12, bf16[2,1024,128]{2,1,0:T(8,128)(2,1)S(1)} %get-tuple-element.20.kv_ref, bf16[2,1024,128]{2,1,0:T(8,128)(2,1)S(1)} %bitcast.14), custom_call_target="tpu_custom_call" | custom-call | flops 402653184 | bytes 1600000 | tf_op jit(solution)/shard_map/prefix/pallas_call | solution.py:170
  17.3 9.3 %all_to_all.10 = bf16[32,5,2,128]{3,2,1,0:T(2,128)(2,1)S(1)} all-to-all(bf16[32,5,2,128]{3,2,1,0:T(2,128)(2,1)S(1)} %bitcast.11), channel_id=1, replica_groups=mesh['grp'=2,'blk'=16] {'grp','blk'}, dimensions={0} | all-to-all | bytes 163840 | tf_op jit(solution)/shard_map/all_to_all | solution.py:198
  26.6 0.8 %merge.1 = bf16[1,64,128]{2,1,0:T(8,128)(2,1)} custom-call(bf16[320,128]{1,0:T(8,128)(2,1)S(1)} %bitcast.10, f32[64,128]{1,0:T(8,128)S(1)} %get-tuple-element.21.suffix_ref, f32[64,128]{1,0:T(8,128)S(1)} %get-tuple-element.22.lse_ref), custom_call_target="tpu_custom_call" | custom-call | tf_op jit(solution)/shard_map/merge/pallas_call | solution.py:170
Async XLA Ops:
  0.0 16.2 %collective-permute-start = (bf16[2,1,1024,128]{3,2,0,1:T(8,128)(2,1)}, bf16[2,1,1024,128]{3,2,0,1:T(8,128)(2,1)S(1)}, u32[]{:S(2)}, u32[]{:S(2)}) collective-permute-start(bf16[2,1,1024,128]{3,2,0,1:T(8,128)(2,1)} %bitcast.16), channel_id=1, source_target_pairs={{0,1},{1,0},{2,3},{3,2},{4,5},{5,4},{6,7},{7,6},{8,9},{9,8},{10,11... | collective-permute-start | bytes 1572872 | tf_op jit(solution)/shard_map/ppermute | solution.py:200
  1.9 14.4 %all-to-all-start = ((bf16[32,8,128]{2,1,0:T(8,128)(2,1)}), bf16[32,8,128]{2,1,0:T(8,128)(2,1)S(1)}, u32[]{:S(2)}, u32[]{:S(2)}) async-start(bf16[32,8,128]{2,1,0:T(8,128)(2,1)} %bitcast.3), calls=%async_computation | async-start | bytes 131072 | tf_op jit(solution)/shard_map/all_to_all | solution.py:198
  9.5 0.7 %copy-start = (bf16[1,2,4,128]{3,2,1,0:T(4,128)(2,1)S(1)}, bf16[1,2,4,128]{3,2,1,0:T(4,128)(2,1)}, u32[]{:S(2)}) copy-start(bf16[1,2,4,128]{3,2,1,0:T(4,128)(2,1)} %param.8) | copy-start | bytes 6148

commit v13 on v12

--- a/solution.py
+++ b/solution.py
@@ -15,7 +15,7 @@
 SCALE2 = HD ** (-0.5) * math.log2(math.e)
 VMEM = pl.BlockSpec(memory_space=pltpu.VMEM)
 ROWS = 256
-CHUNK = 1024
+CHUNK = 512
 CORES = 2
 HALF = SHARE // CORES
 MESSAGE = HALF + 2

time: 27.7 us -> 27.7 us (level)
  no operation moved by 1% of the time
where the time goes in v13:
time: 27.7 us; the launch traced here: 27.4 us
  blocking collectives  9.3 us (34%)
  starting transfers between devices  7.42 us (27%)
  waiting for transfers between devices  5.38 us (19%)
  Pallas kernels  3.92 us (14%)
  between operations  0.69 us (2%)
  local copies, waits for them, and re-layouts  0.68 us (2%)
    all_to_all x1, blocking collectives, exchange(): return lax.all_to_all(array, ('grp', 'blk'), 0, 0, tiled=True)  9.3 us
    all_to_all x1, starting transfers between devices, exchange(): return lax.all_to_all(array, ('grp', 'blk'), 0, 0, tiled=True)  6.97 us
    all_to_all x1, waiting for transfers between devices, exchange(): return lax.all_to_all(array, ('grp', 'blk'), 0, 0, tiled=True)  5.38 us
    pallas_call x3, Pallas kernels, call(): pl.pallas_call(kernel, out_shape=outs, in_specs=specs or [VMEM] * len(ope...  2.52 us
    pallas_call x1, Pallas kernels, local(): pl.pallas_call(fan_kernel, out_shape=[half(groups, KVH, chips, SHARE), ha...  1.4 us
    unnamed x2, local copies, waits for them, and re-layouts  0.68 us
  transfers between devices with their start and end apart: 2, of which 1 were waited for; matrix products, arithmetic and copies ran while one was open for 0% of the time, Pallas kernels for 8%

profile of v13, /device:TPU:0, one launch (start us, length us, event | category | flops | bytes accessed | tf_op | source)
XLA Modules:
  0.0 27.4 jit_solution(5638080318456521026)
XLA Ops:
  0.0 0.5 %collective-permute-start = (bf16[2,1,1024,128]{3,2,0,1:T(8,128)(2,1)}, bf16[2,1,1024,128]{3,2,0,1:T(8,128)(2,1)S(1)}, u32[]{:S(2)}, u32[]{:S(2)}) collective-permute-start(bf16[2,1,1024,128]{3,2,0,1:T(8,128)(2,1)} %bitcast.16), channel_id=1, source_target_pairs={{0,1},{1,0},{2,3},{3,2},{4,5},{5,4},{6,7},{7,6},{8,9},{9,8},{10,11... | collective-permute-start | bytes 1572872 | tf_op jit(solution)/shard_map/ppermute | solution.py:200
  0.5 1.4 %fan.1 = (bf16[2,4,2,16,128]{4,3,2,1,0:T(8,128)(2,1)}, bf16[4,16,128]{2,1,0:T(8,128)(2,1)S(1)}, bf16[2,1024,128]{2,1,0:T(8,128)(2,1)S(1)}, bf16[2048,128]{1,0:T(8,128)(2,1)S(1)}) custom-call(bf16[4,16,128]{2,1,0:T(8,128)(2,1)} %bitcast.18, bf16[2,1024,128]{2,1,0:T(8,128)(2,1)} %bitcast.17, bf16[2048,128]{1,0:T(8,128)(2,1)} %bitcast.15), custom_call_target="tpu_custom_call" | custom-call | tf_op jit(solution)/shard_map/fan/pallas_call | solution.py:209
  1.9 7.0 %all-to-all-start = ((bf16[32,8,128]{2,1,0:T(8,128)(2,1)}), bf16[32,8,128]{2,1,0:T(8,128)(2,1)S(1)}, u32[]{:S(2)}, u32[]{:S(2)}) async-start(bf16[32,8,128]{2,1,0:T(8,128)(2,1)} %bitcast.3), calls=%async_computation | async-start | bytes 131072 | tf_op jit(solution)/shard_map/all_to_all | solution.py:198
  9.5 0.0 copy-start
  9.5 0.7 %copy-done = bf16[1,2,4,128]{3,2,1,0:T(4,128)(2,1)S(1)} copy-done((bf16[1,2,4,128]{3,2,1,0:T(4,128)(2,1)S(1)}, bf16[1,2,4,128]{3,2,1,0:T(4,128)(2,1)}, u32[]{:S(2)}) %copy-start) | copy-done | bytes 2072
  10.2 0.7 %suffix.1 = (f32[64,128]{1,0:T(8,128)S(1)}, f32[64,128]{1,0:T(8,128)S(1)}) custom-call(s32[1]{0:T(128)S(6)} %copy.7.len_ref, bf16[8,128]{1,0:T(8,128)(2,1)S(1)} %bitcast.13, bf16[4,16,128]{2,1,0:T(8,128)(2,1)S(1)} %get-tuple-element.15.q_ref, bf16[2048,128]{1,0:T(8,128)(2,1)S(1)} %get-tuple-element.16.cache_ref), custom_call_target="tpu_custom_call" | custom-call | flops 70000000 | bytes 600000 | tf_op jit(solution)/shard_map/suffix/pallas_call | solution.py:170
  10.9 5.4 %all-to-all-done = bf16[32,8,128]{2,1,0:T(8,128)(2,1)S(1)} async-done(((bf16[32,8,128]{2,1,0:T(8,128)(2,1)}), bf16[32,8,128]{2,1,0:T(8,128)(2,1)S(1)}, u32[]{:S(2)}, u32[]{:S(2)}) %all-to-all-start) | async-done | bytes 65568 | tf_op jit(solution)/shard_map/all_to_all | solution.py:198
  16.2 0.0 collective-permute-done
  16.2 1.0 %prefix.1 = bf16[320,128]{1,0:T(8,128)(2,1)S(1)} custom-call(bf16[256,128]{1,0:T(8,128)(2,1)S(1)} %bitcast.12, bf16[2,1024,128]{2,1,0:T(8,128)(2,1)S(1)} %get-tuple-element.20.kv_ref, bf16[2,1024,128]{2,1,0:T(8,128)(2,1)S(1)} %bitcast.14), custom_call_target="tpu_custom_call" | custom-call | flops 402653184 | bytes 1600000 | tf_op jit(solution)/shard_map/prefix/pallas_call | solution.py:170
  17.3 9.3 %all_to_all.10 = bf16[32,5,2,128]{3,2,1,0:T(2,128)(2,1)S(1)} all-to-all(bf16[32,5,2,128]{3,2,1,0:T(2,128)(2,1)S(1)} %bitcast.11), channel_id=1, replica_groups=mesh['grp'=2,'blk'=16] {'grp','blk'}, dimensions={0} | all-to-all | bytes 163840 | tf_op jit(solution)/shard_map/all_to_all | solution.py:198
  26.6 0.8 %merge.1 = bf16[1,64,128]{2,1,0:T(8,128)(2,1)} custom-call(bf16[320,128]{1,0:T(8,128)(2,1)S(1)} %bitcast.10, f32[64,128]{1,0:T(8,128)S(1)} %get-tuple-element.21.suffix_ref, f32[64,128]{1,0:T(8,128)S(1)} %get-tuple-element.22.lse_ref), custom_call_target="tpu_custom_call" | custom-call | tf_op jit(solution)/shard_map/merge/pallas_call | solution.py:170
Async XLA Ops:
  0.0 16.2 %collective-permute-start = (bf16[2,1,1024,128]{3,2,0,1:T(8,128)(2,1)}, bf16[2,1,1024,128]{3,2,0,1:T(8,128)(2,1)S(1)}, u32[]{:S(2)}, u32[]{:S(2)}) collective-permute-start(bf16[2,1,1024,128]{3,2,0,1:T(8,128)(2,1)} %bitcast.16), channel_id=1, source_target_pairs={{0,1},{1,0},{2,3},{3,2},{4,5},{5,4},{6,7},{7,6},{8,9},{9,8},{10,11... | collective-permute-start | bytes 1572872 | tf_op jit(solution)/shard_map/ppermute | solution.py:200
  1.9 14.4 %all-to-all-start = ((bf16[32,8,128]{2,1,0:T(8,128)(2,1)}), bf16[32,8,128]{2,1,0:T(8,128)(2,1)S(1)}, u32[]{:S(2)}, u32[]{:S(2)}) async-start(bf16[32,8,128]{2,1,0:T(8,128)(2,1)} %bitcast.3), calls=%async_computation | async-start | bytes 131072 | tf_op jit(solution)/shard_map/all_to_all | solution.py:198
  9.5 0.7 %copy-start = (bf16[1,2,4,128]{3,2,1,0:T(4,128)(2,1)S(1)}, bf16[1,2,4,128]{3,2,1,0:T(4,128)(2,1)}, u32[]{:S(2)}) copy-start(bf16[1,2,4,128]{3,2,1,0:T(4,128)(2,1)} %param.8) | copy-start | bytes 6148

commit v14 on v11

--- a/solution.py
+++ b/solution.py
@@ -15,7 +15,8 @@
 SCALE2 = HD ** (-0.5) * math.log2(math.e)
 VMEM = pl.BlockSpec(memory_space=pltpu.VMEM)
 ROWS = 256
-CHUNK = 512
+CHUNK = 256
+AHEAD = 2
 CORES = 2
 HALF = SHARE // CORES
 MESSAGE = HALF + 2
@@ -63,11 +64,11 @@
             return dot_nt(rows, ref[0, first : first + CHUNK])
 
         parts = []
-        ahead = score(*chunks[0])
+        ahead = [score(*chunk) for chunk in chunks[:AHEAD]]
         for index, (ref, first) in enumerate(chunks):
-            scores = ahead
-            if index + 1 < len(chunks):
-                ahead = score(*chunks[index + 1])
+            if index + AHEAD < len(chunks):
+                ahead.append(score(*chunks[index + AHEAD]))
+            scores = ahead.pop(0)
             best = jnp.max(scores, axis=1, keepdims=True)
             weight = jnp.exp2((scores - best) * SCALE2).astype(jnp.bfloat16)
             values = ref[1, first : first + CHUNK]

time: 27.7 us -> 27.7 us (level)
  no operation moved by 1% of the time
where the time goes in v14:
time: 27.7 us; the launch traced here: 27.4 us
  blocking collectives  9.3 us (34%)
  starting transfers between devices  7.42 us (27%)
  waiting for transfers between devices  5.38 us (19%)
  Pallas kernels  3.98 us (14%)
  between operations  0.69 us (2%)
  local copies, waits for them, and re-layouts  0.68 us (2%)
    all_to_all x1, blocking collectives, exchange(): return lax.all_to_all(array, ('grp', 'blk'), 0, 0, tiled=True)  9.3 us
    all_to_all x1, starting transfers between devices, exchange(): return lax.all_to_all(array, ('grp', 'blk'), 0, 0, tiled=True)  6.97 us
    all_to_all x1, waiting for transfers between devices, exchange(): return lax.all_to_all(array, ('grp', 'blk'), 0, 0, tiled=True)  5.38 us
    pallas_call x3, Pallas kernels, call(): pl.pallas_call(kernel, out_shape=outs, in_specs=specs or [VMEM] * len(ope...  2.58 us
    pallas_call x1, Pallas kernels, local(): pl.pallas_call(fan_kernel, out_shape=[half(groups, KVH, chips, SHARE), ha...  1.4 us
    unnamed x2, local copies, waits for them, and re-layouts  0.68 us
  transfers between devices with their start and end apart: 2, of which 1 were waited for; matrix products, arithmetic and copies ran while one was open for 0% of the time, Pallas kernels for 8%

profile of v14, /device:TPU:0, one launch (start us, length us, event | category | flops | bytes accessed | tf_op | source)
XLA Modules:
  0.0 27.4 jit_solution(6472998501853578203)
XLA Ops:
  0.0 0.5 %collective-permute-start = (bf16[2,1,1024,128]{3,2,0,1:T(8,128)(2,1)}, bf16[2,1,1024,128]{3,2,0,1:T(8,128)(2,1)S(1)}, u32[]{:S(2)}, u32[]{:S(2)}) collective-permute-start(bf16[2,1,1024,128]{3,2,0,1:T(8,128)(2,1)} %bitcast.16), channel_id=1, source_target_pairs={{0,1},{1,0},{2,3},{3,2},{4,5},{5,4},{6,7},{7,6},{8,9},{9,8},{10,11... | collective-permute-start | bytes 1572872 | tf_op jit(solution)/shard_map/ppermute | solution.py:195
  0.5 1.4 %fan.1 = (bf16[2,4,2,16,128]{4,3,2,1,0:T(8,128)(2,1)}, bf16[4,16,128]{2,1,0:T(8,128)(2,1)S(1)}, bf16[2,1024,128]{2,1,0:T(8,128)(2,1)S(1)}, bf16[2048,128]{1,0:T(8,128)(2,1)S(1)}) custom-call(bf16[4,16,128]{2,1,0:T(8,128)(2,1)} %bitcast.18, bf16[2,1024,128]{2,1,0:T(8,128)(2,1)} %bitcast.17, bf16[2048,128]{1,0:T(8,128)(2,1)} %bitcast.15), custom_call_target="tpu_custom_call" | custom-call | tf_op jit(solution)/shard_map/fan/pallas_call | solution.py:204
  1.9 7.0 %all-to-all-start = ((bf16[32,8,128]{2,1,0:T(8,128)(2,1)}), bf16[32,8,128]{2,1,0:T(8,128)(2,1)S(1)}, u32[]{:S(2)}, u32[]{:S(2)}) async-start(bf16[32,8,128]{2,1,0:T(8,128)(2,1)} %bitcast.3), calls=%async_computation | async-start | bytes 131072 | tf_op jit(solution)/shard_map/all_to_all | solution.py:193
  9.5 0.0 copy-start
  9.5 0.7 %copy-done = bf16[1,2,4,128]{3,2,1,0:T(4,128)(2,1)S(1)} copy-done((bf16[1,2,4,128]{3,2,1,0:T(4,128)(2,1)S(1)}, bf16[1,2,4,128]{3,2,1,0:T(4,128)(2,1)}, u32[]{:S(2)}) %copy-start) | copy-done | bytes 2072
  10.2 0.7 %suffix.1 = (f32[64,128]{1,0:T(8,128)S(1)}, f32[64,128]{1,0:T(8,128)S(1)}) custom-call(s32[1]{0:T(128)S(6)} %copy.7.len_ref, bf16[8,128]{1,0:T(8,128)(2,1)S(1)} %bitcast.13, bf16[4,16,128]{2,1,0:T(8,128)(2,1)S(1)} %get-tuple-element.15.q_ref, bf16[2048,128]{1,0:T(8,128)(2,1)S(1)} %get-tuple-element.16.cache_ref), custom_call_target="tpu_custom_call" | custom-call | flops 70000000 | bytes 600000 | tf_op jit(solution)/shard_map/suffix/pallas_call | solution.py:165
  10.9 5.4 %all-to-all-done = bf16[32,8,128]{2,1,0:T(8,128)(2,1)S(1)} async-done(((bf16[32,8,128]{2,1,0:T(8,128)(2,1)}), bf16[32,8,128]{2,1,0:T(8,128)(2,1)S(1)}, u32[]{:S(2)}, u32[]{:S(2)}) %all-to-all-start) | async-done | bytes 65568 | tf_op jit(solution)/shard_map/all_to_all | solution.py:193
  16.2 0.0 collective-permute-done
  16.2 1.1 %prefix.1 = bf16[320,128]{1,0:T(8,128)(2,1)S(1)} custom-call(bf16[256,128]{1,0:T(8,128)(2,1)S(1)} %bitcast.12, bf16[2,1024,128]{2,1,0:T(8,128)(2,1)S(1)} %get-tuple-element.20.kv_ref, bf16[2,1024,128]{2,1,0:T(8,128)(2,1)S(1)} %bitcast.14), custom_call_target="tpu_custom_call" | custom-call | flops 402653184 | bytes 1600000 | tf_op jit(solution)/shard_map/prefix/pallas_call | solution.py:165
  17.3 9.3 %all_to_all.10 = bf16[32,5,2,128]{3,2,1,0:T(2,128)(2,1)S(1)} all-to-all(bf16[32,5,2,128]{3,2,1,0:T(2,128)(2,1)S(1)} %bitcast.11), channel_id=1, replica_groups=mesh['grp'=2,'blk'=16] {'grp','blk'}, dimensions={0} | all-to-all | bytes 163840 | tf_op jit(solution)/shard_map/all_to_all | solution.py:193
  26.6 0.8 %merge.1 = bf16[1,64,128]{2,1,0:T(8,128)(2,1)} custom-call(bf16[320,128]{1,0:T(8,128)(2,1)S(1)} %bitcast.10, f32[64,128]{1,0:T(8,128)S(1)} %get-tuple-element.21.suffix_ref, f32[64,128]{1,0:T(8,128)S(1)} %get-tuple-element.22.lse_ref), custom_call_target="tpu_custom_call" | custom-call | tf_op jit(solution)/shard_map/merge/pallas_call | solution.py:165
Async XLA Ops:
  0.0 16.2 %collective-permute-start = (bf16[2,1,1024,128]{3,2,0,1:T(8,128)(2,1)}, bf16[2,1,1024,128]{3,2,0,1:T(8,128)(2,1)S(1)}, u32[]{:S(2)}, u32[]{:S(2)}) collective-permute-start(bf16[2,1,1024,128]{3,2,0,1:T(8,128)(2,1)} %bitcast.16), channel_id=1, source_target_pairs={{0,1},{1,0},{2,3},{3,2},{4,5},{5,4},{6,7},{7,6},{8,9},{9,8},{10,11... | collective-permute-start | bytes 1572872 | tf_op jit(solution)/shard_map/ppermute | solution.py:195
  1.9 14.4 %all-to-all-start = ((bf16[32,8,128]{2,1,0:T(8,128)(2,1)}), bf16[32,8,128]{2,1,0:T(8,128)(2,1)S(1)}, u32[]{:S(2)}, u32[]{:S(2)}) async-start(bf16[32,8,128]{2,1,0:T(8,128)(2,1)} %bitcast.3), calls=%async_computation | async-start | bytes 131072 | tf_op jit(solution)/shard_map/all_to_all | solution.py:193
  9.5 0.7 %copy-start = (bf16[1,2,4,128]{3,2,1,0:T(4,128)(2,1)S(1)}, bf16[1,2,4,128]{3,2,1,0:T(4,128)(2,1)}, u32[]{:S(2)}) copy-start(bf16[1,2,4,128]{3,2,1,0:T(4,128)(2,1)} %param.8) | copy-start | bytes 6148

commit v15 on v11

--- a/solution.py
+++ b/solution.py
@@ -191,7 +191,6 @@
     def exchange(array):
         return lax.all_to_all(array, ("grp", "blk"), 0, 0, tiled=True)
 
-    other = lax.ppermute(prefix_kv, "blk", [(i, i ^ 1) for i in range(members)]).reshape(2, span, HD)
     bound = [
         pltpu.with_memory_space_constraint(array, pltpu.HBM)
         for array in (
@@ -210,6 +209,7 @@
         compiler_params=pltpu.CompilerParams(vmem_limit_bytes=LIMIT),
     )(*bound)
     arrived = exchange(outgoing.reshape(devices, HALF, HD)).reshape(devices * HALF, HD)
+    other = lax.ppermute(kv, "blk", [(i, i ^ 1) for i in range(members)])
     suffix = call(
         suffix_kernel,
         "suffix",

time: 27.7 us -> 27.7 us (level)
  transfers between devices with their start and end apart: 2 -> 2, of which waited for: 1 -> 1; matrix products, arithmetic and copies ran while one was open for 0% -> 0% of each run, Pallas kernels for 8% -> 3%
where the time goes in v15:
time: 27.7 us; the launch traced here: 27.4 us
  blocking collectives  9.3 us (34%)
  starting transfers between devices  7.48 us (27%)
  waiting for transfers between devices  5.38 us (19%)
  Pallas kernels  3.89 us (14%)
  between operations  0.69 us (2%)
  local copies, waits for them, and re-layouts  0.68 us (2%)
    all_to_all x1, blocking collectives, exchange(): return lax.all_to_all(array, ('grp', 'blk'), 0, 0, tiled=True)  9.3 us
    all_to_all x1, starting transfers between devices, exchange(): return lax.all_to_all(array, ('grp', 'blk'), 0, 0, tiled=True)  6.96 us
    all_to_all x1, waiting for transfers between devices, exchange(): return lax.all_to_all(array, ('grp', 'blk'), 0, 0, tiled=True)  5.38 us
    pallas_call x3, Pallas kernels, call(): pl.pallas_call(kernel, out_shape=outs, in_specs=specs or [VMEM] * len(ope...  2.5 us
    pallas_call x1, Pallas kernels, local(): pl.pallas_call(fan_kernel, out_shape=[half(groups, KVH, chips, SHARE), ha...  1.4 us
    unnamed x2, local copies, waits for them, and re-layouts  0.68 us
  transfers between devices with their start and end apart: 2, of which 1 were waited for; matrix products, arithmetic and copies ran while one was open for 0% of the time, Pallas kernels for 3%

profile of v15, /device:TPU:0, one launch (start us, length us, event | category | flops | bytes accessed | tf_op | source)
XLA Modules:
  0.0 27.4 jit_solution(10208209892010755660)
XLA Ops:
  0.0 1.4 %fan.1 = (bf16[2,4,2,16,128]{4,3,2,1,0:T(8,128)(2,1)}, bf16[4,16,128]{2,1,0:T(8,128)(2,1)S(1)}, bf16[2,1024,128]{2,1,0:T(8,128)(2,1)S(1)}, bf16[2048,128]{1,0:T(8,128)(2,1)S(1)}) custom-call(bf16[4,16,128]{2,1,0:T(8,128)(2,1)} %bitcast.14, bf16[2,1024,128]{2,1,0:T(8,128)(2,1)} %bitcast.12, bf16[2048,128]{1,0:T(8,128)(2,1)} %bitcast.13), custom_call_target="tpu_custom_call" | custom-call | tf_op jit(solution)/shard_map/fan/pallas_call | solution.py:202
  1.4 0.5 %collective-permute-start = (bf16[2,1024,128]{2,1,0:T(8,128)(2,1)S(1)}, bf16[2,1024,128]{2,1,0:T(8,128)(2,1)S(1)}, u32[]{:S(2)}, u32[]{:S(2)}) collective-permute-start(bf16[2,1024,128]{2,1,0:T(8,128)(2,1)S(1)} %get-tuple-element.20.kv_ref), channel_id=1, source_target_pairs={{0,1},{1,0},{2,3},{3,2},{4,5},{5,4},{6,7},{7,6},{8,9},{9,8},{10,11... | collective-permute-start | bytes 1572872 | tf_op jit(solution)/shard_map/ppermute | solution.py:212
  1.9 7.0 %all-to-all-start = ((bf16[32,8,128]{2,1,0:T(8,128)(2,1)}), bf16[32,8,128]{2,1,0:T(8,128)(2,1)S(1)}, u32[]{:S(2)}, u32[]{:S(2)}) async-start(bf16[32,8,128]{2,1,0:T(8,128)(2,1)} %bitcast.3), calls=%async_computation | async-start | bytes 131072 | tf_op jit(solution)/shard_map/all_to_all | solution.py:192
  9.5 0.0 copy-start
  9.5 0.7 %copy-done = bf16[1,2,4,128]{3,2,1,0:T(4,128)(2,1)S(1)} copy-done((bf16[1,2,4,128]{3,2,1,0:T(4,128)(2,1)S(1)}, bf16[1,2,4,128]{3,2,1,0:T(4,128)(2,1)}, u32[]{:S(2)}) %copy-start) | copy-done | bytes 2072
  10.2 0.7 %suffix.1 = (f32[64,128]{1,0:T(8,128)S(1)}, f32[64,128]{1,0:T(8,128)S(1)}) custom-call(s32[1]{0:T(128)S(6)} %copy.6.len_ref, bf16[8,128]{1,0:T(8,128)(2,1)S(1)} %bitcast.11, bf16[4,16,128]{2,1,0:T(8,128)(2,1)S(1)} %get-tuple-element.15.q_ref, bf16[2048,128]{1,0:T(8,128)(2,1)S(1)} %get-tuple-element.16.cache_ref), custom_call_target="tpu_custom_call" | custom-call | flops 70000000 | bytes 600000 | tf_op jit(solution)/shard_map/suffix/pallas_call | solution.py:164
  10.9 5.4 %all-to-all-done = bf16[32,8,128]{2,1,0:T(8,128)(2,1)S(1)} async-done(((bf16[32,8,128]{2,1,0:T(8,128)(2,1)}), bf16[32,8,128]{2,1,0:T(8,128)(2,1)S(1)}, u32[]{:S(2)}, u32[]{:S(2)}) %all-to-all-start) | async-done | bytes 65568 | tf_op jit(solution)/shard_map/all_to_all | solution.py:192
  16.3 0.0 collective-permute-done.other_ref
  16.3 1.0 %prefix.1 = bf16[320,128]{1,0:T(8,128)(2,1)S(1)} custom-call(bf16[256,128]{1,0:T(8,128)(2,1)S(1)} %bitcast.10, bf16[2,1024,128]{2,1,0:T(8,128)(2,1)S(1)} %get-tuple-element.20.kv_ref, bf16[2,1024,128]{2,1,0:T(8,128)(2,1)S(1)} %collective-permute-done.other_ref), custom_call_target="tpu_custom_call" | custom-call | flops 402653184 | bytes 1600000 | tf_op jit(solution)/shard_map/prefix/pallas_call | solution.py:164
  17.3 9.3 %all_to_all.10 = bf16[32,5,2,128]{3,2,1,0:T(2,128)(2,1)S(1)} all-to-all(bf16[32,5,2,128]{3,2,1,0:T(2,128)(2,1)S(1)} %bitcast.9), channel_id=1, replica_groups=mesh['grp'=2,'blk'=16] {'grp','blk'}, dimensions={0} | all-to-all | bytes 163840 | tf_op jit(solution)/shard_map/all_to_all | solution.py:192
  26.6 0.8 %merge.1 = bf16[1,64,128]{2,1,0:T(8,128)(2,1)} custom-call(bf16[320,128]{1,0:T(8,128)(2,1)S(1)} %bitcast.8, f32[64,128]{1,0:T(8,128)S(1)} %get-tuple-element.21.suffix_ref, f32[64,128]{1,0:T(8,128)S(1)} %get-tuple-element.22.lse_ref), custom_call_target="tpu_custom_call" | custom-call | tf_op jit(solution)/shard_map/merge/pallas_call | solution.py:164
Async XLA Ops:
  1.4 14.9 %collective-permute-start = (bf16[2,1024,128]{2,1,0:T(8,128)(2,1)S(1)}, bf16[2,1024,128]{2,1,0:T(8,128)(2,1)S(1)}, u32[]{:S(2)}, u32[]{:S(2)}) collective-permute-start(bf16[2,1024,128]{2,1,0:T(8,128)(2,1)S(1)} %get-tuple-element.20.kv_ref), channel_id=1, source_target_pairs={{0,1},{1,0},{2,3},{3,2},{4,5},{5,4},{6,7},{7,6},{8,9},{9,8},{10,11... | collective-permute-start | bytes 1572872 | tf_op jit(solution)/shard_map/ppermute | solution.py:212
  1.9 14.4 %all-to-all-start = ((bf16[32,8,128]{2,1,0:T(8,128)(2,1)}), bf16[32,8,128]{2,1,0:T(8,128)(2,1)S(1)}, u32[]{:S(2)}, u32[]{:S(2)}) async-start(bf16[32,8,128]{2,1,0:T(8,128)(2,1)} %bitcast.3), calls=%async_computation | async-start | bytes 131072 | tf_op jit(solution)/shard_map/all_to_all | solution.py:192
  9.5 0.7 %copy-start = (bf16[1,2,4,128]{3,2,1,0:T(4,128)(2,1)S(1)}, bf16[1,2,4,128]{3,2,1,0:T(4,128)(2,1)}, u32[]{:S(2)}) copy-start(bf16[1,2,4,128]{3,2,1,0:T(4,128)(2,1)} %param.8) | copy-start | bytes 6148

commit v16 on v11

--- a/solution.py
+++ b/solution.py
@@ -70,14 +70,15 @@
                 ahead = score(*chunks[index + 1])
             best = jnp.max(scores, axis=1, keepdims=True)
             weight = jnp.exp2((scores - best) * SCALE2).astype(jnp.bfloat16)
-            values = ref[1, first : first + CHUNK]
-            parts.append((best, dot(weight, jnp.concatenate([values, jnp.ones_like(values)], axis=1))))
+            total = jnp.sum(weight.astype(jnp.float32), axis=1, keepdims=True)
+            parts.append((best, total, dot(weight, ref[1, first : first + CHUNK])))
         best = functools.reduce(jnp.maximum, [part[0] for part in parts])
-        both = sum(jnp.exp2((its - best) * SCALE2) * sums for its, sums in parts)
-        total = both[:, HD:]
-        result = both[:, :HD] / total
+        factors = [jnp.exp2((part[0] - best) * SCALE2) for part in parts]
+        total = sum(factor * part[1] for factor, part in zip(factors, parts))
+        result = sum(factor * part[2] for factor, part in zip(factors, parts)) / total
         slots = ROWS // HALF
-        stats = pack_stats((best * SCALE2 + log2(total)).reshape(slots, HALF, HD))
+        lse = jnp.broadcast_to(best * SCALE2 + log2(total), result.shape)
+        stats = pack_stats(lse.reshape(slots, HALF, HD))
         empty = jnp.zeros((1, HD), jnp.float32)
         pieces = []
         for slot in range(slots):

time: 27.7 us -> 27.7 us (level)
  no operation moved by 1% of the time
where the time goes in v16:
time: 27.7 us; the launch traced here: 27.4 us
  blocking collectives  9.3 us (34%)
  starting transfers between devices  7.42 us (27%)
  waiting for transfers between devices  5.38 us (19%)
  Pallas kernels  3.98 us (14%)
  between operations  0.69 us (2%)
  local copies, waits for them, and re-layouts  0.68 us (2%)
    all_to_all x1, blocking collectives, exchange(): return lax.all_to_all(array, ('grp', 'blk'), 0, 0, tiled=True)  9.3 us
    all_to_all x1, starting transfers between devices, exchange(): return lax.all_to_all(array, ('grp', 'blk'), 0, 0, tiled=True)  6.97 us
    all_to_all x1, waiting for transfers between devices, exchange(): return lax.all_to_all(array, ('grp', 'blk'), 0, 0, tiled=True)  5.38 us
    pallas_call x3, Pallas kernels, call(): pl.pallas_call(kernel, out_shape=outs, in_specs=specs or [VMEM] * len(ope...  2.58 us
    pallas_call x1, Pallas kernels, local(): pl.pallas_call(fan_kernel, out_shape=[half(groups, KVH, chips, SHARE), ha...  1.4 us
    unnamed x2, local copies, waits for them, and re-layouts  0.68 us
  transfers between devices with their start and end apart: 2, of which 1 were waited for; matrix products, arithmetic and copies ran while one was open for 0% of the time, Pallas kernels for 8%

profile of v16, /device:TPU:0, one launch (start us, length us, event | category | flops | bytes accessed | tf_op | source)
XLA Modules:
  0.0 27.4 jit_solution(26119060677428716)
XLA Ops:
  0.0 0.5 %collective-permute-start = (bf16[2,1,1024,128]{3,2,0,1:T(8,128)(2,1)}, bf16[2,1,1024,128]{3,2,0,1:T(8,128)(2,1)S(1)}, u32[]{:S(2)}, u32[]{:S(2)}) collective-permute-start(bf16[2,1,1024,128]{3,2,0,1:T(8,128)(2,1)} %bitcast.16), channel_id=1, source_target_pairs={{0,1},{1,0},{2,3},{3,2},{4,5},{5,4},{6,7},{7,6},{8,9},{9,8},{10,11... | collective-permute-start | bytes 1572872 | tf_op jit(solution)/shard_map/ppermute | solution.py:195
  0.5 1.4 %fan.1 = (bf16[2,4,2,16,128]{4,3,2,1,0:T(8,128)(2,1)}, bf16[4,16,128]{2,1,0:T(8,128)(2,1)S(1)}, bf16[2,1024,128]{2,1,0:T(8,128)(2,1)S(1)}, bf16[2048,128]{1,0:T(8,128)(2,1)S(1)}) custom-call(bf16[4,16,128]{2,1,0:T(8,128)(2,1)} %bitcast.18, bf16[2,1024,128]{2,1,0:T(8,128)(2,1)} %bitcast.17, bf16[2048,128]{1,0:T(8,128)(2,1)} %bitcast.15), custom_call_target="tpu_custom_call" | custom-call | tf_op jit(solution)/shard_map/fan/pallas_call | solution.py:204
  1.9 7.0 %all-to-all-start = ((bf16[32,8,128]{2,1,0:T(8,128)(2,1)}), bf16[32,8,128]{2,1,0:T(8,128)(2,1)S(1)}, u32[]{:S(2)}, u32[]{:S(2)}) async-start(bf16[32,8,128]{2,1,0:T(8,128)(2,1)} %bitcast.3), calls=%async_computation | async-start | bytes 131072 | tf_op jit(solution)/shard_map/all_to_all | solution.py:193
  9.5 0.0 copy-start
  9.5 0.7 %copy-done = bf16[1,2,4,128]{3,2,1,0:T(4,128)(2,1)S(1)} copy-done((bf16[1,2,4,128]{3,2,1,0:T(4,128)(2,1)S(1)}, bf16[1,2,4,128]{3,2,1,0:T(4,128)(2,1)}, u32[]{:S(2)}) %copy-start) | copy-done | bytes 2072
  10.2 0.7 %suffix.1 = (f32[64,128]{1,0:T(8,128)S(1)}, f32[64,128]{1,0:T(8,128)S(1)}) custom-call(s32[1]{0:T(128)S(6)} %copy.7.len_ref, bf16[8,128]{1,0:T(8,128)(2,1)S(1)} %bitcast.13, bf16[4,16,128]{2,1,0:T(8,128)(2,1)S(1)} %get-tuple-element.15.q_ref, bf16[2048,128]{1,0:T(8,128)(2,1)S(1)} %get-tuple-element.16.cache_ref), custom_call_target="tpu_custom_call" | custom-call | flops 70000000 | bytes 600000 | tf_op jit(solution)/shard_map/suffix/pallas_call | solution.py:165
  10.9 5.4 %all-to-all-done = bf16[32,8,128]{2,1,0:T(8,128)(2,1)S(1)} async-done(((bf16[32,8,128]{2,1,0:T(8,128)(2,1)}), bf16[32,8,128]{2,1,0:T(8,128)(2,1)S(1)}, u32[]{:S(2)}, u32[]{:S(2)}) %all-to-all-start) | async-done | bytes 65568 | tf_op jit(solution)/shard_map/all_to_all | solution.py:193
  16.2 0.0 collective-permute-done
  16.2 1.1 %prefix.1 = bf16[320,128]{1,0:T(8,128)(2,1)S(1)} custom-call(bf16[256,128]{1,0:T(8,128)(2,1)S(1)} %bitcast.12, bf16[2,1024,128]{2,1,0:T(8,128)(2,1)S(1)} %get-tuple-element.20.kv_ref, bf16[2,1024,128]{2,1,0:T(8,128)(2,1)S(1)} %bitcast.14), custom_call_target="tpu_custom_call" | custom-call | flops 402653184 | bytes 1600000 | tf_op jit(solution)/shard_map/prefix/pallas_call | solution.py:165
  17.3 9.3 %all_to_all.10 = bf16[32,5,2,128]{3,2,1,0:T(2,128)(2,1)S(1)} all-to-all(bf16[32,5,2,128]{3,2,1,0:T(2,128)(2,1)S(1)} %bitcast.11), channel_id=1, replica_groups=mesh['grp'=2,'blk'=16] {'grp','blk'}, dimensions={0} | all-to-all | bytes 163840 | tf_op jit(solution)/shard_map/all_to_all | solution.py:193
  26.6 0.8 %merge.1 = bf16[1,64,128]{2,1,0:T(8,128)(2,1)} custom-call(bf16[320,128]{1,0:T(8,128)(2,1)S(1)} %bitcast.10, f32[64,128]{1,0:T(8,128)S(1)} %get-tuple-element.21.suffix_ref, f32[64,128]{1,0:T(8,128)S(1)} %get-tuple-element.22.lse_ref), custom_call_target="tpu_custom_call" | custom-call | tf_op jit(solution)/shard_map/merge/pallas_call | solution.py:165
Async XLA Ops:
  0.0 16.2 %collective-permute-start = (bf16[2,1,1024,128]{3,2,0,1:T(8,128)(2,1)}, bf16[2,1,1024,128]{3,2,0,1:T(8,128)(2,1)S(1)}, u32[]{:S(2)}, u32[]{:S(2)}) collective-permute-start(bf16[2,1,1024,128]{3,2,0,1:T(8,128)(2,1)} %bitcast.16), channel_id=1, source_target_pairs={{0,1},{1,0},{2,3},{3,2},{4,5},{5,4},{6,7},{7,6},{8,9},{9,8},{10,11... | collective-permute-start | bytes 1572872 | tf_op jit(solution)/shard_map/ppermute | solution.py:195
  1.9 14.4 %all-to-all-start = ((bf16[32,8,128]{2,1,0:T(8,128)(2,1)}), bf16[32,8,128]{2,1,0:T(8,128)(2,1)S(1)}, u32[]{:S(2)}, u32[]{:S(2)}) async-start(bf16[32,8,128]{2,1,0:T(8,128)(2,1)} %bitcast.3), calls=%async_computation | async-start | bytes 131072 | tf_op jit(solution)/shard_map/all_to_all | solution.py:193
  9.5 0.7 %copy-start = (bf16[1,2,4,128]{3,2,1,0:T(4,128)(2,1)S(1)}, bf16[1,2,4,128]{3,2,1,0:T(4,128)(2,1)}, u32[]{:S(2)}) copy-start(bf16[1,2,4,128]{3,2,1,0:T(4,128)(2,1)} %param.8) | copy-start | bytes 6148

commit v17 on v11

--- a/solution.py
+++ b/solution.py
@@ -20,6 +20,7 @@
 HALF = SHARE // CORES
 MESSAGE = HALF + 2
 LANES = HD // HALF
+PIECES = 3
 LIMIT = 24 * 1024 * 1024
 NT = (((1,), (1,)), ((), ()))
 
@@ -36,21 +37,30 @@
     return jnp.log(x) * math.log2(math.e)
 
 
-def pack_stats(x):
+def split3(x):
     hi = x.astype(jnp.bfloat16).astype(jnp.float32)
     rest = x - hi
     mid = rest.astype(jnp.bfloat16).astype(jnp.float32)
-    low = rest - mid
-    row = lax.broadcasted_iota(jnp.int32, x.shape, 1)
-    lane = lax.broadcasted_iota(jnp.int32, x.shape, 2) - row * LANES
-    return jnp.sum(jnp.where(lane == 0, hi, jnp.where(lane == 1, mid, jnp.where(lane == 2, low, 0.0))), axis=1)
+    return hi, mid, rest - mid
+
+
+def pack_stats(best, total):
+    row = lax.broadcasted_iota(jnp.int32, best.shape, 1)
+    lane = lax.broadcasted_iota(jnp.int32, best.shape, 2) - row * LANES
+    packed = jnp.zeros_like(best)
+    for at, piece in enumerate((*split3(best), *split3(total))):
+        packed = jnp.where(lane == at, piece, packed)
+    return jnp.sum(packed, axis=1)
 
 
 def unpack_stats(rows):
     shape = (HALF, HD)
     mine = lax.broadcasted_iota(jnp.int32, shape, 1) // LANES == lax.broadcasted_iota(jnp.int32, shape, 0)
     pieces = [jnp.where(mine, jnp.broadcast_to(row, shape), 0.0) for row in rows]
-    return dot(jnp.concatenate(pieces, axis=0).astype(jnp.bfloat16), jnp.ones((HD, HD), jnp.bfloat16))
+    shape = (HD, 2 * HD)
+    which = lax.broadcasted_iota(jnp.int32, shape, 0) % LANES // PIECES
+    select = jnp.where(which == lax.broadcasted_iota(jnp.int32, shape, 1) // HD, 1.0, 0.0)
+    return dot(jnp.concatenate(pieces, axis=0).astype(jnp.bfloat16), select.astype(jnp.bfloat16))
 
 
 def prefix_kernel(q_ref, kv_ref, other_ref, out_ref):
@@ -74,14 +84,15 @@
             parts.append((best, dot(weight, jnp.concatenate([values, jnp.ones_like(values)], axis=1))))
         best = functools.reduce(jnp.maximum, [part[0] for part in parts])
         both = sum(jnp.exp2((its - best) * SCALE2) * sums for its, sums in parts)
-        total = both[:, HD:]
-        result = both[:, :HD] / total
+        numerator = both[:, :HD]
         slots = ROWS // HALF
-        stats = pack_stats((best * SCALE2 + log2(total)).reshape(slots, HALF, HD))
+        shape = (slots, HALF, HD)
+        best = jnp.broadcast_to(best * SCALE2, numerator.shape)
+        stats = pack_stats(best.reshape(shape), both[:, HD:].reshape(shape))
         empty = jnp.zeros((1, HD), jnp.float32)
         pieces = []
         for slot in range(slots):
-            pieces += [result[slot * HALF : (slot + 1) * HALF], stats[slot : slot + 1], empty]
+            pieces += [numerator[slot * HALF : (slot + 1) * HALF], stats[slot : slot + 1], empty]
         out_ref[pl.ds(trip * slots * MESSAGE, slots * MESSAGE)] = jnp.concatenate(pieces, axis=0).astype(jnp.bfloat16)
 
     trips = q_ref.shape[0] // ROWS
@@ -141,7 +152,7 @@
     part = part_ref[...].astype(jnp.float32)
     starts = range(0, len(served) * MESSAGE, MESSAGE)
     rows = [part[at : at + HALF] for at in starts]
-    sums = unpack_stats([part[at + HALF : at + HALF + 1] for at in starts]).reshape(len(served), HALF, HD)
+    sums = unpack_stats([part[at + HALF : at + HALF + 1] for at in starts]).reshape(len(served), HALF, 2 * HD)
     blocks = []
     for block in range(H // HALF):
         span = slice(block * HALF, (block + 1) * HALF)
@@ -149,12 +160,12 @@
         own_lse = lse_ref[span]
         best = own_lse
         for slot in own:
-            best = jnp.maximum(best, sums[slot])
+            best = jnp.maximum(best, sums[slot, :, :HD])
         total = jnp.exp2(own_lse - best)
         numerator = total * suffix_ref[span]
         for slot in own:
-            factor = jnp.exp2(sums[slot] - best)
-            total = total + factor
+            factor = jnp.exp2(sums[slot, :, :HD] - best)
+            total = total + factor * sums[slot, :, HD:]
             numerator = numerator + factor * rows[slot]
         blocks.append(numerator / total)
     out_ref[0] = jnp.concatenate(blocks, axis=0).astype(jnp.bfloat16)

time: 27.7 us -> 27.7 us (level)
  no operation moved by 1% of the time
where the time goes in v17:
time: 27.7 us; the launch traced here: 27.4 us
  blocking collectives  9.3 us (34%)
  starting transfers between devices  7.42 us (27%)
  waiting for transfers between devices  5.38 us (19%)
  Pallas kernels  3.91 us (14%)
  between operations  0.69 us (2%)
  local copies, waits for them, and re-layouts  0.68 us (2%)
    all_to_all x1, blocking collectives, exchange(): return lax.all_to_all(array, ('grp', 'blk'), 0, 0, tiled=True)  9.3 us
    all_to_all x1, starting transfers between devices, exchange(): return lax.all_to_all(array, ('grp', 'blk'), 0, 0, tiled=True)  6.97 us
    all_to_all x1, waiting for transfers between devices, exchange(): return lax.all_to_all(array, ('grp', 'blk'), 0, 0, tiled=True)  5.38 us
    pallas_call x3, Pallas kernels, call(): pl.pallas_call(kernel, out_shape=outs, in_specs=specs or [VMEM] * len(ope...  2.51 us
    pallas_call x1, Pallas kernels, local(): pl.pallas_call(fan_kernel, out_shape=[half(groups, KVH, chips, SHARE), ha...  1.4 us
    unnamed x2, local copies, waits for them, and re-layouts  0.68 us
  transfers between devices with their start and end apart: 2, of which 1 were waited for; matrix products, arithmetic and copies ran while one was open for 0% of the time, Pallas kernels for 8%

profile of v17, /device:TPU:0, one launch (start us, length us, event | category | flops | bytes accessed | tf_op | source)
XLA Modules:
  0.0 27.4 jit_solution(8758627849127886099)
XLA Ops:
  0.0 0.5 %collective-permute-start = (bf16[2,1,1024,128]{3,2,0,1:T(8,128)(2,1)}, bf16[2,1,1024,128]{3,2,0,1:T(8,128)(2,1)S(1)}, u32[]{:S(2)}, u32[]{:S(2)}) collective-permute-start(bf16[2,1,1024,128]{3,2,0,1:T(8,128)(2,1)} %bitcast.16), channel_id=1, source_target_pairs={{0,1},{1,0},{2,3},{3,2},{4,5},{5,4},{6,7},{7,6},{8,9},{9,8},{10,11... | collective-permute-start | bytes 1572872 | tf_op jit(solution)/shard_map/ppermute | solution.py:205
  0.5 1.4 %fan.1 = (bf16[2,4,2,16,128]{4,3,2,1,0:T(8,128)(2,1)}, bf16[4,16,128]{2,1,0:T(8,128)(2,1)S(1)}, bf16[2,1024,128]{2,1,0:T(8,128)(2,1)S(1)}, bf16[2048,128]{1,0:T(8,128)(2,1)S(1)}) custom-call(bf16[4,16,128]{2,1,0:T(8,128)(2,1)} %bitcast.18, bf16[2,1024,128]{2,1,0:T(8,128)(2,1)} %bitcast.17, bf16[2048,128]{1,0:T(8,128)(2,1)} %bitcast.15), custom_call_target="tpu_custom_call" | custom-call | tf_op jit(solution)/shard_map/fan/pallas_call | solution.py:214
  1.9 7.0 %all-to-all-start = ((bf16[32,8,128]{2,1,0:T(8,128)(2,1)}), bf16[32,8,128]{2,1,0:T(8,128)(2,1)S(1)}, u32[]{:S(2)}, u32[]{:S(2)}) async-start(bf16[32,8,128]{2,1,0:T(8,128)(2,1)} %bitcast.3), calls=%async_computation | async-start | bytes 131072 | tf_op jit(solution)/shard_map/all_to_all | solution.py:203
  9.5 0.0 copy-start
  9.5 0.7 %copy-done = bf16[1,2,4,128]{3,2,1,0:T(4,128)(2,1)S(1)} copy-done((bf16[1,2,4,128]{3,2,1,0:T(4,128)(2,1)S(1)}, bf16[1,2,4,128]{3,2,1,0:T(4,128)(2,1)}, u32[]{:S(2)}) %copy-start) | copy-done | bytes 2072
  10.2 0.7 %suffix.1 = (f32[64,128]{1,0:T(8,128)S(1)}, f32[64,128]{1,0:T(8,128)S(1)}) custom-call(s32[1]{0:T(128)S(6)} %copy.7.len_ref, bf16[8,128]{1,0:T(8,128)(2,1)S(1)} %bitcast.13, bf16[4,16,128]{2,1,0:T(8,128)(2,1)S(1)} %get-tuple-element.15.q_ref, bf16[2048,128]{1,0:T(8,128)(2,1)S(1)} %get-tuple-element.16.cache_ref), custom_call_target="tpu_custom_call" | custom-call | flops 70000000 | bytes 600000 | tf_op jit(solution)/shard_map/suffix/pallas_call | solution.py:175
  10.9 5.4 %all-to-all-done = bf16[32,8,128]{2,1,0:T(8,128)(2,1)S(1)} async-done(((bf16[32,8,128]{2,1,0:T(8,128)(2,1)}), bf16[32,8,128]{2,1,0:T(8,128)(2,1)S(1)}, u32[]{:S(2)}, u32[]{:S(2)}) %all-to-all-start) | async-done | bytes 65568 | tf_op jit(solution)/shard_map/all_to_all | solution.py:203
  16.2 0.0 collective-permute-done
  16.2 1.0 %prefix.1 = bf16[320,128]{1,0:T(8,128)(2,1)S(1)} custom-call(bf16[256,128]{1,0:T(8,128)(2,1)S(1)} %bitcast.12, bf16[2,1024,128]{2,1,0:T(8,128)(2,1)S(1)} %get-tuple-element.20.kv_ref, bf16[2,1024,128]{2,1,0:T(8,128)(2,1)S(1)} %bitcast.14), custom_call_target="tpu_custom_call" | custom-call | flops 402653184 | bytes 1600000 | tf_op jit(solution)/shard_map/prefix/pallas_call | solution.py:175
  17.2 9.3 %all_to_all.10 = bf16[32,5,2,128]{3,2,1,0:T(2,128)(2,1)S(1)} all-to-all(bf16[32,5,2,128]{3,2,1,0:T(2,128)(2,1)S(1)} %bitcast.11), channel_id=1, replica_groups=mesh['grp'=2,'blk'=16] {'grp','blk'}, dimensions={0} | all-to-all | bytes 163840 | tf_op jit(solution)/shard_map/all_to_all | solution.py:203
  26.5 0.8 %merge.1 = bf16[1,64,128]{2,1,0:T(8,128)(2,1)} custom-call(bf16[320,128]{1,0:T(8,128)(2,1)S(1)} %bitcast.10, f32[64,128]{1,0:T(8,128)S(1)} %get-tuple-element.21.suffix_ref, f32[64,128]{1,0:T(8,128)S(1)} %get-tuple-element.22.lse_ref), custom_call_target="tpu_custom_call" | custom-call | tf_op jit(solution)/shard_map/merge/pallas_call | solution.py:175
Async XLA Ops:
  0.0 16.2 %collective-permute-start = (bf16[2,1,1024,128]{3,2,0,1:T(8,128)(2,1)}, bf16[2,1,1024,128]{3,2,0,1:T(8,128)(2,1)S(1)}, u32[]{:S(2)}, u32[]{:S(2)}) collective-permute-start(bf16[2,1,1024,128]{3,2,0,1:T(8,128)(2,1)} %bitcast.16), channel_id=1, source_target_pairs={{0,1},{1,0},{2,3},{3,2},{4,5},{5,4},{6,7},{7,6},{8,9},{9,8},{10,11... | collective-permute-start | bytes 1572872 | tf_op jit(solution)/shard_map/ppermute | solution.py:205
  1.9 14.4 %all-to-all-start = ((bf16[32,8,128]{2,1,0:T(8,128)(2,1)}), bf16[32,8,128]{2,1,0:T(8,128)(2,1)S(1)}, u32[]{:S(2)}, u32[]{:S(2)}) async-start(bf16[32,8,128]{2,1,0:T(8,128)(2,1)} %bitcast.3), calls=%async_computation | async-start | bytes 131072 | tf_op jit(solution)/shard_map/all_to_all | solution.py:203
  9.5 0.7 %copy-start = (bf16[1,2,4,128]{3,2,1,0:T(4,128)(2,1)S(1)}, bf16[1,2,4,128]{3,2,1,0:T(4,128)(2,1)}, u32[]{:S(2)}) copy-start(bf16[1,2,4,128]{3,2,1,0:T(4,128)(2,1)} %param.8) | copy-start | bytes 6148

commit v18 on v14

--- a/solution.py
+++ b/solution.py
@@ -15,7 +15,7 @@
 SCALE2 = HD ** (-0.5) * math.log2(math.e)
 VMEM = pl.BlockSpec(memory_space=pltpu.VMEM)
 ROWS = 256
-CHUNK = 256
+CHUNK = 512
 AHEAD = 2
 CORES = 2
 HALF = SHARE // CORES
@@ -203,9 +203,14 @@
     ]
     outgoing, q, kv, cache = pl.pallas_call(
         fan_kernel,
-        out_shape=[half(groups, KVH, chips, SHARE), half(KVH, SHARE), half(2, span), half(cache_rows)],
+        out_shape=[
+            pltpu.HBM((groups, KVH, chips, SHARE, HD), jnp.bfloat16),
+            half(KVH, SHARE),
+            half(2, span),
+            half(cache_rows),
+        ],
         in_specs=[pl.BlockSpec(memory_space=pltpu.HBM)] * 3,
-        out_specs=[pl.BlockSpec(memory_space=pl.ANY), VMEM, VMEM, VMEM],
+        out_specs=[pl.BlockSpec(memory_space=pltpu.HBM), VMEM, VMEM, VMEM],
         scratch_shapes=[pltpu.SemaphoreType.DMA((3,)), pltpu.SemaphoreType.DMA((groups, chips))],
         name="fan",
         compiler_params=pltpu.CompilerParams(vmem_limit_bytes=LIMIT),

time: 27.7 us -> 27.7 us (level)
  no operation moved by 1% of the time
where the time goes in v18:
time: 27.7 us; the launch traced here: 27.4 us
  blocking collectives  9.3 us (34%)
  starting transfers between devices  7.42 us (27%)
  waiting for transfers between devices  5.38 us (19%)
  Pallas kernels  3.92 us (14%)
  between operations  0.69 us (2%)
  local copies, waits for them, and re-layouts  0.68 us (2%)
    all_to_all x1, blocking collectives, exchange(): return lax.all_to_all(array, ('grp', 'blk'), 0, 0, tiled=True)  9.3 us
    all_to_all x1, starting transfers between devices, exchange(): return lax.all_to_all(array, ('grp', 'blk'), 0, 0, tiled=True)  6.97 us
    all_to_all x1, waiting for transfers between devices, exchange(): return lax.all_to_all(array, ('grp', 'blk'), 0, 0, tiled=True)  5.38 us
    pallas_call x3, Pallas kernels, call(): pl.pallas_call(kernel, out_shape=outs, in_specs=specs or [VMEM] * len(ope...  2.52 us
    pallas_call x1, Pallas kernels, local(): pl.pallas_call(fan_kernel, out_shape=[pltpu.HBM((groups, KVH, chips, SHAR...  1.4 us
    unnamed x2, local copies, waits for them, and re-layouts  0.68 us
  transfers between devices with their start and end apart: 2, of which 1 were waited for; matrix products, arithmetic and copies ran while one was open for 0% of the time, Pallas kernels for 8%

profile of v18, /device:TPU:0, one launch (start us, length us, event | category | flops | bytes accessed | tf_op | source)
XLA Modules:
  0.0 27.4 jit_solution(9586194034751332270)
XLA Ops:
  0.0 0.5 %collective-permute-start = (bf16[2,1,1024,128]{3,2,0,1:T(8,128)(2,1)}, bf16[2,1,1024,128]{3,2,0,1:T(8,128)(2,1)S(1)}, u32[]{:S(2)}, u32[]{:S(2)}) collective-permute-start(bf16[2,1,1024,128]{3,2,0,1:T(8,128)(2,1)} %bitcast.16), channel_id=1, source_target_pairs={{0,1},{1,0},{2,3},{3,2},{4,5},{5,4},{6,7},{7,6},{8,9},{9,8},{10,11... | collective-permute-start | bytes 1572872 | tf_op jit(solution)/shard_map/ppermute | solution.py:195
  0.5 1.4 %fan.1 = (bf16[2,4,2,16,128]{4,3,2,1,0:T(8,128)(2,1)}, bf16[4,16,128]{2,1,0:T(8,128)(2,1)S(1)}, bf16[2,1024,128]{2,1,0:T(8,128)(2,1)S(1)}, bf16[2048,128]{1,0:T(8,128)(2,1)S(1)}) custom-call(bf16[4,16,128]{2,1,0:T(8,128)(2,1)} %bitcast.19, bf16[2,1024,128]{2,1,0:T(8,128)(2,1)} %bitcast.17, bf16[2048,128]{1,0:T(8,128)(2,1)} %bitcast.15), custom_call_target="tpu_custom_call" | custom-call | tf_op jit(solution)/shard_map/fan/pallas_call | solution.py:204
  1.9 7.0 %all-to-all-start = ((bf16[32,8,128]{2,1,0:T(8,128)(2,1)}), bf16[32,8,128]{2,1,0:T(8,128)(2,1)S(1)}, u32[]{:S(2)}, u32[]{:S(2)}) async-start(bf16[32,8,128]{2,1,0:T(8,128)(2,1)} %bitcast.18), calls=%async_computation | async-start | bytes 131072 | tf_op jit(solution)/shard_map/all_to_all | solution.py:193
  9.5 0.0 copy-start
  9.5 0.7 %copy-done = bf16[1,2,4,128]{3,2,1,0:T(4,128)(2,1)S(1)} copy-done((bf16[1,2,4,128]{3,2,1,0:T(4,128)(2,1)S(1)}, bf16[1,2,4,128]{3,2,1,0:T(4,128)(2,1)}, u32[]{:S(2)}) %copy-start) | copy-done | bytes 2072
  10.2 0.7 %suffix.1 = (f32[64,128]{1,0:T(8,128)S(1)}, f32[64,128]{1,0:T(8,128)S(1)}) custom-call(s32[1]{0:T(128)S(6)} %copy.7.len_ref, bf16[8,128]{1,0:T(8,128)(2,1)S(1)} %bitcast.13, bf16[4,16,128]{2,1,0:T(8,128)(2,1)S(1)} %get-tuple-element.15.q_ref, bf16[2048,128]{1,0:T(8,128)(2,1)S(1)} %get-tuple-element.16.cache_ref), custom_call_target="tpu_custom_call" | custom-call | flops 70000000 | bytes 600000 | tf_op jit(solution)/shard_map/suffix/pallas_call | solution.py:165
  10.9 5.4 %all-to-all-done = bf16[32,8,128]{2,1,0:T(8,128)(2,1)S(1)} async-done(((bf16[32,8,128]{2,1,0:T(8,128)(2,1)}), bf16[32,8,128]{2,1,0:T(8,128)(2,1)S(1)}, u32[]{:S(2)}, u32[]{:S(2)}) %all-to-all-start) | async-done | bytes 65568 | tf_op jit(solution)/shard_map/all_to_all | solution.py:193
  16.2 0.0 collective-permute-done
  16.2 1.0 %prefix.1 = bf16[320,128]{1,0:T(8,128)(2,1)S(1)} custom-call(bf16[256,128]{1,0:T(8,128)(2,1)S(1)} %bitcast.12, bf16[2,1024,128]{2,1,0:T(8,128)(2,1)S(1)} %get-tuple-element.20.kv_ref, bf16[2,1024,128]{2,1,0:T(8,128)(2,1)S(1)} %bitcast.14), custom_call_target="tpu_custom_call" | custom-call | flops 402653184 | bytes 1600000 | tf_op jit(solution)/shard_map/prefix/pallas_call | solution.py:165
  17.3 9.3 %all_to_all.10 = bf16[32,5,2,128]{3,2,1,0:T(2,128)(2,1)S(1)} all-to-all(bf16[32,5,2,128]{3,2,1,0:T(2,128)(2,1)S(1)} %bitcast.11), channel_id=1, replica_groups=mesh['grp'=2,'blk'=16] {'grp','blk'}, dimensions={0} | all-to-all | bytes 163840 | tf_op jit(solution)/shard_map/all_to_all | solution.py:193
  26.6 0.8 %merge.1 = bf16[1,64,128]{2,1,0:T(8,128)(2,1)} custom-call(bf16[320,128]{1,0:T(8,128)(2,1)S(1)} %bitcast.10, f32[64,128]{1,0:T(8,128)S(1)} %get-tuple-element.21.suffix_ref, f32[64,128]{1,0:T(8,128)S(1)} %get-tuple-element.22.lse_ref), custom_call_target="tpu_custom_call" | custom-call | tf_op jit(solution)/shard_map/merge/pallas_call | solution.py:165
Async XLA Ops:
  0.0 16.2 %collective-permute-start = (bf16[2,1,1024,128]{3,2,0,1:T(8,128)(2,1)}, bf16[2,1,1024,128]{3,2,0,1:T(8,128)(2,1)S(1)}, u32[]{:S(2)}, u32[]{:S(2)}) collective-permute-start(bf16[2,1,1024,128]{3,2,0,1:T(8,128)(2,1)} %bitcast.16), channel_id=1, source_target_pairs={{0,1},{1,0},{2,3},{3,2},{4,5},{5,4},{6,7},{7,6},{8,9},{9,8},{10,11... | collective-permute-start | bytes 1572872 | tf_op jit(solution)/shard_map/ppermute | solution.py:195
  1.9 14.4 %all-to-all-start = ((bf16[32,8,128]{2,1,0:T(8,128)(2,1)}), bf16[32,8,128]{2,1,0:T(8,128)(2,1)S(1)}, u32[]{:S(2)}, u32[]{:S(2)}) async-start(bf16[32,8,128]{2,1,0:T(8,128)(2,1)} %bitcast.18), calls=%async_computation | async-start | bytes 131072 | tf_op jit(solution)/shard_map/all_to_all | solution.py:193
  9.5 0.7 %copy-start = (bf16[1,2,4,128]{3,2,1,0:T(4,128)(2,1)S(1)}, bf16[1,2,4,128]{3,2,1,0:T(4,128)(2,1)}, u32[]{:S(2)}) copy-start(bf16[1,2,4,128]{3,2,1,0:T(4,128)(2,1)} %param.8) | copy-start | bytes 6148

commit v19 on v18

--- a/solution.py
+++ b/solution.py
@@ -16,7 +16,6 @@
 VMEM = pl.BlockSpec(memory_space=pltpu.VMEM)
 ROWS = 256
 CHUNK = 512
-AHEAD = 2
 CORES = 2
 HALF = SHARE // CORES
 MESSAGE = HALF + 2
@@ -64,11 +63,11 @@
             return dot_nt(rows, ref[0, first : first + CHUNK])
 
         parts = []
-        ahead = [score(*chunk) for chunk in chunks[:AHEAD]]
+        ahead = score(*chunks[0])
         for index, (ref, first) in enumerate(chunks):
-            if index + AHEAD < len(chunks):
-                ahead.append(score(*chunks[index + AHEAD]))
-            scores = ahead.pop(0)
+            scores = ahead
+            if index + 1 < len(chunks):
+                ahead = score(*chunks[index + 1])
             best = jnp.max(scores, axis=1, keepdims=True)
             weight = jnp.exp2((scores - best) * SCALE2).astype(jnp.bfloat16)
             values = ref[1, first : first + CHUNK]

time: 27.7 us -> 27.7 us (level)
  no operation moved by 1% of the time
where the time goes in v19:
time: 27.7 us; the launch traced here: 27.4 us
  blocking collectives  9.3 us (34%)
  starting transfers between devices  7.42 us (27%)
  waiting for transfers between devices  5.38 us (19%)
  Pallas kernels  3.89 us (14%)
  between operations  0.69 us (2%)
  local copies, waits for them, and re-layouts  0.68 us (2%)
    all_to_all x1, blocking collectives, exchange(): return lax.all_to_all(array, ('grp', 'blk'), 0, 0, tiled=True)  9.3 us
    all_to_all x1, starting transfers between devices, exchange(): return lax.all_to_all(array, ('grp', 'blk'), 0, 0, tiled=True)  6.97 us
    all_to_all x1, waiting for transfers between devices, exchange(): return lax.all_to_all(array, ('grp', 'blk'), 0, 0, tiled=True)  5.38 us
    pallas_call x3, Pallas kernels, call(): pl.pallas_call(kernel, out_shape=outs, in_specs=specs or [VMEM] * len(ope...  2.5 us
    pallas_call x1, Pallas kernels, local(): pl.pallas_call(fan_kernel, out_shape=[pltpu.HBM((groups, KVH, chips, SHAR...  1.4 us
    unnamed x2, local copies, waits for them, and re-layouts  0.68 us
  transfers between devices with their start and end apart: 2, of which 1 were waited for; matrix products, arithmetic and copies ran while one was open for 0% of the time, Pallas kernels for 8%

profile of v19, /device:TPU:0, one launch (start us, length us, event | category | flops | bytes accessed | tf_op | source)
XLA Modules:
  0.0 27.4 jit_solution(17492965141629054102)
XLA Ops:
  0.0 0.5 %collective-permute-start = (bf16[2,1,1024,128]{3,2,0,1:T(8,128)(2,1)}, bf16[2,1,1024,128]{3,2,0,1:T(8,128)(2,1)S(1)}, u32[]{:S(2)}, u32[]{:S(2)}) collective-permute-start(bf16[2,1,1024,128]{3,2,0,1:T(8,128)(2,1)} %bitcast.16), channel_id=1, source_target_pairs={{0,1},{1,0},{2,3},{3,2},{4,5},{5,4},{6,7},{7,6},{8,9},{9,8},{10,11... | collective-permute-start | bytes 1572872 | tf_op jit(solution)/shard_map/ppermute | solution.py:194
  0.5 1.4 %fan.1 = (bf16[2,4,2,16,128]{4,3,2,1,0:T(8,128)(2,1)}, bf16[4,16,128]{2,1,0:T(8,128)(2,1)S(1)}, bf16[2,1024,128]{2,1,0:T(8,128)(2,1)S(1)}, bf16[2048,128]{1,0:T(8,128)(2,1)S(1)}) custom-call(bf16[4,16,128]{2,1,0:T(8,128)(2,1)} %bitcast.19, bf16[2,1024,128]{2,1,0:T(8,128)(2,1)} %bitcast.17, bf16[2048,128]{1,0:T(8,128)(2,1)} %bitcast.15), custom_call_target="tpu_custom_call" | custom-call | tf_op jit(solution)/shard_map/fan/pallas_call | solution.py:203
  1.9 7.0 %all-to-all-start = ((bf16[32,8,128]{2,1,0:T(8,128)(2,1)}), bf16[32,8,128]{2,1,0:T(8,128)(2,1)S(1)}, u32[]{:S(2)}, u32[]{:S(2)}) async-start(bf16[32,8,128]{2,1,0:T(8,128)(2,1)} %bitcast.18), calls=%async_computation | async-start | bytes 131072 | tf_op jit(solution)/shard_map/all_to_all | solution.py:192
  9.5 0.0 copy-start
  9.5 0.7 %copy-done = bf16[1,2,4,128]{3,2,1,0:T(4,128)(2,1)S(1)} copy-done((bf16[1,2,4,128]{3,2,1,0:T(4,128)(2,1)S(1)}, bf16[1,2,4,128]{3,2,1,0:T(4,128)(2,1)}, u32[]{:S(2)}) %copy-start) | copy-done | bytes 2072
  10.2 0.7 %suffix.1 = (f32[64,128]{1,0:T(8,128)S(1)}, f32[64,128]{1,0:T(8,128)S(1)}) custom-call(s32[1]{0:T(128)S(6)} %copy.7.len_ref, bf16[8,128]{1,0:T(8,128)(2,1)S(1)} %bitcast.13, bf16[4,16,128]{2,1,0:T(8,128)(2,1)S(1)} %get-tuple-element.15.q_ref, bf16[2048,128]{1,0:T(8,128)(2,1)S(1)} %get-tuple-element.16.cache_ref), custom_call_target="tpu_custom_call" | custom-call | flops 70000000 | bytes 600000 | tf_op jit(solution)/shard_map/suffix/pallas_call | solution.py:164
  10.9 5.4 %all-to-all-done = bf16[32,8,128]{2,1,0:T(8,128)(2,1)S(1)} async-done(((bf16[32,8,128]{2,1,0:T(8,128)(2,1)}), bf16[32,8,128]{2,1,0:T(8,128)(2,1)S(1)}, u32[]{:S(2)}, u32[]{:S(2)}) %all-to-all-start) | async-done | bytes 65568 | tf_op jit(solution)/shard_map/all_to_all | solution.py:192
  16.2 0.0 collective-permute-done
  16.2 1.0 %prefix.1 = bf16[320,128]{1,0:T(8,128)(2,1)S(1)} custom-call(bf16[256,128]{1,0:T(8,128)(2,1)S(1)} %bitcast.12, bf16[2,1024,128]{2,1,0:T(8,128)(2,1)S(1)} %get-tuple-element.20.kv_ref, bf16[2,1024,128]{2,1,0:T(8,128)(2,1)S(1)} %bitcast.14), custom_call_target="tpu_custom_call" | custom-call | flops 402653184 | bytes 1600000 | tf_op jit(solution)/shard_map/prefix/pallas_call | solution.py:164
  17.3 9.3 %all_to_all.10 = bf16[32,5,2,128]{3,2,1,0:T(2,128)(2,1)S(1)} all-to-all(bf16[32,5,2,128]{3,2,1,0:T(2,128)(2,1)S(1)} %bitcast.11), channel_id=1, replica_groups=mesh['grp'=2,'blk'=16] {'grp','blk'}, dimensions={0} | all-to-all | bytes 163840 | tf_op jit(solution)/shard_map/all_to_all | solution.py:192
  26.6 0.8 %merge.1 = bf16[1,64,128]{2,1,0:T(8,128)(2,1)} custom-call(bf16[320,128]{1,0:T(8,128)(2,1)S(1)} %bitcast.10, f32[64,128]{1,0:T(8,128)S(1)} %get-tuple-element.21.suffix_ref, f32[64,128]{1,0:T(8,128)S(1)} %get-tuple-element.22.lse_ref), custom_call_target="tpu_custom_call" | custom-call | tf_op jit(solution)/shard_map/merge/pallas_call | solution.py:164
Async XLA Ops:
  0.0 16.2 %collective-permute-start = (bf16[2,1,1024,128]{3,2,0,1:T(8,128)(2,1)}, bf16[2,1,1024,128]{3,2,0,1:T(8,128)(2,1)S(1)}, u32[]{:S(2)}, u32[]{:S(2)}) collective-permute-start(bf16[2,1,1024,128]{3,2,0,1:T(8,128)(2,1)} %bitcast.16), channel_id=1, source_target_pairs={{0,1},{1,0},{2,3},{3,2},{4,5},{5,4},{6,7},{7,6},{8,9},{9,8},{10,11... | collective-permute-start | bytes 1572872 | tf_op jit(solution)/shard_map/ppermute | solution.py:194
  1.9 14.4 %all-to-all-start = ((bf16[32,8,128]{2,1,0:T(8,128)(2,1)}), bf16[32,8,128]{2,1,0:T(8,128)(2,1)S(1)}, u32[]{:S(2)}, u32[]{:S(2)}) async-start(bf16[32,8,128]{2,1,0:T(8,128)(2,1)} %bitcast.18), calls=%async_computation | async-start | bytes 131072 | tf_op jit(solution)/shard_map/all_to_all | solution.py:192
  9.5 0.7 %copy-start = (bf16[1,2,4,128]{3,2,1,0:T(4,128)(2,1)S(1)}, bf16[1,2,4,128]{3,2,1,0:T(4,128)(2,1)}, u32[]{:S(2)}) copy-start(bf16[1,2,4,128]{3,2,1,0:T(4,128)(2,1)} %param.8) | copy-start | bytes 6148

commit v20 on v11

--- a/solution.py
+++ b/solution.py
@@ -16,6 +16,7 @@
 VMEM = pl.BlockSpec(memory_space=pltpu.VMEM)
 ROWS = 256
 CHUNK = 512
+PIECE = 256
 CORES = 2
 HALF = SHARE // CORES
 MESSAGE = HALF + 2
@@ -120,20 +121,19 @@
     lse_ref[...] = jnp.broadcast_to(best * SCALE2 + log2(total), lse_ref.shape)
 
 
-def fan_kernel(q_hbm, kv_hbm, cache_hbm, out_ref, q_ref, kv_ref, cache_ref, sems, fan_sems):
-    pairs = [(q_hbm, q_ref), (cache_hbm, cache_ref), (kv_hbm, kv_ref)]
-    loads = [pltpu.make_async_copy(source, target, sems.at[i]) for i, (source, target) in enumerate(pairs)]
-    for load in loads:
-        load.start()
-    loads[0].wait()
-    copies = [
-        pltpu.make_async_copy(q_ref, out_ref.at[group, :, chip], fan_sems.at[group, chip])
-        for group in range(out_ref.shape[0])
-        for chip in range(out_ref.shape[2])
-    ]
+def fan_kernel(q_hbm, kv_hbm, cache_hbm, out_ref, q_ref, kv_ref, cache_ref, sems):
+    groups, heads, chips = out_ref.shape[:3]
+    places = [(group, head, chip) for group in range(groups) for chip in range(chips) for head in range(heads)]
+    pairs = [(q_hbm.at[head], out_ref.at[group, head, chip]) for group, head, chip in places]
+    pairs.append((q_hbm, q_ref))
+    spans = [(i, pl.ds(at, PIECE)) for at in range(0, kv_ref.shape[1], PIECE) for i in range(2)]
+    pairs += [(kv_hbm.at[i, span], kv_ref.at[i, span]) for i, span in spans]
+    spans = [pl.ds(at, PIECE) for at in range(0, cache_ref.shape[0], PIECE)]
+    pairs += [(cache_hbm.at[span], cache_ref.at[span]) for span in spans]
+    copies = [pltpu.make_async_copy(source, target, sems.at[i]) for i, (source, target) in enumerate(pairs)]
     for copy in copies:
         copy.start()
-    for copy in copies + loads[1:]:
+    for copy in copies:
         copy.wait()
 
 
@@ -205,7 +205,7 @@
         out_shape=[half(groups, KVH, chips, SHARE), half(KVH, SHARE), half(2, span), half(cache_rows)],
         in_specs=[pl.BlockSpec(memory_space=pltpu.HBM)] * 3,
         out_specs=[pl.BlockSpec(memory_space=pl.ANY), VMEM, VMEM, VMEM],
-        scratch_shapes=[pltpu.SemaphoreType.DMA((3,)), pltpu.SemaphoreType.DMA((groups, chips))],
+        scratch_shapes=[pltpu.SemaphoreType.DMA((groups * KVH * chips + 1 + 2 * span // PIECE + cache_rows // PIECE,))],
         name="fan",
         compiler_params=pltpu.CompilerParams(vmem_limit_bytes=LIMIT),
     )(*bound)

time: 27.7 us -> 29.6 us (1.069)
  Pallas kernels: 3.89 us -> 5.9 us
    pallas_call x1, Pallas kernels: 1.4 us -> 3.41 us  [local(): pl.pallas_call(fan_kernel, out_shape=[half(groups, KVH, chips, SHARE), ha...]
  transfers between devices with their start and end apart: 2 -> 2, of which waited for: 1 -> 1; matrix products, arithmetic and copies ran while one was open for 0% -> 0% of each run, Pallas kernels for 8% -> 14%
where the time goes in v20:
time: 29.6 us; the launch traced here: 29.4 us
  blocking collectives  9.3 us (31%)
  starting transfers between devices  7.42 us (25%)
  Pallas kernels  5.9 us (20%)
  waiting for transfers between devices  5.38 us (18%)
  between operations  0.69 us (2%)
  local copies, waits for them, and re-layouts  0.68 us (2%)
    all_to_all x1, blocking collectives, exchange(): return lax.all_to_all(array, ('grp', 'blk'), 0, 0, tiled=True)  9.3 us
    all_to_all x1, starting transfers between devices, exchange(): return lax.all_to_all(array, ('grp', 'blk'), 0, 0, tiled=True)  6.97 us
    all_to_all x1, waiting for transfers between devices, exchange(): return lax.all_to_all(array, ('grp', 'blk'), 0, 0, tiled=True)  5.38 us
    pallas_call x1, Pallas kernels, local(): pl.pallas_call(fan_kernel, out_shape=[half(groups, KVH, chips, SHARE), ha...  3.41 us
    pallas_call x3, Pallas kernels, call(): pl.pallas_call(kernel, out_shape=outs, in_specs=specs or [VMEM] * len(ope...  2.5 us
    unnamed x2, local copies, waits for them, and re-layouts  0.68 us
  transfers between devices with their start and end apart: 2, of which 1 were waited for; matrix products, arithmetic and copies ran while one was open for 0% of the time, Pallas kernels for 14%

profile of v20, /device:TPU:0, one launch (start us, length us, event | category | flops | bytes accessed | tf_op | source)
XLA Modules:
  0.0 29.4 jit_solution(2687501266295348281)
XLA Ops:
  0.0 0.5 %collective-permute-start = (bf16[2,1,1024,128]{3,2,0,1:T(8,128)(2,1)}, bf16[2,1,1024,128]{3,2,0,1:T(8,128)(2,1)S(1)}, u32[]{:S(2)}, u32[]{:S(2)}) collective-permute-start(bf16[2,1,1024,128]{3,2,0,1:T(8,128)(2,1)} %bitcast.16), channel_id=1, source_target_pairs={{0,1},{1,0},{2,3},{3,2},{4,5},{5,4},{6,7},{7,6},{8,9},{9,8},{10,11... | collective-permute-start | bytes 1572872 | tf_op jit(solution)/shard_map/ppermute | solution.py:194
  0.5 3.4 %fan.1 = (bf16[2,4,2,16,128]{4,3,2,1,0:T(8,128)(2,1)}, bf16[4,16,128]{2,1,0:T(8,128)(2,1)S(1)}, bf16[2,1024,128]{2,1,0:T(8,128)(2,1)S(1)}, bf16[2048,128]{1,0:T(8,128)(2,1)S(1)}) custom-call(bf16[4,16,128]{2,1,0:T(8,128)(2,1)} %bitcast.18, bf16[2,1024,128]{2,1,0:T(8,128)(2,1)} %bitcast.17, bf16[2048,128]{1,0:T(8,128)(2,1)} %bitcast.15), custom_call_target="tpu_custom_call" | custom-call | tf_op jit(solution)/shard_map/fan/pallas_call | solution.py:203
  3.9 7.0 %all-to-all-start = ((bf16[32,8,128]{2,1,0:T(8,128)(2,1)}), bf16[32,8,128]{2,1,0:T(8,128)(2,1)S(1)}, u32[]{:S(2)}, u32[]{:S(2)}) async-start(bf16[32,8,128]{2,1,0:T(8,128)(2,1)} %bitcast.3), calls=%async_computation | async-start | bytes 131072 | tf_op jit(solution)/shard_map/all_to_all | solution.py:192
  11.5 0.0 copy-start
  11.5 0.7 %copy-done = bf16[1,2,4,128]{3,2,1,0:T(4,128)(2,1)S(1)} copy-done((bf16[1,2,4,128]{3,2,1,0:T(4,128)(2,1)S(1)}, bf16[1,2,4,128]{3,2,1,0:T(4,128)(2,1)}, u32[]{:S(2)}) %copy-start) | copy-done | bytes 2072
  12.2 0.7 %suffix.1 = (f32[64,128]{1,0:T(8,128)S(1)}, f32[64,128]{1,0:T(8,128)S(1)}) custom-call(s32[1]{0:T(128)S(6)} %copy.7.len_ref, bf16[8,128]{1,0:T(8,128)(2,1)S(1)} %bitcast.13, bf16[4,16,128]{2,1,0:T(8,128)(2,1)S(1)} %get-tuple-element.15.q_ref, bf16[2048,128]{1,0:T(8,128)(2,1)S(1)} %get-tuple-element.16.cache_ref), custom_call_target="tpu_custom_call" | custom-call | flops 70000000 | bytes 600000 | tf_op jit(solution)/shard_map/suffix/pallas_call | solution.py:164
  12.9 5.4 %all-to-all-done = bf16[32,8,128]{2,1,0:T(8,128)(2,1)S(1)} async-done(((bf16[32,8,128]{2,1,0:T(8,128)(2,1)}), bf16[32,8,128]{2,1,0:T(8,128)(2,1)S(1)}, u32[]{:S(2)}, u32[]{:S(2)}) %all-to-all-start) | async-done | bytes 65568 | tf_op jit(solution)/shard_map/all_to_all | solution.py:192
  18.3 0.0 collective-permute-done
  18.3 1.0 %prefix.1 = bf16[320,128]{1,0:T(8,128)(2,1)S(1)} custom-call(bf16[256,128]{1,0:T(8,128)(2,1)S(1)} %bitcast.12, bf16[2,1024,128]{2,1,0:T(8,128)(2,1)S(1)} %get-tuple-element.20.kv_ref, bf16[2,1024,128]{2,1,0:T(8,128)(2,1)S(1)} %bitcast.14), custom_call_target="tpu_custom_call" | custom-call | flops 402653184 | bytes 1600000 | tf_op jit(solution)/shard_map/prefix/pallas_call | solution.py:164
  19.3 9.3 %all_to_all.10 = bf16[32,5,2,128]{3,2,1,0:T(2,128)(2,1)S(1)} all-to-all(bf16[32,5,2,128]{3,2,1,0:T(2,128)(2,1)S(1)} %bitcast.11), channel_id=1, replica_groups=mesh['grp'=2,'blk'=16] {'grp','blk'}, dimensions={0} | all-to-all | bytes 163840 | tf_op jit(solution)/shard_map/all_to_all | solution.py:192
  28.6 0.8 %merge.1 = bf16[1,64,128]{2,1,0:T(8,128)(2,1)} custom-call(bf16[320,128]{1,0:T(8,128)(2,1)S(1)} %bitcast.10, f32[64,128]{1,0:T(8,128)S(1)} %get-tuple-element.21.suffix_ref, f32[64,128]{1,0:T(8,128)S(1)} %get-tuple-element.22.lse_ref), custom_call_target="tpu_custom_call" | custom-call | tf_op jit(solution)/shard_map/merge/pallas_call | solution.py:164
Async XLA Ops:
  0.0 18.3 %collective-permute-start = (bf16[2,1,1024,128]{3,2,0,1:T(8,128)(2,1)}, bf16[2,1,1024,128]{3,2,0,1:T(8,128)(2,1)S(1)}, u32[]{:S(2)}, u32[]{:S(2)}) collective-permute-start(bf16[2,1,1024,128]{3,2,0,1:T(8,128)(2,1)} %bitcast.16), channel_id=1, source_target_pairs={{0,1},{1,0},{2,3},{3,2},{4,5},{5,4},{6,7},{7,6},{8,9},{9,8},{10,11... | collective-permute-start | bytes 1572872 | tf_op jit(solution)/shard_map/ppermute | solution.py:194
  3.9 14.4 %all-to-all-start = ((bf16[32,8,128]{2,1,0:T(8,128)(2,1)}), bf16[32,8,128]{2,1,0:T(8,128)(2,1)S(1)}, u32[]{:S(2)}, u32[]{:S(2)}) async-start(bf16[32,8,128]{2,1,0:T(8,128)(2,1)} %bitcast.3), calls=%async_computation | async-start | bytes 131072 | tf_op jit(solution)/shard_map/all_to_all | solution.py:192
  11.5 0.7 %copy-start = (bf16[1,2,4,128]{3,2,1,0:T(4,128)(2,1)S(1)}, bf16[1,2,4,128]{3,2,1,0:T(4,128)(2,1)}, u32[]{:S(2)}) copy-start(bf16[1,2,4,128]{3,2,1,0:T(4,128)(2,1)} %param.8) | copy-start | bytes 6148

commit v21 on v11

--- a/solution.py
+++ b/solution.py
@@ -103,7 +103,7 @@
 
 
 def suffix_kernel(len_ref, new_ref, q_ref, cache_ref, out_ref, lse_ref):
-    q = q_ref[...].reshape(H, HD)
+    q = q_ref[...]
     cache = cache_ref[...]
     new = new_ref[...]
     raw = dot_nt(q, cache)
@@ -126,11 +126,7 @@
     for load in loads:
         load.start()
     loads[0].wait()
-    copies = [
-        pltpu.make_async_copy(q_ref, out_ref.at[group, :, chip], fan_sems.at[group, chip])
-        for group in range(out_ref.shape[0])
-        for chip in range(out_ref.shape[2])
-    ]
+    copies = [pltpu.make_async_copy(q_ref, out_ref.at[i], fan_sems.at[i]) for i in range(out_ref.shape[0])]
     for copy in copies:
         copy.start()
     for copy in copies + loads[1:]:
@@ -180,7 +176,14 @@
     span = prefix_kv.shape[2]
     cache_rows = suffix_kv.shape[1] * 2 * KVH
     chips = per_head // CORES
-    served = [device % members // per_head * CORES + device % CORES for device in range(devices)]
+    order = [
+        g * members + (head * chips + chip) * CORES + core
+        for g in range(groups)
+        for chip in range(chips)
+        for head in range(KVH)
+        for core in range(CORES)
+    ]
+    served = [device % members // per_head * CORES + device % CORES for device in order]
 
     def one(rows):
         return jax.ShapeDtypeStruct((rows, HD), jnp.float32)
@@ -189,23 +192,23 @@
         return jax.ShapeDtypeStruct((*shape, HD), jnp.bfloat16)
 
     def exchange(array):
-        return lax.all_to_all(array, ("grp", "blk"), 0, 0, tiled=True)
+        return lax.all_to_all(array, ("grp", "blk"), 0, 0, axis_index_groups=[order], tiled=True)
 
     other = lax.ppermute(prefix_kv, "blk", [(i, i ^ 1) for i in range(members)]).reshape(2, span, HD)
     bound = [
         pltpu.with_memory_space_constraint(array, pltpu.HBM)
         for array in (
-            queries.reshape(KVH, SHARE, HD),
+            queries.reshape(H, HD),
             prefix_kv.reshape(2, span, HD),
             suffix_kv.reshape(cache_rows, HD),
         )
     ]
     outgoing, q, kv, cache = pl.pallas_call(
         fan_kernel,
-        out_shape=[half(groups, KVH, chips, SHARE), half(KVH, SHARE), half(2, span), half(cache_rows)],
+        out_shape=[half(groups * chips, H), half(H), half(2, span), half(cache_rows)],
         in_specs=[pl.BlockSpec(memory_space=pltpu.HBM)] * 3,
         out_specs=[pl.BlockSpec(memory_space=pl.ANY), VMEM, VMEM, VMEM],
-        scratch_shapes=[pltpu.SemaphoreType.DMA((3,)), pltpu.SemaphoreType.DMA((groups, chips))],
+        scratch_shapes=[pltpu.SemaphoreType.DMA((3,)), pltpu.SemaphoreType.DMA((groups * chips,))],
         name="fan",
         compiler_params=pltpu.CompilerParams(vmem_limit_bytes=LIMIT),
     )(*bound)

time: 27.7 us -> 27.6 us (level)
  no operation moved by 1% of the time
where the time goes in v21:
time: 27.6 us; the launch traced here: 27.3 us
  blocking collectives  9.27 us (34%)
  starting transfers between devices  7.42 us (27%)
  waiting for transfers between devices  5.36 us (19%)
  Pallas kernels  3.9 us (14%)
  between operations  0.69 us (2%)
  local copies, waits for them, and re-layouts  0.68 us (2%)
    all_to_all x1, blocking collectives, exchange(): lax.all_to_all(array, ('grp', 'blk'), 0, 0, axis_index_groups=[order], ti...  9.27 us
    all_to_all x1, starting transfers between devices, exchange(): lax.all_to_all(array, ('grp', 'blk'), 0, 0, axis_index_groups=[order], ti...  6.97 us
    all_to_all x1, waiting for transfers between devices, exchange(): lax.all_to_all(array, ('grp', 'blk'), 0, 0, axis_index_groups=[order], ti...  5.35 us
    pallas_call x3, Pallas kernels, call(): pl.pallas_call(kernel, out_shape=outs, in_specs=specs or [VMEM] * len(ope...  2.5 us
    pallas_call x1, Pallas kernels, local(): pl.pallas_call(fan_kernel, out_shape=[half(groups * chips, H), half(H), h...  1.4 us
    unnamed x2, local copies, waits for them, and re-layouts  0.68 us
  transfers between devices with their start and end apart: 2, of which 1 were waited for; matrix products, arithmetic and copies ran while one was open for 0% of the time, Pallas kernels for 8%

profile of v21, /device:TPU:0, one launch (start us, length us, event | category | flops | bytes accessed | tf_op | source)
XLA Modules:
  0.0 27.3 jit_solution(5872502405887993885)
XLA Ops:
  0.0 0.5 %collective-permute-start = (bf16[2,1,1024,128]{3,2,0,1:T(8,128)(2,1)}, bf16[2,1,1024,128]{3,2,0,1:T(8,128)(2,1)S(1)}, u32[]{:S(2)}, u32[]{:S(2)}) collective-permute-start(bf16[2,1,1024,128]{3,2,0,1:T(8,128)(2,1)} %bitcast.16), channel_id=1, source_target_pairs={{0,1},{1,0},{2,3},{3,2},{4,5},{5,4},{6,7},{7,6},{8,9},{9,8},{10,11... | collective-permute-start | bytes 1572872 | tf_op jit(solution)/shard_map/ppermute | solution.py:197
  0.5 1.4 %fan.1 = (bf16[4,64,128]{2,1,0:T(8,128)(2,1)}, bf16[64,128]{1,0:T(8,128)(2,1)S(1)}, bf16[2,1024,128]{2,1,0:T(8,128)(2,1)S(1)}, bf16[2048,128]{1,0:T(8,128)(2,1)S(1)}) custom-call(bf16[64,128]{1,0:T(8,128)(2,1)} %bitcast.18, bf16[2,1024,128]{2,1,0:T(8,128)(2,1)} %bitcast.17, bf16[2048,128]{1,0:T(8,128)(2,1)} %bitcast.15), custom_call_target="tpu_custom_call" | custom-call | tf_op jit(solution)/shard_map/fan/pallas_call | solution.py:206
  1.9 7.0 %all-to-all-start = ((bf16[32,8,128]{2,1,0:T(8,128)(2,1)}), bf16[32,8,128]{2,1,0:T(8,128)(2,1)S(1)}, u32[]{:S(2)}, u32[]{:S(2)}) async-start(bf16[32,8,128]{2,1,0:T(8,128)(2,1)} %bitcast.3), calls=%async_computation | async-start | bytes 131072 | tf_op jit(solution)/shard_map/all_to_all | solution.py:195
  9.5 0.0 copy-start
  9.5 0.7 %copy-done = bf16[1,2,4,128]{3,2,1,0:T(4,128)(2,1)S(1)} copy-done((bf16[1,2,4,128]{3,2,1,0:T(4,128)(2,1)S(1)}, bf16[1,2,4,128]{3,2,1,0:T(4,128)(2,1)}, u32[]{:S(2)}) %copy-start) | copy-done | bytes 2072
  10.2 0.7 %suffix.1 = (f32[64,128]{1,0:T(8,128)S(1)}, f32[64,128]{1,0:T(8,128)S(1)}) custom-call(s32[1]{0:T(128)S(6)} %copy.7.len_ref, bf16[8,128]{1,0:T(8,128)(2,1)S(1)} %bitcast.13, bf16[64,128]{1,0:T(8,128)(2,1)S(1)} %get-tuple-element.15.q_ref, bf16[2048,128]{1,0:T(8,128)(2,1)S(1)} %get-tuple-element.16.cache_ref), custom_call_target="tpu_custom_call" | custom-call | flops 70000000 | bytes 600000 | tf_op jit(solution)/shard_map/suffix/pallas_call | solution.py:160
  10.9 5.4 %all-to-all-done = bf16[32,8,128]{2,1,0:T(8,128)(2,1)S(1)} async-done(((bf16[32,8,128]{2,1,0:T(8,128)(2,1)}), bf16[32,8,128]{2,1,0:T(8,128)(2,1)S(1)}, u32[]{:S(2)}, u32[]{:S(2)}) %all-to-all-start) | async-done | bytes 65568 | tf_op jit(solution)/shard_map/all_to_all | solution.py:195
  16.2 0.0 collective-permute-done
  16.2 1.0 %prefix.1 = bf16[320,128]{1,0:T(8,128)(2,1)S(1)} custom-call(bf16[256,128]{1,0:T(8,128)(2,1)S(1)} %bitcast.12, bf16[2,1024,128]{2,1,0:T(8,128)(2,1)S(1)} %get-tuple-element.20.kv_ref, bf16[2,1024,128]{2,1,0:T(8,128)(2,1)S(1)} %bitcast.14), custom_call_target="tpu_custom_call" | custom-call | flops 402653184 | bytes 1600000 | tf_op jit(solution)/shard_map/prefix/pallas_call | solution.py:160
  17.2 9.3 %all_to_all.10 = bf16[32,5,2,128]{3,2,1,0:T(2,128)(2,1)S(1)} all-to-all(bf16[32,5,2,128]{3,2,1,0:T(2,128)(2,1)S(1)} %bitcast.11), channel_id=1, replica_groups={{0,1,4,5,8,9,12,13,2,3,6,7,10,11,14,15,16,17,20,21,24,25,28,29,18,19,22..., dimensions={0} | all-to-all | bytes 163840 | tf_op jit(solution)/shard_map/all_to_all | solution.py:195
  26.5 0.8 %merge.1 = bf16[1,64,128]{2,1,0:T(8,128)(2,1)} custom-call(bf16[320,128]{1,0:T(8,128)(2,1)S(1)} %bitcast.10, f32[64,128]{1,0:T(8,128)S(1)} %get-tuple-element.21.suffix_ref, f32[64,128]{1,0:T(8,128)S(1)} %get-tuple-element.22.lse_ref), custom_call_target="tpu_custom_call" | custom-call | tf_op jit(solution)/shard_map/merge/pallas_call | solution.py:160
Async XLA Ops:
  0.0 16.2 %collective-permute-start = (bf16[2,1,1024,128]{3,2,0,1:T(8,128)(2,1)}, bf16[2,1,1024,128]{3,2,0,1:T(8,128)(2,1)S(1)}, u32[]{:S(2)}, u32[]{:S(2)}) collective-permute-start(bf16[2,1,1024,128]{3,2,0,1:T(8,128)(2,1)} %bitcast.16), channel_id=1, source_target_pairs={{0,1},{1,0},{2,3},{3,2},{4,5},{5,4},{6,7},{7,6},{8,9},{9,8},{10,11... | collective-permute-start | bytes 1572872 | tf_op jit(solution)/shard_map/ppermute | solution.py:197
  1.9 14.4 %all-to-all-start = ((bf16[32,8,128]{2,1,0:T(8,128)(2,1)}), bf16[32,8,128]{2,1,0:T(8,128)(2,1)S(1)}, u32[]{:S(2)}, u32[]{:S(2)}) async-start(bf16[32,8,128]{2,1,0:T(8,128)(2,1)} %bitcast.3), calls=%async_computation | async-start | bytes 131072 | tf_op jit(solution)/shard_map/all_to_all | solution.py:195
  9.5 0.7 %copy-start = (bf16[1,2,4,128]{3,2,1,0:T(4,128)(2,1)S(1)}, bf16[1,2,4,128]{3,2,1,0:T(4,128)(2,1)}, u32[]{:S(2)}) copy-start(bf16[1,2,4,128]{3,2,1,0:T(4,128)(2,1)} %param.8) | copy-start | bytes 6148

commit v22 on v21

--- a/solution.py
+++ b/solution.py
@@ -103,7 +103,7 @@
 
 
 def suffix_kernel(len_ref, new_ref, q_ref, cache_ref, out_ref, lse_ref):
-    q = q_ref[...]
+    q = q_ref[...].reshape(H, HD)
     cache = cache_ref[...]
     new = new_ref[...]
     raw = dot_nt(q, cache)
@@ -126,7 +126,11 @@
     for load in loads:
         load.start()
     loads[0].wait()
-    copies = [pltpu.make_async_copy(q_ref, out_ref.at[i], fan_sems.at[i]) for i in range(out_ref.shape[0])]
+    copies = [
+        pltpu.make_async_copy(q_ref, out_ref.at[chip, :, group], fan_sems.at[chip, group])
+        for chip in range(out_ref.shape[0])
+        for group in range(out_ref.shape[2])
+    ]
     for copy in copies:
         copy.start()
     for copy in copies + loads[1:]:
@@ -178,9 +182,9 @@
     chips = per_head // CORES
     order = [
         g * members + (head * chips + chip) * CORES + core
-        for g in range(groups)
         for chip in range(chips)
         for head in range(KVH)
+        for g in range(groups)
         for core in range(CORES)
     ]
     served = [device % members // per_head * CORES + device % CORES for device in order]
@@ -198,17 +202,17 @@
     bound = [
         pltpu.with_memory_space_constraint(array, pltpu.HBM)
         for array in (
-            queries.reshape(H, HD),
+            queries.reshape(KVH, SHARE, HD),
             prefix_kv.reshape(2, span, HD),
             suffix_kv.reshape(cache_rows, HD),
         )
     ]
     outgoing, q, kv, cache = pl.pallas_call(
         fan_kernel,
-        out_shape=[half(groups * chips, H), half(H), half(2, span), half(cache_rows)],
+        out_shape=[half(chips, KVH, groups, SHARE), half(KVH, SHARE), half(2, span), half(cache_rows)],
         in_specs=[pl.BlockSpec(memory_space=pltpu.HBM)] * 3,
         out_specs=[pl.BlockSpec(memory_space=pl.ANY), VMEM, VMEM, VMEM],
-        scratch_shapes=[pltpu.SemaphoreType.DMA((3,)), pltpu.SemaphoreType.DMA((groups * chips,))],
+        scratch_shapes=[pltpu.SemaphoreType.DMA((3,)), pltpu.SemaphoreType.DMA((chips, groups))],
         name="fan",
         compiler_params=pltpu.CompilerParams(vmem_limit_bytes=LIMIT),
     )(*bound)

time: 27.6 us -> 27.7 us (level)
  no operation moved by 1% of the time
where the time goes in v22:
time: 27.7 us; the launch traced here: 27.4 us
  blocking collectives  9.3 us (34%)
  starting transfers between devices  7.42 us (27%)
  waiting for transfers between devices  5.38 us (19%)
  Pallas kernels  3.89 us (14%)
  between operations  0.69 us (2%)
  local copies, waits for them, and re-layouts  0.68 us (2%)
    all_to_all x1, blocking collectives, exchange(): lax.all_to_all(array, ('grp', 'blk'), 0, 0, axis_index_groups=[order], ti...  9.3 us
    all_to_all x1, starting transfers between devices, exchange(): lax.all_to_all(array, ('grp', 'blk'), 0, 0, axis_index_groups=[order], ti...  6.97 us
    all_to_all x1, waiting for transfers between devices, exchange(): lax.all_to_all(array, ('grp', 'blk'), 0, 0, axis_index_groups=[order], ti...  5.38 us
    pallas_call x3, Pallas kernels, call(): pl.pallas_call(kernel, out_shape=outs, in_specs=specs or [VMEM] * len(ope...  2.5 us
    pallas_call x1, Pallas kernels, local(): pl.pallas_call(fan_kernel, out_shape=[half(chips, KVH, groups, SHARE), ha...  1.4 us
    unnamed x2, local copies, waits for them, and re-layouts  0.68 us
  transfers between devices with their start and end apart: 2, of which 1 were waited for; matrix products, arithmetic and copies ran while one was open for 0% of the time, Pallas kernels for 8%

profile of v22, /device:TPU:0, one launch (start us, length us, event | category | flops | bytes accessed | tf_op | source)
XLA Modules:
  0.0 27.4 jit_solution(12174524057679609272)
XLA Ops:
  0.0 0.5 %collective-permute-start = (bf16[2,1,1024,128]{3,2,0,1:T(8,128)(2,1)}, bf16[2,1,1024,128]{3,2,0,1:T(8,128)(2,1)S(1)}, u32[]{:S(2)}, u32[]{:S(2)}) collective-permute-start(bf16[2,1,1024,128]{3,2,0,1:T(8,128)(2,1)} %bitcast.16), channel_id=1, source_target_pairs={{0,1},{1,0},{2,3},{3,2},{4,5},{5,4},{6,7},{7,6},{8,9},{9,8},{10,11... | collective-permute-start | bytes 1572872 | tf_op jit(solution)/shard_map/ppermute | solution.py:201
  0.5 1.4 %fan.1 = (bf16[2,4,2,16,128]{4,3,2,1,0:T(8,128)(2,1)}, bf16[4,16,128]{2,1,0:T(8,128)(2,1)S(1)}, bf16[2,1024,128]{2,1,0:T(8,128)(2,1)S(1)}, bf16[2048,128]{1,0:T(8,128)(2,1)S(1)}) custom-call(bf16[4,16,128]{2,1,0:T(8,128)(2,1)} %bitcast.18, bf16[2,1024,128]{2,1,0:T(8,128)(2,1)} %bitcast.17, bf16[2048,128]{1,0:T(8,128)(2,1)} %bitcast.15), custom_call_target="tpu_custom_call" | custom-call | tf_op jit(solution)/shard_map/fan/pallas_call | solution.py:210
  1.9 7.0 %all-to-all-start = ((bf16[32,8,128]{2,1,0:T(8,128)(2,1)}), bf16[32,8,128]{2,1,0:T(8,128)(2,1)S(1)}, u32[]{:S(2)}, u32[]{:S(2)}) async-start(bf16[32,8,128]{2,1,0:T(8,128)(2,1)} %bitcast.3), calls=%async_computation | async-start | bytes 131072 | tf_op jit(solution)/shard_map/all_to_all | solution.py:199
  9.5 0.0 copy-start
  9.5 0.7 %copy-done = bf16[1,2,4,128]{3,2,1,0:T(4,128)(2,1)S(1)} copy-done((bf16[1,2,4,128]{3,2,1,0:T(4,128)(2,1)S(1)}, bf16[1,2,4,128]{3,2,1,0:T(4,128)(2,1)}, u32[]{:S(2)}) %copy-start) | copy-done | bytes 2072
  10.2 0.7 %suffix.1 = (f32[64,128]{1,0:T(8,128)S(1)}, f32[64,128]{1,0:T(8,128)S(1)}) custom-call(s32[1]{0:T(128)S(6)} %copy.7.len_ref, bf16[8,128]{1,0:T(8,128)(2,1)S(1)} %bitcast.13, bf16[4,16,128]{2,1,0:T(8,128)(2,1)S(1)} %get-tuple-element.15.q_ref, bf16[2048,128]{1,0:T(8,128)(2,1)S(1)} %get-tuple-element.16.cache_ref), custom_call_target="tpu_custom_call" | custom-call | flops 70000000 | bytes 600000 | tf_op jit(solution)/shard_map/suffix/pallas_call | solution.py:164
  10.9 5.4 %all-to-all-done = bf16[32,8,128]{2,1,0:T(8,128)(2,1)S(1)} async-done(((bf16[32,8,128]{2,1,0:T(8,128)(2,1)}), bf16[32,8,128]{2,1,0:T(8,128)(2,1)S(1)}, u32[]{:S(2)}, u32[]{:S(2)}) %all-to-all-start) | async-done | bytes 65568 | tf_op jit(solution)/shard_map/all_to_all | solution.py:199
  16.2 0.0 collective-permute-done
  16.2 1.0 %prefix.1 = bf16[320,128]{1,0:T(8,128)(2,1)S(1)} custom-call(bf16[256,128]{1,0:T(8,128)(2,1)S(1)} %bitcast.12, bf16[2,1024,128]{2,1,0:T(8,128)(2,1)S(1)} %get-tuple-element.20.kv_ref, bf16[2,1024,128]{2,1,0:T(8,128)(2,1)S(1)} %bitcast.14), custom_call_target="tpu_custom_call" | custom-call | flops 402653184 | bytes 1600000 | tf_op jit(solution)/shard_map/prefix/pallas_call | solution.py:164
  17.3 9.3 %all_to_all.10 = bf16[32,5,2,128]{3,2,1,0:T(2,128)(2,1)S(1)} all-to-all(bf16[32,5,2,128]{3,2,1,0:T(2,128)(2,1)S(1)} %bitcast.11), channel_id=1, replica_groups={{0,1,16,17,4,5,20,21,8,9,24,25,12,13,28,29,2,3,18,19,6,7,22,23,10,11,26..., dimensions={0} | all-to-all | bytes 163840 | tf_op jit(solution)/shard_map/all_to_all | solution.py:199
  26.6 0.8 %merge.1 = bf16[1,64,128]{2,1,0:T(8,128)(2,1)} custom-call(bf16[320,128]{1,0:T(8,128)(2,1)S(1)} %bitcast.10, f32[64,128]{1,0:T(8,128)S(1)} %get-tuple-element.21.suffix_ref, f32[64,128]{1,0:T(8,128)S(1)} %get-tuple-element.22.lse_ref), custom_call_target="tpu_custom_call" | custom-call | tf_op jit(solution)/shard_map/merge/pallas_call | solution.py:164
Async XLA Ops:
  0.0 16.2 %collective-permute-start = (bf16[2,1,1024,128]{3,2,0,1:T(8,128)(2,1)}, bf16[2,1,1024,128]{3,2,0,1:T(8,128)(2,1)S(1)}, u32[]{:S(2)}, u32[]{:S(2)}) collective-permute-start(bf16[2,1,1024,128]{3,2,0,1:T(8,128)(2,1)} %bitcast.16), channel_id=1, source_target_pairs={{0,1},{1,0},{2,3},{3,2},{4,5},{5,4},{6,7},{7,6},{8,9},{9,8},{10,11... | collective-permute-start | bytes 1572872 | tf_op jit(solution)/shard_map/ppermute | solution.py:201
  1.9 14.4 %all-to-all-start = ((bf16[32,8,128]{2,1,0:T(8,128)(2,1)}), bf16[32,8,128]{2,1,0:T(8,128)(2,1)S(1)}, u32[]{:S(2)}, u32[]{:S(2)}) async-start(bf16[32,8,128]{2,1,0:T(8,128)(2,1)} %bitcast.3), calls=%async_computation | async-start | bytes 131072 | tf_op jit(solution)/shard_map/all_to_all | solution.py:199
  9.5 0.7 %copy-start = (bf16[1,2,4,128]{3,2,1,0:T(4,128)(2,1)S(1)}, bf16[1,2,4,128]{3,2,1,0:T(4,128)(2,1)}, u32[]{:S(2)}) copy-start(bf16[1,2,4,128]{3,2,1,0:T(4,128)(2,1)} %param.8) | copy-start | bytes 6148

commit v23 on v11

--- a/solution.py
+++ b/solution.py
@@ -53,7 +53,7 @@
     return dot(jnp.concatenate(pieces, axis=0).astype(jnp.bfloat16), jnp.ones((HD, HD), jnp.bfloat16))
 
 
-def prefix_kernel(q_ref, kv_ref, other_ref, out_ref):
+def prefix_kernel(q_ref, kv_ref, other_ref, out_ref, message_ref):
     chunks = [(ref, at) for ref in (other_ref, kv_ref) for at in range(0, ref.shape[1], CHUNK)]
 
     def block(trip):
@@ -79,10 +79,11 @@
         slots = ROWS // HALF
         stats = pack_stats((best * SCALE2 + log2(total)).reshape(slots, HALF, HD))
         empty = jnp.zeros((1, HD), jnp.float32)
-        pieces = []
         for slot in range(slots):
-            pieces += [result[slot * HALF : (slot + 1) * HALF], stats[slot : slot + 1], empty]
-        out_ref[pl.ds(trip * slots * MESSAGE, slots * MESSAGE)] = jnp.concatenate(pieces, axis=0).astype(jnp.bfloat16)
+            at = slot * MESSAGE
+            message_ref[at : at + HALF] = result[slot * HALF : (slot + 1) * HALF]
+            message_ref[at + HALF : at + MESSAGE] = jnp.concatenate([stats[slot : slot + 1], empty], axis=0)
+        out_ref[pl.ds(trip * slots * MESSAGE, slots * MESSAGE)] = message_ref[...].astype(jnp.bfloat16)
 
     trips = q_ref.shape[0] // ROWS
     if trips == 1:
@@ -137,11 +138,11 @@
         copy.wait()
 
 
-def merge_kernel(served, part_ref, suffix_ref, lse_ref, out_ref):
-    part = part_ref[...].astype(jnp.float32)
+def merge_kernel(served, part_ref, suffix_ref, lse_ref, out_ref, message_ref):
+    message_ref[...] = part_ref[...].astype(jnp.float32)
     starts = range(0, len(served) * MESSAGE, MESSAGE)
-    rows = [part[at : at + HALF] for at in starts]
-    sums = unpack_stats([part[at + HALF : at + HALF + 1] for at in starts]).reshape(len(served), HALF, HD)
+    rows = [message_ref[at : at + HALF] for at in starts]
+    sums = unpack_stats([message_ref[at + HALF : at + HALF + 1] for at in starts]).reshape(len(served), HALF, HD)
     blocks = []
     for block in range(H // HALF):
         span = slice(block * HALF, (block + 1) * HALF)
@@ -160,12 +161,13 @@
     out_ref[0] = jnp.concatenate(blocks, axis=0).astype(jnp.bfloat16)
 
 
-def call(kernel, name, outs, operands, specs=None, **cost):
+def call(kernel, name, outs, operands, specs=None, scratch=(), **cost):
     return pl.pallas_call(
         kernel,
         out_shape=outs,
         in_specs=specs or [VMEM] * len(operands),
         out_specs=jax.tree.map(lambda _: VMEM, outs),
+        scratch_shapes=scratch,
         name=name,
         compiler_params=pltpu.CompilerParams(vmem_limit_bytes=LIMIT),
         cost_estimate=pl.CostEstimate(**cost) if cost else None,
@@ -226,6 +228,7 @@
         "prefix",
         half(devices * MESSAGE),
         (arrived, kv, other),
+        scratch=[pltpu.VMEM((ROWS // HALF * MESSAGE, HD), jnp.float32)],
         flops=12 * devices * HALF * span * HD,
         bytes_accessed=1_600_000,
         transcendentals=2 * devices * HALF * span,
@@ -236,6 +239,7 @@
         "merge",
         jax.ShapeDtypeStruct((1, H, HD), jnp.bfloat16),
         (returned, *suffix),
+        scratch=[pltpu.VMEM((devices * MESSAGE, HD), jnp.float32)],
     )
 
 

time: 27.7 us -> 27.7 us (level)
  no operation moved by 1% of the time
where the time goes in v23:
time: 27.7 us; the launch traced here: 27.4 us
  blocking collectives  9.3 us (34%)
  starting transfers between devices  7.42 us (27%)
  waiting for transfers between devices  5.38 us (19%)
  Pallas kernels  3.91 us (14%)
  local copies, waits for them, and re-layouts  0.68 us (2%)
  between operations  0.68 us (2%)
    all_to_all x1, blocking collectives, exchange(): return lax.all_to_all(array, ('grp', 'blk'), 0, 0, tiled=True)  9.3 us
    all_to_all x1, starting transfers between devices, exchange(): return lax.all_to_all(array, ('grp', 'blk'), 0, 0, tiled=True)  6.97 us
    all_to_all x1, waiting for transfers between devices, exchange(): return lax.all_to_all(array, ('grp', 'blk'), 0, 0, tiled=True)  5.38 us
    pallas_call x3, Pallas kernels, call(): pl.pallas_call(kernel, out_shape=outs, in_specs=specs or [VMEM] * len(ope...  2.52 us
    pallas_call x1, Pallas kernels, local(): pl.pallas_call(fan_kernel, out_shape=[half(groups, KVH, chips, SHARE), ha...  1.4 us
    unnamed x2, local copies, waits for them, and re-layouts  0.68 us
  transfers between devices with their start and end apart: 2, of which 1 were waited for; matrix products, arithmetic and copies ran while one was open for 0% of the time, Pallas kernels for 8%

profile of v23, /device:TPU:0, one launch (start us, length us, event | category | flops | bytes accessed | tf_op | source)
XLA Modules:
  0.0 27.4 jit_solution(14630894573064187405)
XLA Ops:
  0.0 0.5 %collective-permute-start = (bf16[2,1,1024,128]{3,2,0,1:T(8,128)(2,1)}, bf16[2,1,1024,128]{3,2,0,1:T(8,128)(2,1)S(1)}, u32[]{:S(2)}, u32[]{:S(2)}) collective-permute-start(bf16[2,1,1024,128]{3,2,0,1:T(8,128)(2,1)} %bitcast.16), channel_id=1, source_target_pairs={{0,1},{1,0},{2,3},{3,2},{4,5},{5,4},{6,7},{7,6},{8,9},{9,8},{10,11... | collective-permute-start | bytes 1572872 | tf_op jit(solution)/shard_map/ppermute | solution.py:196
  0.5 1.4 %fan.1 = (bf16[2,4,2,16,128]{4,3,2,1,0:T(8,128)(2,1)}, bf16[4,16,128]{2,1,0:T(8,128)(2,1)S(1)}, bf16[2,1024,128]{2,1,0:T(8,128)(2,1)S(1)}, bf16[2048,128]{1,0:T(8,128)(2,1)S(1)}) custom-call(bf16[4,16,128]{2,1,0:T(8,128)(2,1)} %bitcast.18, bf16[2,1024,128]{2,1,0:T(8,128)(2,1)} %bitcast.17, bf16[2048,128]{1,0:T(8,128)(2,1)} %bitcast.15), custom_call_target="tpu_custom_call" | custom-call | tf_op jit(solution)/shard_map/fan/pallas_call | solution.py:205
  1.9 7.0 %all-to-all-start = ((bf16[32,8,128]{2,1,0:T(8,128)(2,1)}), bf16[32,8,128]{2,1,0:T(8,128)(2,1)S(1)}, u32[]{:S(2)}, u32[]{:S(2)}) async-start(bf16[32,8,128]{2,1,0:T(8,128)(2,1)} %bitcast.3), calls=%async_computation | async-start | bytes 131072 | tf_op jit(solution)/shard_map/all_to_all | solution.py:194
  9.5 0.0 copy-start
  9.5 0.7 %copy-done = bf16[1,2,4,128]{3,2,1,0:T(4,128)(2,1)S(1)} copy-done((bf16[1,2,4,128]{3,2,1,0:T(4,128)(2,1)S(1)}, bf16[1,2,4,128]{3,2,1,0:T(4,128)(2,1)}, u32[]{:S(2)}) %copy-start) | copy-done | bytes 2072
  10.2 0.7 %suffix.1 = (f32[64,128]{1,0:T(8,128)S(1)}, f32[64,128]{1,0:T(8,128)S(1)}) custom-call(s32[1]{0:T(128)S(6)} %copy.7.len_ref, bf16[8,128]{1,0:T(8,128)(2,1)S(1)} %bitcast.13, bf16[4,16,128]{2,1,0:T(8,128)(2,1)S(1)} %get-tuple-element.15.q_ref, bf16[2048,128]{1,0:T(8,128)(2,1)S(1)} %get-tuple-element.16.cache_ref), custom_call_target="tpu_custom_call" | custom-call | flops 70000000 | bytes 600000 | tf_op jit(solution)/shard_map/suffix/pallas_call | solution.py:165
  10.9 5.4 %all-to-all-done = bf16[32,8,128]{2,1,0:T(8,128)(2,1)S(1)} async-done(((bf16[32,8,128]{2,1,0:T(8,128)(2,1)}), bf16[32,8,128]{2,1,0:T(8,128)(2,1)S(1)}, u32[]{:S(2)}, u32[]{:S(2)}) %all-to-all-start) | async-done | bytes 65568 | tf_op jit(solution)/shard_map/all_to_all | solution.py:194
  16.2 0.0 collective-permute-done
  16.2 1.0 %prefix.1 = bf16[320,128]{1,0:T(8,128)(2,1)S(1)} custom-call(bf16[256,128]{1,0:T(8,128)(2,1)S(1)} %bitcast.12, bf16[2,1024,128]{2,1,0:T(8,128)(2,1)S(1)} %get-tuple-element.20.kv_ref, bf16[2,1024,128]{2,1,0:T(8,128)(2,1)S(1)} %bitcast.14), custom_call_target="tpu_custom_call" | custom-call | flops 402653184 | bytes 1600000 | tf_op jit(solution)/shard_map/prefix/pallas_call | solution.py:165
  17.3 9.3 %all_to_all.10 = bf16[32,5,2,128]{3,2,1,0:T(2,128)(2,1)S(1)} all-to-all(bf16[32,5,2,128]{3,2,1,0:T(2,128)(2,1)S(1)} %bitcast.11), channel_id=1, replica_groups=mesh['grp'=2,'blk'=16] {'grp','blk'}, dimensions={0} | all-to-all | bytes 163840 | tf_op jit(solution)/shard_map/all_to_all | solution.py:194
  26.6 0.8 %merge.1 = bf16[1,64,128]{2,1,0:T(8,128)(2,1)} custom-call(bf16[320,128]{1,0:T(8,128)(2,1)S(1)} %bitcast.10, f32[64,128]{1,0:T(8,128)S(1)} %get-tuple-element.21.suffix_ref, f32[64,128]{1,0:T(8,128)S(1)} %get-tuple-element.22.lse_ref), custom_call_target="tpu_custom_call" | custom-call | tf_op jit(solution)/shard_map/merge/pallas_call | solution.py:165
Async XLA Ops:
  0.0 16.2 %collective-permute-start = (bf16[2,1,1024,128]{3,2,0,1:T(8,128)(2,1)}, bf16[2,1,1024,128]{3,2,0,1:T(8,128)(2,1)S(1)}, u32[]{:S(2)}, u32[]{:S(2)}) collective-permute-start(bf16[2,1,1024,128]{3,2,0,1:T(8,128)(2,1)} %bitcast.16), channel_id=1, source_target_pairs={{0,1},{1,0},{2,3},{3,2},{4,5},{5,4},{6,7},{7,6},{8,9},{9,8},{10,11... | collective-permute-start | bytes 1572872 | tf_op jit(solution)/shard_map/ppermute | solution.py:196
  1.9 14.4 %all-to-all-start = ((bf16[32,8,128]{2,1,0:T(8,128)(2,1)}), bf16[32,8,128]{2,1,0:T(8,128)(2,1)S(1)}, u32[]{:S(2)}, u32[]{:S(2)}) async-start(bf16[32,8,128]{2,1,0:T(8,128)(2,1)} %bitcast.3), calls=%async_computation | async-start | bytes 131072 | tf_op jit(solution)/shard_map/all_to_all | solution.py:194
  9.5 0.7 %copy-start = (bf16[1,2,4,128]{3,2,1,0:T(4,128)(2,1)S(1)}, bf16[1,2,4,128]{3,2,1,0:T(4,128)(2,1)}, u32[]{:S(2)}) copy-start(bf16[1,2,4,128]{3,2,1,0:T(4,128)(2,1)} %param.8) | copy-start | bytes 6148

commit v24 on v11

--- a/solution.py
+++ b/solution.py
@@ -20,6 +20,7 @@
 HALF = SHARE // CORES
 MESSAGE = HALF + 2
 LANES = HD // HALF
+ONES = 16
 LIMIT = 24 * 1024 * 1024
 NT = (((1,), (1,)), ((), ()))
 
@@ -53,31 +54,32 @@
     return dot(jnp.concatenate(pieces, axis=0).astype(jnp.bfloat16), jnp.ones((HD, HD), jnp.bfloat16))
 
 
-def prefix_kernel(q_ref, kv_ref, other_ref, out_ref):
-    chunks = [(ref, at) for ref in (other_ref, kv_ref) for at in range(0, ref.shape[1], CHUNK)]
+def prefix_kernel(q_ref, kv_ref, other_ref, values_ref, other_values_ref, out_ref):
+    pairs = [(other_ref, other_values_ref), (kv_ref, values_ref)]
+    chunks = [(ref, values, at) for ref, values in pairs for at in range(0, ref.shape[1], CHUNK)]
 
     def block(trip):
         rows = q_ref[pl.ds(trip * ROWS, ROWS)]
 
-        def score(ref, first):
-            return dot_nt(rows, ref[0, first : first + CHUNK])
+        def score(ref, values, first):
+            return dot_nt(ref[0, first : first + CHUNK], rows)
 
         parts = []
         ahead = score(*chunks[0])
-        for index, (ref, first) in enumerate(chunks):
+        for index, (ref, values, first) in enumerate(chunks):
             scores = ahead
             if index + 1 < len(chunks):
                 ahead = score(*chunks[index + 1])
-            best = jnp.max(scores, axis=1, keepdims=True)
+            best = jnp.max(scores, axis=0, keepdims=True)
             weight = jnp.exp2((scores - best) * SCALE2).astype(jnp.bfloat16)
-            values = ref[1, first : first + CHUNK]
-            parts.append((best, dot(weight, jnp.concatenate([values, jnp.ones_like(values)], axis=1))))
+            parts.append((best, dot(values[:, first : first + CHUNK], weight)))
         best = functools.reduce(jnp.maximum, [part[0] for part in parts])
         both = sum(jnp.exp2((its - best) * SCALE2) * sums for its, sums in parts)
-        total = both[:, HD:]
-        result = both[:, :HD] / total
+        total = both[HD : HD + 1]
+        result = (both[:HD] / total).T
+        lse = jnp.broadcast_to(best * SCALE2 + log2(total), (HD, ROWS)).T
         slots = ROWS // HALF
-        stats = pack_stats((best * SCALE2 + log2(total)).reshape(slots, HALF, HD))
+        stats = pack_stats(lse.reshape(slots, HALF, HD))
         empty = jnp.zeros((1, HD), jnp.float32)
         pieces = []
         for slot in range(slots):
@@ -102,7 +104,10 @@
     return (at % (2 * KVH) == head) & (at < limit * (2 * KVH))
 
 
-def suffix_kernel(len_ref, new_ref, q_ref, cache_ref, out_ref, lse_ref):
+def suffix_kernel(len_ref, new_ref, q_ref, cache_ref, kv_ref, other_ref, out_ref, lse_ref, values_ref, other_values_ref):
+    for ref, transposed in ((kv_ref, values_ref), (other_ref, other_values_ref)):
+        transposed[:HD] = ref[1].T
+        transposed[HD:] = jnp.ones((ONES, ref.shape[1]), jnp.bfloat16)
     q = q_ref[...].reshape(H, HD)
     cache = cache_ref[...]
     new = new_ref[...]
@@ -210,12 +215,13 @@
         compiler_params=pltpu.CompilerParams(vmem_limit_bytes=LIMIT),
     )(*bound)
     arrived = exchange(outgoing.reshape(devices, HALF, HD)).reshape(devices * HALF, HD)
+    transposed = jax.ShapeDtypeStruct((HD + ONES, span), jnp.bfloat16)
     suffix = call(
         suffix_kernel,
         "suffix",
-        [one(H)] * 2,
-        (suffix_len, new_kv.reshape(2 * KVH, HD), q, cache),
-        [pl.BlockSpec(memory_space=pltpu.SMEM), VMEM, VMEM, VMEM],
+        [one(H), one(H), transposed, transposed],
+        (suffix_len, new_kv.reshape(2 * KVH, HD), q, cache, kv, other),
+        [pl.BlockSpec(memory_space=pltpu.SMEM)] + [VMEM] * 5,
         flops=70_000_000,
         bytes_accessed=600_000,
         transcendentals=140_000,
@@ -225,7 +231,7 @@
         prefix_kernel,
         "prefix",
         half(devices * MESSAGE),
-        (arrived, kv, other),
+        (arrived, kv, other, *suffix[2:]),
         flops=12 * devices * HALF * span * HD,
         bytes_accessed=1_600_000,
         transcendentals=2 * devices * HALF * span,
@@ -235,7 +241,7 @@
         functools.partial(merge_kernel, served),
         "merge",
         jax.ShapeDtypeStruct((1, H, HD), jnp.bfloat16),
-        (returned, *suffix),
+        (returned, *suffix[:2]),
     )
 
 

time: 27.7 us -> 27.8 us (level)
  no operation moved by 1% of the time
where the time goes in v24:
time: 27.8 us; the launch traced here: 27.5 us
  blocking collectives  9.3 us (33%)
  starting transfers between devices  7.42 us (27%)
  waiting for transfers between devices  5.35 us (19%)
  Pallas kernels  4.06 us (15%)
  between operations  0.7 us (3%)
  local copies, waits for them, and re-layouts  0.68 us (2%)
    all_to_all x1, blocking collectives, exchange(): return lax.all_to_all(array, ('grp', 'blk'), 0, 0, tiled=True)  9.3 us
    all_to_all x1, starting transfers between devices, exchange(): return lax.all_to_all(array, ('grp', 'blk'), 0, 0, tiled=True)  6.97 us
    all_to_all x1, waiting for transfers between devices, exchange(): return lax.all_to_all(array, ('grp', 'blk'), 0, 0, tiled=True)  5.34 us
    pallas_call x3, Pallas kernels, call(): pl.pallas_call(kernel, out_shape=outs, in_specs=specs or [VMEM] * len(ope...  2.66 us
    pallas_call x1, Pallas kernels, local(): pl.pallas_call(fan_kernel, out_shape=[half(groups, KVH, chips, SHARE), ha...  1.4 us
    unnamed x2, local copies, waits for them, and re-layouts  0.68 us
  transfers between devices with their start and end apart: 2, of which 1 were waited for; matrix products, arithmetic and copies ran while one was open for 0% of the time, Pallas kernels for 8%

profile of v24, /device:TPU:0, one launch (start us, length us, event | category | flops | bytes accessed | tf_op | source)
XLA Modules:
  0.0 27.5 jit_solution(17907144693310905185)
XLA Ops:
  0.0 0.5 %collective-permute-start = (bf16[2,1,1024,128]{3,2,0,1:T(8,128)(2,1)}, bf16[2,1,1024,128]{3,2,0,1:T(8,128)(2,1)S(1)}, u32[]{:S(2)}, u32[]{:S(2)}) collective-permute-start(bf16[2,1,1024,128]{3,2,0,1:T(8,128)(2,1)} %bitcast.17), channel_id=1, source_target_pairs={{0,1},{1,0},{2,3},{3,2},{4,5},{5,4},{6,7},{7,6},{8,9},{9,8},{10,11... | collective-permute-start | bytes 1572872 | tf_op jit(solution)/shard_map/ppermute | solution.py:199
  0.5 1.4 %fan.1 = (bf16[2,4,2,16,128]{4,3,2,1,0:T(8,128)(2,1)}, bf16[4,16,128]{2,1,0:T(8,128)(2,1)S(1)}, bf16[2,1024,128]{2,1,0:T(8,128)(2,1)S(1)}, bf16[2048,128]{1,0:T(8,128)(2,1)S(1)}) custom-call(bf16[4,16,128]{2,1,0:T(8,128)(2,1)} %bitcast.19, bf16[2,1024,128]{2,1,0:T(8,128)(2,1)} %bitcast.18, bf16[2048,128]{1,0:T(8,128)(2,1)} %bitcast.16), custom_call_target="tpu_custom_call" | custom-call | tf_op jit(solution)/shard_map/fan/pallas_call | solution.py:208
  1.9 7.0 %all-to-all-start = ((bf16[32,8,128]{2,1,0:T(8,128)(2,1)}), bf16[32,8,128]{2,1,0:T(8,128)(2,1)S(1)}, u32[]{:S(2)}, u32[]{:S(2)}) async-start(bf16[32,8,128]{2,1,0:T(8,128)(2,1)} %bitcast.3), calls=%async_computation | async-start | bytes 131072 | tf_op jit(solution)/shard_map/all_to_all | solution.py:197
  9.5 0.0 collective-permute-done
  9.5 0.0 copy-start
  9.5 0.7 %copy-done = bf16[1,2,4,128]{3,2,1,0:T(4,128)(2,1)S(1)} copy-done((bf16[1,2,4,128]{3,2,1,0:T(4,128)(2,1)S(1)}, bf16[1,2,4,128]{3,2,1,0:T(4,128)(2,1)}, u32[]{:S(2)}) %copy-start) | copy-done | bytes 2072
  10.2 0.7 %suffix.1 = (f32[64,128]{1,0:T(8,128)S(1)}, f32[64,128]{1,0:T(8,128)S(1)}, bf16[144,1024]{1,0:T(8,128)(2,1)S(1)}, bf16[144,1024]{1,0:T(8,128)(2,1)S(1)}) custom-call(s32[1]{0:T(128)S(6)} %copy.7.len_ref, bf16[8,128]{1,0:T(8,128)(2,1)S(1)} %bitcast.15, bf16[4,16,128]{2,1,0:T(8,128)(2,1)S(1)} %get-tuple-element.19.q_ref, ...), custom_call_target="tpu_custom_call" | custom-call | flops 70000000 | bytes 600000 | tf_op jit(solution)/shard_map/suffix/pallas_call | solution.py:169
  10.9 5.3 %all-to-all-done = bf16[32,8,128]{2,1,0:T(8,128)(2,1)S(1)} async-done(((bf16[32,8,128]{2,1,0:T(8,128)(2,1)}), bf16[32,8,128]{2,1,0:T(8,128)(2,1)S(1)}, u32[]{:S(2)}, u32[]{:S(2)}) %all-to-all-start) | async-done | bytes 65568 | tf_op jit(solution)/shard_map/all_to_all | solution.py:197
  16.2 1.2 %prefix.1 = bf16[320,128]{1,0:T(8,128)(2,1)S(1)} custom-call(bf16[256,128]{1,0:T(8,128)(2,1)S(1)} %bitcast.14, bf16[2,1024,128]{2,1,0:T(8,128)(2,1)S(1)} %get-tuple-element.21.kv_ref, bf16[2,1024,128]{2,1,0:T(8,128)(2,1)S(1)} %bitcast.11, bf16[144,1024]{1,0:T(8,128)(2,1)S(1)} %get-tuple-element.27.values_ref, ...), custom_call_target="tpu_custom_call" | custom-call | flops 402653184 | bytes 1600000 | tf_op jit(solution)/shard_map/prefix/pallas_call | solution.py:169
  17.4 9.3 %all_to_all.10 = bf16[32,5,2,128]{3,2,1,0:T(2,128)(2,1)S(1)} all-to-all(bf16[32,5,2,128]{3,2,1,0:T(2,128)(2,1)S(1)} %bitcast.12), channel_id=1, replica_groups=mesh['grp'=2,'blk'=16] {'grp','blk'}, dimensions={0} | all-to-all | bytes 163840 | tf_op jit(solution)/shard_map/all_to_all | solution.py:197
  26.7 0.8 %merge.1 = bf16[1,64,128]{2,1,0:T(8,128)(2,1)} custom-call(bf16[320,128]{1,0:T(8,128)(2,1)S(1)} %bitcast.13, f32[64,128]{1,0:T(8,128)S(1)} %get-tuple-element.29.suffix_ref, f32[64,128]{1,0:T(8,128)S(1)} %get-tuple-element.30.lse_ref), custom_call_target="tpu_custom_call" | custom-call | tf_op jit(solution)/shard_map/merge/pallas_call | solution.py:169
Async XLA Ops:
  0.0 9.5 %collective-permute-start = (bf16[2,1,1024,128]{3,2,0,1:T(8,128)(2,1)}, bf16[2,1,1024,128]{3,2,0,1:T(8,128)(2,1)S(1)}, u32[]{:S(2)}, u32[]{:S(2)}) collective-permute-start(bf16[2,1,1024,128]{3,2,0,1:T(8,128)(2,1)} %bitcast.17), channel_id=1, source_target_pairs={{0,1},{1,0},{2,3},{3,2},{4,5},{5,4},{6,7},{7,6},{8,9},{9,8},{10,11... | collective-permute-start | bytes 1572872 | tf_op jit(solution)/shard_map/ppermute | solution.py:199
  1.9 14.4 %all-to-all-start = ((bf16[32,8,128]{2,1,0:T(8,128)(2,1)}), bf16[32,8,128]{2,1,0:T(8,128)(2,1)S(1)}, u32[]{:S(2)}, u32[]{:S(2)}) async-start(bf16[32,8,128]{2,1,0:T(8,128)(2,1)} %bitcast.3), calls=%async_computation | async-start | bytes 131072 | tf_op jit(solution)/shard_map/all_to_all | solution.py:197
  9.5 0.7 %copy-start = (bf16[1,2,4,128]{3,2,1,0:T(4,128)(2,1)S(1)}, bf16[1,2,4,128]{3,2,1,0:T(4,128)(2,1)}, u32[]{:S(2)}) copy-start(bf16[1,2,4,128]{3,2,1,0:T(4,128)(2,1)} %param.8) | copy-start | bytes 6148

commit v25 on v11

--- a/solution.py
+++ b/solution.py
@@ -15,7 +15,7 @@
 SCALE2 = HD ** (-0.5) * math.log2(math.e)
 VMEM = pl.BlockSpec(memory_space=pltpu.VMEM)
 ROWS = 256
-CHUNK = 512
+EDGE = 256
 CORES = 2
 HALF = SHARE // CORES
 MESSAGE = HALF + 2
@@ -54,23 +54,29 @@
 
 
 def prefix_kernel(q_ref, kv_ref, other_ref, out_ref):
-    chunks = [(ref, at) for ref in (other_ref, kv_ref) for at in range(0, ref.shape[1], CHUNK)]
+    span = kv_ref.shape[1]
+    chunks = [
+        (other_ref, slice(0, EDGE)),
+        (other_ref, slice(EDGE, span)),
+        (kv_ref, slice(0, span - EDGE)),
+        (kv_ref, slice(span - EDGE, span)),
+    ]
 
     def block(trip):
         rows = q_ref[pl.ds(trip * ROWS, ROWS)]
 
-        def score(ref, first):
-            return dot_nt(rows, ref[0, first : first + CHUNK])
+        def score(ref, positions):
+            return dot_nt(rows, ref[0, positions])
 
         parts = []
         ahead = score(*chunks[0])
-        for index, (ref, first) in enumerate(chunks):
+        for index, (ref, positions) in enumerate(chunks):
             scores = ahead
             if index + 1 < len(chunks):
                 ahead = score(*chunks[index + 1])
             best = jnp.max(scores, axis=1, keepdims=True)
             weight = jnp.exp2((scores - best) * SCALE2).astype(jnp.bfloat16)
-            values = ref[1, first : first + CHUNK]
+            values = ref[1, positions]
             parts.append((best, dot(weight, jnp.concatenate([values, jnp.ones_like(values)], axis=1))))
         best = functools.reduce(jnp.maximum, [part[0] for part in parts])
         both = sum(jnp.exp2((its - best) * SCALE2) * sums for its, sums in parts)

time: 27.7 us -> 27.6 us (level)
  no operation moved by 1% of the time
where the time goes in v25:
time: 27.6 us; the launch traced here: 27.3 us
  blocking collectives  9.3 us (34%)
  starting transfers between devices  7.42 us (27%)
  waiting for transfers between devices  5.38 us (19%)
  Pallas kernels  3.88 us (14%)
  local copies, waits for them, and re-layouts  0.68 us (2%)
  between operations  0.68 us (2%)
    all_to_all x1, blocking collectives, exchange(): return lax.all_to_all(array, ('grp', 'blk'), 0, 0, tiled=True)  9.3 us
    all_to_all x1, starting transfers between devices, exchange(): return lax.all_to_all(array, ('grp', 'blk'), 0, 0, tiled=True)  6.97 us
    all_to_all x1, waiting for transfers between devices, exchange(): return lax.all_to_all(array, ('grp', 'blk'), 0, 0, tiled=True)  5.38 us
    pallas_call x3, Pallas kernels, call(): pl.pallas_call(kernel, out_shape=outs, in_specs=specs or [VMEM] * len(ope...  2.48 us
    pallas_call x1, Pallas kernels, local(): pl.pallas_call(fan_kernel, out_shape=[half(groups, KVH, chips, SHARE), ha...  1.4 us
    unnamed x2, local copies, waits for them, and re-layouts  0.68 us
  transfers between devices with their start and end apart: 2, of which 1 were waited for; matrix products, arithmetic and copies ran while one was open for 0% of the time, Pallas kernels for 8%

profile of v25, /device:TPU:0, one launch (start us, length us, event | category | flops | bytes accessed | tf_op | source)
XLA Modules:
  0.0 27.3 jit_solution(6805884536055970932)
XLA Ops:
  0.0 0.5 %collective-permute-start = (bf16[2,1,1024,128]{3,2,0,1:T(8,128)(2,1)}, bf16[2,1,1024,128]{3,2,0,1:T(8,128)(2,1)S(1)}, u32[]{:S(2)}, u32[]{:S(2)}) collective-permute-start(bf16[2,1,1024,128]{3,2,0,1:T(8,128)(2,1)} %bitcast.16), channel_id=1, source_target_pairs={{0,1},{1,0},{2,3},{3,2},{4,5},{5,4},{6,7},{7,6},{8,9},{9,8},{10,11... | collective-permute-start | bytes 1572872 | tf_op jit(solution)/shard_map/ppermute | solution.py:200
  0.5 1.4 %fan.1 = (bf16[2,4,2,16,128]{4,3,2,1,0:T(8,128)(2,1)}, bf16[4,16,128]{2,1,0:T(8,128)(2,1)S(1)}, bf16[2,1024,128]{2,1,0:T(8,128)(2,1)S(1)}, bf16[2048,128]{1,0:T(8,128)(2,1)S(1)}) custom-call(bf16[4,16,128]{2,1,0:T(8,128)(2,1)} %bitcast.18, bf16[2,1024,128]{2,1,0:T(8,128)(2,1)} %bitcast.17, bf16[2048,128]{1,0:T(8,128)(2,1)} %bitcast.15), custom_call_target="tpu_custom_call" | custom-call | tf_op jit(solution)/shard_map/fan/pallas_call | solution.py:209
  1.9 7.0 %all-to-all-start = ((bf16[32,8,128]{2,1,0:T(8,128)(2,1)}), bf16[32,8,128]{2,1,0:T(8,128)(2,1)S(1)}, u32[]{:S(2)}, u32[]{:S(2)}) async-start(bf16[32,8,128]{2,1,0:T(8,128)(2,1)} %bitcast.3), calls=%async_computation | async-start | bytes 131072 | tf_op jit(solution)/shard_map/all_to_all | solution.py:198
  9.5 0.0 copy-start
  9.5 0.7 %copy-done = bf16[1,2,4,128]{3,2,1,0:T(4,128)(2,1)S(1)} copy-done((bf16[1,2,4,128]{3,2,1,0:T(4,128)(2,1)S(1)}, bf16[1,2,4,128]{3,2,1,0:T(4,128)(2,1)}, u32[]{:S(2)}) %copy-start) | copy-done | bytes 2072
  10.2 0.7 %suffix.1 = (f32[64,128]{1,0:T(8,128)S(1)}, f32[64,128]{1,0:T(8,128)S(1)}) custom-call(s32[1]{0:T(128)S(6)} %copy.7.len_ref, bf16[8,128]{1,0:T(8,128)(2,1)S(1)} %bitcast.13, bf16[4,16,128]{2,1,0:T(8,128)(2,1)S(1)} %get-tuple-element.15.q_ref, bf16[2048,128]{1,0:T(8,128)(2,1)S(1)} %get-tuple-element.16.cache_ref), custom_call_target="tpu_custom_call" | custom-call | flops 70000000 | bytes 600000 | tf_op jit(solution)/shard_map/suffix/pallas_call | solution.py:170
  10.9 5.4 %all-to-all-done = bf16[32,8,128]{2,1,0:T(8,128)(2,1)S(1)} async-done(((bf16[32,8,128]{2,1,0:T(8,128)(2,1)}), bf16[32,8,128]{2,1,0:T(8,128)(2,1)S(1)}, u32[]{:S(2)}, u32[]{:S(2)}) %all-to-all-start) | async-done | bytes 65568 | tf_op jit(solution)/shard_map/all_to_all | solution.py:198
  16.2 0.0 collective-permute-done
  16.2 1.0 %prefix.1 = bf16[320,128]{1,0:T(8,128)(2,1)S(1)} custom-call(bf16[256,128]{1,0:T(8,128)(2,1)S(1)} %bitcast.12, bf16[2,1024,128]{2,1,0:T(8,128)(2,1)S(1)} %get-tuple-element.20.kv_ref, bf16[2,1024,128]{2,1,0:T(8,128)(2,1)S(1)} %bitcast.14), custom_call_target="tpu_custom_call" | custom-call | flops 402653184 | bytes 1600000 | tf_op jit(solution)/shard_map/prefix/pallas_call | solution.py:170
  17.2 9.3 %all_to_all.10 = bf16[32,5,2,128]{3,2,1,0:T(2,128)(2,1)S(1)} all-to-all(bf16[32,5,2,128]{3,2,1,0:T(2,128)(2,1)S(1)} %bitcast.11), channel_id=1, replica_groups=mesh['grp'=2,'blk'=16] {'grp','blk'}, dimensions={0} | all-to-all | bytes 163840 | tf_op jit(solution)/shard_map/all_to_all | solution.py:198
  26.5 0.8 %merge.1 = bf16[1,64,128]{2,1,0:T(8,128)(2,1)} custom-call(bf16[320,128]{1,0:T(8,128)(2,1)S(1)} %bitcast.10, f32[64,128]{1,0:T(8,128)S(1)} %get-tuple-element.21.suffix_ref, f32[64,128]{1,0:T(8,128)S(1)} %get-tuple-element.22.lse_ref), custom_call_target="tpu_custom_call" | custom-call | tf_op jit(solution)/shard_map/merge/pallas_call | solution.py:170
Async XLA Ops:
  0.0 16.2 %collective-permute-start = (bf16[2,1,1024,128]{3,2,0,1:T(8,128)(2,1)}, bf16[2,1,1024,128]{3,2,0,1:T(8,128)(2,1)S(1)}, u32[]{:S(2)}, u32[]{:S(2)}) collective-permute-start(bf16[2,1,1024,128]{3,2,0,1:T(8,128)(2,1)} %bitcast.16), channel_id=1, source_target_pairs={{0,1},{1,0},{2,3},{3,2},{4,5},{5,4},{6,7},{7,6},{8,9},{9,8},{10,11... | collective-permute-start | bytes 1572872 | tf_op jit(solution)/shard_map/ppermute | solution.py:200
  1.9 14.4 %all-to-all-start = ((bf16[32,8,128]{2,1,0:T(8,128)(2,1)}), bf16[32,8,128]{2,1,0:T(8,128)(2,1)S(1)}, u32[]{:S(2)}, u32[]{:S(2)}) async-start(bf16[32,8,128]{2,1,0:T(8,128)(2,1)} %bitcast.3), calls=%async_computation | async-start | bytes 131072 | tf_op jit(solution)/shard_map/all_to_all | solution.py:198
  9.5 0.7 %copy-start = (bf16[1,2,4,128]{3,2,1,0:T(4,128)(2,1)S(1)}, bf16[1,2,4,128]{3,2,1,0:T(4,128)(2,1)}, u32[]{:S(2)}) copy-start(bf16[1,2,4,128]{3,2,1,0:T(4,128)(2,1)} %param.8) | copy-start | bytes 6148

commit v26 on v15

--- a/solution.py
+++ b/solution.py
@@ -216,7 +216,7 @@
         [one(H)] * 2,
         (suffix_len, new_kv.reshape(2 * KVH, HD), q, cache),
         [pl.BlockSpec(memory_space=pltpu.SMEM), VMEM, VMEM, VMEM],
-        flops=70_000_000,
+        flops=20_000_000_000,
         bytes_accessed=600_000,
         transcendentals=140_000,
     )

time: 27.7 us -> 27.5 us (level)
  waiting for transfers between devices: 5.38 us -> 5.06 us
    all_to_all x1, starting transfers between devices: 6.96 us -> 7.3 us  [exchange(): return lax.all_to_all(array, ('grp', 'blk'), 0, 0, tiled=True)]
    all_to_all x1, waiting for transfers between devices: 5.38 us -> 5.05 us  [exchange(): return lax.all_to_all(array, ('grp', 'blk'), 0, 0, tiled=True)]
where the time goes in v26:
time: 27.5 us; the launch traced here: 27.2 us
  blocking collectives  9.3 us (34%)
  starting transfers between devices  7.62 us (28%)
  waiting for transfers between devices  5.06 us (18%)
  Pallas kernels  3.89 us (14%)
  between operations  0.69 us (3%)
  local copies, waits for them, and re-layouts  0.68 us (2%)
    all_to_all x1, blocking collectives, exchange(): return lax.all_to_all(array, ('grp', 'blk'), 0, 0, tiled=True)  9.3 us
    all_to_all x1, starting transfers between devices, exchange(): return lax.all_to_all(array, ('grp', 'blk'), 0, 0, tiled=True)  7.3 us
    all_to_all x1, waiting for transfers between devices, exchange(): return lax.all_to_all(array, ('grp', 'blk'), 0, 0, tiled=True)  5.05 us
    pallas_call x3, Pallas kernels, call(): pl.pallas_call(kernel, out_shape=outs, in_specs=specs or [VMEM] * len(ope...  2.49 us
    pallas_call x1, Pallas kernels, local(): pl.pallas_call(fan_kernel, out_shape=[half(groups, KVH, chips, SHARE), ha...  1.4 us
    unnamed x2, local copies, waits for them, and re-layouts  0.68 us
  transfers between devices with their start and end apart: 2, of which 1 were waited for; matrix products, arithmetic and copies ran while one was open for 0% of the time, Pallas kernels for 3%

profile of v26, /device:TPU:0, one launch (start us, length us, event | category | flops | bytes accessed | tf_op | source)
XLA Modules:
  0.0 27.2 jit_solution(5134822426708025487)
XLA Ops:
  0.0 1.4 %fan.1 = (bf16[2,4,2,16,128]{4,3,2,1,0:T(8,128)(2,1)}, bf16[4,16,128]{2,1,0:T(8,128)(2,1)S(1)}, bf16[2,1024,128]{2,1,0:T(8,128)(2,1)S(1)}, bf16[2048,128]{1,0:T(8,128)(2,1)S(1)}) custom-call(bf16[4,16,128]{2,1,0:T(8,128)(2,1)} %bitcast.14, bf16[2,1024,128]{2,1,0:T(8,128)(2,1)} %bitcast.12, bf16[2048,128]{1,0:T(8,128)(2,1)} %bitcast.13), custom_call_target="tpu_custom_call" | custom-call | tf_op jit(solution)/shard_map/fan/pallas_call | solution.py:202
  1.4 7.3 %all-to-all-start = ((bf16[32,8,128]{2,1,0:T(8,128)(2,1)}), bf16[32,8,128]{2,1,0:T(8,128)(2,1)S(1)}, u32[]{:S(2)}, u32[]{:S(2)}) async-start(bf16[32,8,128]{2,1,0:T(8,128)(2,1)} %bitcast.3), calls=%async_computation | async-start | bytes 131072 | tf_op jit(solution)/shard_map/all_to_all | solution.py:192
  8.7 0.3 %collective-permute-start = (bf16[2,1024,128]{2,1,0:T(8,128)(2,1)S(1)}, bf16[2,1024,128]{2,1,0:T(8,128)(2,1)S(1)}, u32[]{:S(2)}, u32[]{:S(2)}) collective-permute-start(bf16[2,1024,128]{2,1,0:T(8,128)(2,1)S(1)} %get-tuple-element.20.kv_ref), channel_id=1, source_target_pairs={{0,1},{1,0},{2,3},{3,2},{4,5},{5,4},{6,7},{7,6},{8,9},{9,8},{10,11... | collective-permute-start | bytes 1572872 | tf_op jit(solution)/shard_map/ppermute | solution.py:212
  9.7 0.0 copy-start
  9.7 0.7 %copy-done = bf16[1,2,4,128]{3,2,1,0:T(4,128)(2,1)S(1)} copy-done((bf16[1,2,4,128]{3,2,1,0:T(4,128)(2,1)S(1)}, bf16[1,2,4,128]{3,2,1,0:T(4,128)(2,1)}, u32[]{:S(2)}) %copy-start) | copy-done | bytes 2072
  10.4 0.7 %suffix.1 = (f32[64,128]{1,0:T(8,128)S(1)}, f32[64,128]{1,0:T(8,128)S(1)}) custom-call(s32[1]{0:T(128)S(6)} %copy.6.len_ref, bf16[8,128]{1,0:T(8,128)(2,1)S(1)} %bitcast.11, bf16[4,16,128]{2,1,0:T(8,128)(2,1)S(1)} %get-tuple-element.15.q_ref, bf16[2048,128]{1,0:T(8,128)(2,1)S(1)} %get-tuple-element.16.cache_ref), custom_call_target="tpu_custom_call" | custom-call | flops 20000000000 | bytes 600000 | tf_op jit(solution)/shard_map/suffix/pallas_call | solution.py:164
  11.1 5.1 %all-to-all-done = bf16[32,8,128]{2,1,0:T(8,128)(2,1)S(1)} async-done(((bf16[32,8,128]{2,1,0:T(8,128)(2,1)}), bf16[32,8,128]{2,1,0:T(8,128)(2,1)S(1)}, u32[]{:S(2)}, u32[]{:S(2)}) %all-to-all-start) | async-done | bytes 65568 | tf_op jit(solution)/shard_map/all_to_all | solution.py:192
  16.1 0.0 collective-permute-done.other_ref
  16.1 1.0 %prefix.1 = bf16[320,128]{1,0:T(8,128)(2,1)S(1)} custom-call(bf16[256,128]{1,0:T(8,128)(2,1)S(1)} %bitcast.10, bf16[2,1024,128]{2,1,0:T(8,128)(2,1)S(1)} %get-tuple-element.20.kv_ref, bf16[2,1024,128]{2,1,0:T(8,128)(2,1)S(1)} %collective-permute-done.other_ref), custom_call_target="tpu_custom_call" | custom-call | flops 402653184 | bytes 1600000 | tf_op jit(solution)/shard_map/prefix/pallas_call | solution.py:164
  17.1 9.3 %all_to_all.10 = bf16[32,5,2,128]{3,2,1,0:T(2,128)(2,1)S(1)} all-to-all(bf16[32,5,2,128]{3,2,1,0:T(2,128)(2,1)S(1)} %bitcast.9), channel_id=1, replica_groups=mesh['grp'=2,'blk'=16] {'grp','blk'}, dimensions={0} | all-to-all | bytes 163840 | tf_op jit(solution)/shard_map/all_to_all | solution.py:192
  26.4 0.8 %merge.1 = bf16[1,64,128]{2,1,0:T(8,128)(2,1)} custom-call(bf16[320,128]{1,0:T(8,128)(2,1)S(1)} %bitcast.8, f32[64,128]{1,0:T(8,128)S(1)} %get-tuple-element.21.suffix_ref, f32[64,128]{1,0:T(8,128)S(1)} %get-tuple-element.22.lse_ref), custom_call_target="tpu_custom_call" | custom-call | tf_op jit(solution)/shard_map/merge/pallas_call | solution.py:164
Async XLA Ops:
  1.4 14.7 %all-to-all-start = ((bf16[32,8,128]{2,1,0:T(8,128)(2,1)}), bf16[32,8,128]{2,1,0:T(8,128)(2,1)S(1)}, u32[]{:S(2)}, u32[]{:S(2)}) async-start(bf16[32,8,128]{2,1,0:T(8,128)(2,1)} %bitcast.3), calls=%async_computation | async-start | bytes 131072 | tf_op jit(solution)/shard_map/all_to_all | solution.py:192
  8.7 7.4 %collective-permute-start = (bf16[2,1024,128]{2,1,0:T(8,128)(2,1)S(1)}, bf16[2,1024,128]{2,1,0:T(8,128)(2,1)S(1)}, u32[]{:S(2)}, u32[]{:S(2)}) collective-permute-start(bf16[2,1024,128]{2,1,0:T(8,128)(2,1)S(1)} %get-tuple-element.20.kv_ref), channel_id=1, source_target_pairs={{0,1},{1,0},{2,3},{3,2},{4,5},{5,4},{6,7},{7,6},{8,9},{9,8},{10,11... | collective-permute-start | bytes 1572872 | tf_op jit(solution)/shard_map/ppermute | solution.py:212
  9.7 0.7 %copy-start = (bf16[1,2,4,128]{3,2,1,0:T(4,128)(2,1)S(1)}, bf16[1,2,4,128]{3,2,1,0:T(4,128)(2,1)}, u32[]{:S(2)}) copy-start(bf16[1,2,4,128]{3,2,1,0:T(4,128)(2,1)} %param.8) | copy-start | bytes 6148

commit v27 on v25

--- a/solution.py
+++ b/solution.py
@@ -197,7 +197,6 @@
     def exchange(array):
         return lax.all_to_all(array, ("grp", "blk"), 0, 0, tiled=True)
 
-    other = lax.ppermute(prefix_kv, "blk", [(i, i ^ 1) for i in range(members)]).reshape(2, span, HD)
     bound = [
         pltpu.with_memory_space_constraint(array, pltpu.HBM)
         for array in (
@@ -216,13 +215,14 @@
         compiler_params=pltpu.CompilerParams(vmem_limit_bytes=LIMIT),
     )(*bound)
     arrived = exchange(outgoing.reshape(devices, HALF, HD)).reshape(devices * HALF, HD)
+    other = lax.ppermute(kv, "blk", [(i, i ^ 1) for i in range(members)])
     suffix = call(
         suffix_kernel,
         "suffix",
         [one(H)] * 2,
         (suffix_len, new_kv.reshape(2 * KVH, HD), q, cache),
         [pl.BlockSpec(memory_space=pltpu.SMEM), VMEM, VMEM, VMEM],
-        flops=70_000_000,
+        flops=20_000_000_000,
         bytes_accessed=600_000,
         transcendentals=140_000,
     )

time: 27.6 us -> 27.5 us (level)
  waiting for transfers between devices: 5.38 us -> 5.06 us
    all_to_all x1, starting transfers between devices: 6.97 us -> 7.3 us  [exchange(): return lax.all_to_all(array, ('grp', 'blk'), 0, 0, tiled=True)]
    all_to_all x1, waiting for transfers between devices: 5.38 us -> 5.05 us  [exchange(): return lax.all_to_all(array, ('grp', 'blk'), 0, 0, tiled=True)]
  transfers between devices with their start and end apart: 2 -> 2, of which waited for: 1 -> 1; matrix products, arithmetic and copies ran while one was open for 0% -> 0% of each run, Pallas kernels for 8% -> 3%
where the time goes in v27:
time: 27.5 us; the launch traced here: 27.2 us
  blocking collectives  9.3 us (34%)
  starting transfers between devices  7.62 us (28%)
  waiting for transfers between devices  5.06 us (18%)
  Pallas kernels  3.88 us (14%)
  between operations  0.69 us (3%)
  local copies, waits for them, and re-layouts  0.68 us (2%)
    all_to_all x1, blocking collectives, exchange(): return lax.all_to_all(array, ('grp', 'blk'), 0, 0, tiled=True)  9.3 us
    all_to_all x1, starting transfers between devices, exchange(): return lax.all_to_all(array, ('grp', 'blk'), 0, 0, tiled=True)  7.3 us
    all_to_all x1, waiting for transfers between devices, exchange(): return lax.all_to_all(array, ('grp', 'blk'), 0, 0, tiled=True)  5.05 us
    pallas_call x3, Pallas kernels, call(): pl.pallas_call(kernel, out_shape=outs, in_specs=specs or [VMEM] * len(ope...  2.48 us
    pallas_call x1, Pallas kernels, local(): pl.pallas_call(fan_kernel, out_shape=[half(groups, KVH, chips, SHARE), ha...  1.4 us
    unnamed x2, local copies, waits for them, and re-layouts  0.68 us
  transfers between devices with their start and end apart: 2, of which 1 were waited for; matrix products, arithmetic and copies ran while one was open for 0% of the time, Pallas kernels for 3%

profile of v27, /device:TPU:0, one launch (start us, length us, event | category | flops | bytes accessed | tf_op | source)
XLA Modules:
  0.0 27.2 jit_solution(3833965169509217529)
XLA Ops:
  0.0 1.4 %fan.1 = (bf16[2,4,2,16,128]{4,3,2,1,0:T(8,128)(2,1)}, bf16[4,16,128]{2,1,0:T(8,128)(2,1)S(1)}, bf16[2,1024,128]{2,1,0:T(8,128)(2,1)S(1)}, bf16[2048,128]{1,0:T(8,128)(2,1)S(1)}) custom-call(bf16[4,16,128]{2,1,0:T(8,128)(2,1)} %bitcast.14, bf16[2,1024,128]{2,1,0:T(8,128)(2,1)} %bitcast.12, bf16[2048,128]{1,0:T(8,128)(2,1)} %bitcast.13), custom_call_target="tpu_custom_call" | custom-call | tf_op jit(solution)/shard_map/fan/pallas_call | solution.py:208
  1.4 7.3 %all-to-all-start = ((bf16[32,8,128]{2,1,0:T(8,128)(2,1)}), bf16[32,8,128]{2,1,0:T(8,128)(2,1)S(1)}, u32[]{:S(2)}, u32[]{:S(2)}) async-start(bf16[32,8,128]{2,1,0:T(8,128)(2,1)} %bitcast.3), calls=%async_computation | async-start | bytes 131072 | tf_op jit(solution)/shard_map/all_to_all | solution.py:198
  8.7 0.3 %collective-permute-start = (bf16[2,1024,128]{2,1,0:T(8,128)(2,1)S(1)}, bf16[2,1024,128]{2,1,0:T(8,128)(2,1)S(1)}, u32[]{:S(2)}, u32[]{:S(2)}) collective-permute-start(bf16[2,1024,128]{2,1,0:T(8,128)(2,1)S(1)} %get-tuple-element.20.kv_ref), channel_id=1, source_target_pairs={{0,1},{1,0},{2,3},{3,2},{4,5},{5,4},{6,7},{7,6},{8,9},{9,8},{10,11... | collective-permute-start | bytes 1572872 | tf_op jit(solution)/shard_map/ppermute | solution.py:218
  9.7 0.0 copy-start
  9.7 0.7 %copy-done = bf16[1,2,4,128]{3,2,1,0:T(4,128)(2,1)S(1)} copy-done((bf16[1,2,4,128]{3,2,1,0:T(4,128)(2,1)S(1)}, bf16[1,2,4,128]{3,2,1,0:T(4,128)(2,1)}, u32[]{:S(2)}) %copy-start) | copy-done | bytes 2072
  10.4 0.7 %suffix.1 = (f32[64,128]{1,0:T(8,128)S(1)}, f32[64,128]{1,0:T(8,128)S(1)}) custom-call(s32[1]{0:T(128)S(6)} %copy.6.len_ref, bf16[8,128]{1,0:T(8,128)(2,1)S(1)} %bitcast.11, bf16[4,16,128]{2,1,0:T(8,128)(2,1)S(1)} %get-tuple-element.15.q_ref, bf16[2048,128]{1,0:T(8,128)(2,1)S(1)} %get-tuple-element.16.cache_ref), custom_call_target="tpu_custom_call" | custom-call | flops 20000000000 | bytes 600000 | tf_op jit(solution)/shard_map/suffix/pallas_call | solution.py:170
  11.1 5.1 %all-to-all-done = bf16[32,8,128]{2,1,0:T(8,128)(2,1)S(1)} async-done(((bf16[32,8,128]{2,1,0:T(8,128)(2,1)}), bf16[32,8,128]{2,1,0:T(8,128)(2,1)S(1)}, u32[]{:S(2)}, u32[]{:S(2)}) %all-to-all-start) | async-done | bytes 65568 | tf_op jit(solution)/shard_map/all_to_all | solution.py:198
  16.1 0.0 collective-permute-done.other_ref
  16.1 1.0 %prefix.1 = bf16[320,128]{1,0:T(8,128)(2,1)S(1)} custom-call(bf16[256,128]{1,0:T(8,128)(2,1)S(1)} %bitcast.10, bf16[2,1024,128]{2,1,0:T(8,128)(2,1)S(1)} %get-tuple-element.20.kv_ref, bf16[2,1024,128]{2,1,0:T(8,128)(2,1)S(1)} %collective-permute-done.other_ref), custom_call_target="tpu_custom_call" | custom-call | flops 402653184 | bytes 1600000 | tf_op jit(solution)/shard_map/prefix/pallas_call | solution.py:170
  17.1 9.3 %all_to_all.10 = bf16[32,5,2,128]{3,2,1,0:T(2,128)(2,1)S(1)} all-to-all(bf16[32,5,2,128]{3,2,1,0:T(2,128)(2,1)S(1)} %bitcast.9), channel_id=1, replica_groups=mesh['grp'=2,'blk'=16] {'grp','blk'}, dimensions={0} | all-to-all | bytes 163840 | tf_op jit(solution)/shard_map/all_to_all | solution.py:198
  26.4 0.8 %merge.1 = bf16[1,64,128]{2,1,0:T(8,128)(2,1)} custom-call(bf16[320,128]{1,0:T(8,128)(2,1)S(1)} %bitcast.8, f32[64,128]{1,0:T(8,128)S(1)} %get-tuple-element.21.suffix_ref, f32[64,128]{1,0:T(8,128)S(1)} %get-tuple-element.22.lse_ref), custom_call_target="tpu_custom_call" | custom-call | tf_op jit(solution)/shard_map/merge/pallas_call | solution.py:170
Async XLA Ops:
  1.4 14.7 %all-to-all-start = ((bf16[32,8,128]{2,1,0:T(8,128)(2,1)}), bf16[32,8,128]{2,1,0:T(8,128)(2,1)S(1)}, u32[]{:S(2)}, u32[]{:S(2)}) async-start(bf16[32,8,128]{2,1,0:T(8,128)(2,1)} %bitcast.3), calls=%async_computation | async-start | bytes 131072 | tf_op jit(solution)/shard_map/all_to_all | solution.py:198
  8.7 7.4 %collective-permute-start = (bf16[2,1024,128]{2,1,0:T(8,128)(2,1)S(1)}, bf16[2,1024,128]{2,1,0:T(8,128)(2,1)S(1)}, u32[]{:S(2)}, u32[]{:S(2)}) collective-permute-start(bf16[2,1024,128]{2,1,0:T(8,128)(2,1)S(1)} %get-tuple-element.20.kv_ref), channel_id=1, source_target_pairs={{0,1},{1,0},{2,3},{3,2},{4,5},{5,4},{6,7},{7,6},{8,9},{9,8},{10,11... | collective-permute-start | bytes 1572872 | tf_op jit(solution)/shard_map/ppermute | solution.py:218
  9.7 0.7 %copy-start = (bf16[1,2,4,128]{3,2,1,0:T(4,128)(2,1)S(1)}, bf16[1,2,4,128]{3,2,1,0:T(4,128)(2,1)}, u32[]{:S(2)}) copy-start(bf16[1,2,4,128]{3,2,1,0:T(4,128)(2,1)} %param.8) | copy-start | bytes 6148

commit v28 on v27

--- a/solution.py
+++ b/solution.py
@@ -129,8 +129,9 @@
 def fan_kernel(q_hbm, kv_hbm, cache_hbm, out_ref, q_ref, kv_ref, cache_ref, sems, fan_sems):
     pairs = [(q_hbm, q_ref), (cache_hbm, cache_ref), (kv_hbm, kv_ref)]
     loads = [pltpu.make_async_copy(source, target, sems.at[i]) for i, (source, target) in enumerate(pairs)]
-    for load in loads:
-        load.start()
+    loads[0].start()
+    for load in loads[1:]:
+        load.start(priority=1)
     loads[0].wait()
     copies = [
         pltpu.make_async_copy(q_ref, out_ref.at[group, :, chip], fan_sems.at[group, chip])

time: 27.5 us -> 27.5 us (level)
  no operation moved by 1% of the time
where the time goes in v28:
time: 27.5 us; the launch traced here: 27.2 us
  blocking collectives  9.3 us (34%)
  starting transfers between devices  7.62 us (28%)
  waiting for transfers between devices  5.06 us (18%)
  Pallas kernels  3.88 us (14%)
  between operations  0.69 us (3%)
  local copies, waits for them, and re-layouts  0.68 us (2%)
    all_to_all x1, blocking collectives, exchange(): return lax.all_to_all(array, ('grp', 'blk'), 0, 0, tiled=True)  9.3 us
    all_to_all x1, starting transfers between devices, exchange(): return lax.all_to_all(array, ('grp', 'blk'), 0, 0, tiled=True)  7.3 us
    all_to_all x1, waiting for transfers between devices, exchange(): return lax.all_to_all(array, ('grp', 'blk'), 0, 0, tiled=True)  5.05 us
    pallas_call x3, Pallas kernels, call(): pl.pallas_call(kernel, out_shape=outs, in_specs=specs or [VMEM] * len(ope...  2.48 us
    pallas_call x1, Pallas kernels, local(): pl.pallas_call(fan_kernel, out_shape=[half(groups, KVH, chips, SHARE), ha...  1.4 us
    unnamed x2, local copies, waits for them, and re-layouts  0.68 us
  transfers between devices with their start and end apart: 2, of which 1 were waited for; matrix products, arithmetic and copies ran while one was open for 0% of the time, Pallas kernels for 3%

profile of v28, /device:TPU:0, one launch (start us, length us, event | category | flops | bytes accessed | tf_op | source)
XLA Modules:
  0.0 27.2 jit_solution(5520487498358057046)
XLA Ops:
  0.0 1.4 %fan.1 = (bf16[2,4,2,16,128]{4,3,2,1,0:T(8,128)(2,1)}, bf16[4,16,128]{2,1,0:T(8,128)(2,1)S(1)}, bf16[2,1024,128]{2,1,0:T(8,128)(2,1)S(1)}, bf16[2048,128]{1,0:T(8,128)(2,1)S(1)}) custom-call(bf16[4,16,128]{2,1,0:T(8,128)(2,1)} %bitcast.14, bf16[2,1024,128]{2,1,0:T(8,128)(2,1)} %bitcast.12, bf16[2048,128]{1,0:T(8,128)(2,1)} %bitcast.13), custom_call_target="tpu_custom_call" | custom-call | tf_op jit(solution)/shard_map/fan/pallas_call | solution.py:209
  1.4 7.3 %all-to-all-start = ((bf16[32,8,128]{2,1,0:T(8,128)(2,1)}), bf16[32,8,128]{2,1,0:T(8,128)(2,1)S(1)}, u32[]{:S(2)}, u32[]{:S(2)}) async-start(bf16[32,8,128]{2,1,0:T(8,128)(2,1)} %bitcast.3), calls=%async_computation | async-start | bytes 131072 | tf_op jit(solution)/shard_map/all_to_all | solution.py:199
  8.7 0.3 %collective-permute-start = (bf16[2,1024,128]{2,1,0:T(8,128)(2,1)S(1)}, bf16[2,1024,128]{2,1,0:T(8,128)(2,1)S(1)}, u32[]{:S(2)}, u32[]{:S(2)}) collective-permute-start(bf16[2,1024,128]{2,1,0:T(8,128)(2,1)S(1)} %get-tuple-element.20.kv_ref), channel_id=1, source_target_pairs={{0,1},{1,0},{2,3},{3,2},{4,5},{5,4},{6,7},{7,6},{8,9},{9,8},{10,11... | collective-permute-start | bytes 1572872 | tf_op jit(solution)/shard_map/ppermute | solution.py:219
  9.7 0.0 copy-start
  9.7 0.7 %copy-done = bf16[1,2,4,128]{3,2,1,0:T(4,128)(2,1)S(1)} copy-done((bf16[1,2,4,128]{3,2,1,0:T(4,128)(2,1)S(1)}, bf16[1,2,4,128]{3,2,1,0:T(4,128)(2,1)}, u32[]{:S(2)}) %copy-start) | copy-done | bytes 2072
  10.4 0.7 %suffix.1 = (f32[64,128]{1,0:T(8,128)S(1)}, f32[64,128]{1,0:T(8,128)S(1)}) custom-call(s32[1]{0:T(128)S(6)} %copy.6.len_ref, bf16[8,128]{1,0:T(8,128)(2,1)S(1)} %bitcast.11, bf16[4,16,128]{2,1,0:T(8,128)(2,1)S(1)} %get-tuple-element.15.q_ref, bf16[2048,128]{1,0:T(8,128)(2,1)S(1)} %get-tuple-element.16.cache_ref), custom_call_target="tpu_custom_call" | custom-call | flops 20000000000 | bytes 600000 | tf_op jit(solution)/shard_map/suffix/pallas_call | solution.py:171
  11.1 5.1 %all-to-all-done = bf16[32,8,128]{2,1,0:T(8,128)(2,1)S(1)} async-done(((bf16[32,8,128]{2,1,0:T(8,128)(2,1)}), bf16[32,8,128]{2,1,0:T(8,128)(2,1)S(1)}, u32[]{:S(2)}, u32[]{:S(2)}) %all-to-all-start) | async-done | bytes 65568 | tf_op jit(solution)/shard_map/all_to_all | solution.py:199
  16.1 0.0 collective-permute-done.other_ref
  16.1 1.0 %prefix.1 = bf16[320,128]{1,0:T(8,128)(2,1)S(1)} custom-call(bf16[256,128]{1,0:T(8,128)(2,1)S(1)} %bitcast.10, bf16[2,1024,128]{2,1,0:T(8,128)(2,1)S(1)} %get-tuple-element.20.kv_ref, bf16[2,1024,128]{2,1,0:T(8,128)(2,1)S(1)} %collective-permute-done.other_ref), custom_call_target="tpu_custom_call" | custom-call | flops 402653184 | bytes 1600000 | tf_op jit(solution)/shard_map/prefix/pallas_call | solution.py:171
  17.1 9.3 %all_to_all.10 = bf16[32,5,2,128]{3,2,1,0:T(2,128)(2,1)S(1)} all-to-all(bf16[32,5,2,128]{3,2,1,0:T(2,128)(2,1)S(1)} %bitcast.9), channel_id=1, replica_groups=mesh['grp'=2,'blk'=16] {'grp','blk'}, dimensions={0} | all-to-all | bytes 163840 | tf_op jit(solution)/shard_map/all_to_all | solution.py:199
  26.4 0.8 %merge.1 = bf16[1,64,128]{2,1,0:T(8,128)(2,1)} custom-call(bf16[320,128]{1,0:T(8,128)(2,1)S(1)} %bitcast.8, f32[64,128]{1,0:T(8,128)S(1)} %get-tuple-element.21.suffix_ref, f32[64,128]{1,0:T(8,128)S(1)} %get-tuple-element.22.lse_ref), custom_call_target="tpu_custom_call" | custom-call | tf_op jit(solution)/shard_map/merge/pallas_call | solution.py:171
Async XLA Ops:
  1.4 14.7 %all-to-all-start = ((bf16[32,8,128]{2,1,0:T(8,128)(2,1)}), bf16[32,8,128]{2,1,0:T(8,128)(2,1)S(1)}, u32[]{:S(2)}, u32[]{:S(2)}) async-start(bf16[32,8,128]{2,1,0:T(8,128)(2,1)} %bitcast.3), calls=%async_computation | async-start | bytes 131072 | tf_op jit(solution)/shard_map/all_to_all | solution.py:199
  8.7 7.4 %collective-permute-start = (bf16[2,1024,128]{2,1,0:T(8,128)(2,1)S(1)}, bf16[2,1024,128]{2,1,0:T(8,128)(2,1)S(1)}, u32[]{:S(2)}, u32[]{:S(2)}) collective-permute-start(bf16[2,1024,128]{2,1,0:T(8,128)(2,1)S(1)} %get-tuple-element.20.kv_ref), channel_id=1, source_target_pairs={{0,1},{1,0},{2,3},{3,2},{4,5},{5,4},{6,7},{7,6},{8,9},{9,8},{10,11... | collective-permute-start | bytes 1572872 | tf_op jit(solution)/shard_map/ppermute | solution.py:219
  9.7 0.7 %copy-start = (bf16[1,2,4,128]{3,2,1,0:T(4,128)(2,1)S(1)}, bf16[1,2,4,128]{3,2,1,0:T(4,128)(2,1)}, u32[]{:S(2)}) copy-start(bf16[1,2,4,128]{3,2,1,0:T(4,128)(2,1)} %param.8) | copy-start | bytes 6148

commit v29 on v27

--- a/solution.py
+++ b/solution.py
@@ -127,19 +127,20 @@
 
 
 def fan_kernel(q_hbm, kv_hbm, cache_hbm, out_ref, q_ref, kv_ref, cache_ref, sems, fan_sems):
-    pairs = [(q_hbm, q_ref), (cache_hbm, cache_ref), (kv_hbm, kv_ref)]
+    groups, heads, chips = out_ref.shape[:3]
+    pairs = [(q_hbm.at[head], q_ref.at[head]) for head in range(heads)] + [(cache_hbm, cache_ref), (kv_hbm, kv_ref)]
     loads = [pltpu.make_async_copy(source, target, sems.at[i]) for i, (source, target) in enumerate(pairs)]
     for load in loads:
         load.start()
-    loads[0].wait()
-    copies = [
-        pltpu.make_async_copy(q_ref, out_ref.at[group, :, chip], fan_sems.at[group, chip])
-        for group in range(out_ref.shape[0])
-        for chip in range(out_ref.shape[2])
-    ]
-    for copy in copies:
-        copy.start()
-    for copy in copies + loads[1:]:
+    copies = []
+    for head in range(heads):
+        loads[head].wait()
+        for group in range(groups):
+            for chip in range(chips):
+                sem = fan_sems.at[group, head, chip]
+                copies.append(pltpu.make_async_copy(q_ref.at[head], out_ref.at[group, head, chip], sem))
+                copies[-1].start()
+    for copy in copies + loads[heads:]:
         copy.wait()
 
 
@@ -210,7 +211,7 @@
         out_shape=[half(groups, KVH, chips, SHARE), half(KVH, SHARE), half(2, span), half(cache_rows)],
         in_specs=[pl.BlockSpec(memory_space=pltpu.HBM)] * 3,
         out_specs=[pl.BlockSpec(memory_space=pl.ANY), VMEM, VMEM, VMEM],
-        scratch_shapes=[pltpu.SemaphoreType.DMA((3,)), pltpu.SemaphoreType.DMA((groups, chips))],
+        scratch_shapes=[pltpu.SemaphoreType.DMA((KVH + 2,)), pltpu.SemaphoreType.DMA((groups, KVH, chips))],
         name="fan",
         compiler_params=pltpu.CompilerParams(vmem_limit_bytes=LIMIT),
     )(*bound)

time: 27.5 us -> 27.6 us (level)
  no operation moved by 1% of the time
where the time goes in v29:
time: 27.6 us; the launch traced here: 27.4 us
  blocking collectives  9.3 us (34%)
  starting transfers between devices  7.62 us (28%)
  waiting for transfers between devices  5.05 us (18%)
  Pallas kernels  4.02 us (15%)
  between operations  0.69 us (2%)
  local copies, waits for them, and re-layouts  0.68 us (2%)
    all_to_all x1, blocking collectives, exchange(): return lax.all_to_all(array, ('grp', 'blk'), 0, 0, tiled=True)  9.3 us
    all_to_all x1, starting transfers between devices, exchange(): return lax.all_to_all(array, ('grp', 'blk'), 0, 0, tiled=True)  7.3 us
    all_to_all x1, waiting for transfers between devices, exchange(): return lax.all_to_all(array, ('grp', 'blk'), 0, 0, tiled=True)  5.05 us
    pallas_call x3, Pallas kernels, call(): pl.pallas_call(kernel, out_shape=outs, in_specs=specs or [VMEM] * len(ope...  2.48 us
    pallas_call x1, Pallas kernels, local(): pl.pallas_call(fan_kernel, out_shape=[half(groups, KVH, chips, SHARE), ha...  1.54 us
    unnamed x2, local copies, waits for them, and re-layouts  0.68 us
  transfers between devices with their start and end apart: 2, of which 1 were waited for; matrix products, arithmetic and copies ran while one was open for 0% of the time, Pallas kernels for 3%

profile of v29, /device:TPU:0, one launch (start us, length us, event | category | flops | bytes accessed | tf_op | source)
XLA Modules:
  0.0 27.4 jit_solution(11967255814434829489)
XLA Ops:
  0.0 1.5 %fan.1 = (bf16[2,4,2,16,128]{4,3,2,1,0:T(8,128)(2,1)}, bf16[4,16,128]{2,1,0:T(8,128)(2,1)S(1)}, bf16[2,1024,128]{2,1,0:T(8,128)(2,1)S(1)}, bf16[2048,128]{1,0:T(8,128)(2,1)S(1)}) custom-call(bf16[4,16,128]{2,1,0:T(8,128)(2,1)} %bitcast.14, bf16[2,1024,128]{2,1,0:T(8,128)(2,1)} %bitcast.12, bf16[2048,128]{1,0:T(8,128)(2,1)} %bitcast.13), custom_call_target="tpu_custom_call" | custom-call | tf_op jit(solution)/shard_map/fan/pallas_call | solution.py:209
  1.6 7.3 %all-to-all-start = ((bf16[32,8,128]{2,1,0:T(8,128)(2,1)}), bf16[32,8,128]{2,1,0:T(8,128)(2,1)S(1)}, u32[]{:S(2)}, u32[]{:S(2)}) async-start(bf16[32,8,128]{2,1,0:T(8,128)(2,1)} %bitcast.3), calls=%async_computation | async-start | bytes 131072 | tf_op jit(solution)/shard_map/all_to_all | solution.py:199
  8.9 0.3 %collective-permute-start = (bf16[2,1024,128]{2,1,0:T(8,128)(2,1)S(1)}, bf16[2,1024,128]{2,1,0:T(8,128)(2,1)S(1)}, u32[]{:S(2)}, u32[]{:S(2)}) collective-permute-start(bf16[2,1024,128]{2,1,0:T(8,128)(2,1)S(1)} %get-tuple-element.20.kv_ref), channel_id=1, source_target_pairs={{0,1},{1,0},{2,3},{3,2},{4,5},{5,4},{6,7},{7,6},{8,9},{9,8},{10,11... | collective-permute-start | bytes 1572872 | tf_op jit(solution)/shard_map/ppermute | solution.py:219
  9.8 0.0 copy-start
  9.8 0.7 %copy-done = bf16[1,2,4,128]{3,2,1,0:T(4,128)(2,1)S(1)} copy-done((bf16[1,2,4,128]{3,2,1,0:T(4,128)(2,1)S(1)}, bf16[1,2,4,128]{3,2,1,0:T(4,128)(2,1)}, u32[]{:S(2)}) %copy-start) | copy-done | bytes 2072
  10.5 0.7 %suffix.1 = (f32[64,128]{1,0:T(8,128)S(1)}, f32[64,128]{1,0:T(8,128)S(1)}) custom-call(s32[1]{0:T(128)S(6)} %copy.6.len_ref, bf16[8,128]{1,0:T(8,128)(2,1)S(1)} %bitcast.11, bf16[4,16,128]{2,1,0:T(8,128)(2,1)S(1)} %get-tuple-element.15.q_ref, bf16[2048,128]{1,0:T(8,128)(2,1)S(1)} %get-tuple-element.16.cache_ref), custom_call_target="tpu_custom_call" | custom-call | flops 20000000000 | bytes 600000 | tf_op jit(solution)/shard_map/suffix/pallas_call | solution.py:171
  11.2 5.1 %all-to-all-done = bf16[32,8,128]{2,1,0:T(8,128)(2,1)S(1)} async-done(((bf16[32,8,128]{2,1,0:T(8,128)(2,1)}), bf16[32,8,128]{2,1,0:T(8,128)(2,1)S(1)}, u32[]{:S(2)}, u32[]{:S(2)}) %all-to-all-start) | async-done | bytes 65568 | tf_op jit(solution)/shard_map/all_to_all | solution.py:199
  16.3 0.0 collective-permute-done.other_ref
  16.3 1.0 %prefix.1 = bf16[320,128]{1,0:T(8,128)(2,1)S(1)} custom-call(bf16[256,128]{1,0:T(8,128)(2,1)S(1)} %bitcast.10, bf16[2,1024,128]{2,1,0:T(8,128)(2,1)S(1)} %get-tuple-element.20.kv_ref, bf16[2,1024,128]{2,1,0:T(8,128)(2,1)S(1)} %collective-permute-done.other_ref), custom_call_target="tpu_custom_call" | custom-call | flops 402653184 | bytes 1600000 | tf_op jit(solution)/shard_map/prefix/pallas_call | solution.py:171
  17.3 9.3 %all_to_all.10 = bf16[32,5,2,128]{3,2,1,0:T(2,128)(2,1)S(1)} all-to-all(bf16[32,5,2,128]{3,2,1,0:T(2,128)(2,1)S(1)} %bitcast.9), channel_id=1, replica_groups=mesh['grp'=2,'blk'=16] {'grp','blk'}, dimensions={0} | all-to-all | bytes 163840 | tf_op jit(solution)/shard_map/all_to_all | solution.py:199
  26.6 0.8 %merge.1 = bf16[1,64,128]{2,1,0:T(8,128)(2,1)} custom-call(bf16[320,128]{1,0:T(8,128)(2,1)S(1)} %bitcast.8, f32[64,128]{1,0:T(8,128)S(1)} %get-tuple-element.21.suffix_ref, f32[64,128]{1,0:T(8,128)S(1)} %get-tuple-element.22.lse_ref), custom_call_target="tpu_custom_call" | custom-call | tf_op jit(solution)/shard_map/merge/pallas_call | solution.py:171
Async XLA Ops:
  1.6 14.7 %all-to-all-start = ((bf16[32,8,128]{2,1,0:T(8,128)(2,1)}), bf16[32,8,128]{2,1,0:T(8,128)(2,1)S(1)}, u32[]{:S(2)}, u32[]{:S(2)}) async-start(bf16[32,8,128]{2,1,0:T(8,128)(2,1)} %bitcast.3), calls=%async_computation | async-start | bytes 131072 | tf_op jit(solution)/shard_map/all_to_all | solution.py:199
  8.9 7.4 %collective-permute-start = (bf16[2,1024,128]{2,1,0:T(8,128)(2,1)S(1)}, bf16[2,1024,128]{2,1,0:T(8,128)(2,1)S(1)}, u32[]{:S(2)}, u32[]{:S(2)}) collective-permute-start(bf16[2,1024,128]{2,1,0:T(8,128)(2,1)S(1)} %get-tuple-element.20.kv_ref), channel_id=1, source_target_pairs={{0,1},{1,0},{2,3},{3,2},{4,5},{5,4},{6,7},{7,6},{8,9},{9,8},{10,11... | collective-permute-start | bytes 1572872 | tf_op jit(solution)/shard_map/ppermute | solution.py:219
  9.8 0.7 %copy-start = (bf16[1,2,4,128]{3,2,1,0:T(4,128)(2,1)S(1)}, bf16[1,2,4,128]{3,2,1,0:T(4,128)(2,1)}, u32[]{:S(2)}) copy-start(bf16[1,2,4,128]{3,2,1,0:T(4,128)(2,1)} %param.8) | copy-start | bytes 6148

commit v30 on v27

--- a/solution.py
+++ b/solution.py
@@ -126,21 +126,20 @@
     lse_ref[...] = jnp.broadcast_to(best * SCALE2 + log2(total), lse_ref.shape)
 
 
-def fan_kernel(q_hbm, kv_hbm, cache_hbm, out_ref, q_ref, kv_ref, cache_ref, sems, fan_sems):
+def fan_kernel(q_hbm, kv_hbm, cache_hbm, out_ref, q_ref, kv_ref, cache_ref, fan_ref, sems):
     pairs = [(q_hbm, q_ref), (cache_hbm, cache_ref), (kv_hbm, kv_ref)]
     loads = [pltpu.make_async_copy(source, target, sems.at[i]) for i, (source, target) in enumerate(pairs)]
     for load in loads:
         load.start()
     loads[0].wait()
-    copies = [
-        pltpu.make_async_copy(q_ref, out_ref.at[group, :, chip], fan_sems.at[group, chip])
-        for group in range(out_ref.shape[0])
-        for chip in range(out_ref.shape[2])
-    ]
-    for copy in copies:
-        copy.start()
-    for copy in copies + loads[1:]:
-        copy.wait()
+    for group in range(out_ref.shape[0]):
+        for chip in range(out_ref.shape[2]):
+            fan_ref[group, :, chip] = q_ref[...]
+    copy = pltpu.make_async_copy(fan_ref, out_ref, sems.at[len(loads)])
+    copy.start()
+    for load in loads[1:]:
+        load.wait()
+    copy.wait()
 
 
 def merge_kernel(served, part_ref, suffix_ref, lse_ref, out_ref):
@@ -210,7 +209,7 @@
         out_shape=[half(groups, KVH, chips, SHARE), half(KVH, SHARE), half(2, span), half(cache_rows)],
         in_specs=[pl.BlockSpec(memory_space=pltpu.HBM)] * 3,
         out_specs=[pl.BlockSpec(memory_space=pl.ANY), VMEM, VMEM, VMEM],
-        scratch_shapes=[pltpu.SemaphoreType.DMA((3,)), pltpu.SemaphoreType.DMA((groups, chips))],
+        scratch_shapes=[pltpu.VMEM((groups, KVH, chips, SHARE, HD), jnp.bfloat16), pltpu.SemaphoreType.DMA((4,))],
         name="fan",
         compiler_params=pltpu.CompilerParams(vmem_limit_bytes=LIMIT),
     )(*bound)

time: 27.5 us -> 27.5 us (level)
  no operation moved by 1% of the time
where the time goes in v30:
time: 27.5 us; the launch traced here: 27.2 us
  blocking collectives  9.3 us (34%)
  starting transfers between devices  7.62 us (28%)
  waiting for transfers between devices  5.06 us (18%)
  Pallas kernels  3.86 us (14%)
  between operations  0.69 us (3%)
  local copies, waits for them, and re-layouts  0.68 us (2%)
    all_to_all x1, blocking collectives, exchange(): return lax.all_to_all(array, ('grp', 'blk'), 0, 0, tiled=True)  9.3 us
    all_to_all x1, starting transfers between devices, exchange(): return lax.all_to_all(array, ('grp', 'blk'), 0, 0, tiled=True)  7.3 us
    all_to_all x1, waiting for transfers between devices, exchange(): return lax.all_to_all(array, ('grp', 'blk'), 0, 0, tiled=True)  5.05 us
    pallas_call x3, Pallas kernels, call(): pl.pallas_call(kernel, out_shape=outs, in_specs=specs or [VMEM] * len(ope...  2.48 us
    pallas_call x1, Pallas kernels, local(): pl.pallas_call(fan_kernel, out_shape=[half(groups, KVH, chips, SHARE), ha...  1.37 us
    unnamed x2, local copies, waits for them, and re-layouts  0.68 us
  transfers between devices with their start and end apart: 2, of which 1 were waited for; matrix products, arithmetic and copies ran while one was open for 0% of the time, Pallas kernels for 3%

profile of v30, /device:TPU:0, one launch (start us, length us, event | category | flops | bytes accessed | tf_op | source)
XLA Modules:
  0.0 27.2 jit_solution(13195261596890062329)
XLA Ops:
  0.0 1.4 %fan.1 = (bf16[2,4,2,16,128]{4,3,2,1,0:T(8,128)(2,1)}, bf16[4,16,128]{2,1,0:T(8,128)(2,1)S(1)}, bf16[2,1024,128]{2,1,0:T(8,128)(2,1)S(1)}, bf16[2048,128]{1,0:T(8,128)(2,1)S(1)}) custom-call(bf16[4,16,128]{2,1,0:T(8,128)(2,1)} %bitcast.14, bf16[2,1024,128]{2,1,0:T(8,128)(2,1)} %bitcast.12, bf16[2048,128]{1,0:T(8,128)(2,1)} %bitcast.13), custom_call_target="tpu_custom_call" | custom-call | tf_op jit(solution)/shard_map/fan/pallas_call | solution.py:207
  1.4 7.3 %all-to-all-start = ((bf16[32,8,128]{2,1,0:T(8,128)(2,1)}), bf16[32,8,128]{2,1,0:T(8,128)(2,1)S(1)}, u32[]{:S(2)}, u32[]{:S(2)}) async-start(bf16[32,8,128]{2,1,0:T(8,128)(2,1)} %bitcast.3), calls=%async_computation | async-start | bytes 131072 | tf_op jit(solution)/shard_map/all_to_all | solution.py:197
  8.7 0.3 %collective-permute-start = (bf16[2,1024,128]{2,1,0:T(8,128)(2,1)S(1)}, bf16[2,1024,128]{2,1,0:T(8,128)(2,1)S(1)}, u32[]{:S(2)}, u32[]{:S(2)}) collective-permute-start(bf16[2,1024,128]{2,1,0:T(8,128)(2,1)S(1)} %get-tuple-element.20.kv_ref), channel_id=1, source_target_pairs={{0,1},{1,0},{2,3},{3,2},{4,5},{5,4},{6,7},{7,6},{8,9},{9,8},{10,11... | collective-permute-start | bytes 1572872 | tf_op jit(solution)/shard_map/ppermute | solution.py:217
  9.7 0.0 copy-start
  9.7 0.7 %copy-done = bf16[1,2,4,128]{3,2,1,0:T(4,128)(2,1)S(1)} copy-done((bf16[1,2,4,128]{3,2,1,0:T(4,128)(2,1)S(1)}, bf16[1,2,4,128]{3,2,1,0:T(4,128)(2,1)}, u32[]{:S(2)}) %copy-start) | copy-done | bytes 2072
  10.3 0.7 %suffix.1 = (f32[64,128]{1,0:T(8,128)S(1)}, f32[64,128]{1,0:T(8,128)S(1)}) custom-call(s32[1]{0:T(128)S(6)} %copy.6.len_ref, bf16[8,128]{1,0:T(8,128)(2,1)S(1)} %bitcast.11, bf16[4,16,128]{2,1,0:T(8,128)(2,1)S(1)} %get-tuple-element.15.q_ref, bf16[2048,128]{1,0:T(8,128)(2,1)S(1)} %get-tuple-element.16.cache_ref), custom_call_target="tpu_custom_call" | custom-call | flops 20000000000 | bytes 600000 | tf_op jit(solution)/shard_map/suffix/pallas_call | solution.py:169
  11.0 5.1 %all-to-all-done = bf16[32,8,128]{2,1,0:T(8,128)(2,1)S(1)} async-done(((bf16[32,8,128]{2,1,0:T(8,128)(2,1)}), bf16[32,8,128]{2,1,0:T(8,128)(2,1)S(1)}, u32[]{:S(2)}, u32[]{:S(2)}) %all-to-all-start) | async-done | bytes 65568 | tf_op jit(solution)/shard_map/all_to_all | solution.py:197
  16.1 0.0 collective-permute-done.other_ref
  16.1 1.0 %prefix.1 = bf16[320,128]{1,0:T(8,128)(2,1)S(1)} custom-call(bf16[256,128]{1,0:T(8,128)(2,1)S(1)} %bitcast.10, bf16[2,1024,128]{2,1,0:T(8,128)(2,1)S(1)} %get-tuple-element.20.kv_ref, bf16[2,1024,128]{2,1,0:T(8,128)(2,1)S(1)} %collective-permute-done.other_ref), custom_call_target="tpu_custom_call" | custom-call | flops 402653184 | bytes 1600000 | tf_op jit(solution)/shard_map/prefix/pallas_call | solution.py:169
  17.1 9.3 %all_to_all.10 = bf16[32,5,2,128]{3,2,1,0:T(2,128)(2,1)S(1)} all-to-all(bf16[32,5,2,128]{3,2,1,0:T(2,128)(2,1)S(1)} %bitcast.9), channel_id=1, replica_groups=mesh['grp'=2,'blk'=16] {'grp','blk'}, dimensions={0} | all-to-all | bytes 163840 | tf_op jit(solution)/shard_map/all_to_all | solution.py:197
  26.4 0.8 %merge.1 = bf16[1,64,128]{2,1,0:T(8,128)(2,1)} custom-call(bf16[320,128]{1,0:T(8,128)(2,1)S(1)} %bitcast.8, f32[64,128]{1,0:T(8,128)S(1)} %get-tuple-element.21.suffix_ref, f32[64,128]{1,0:T(8,128)S(1)} %get-tuple-element.22.lse_ref), custom_call_target="tpu_custom_call" | custom-call | tf_op jit(solution)/shard_map/merge/pallas_call | solution.py:169
Async XLA Ops:
  1.4 14.7 %all-to-all-start = ((bf16[32,8,128]{2,1,0:T(8,128)(2,1)}), bf16[32,8,128]{2,1,0:T(8,128)(2,1)S(1)}, u32[]{:S(2)}, u32[]{:S(2)}) async-start(bf16[32,8,128]{2,1,0:T(8,128)(2,1)} %bitcast.3), calls=%async_computation | async-start | bytes 131072 | tf_op jit(solution)/shard_map/all_to_all | solution.py:197
  8.7 7.4 %collective-permute-start = (bf16[2,1024,128]{2,1,0:T(8,128)(2,1)S(1)}, bf16[2,1024,128]{2,1,0:T(8,128)(2,1)S(1)}, u32[]{:S(2)}, u32[]{:S(2)}) collective-permute-start(bf16[2,1024,128]{2,1,0:T(8,128)(2,1)S(1)} %get-tuple-element.20.kv_ref), channel_id=1, source_target_pairs={{0,1},{1,0},{2,3},{3,2},{4,5},{5,4},{6,7},{7,6},{8,9},{9,8},{10,11... | collective-permute-start | bytes 1572872 | tf_op jit(solution)/shard_map/ppermute | solution.py:217
  9.7 0.7 %copy-start = (bf16[1,2,4,128]{3,2,1,0:T(4,128)(2,1)S(1)}, bf16[1,2,4,128]{3,2,1,0:T(4,128)(2,1)}, u32[]{:S(2)}) copy-start(bf16[1,2,4,128]{3,2,1,0:T(4,128)(2,1)} %param.8) | copy-start | bytes 6148

commit v31 on v30

--- a/solution.py
+++ b/solution.py
@@ -20,6 +20,7 @@
 HALF = SHARE // CORES
 MESSAGE = HALF + 2
 LANES = HD // HALF
+PIECES = 3
 LIMIT = 24 * 1024 * 1024
 NT = (((1,), (1,)), ((), ()))
 
@@ -36,21 +37,30 @@
     return jnp.log(x) * math.log2(math.e)
 
 
-def pack_stats(x):
+def split3(x):
     hi = x.astype(jnp.bfloat16).astype(jnp.float32)
     rest = x - hi
     mid = rest.astype(jnp.bfloat16).astype(jnp.float32)
-    low = rest - mid
-    row = lax.broadcasted_iota(jnp.int32, x.shape, 1)
-    lane = lax.broadcasted_iota(jnp.int32, x.shape, 2) - row * LANES
-    return jnp.sum(jnp.where(lane == 0, hi, jnp.where(lane == 1, mid, jnp.where(lane == 2, low, 0.0))), axis=1)
+    return hi, mid, rest - mid
+
+
+def pack_stats(best, total):
+    row = lax.broadcasted_iota(jnp.int32, best.shape, 1)
+    lane = lax.broadcasted_iota(jnp.int32, best.shape, 2) - row * LANES
+    packed = jnp.zeros_like(best)
+    for at, piece in enumerate((*split3(best), *split3(total))):
+        packed = jnp.where(lane == at, piece, packed)
+    return jnp.sum(packed, axis=1)
 
 
 def unpack_stats(rows):
     shape = (HALF, HD)
     mine = lax.broadcasted_iota(jnp.int32, shape, 1) // LANES == lax.broadcasted_iota(jnp.int32, shape, 0)
     pieces = [jnp.where(mine, jnp.broadcast_to(row, shape), 0.0) for row in rows]
-    return dot(jnp.concatenate(pieces, axis=0).astype(jnp.bfloat16), jnp.ones((HD, HD), jnp.bfloat16))
+    shape = (HD, 2 * HD)
+    which = lax.broadcasted_iota(jnp.int32, shape, 0) % LANES // PIECES
+    select = jnp.where(which == lax.broadcasted_iota(jnp.int32, shape, 1) // HD, 1.0, 0.0)
+    return dot(jnp.concatenate(pieces, axis=0).astype(jnp.bfloat16), select.astype(jnp.bfloat16))
 
 
 def prefix_kernel(q_ref, kv_ref, other_ref, out_ref):
@@ -80,14 +90,15 @@
             parts.append((best, dot(weight, jnp.concatenate([values, jnp.ones_like(values)], axis=1))))
         best = functools.reduce(jnp.maximum, [part[0] for part in parts])
         both = sum(jnp.exp2((its - best) * SCALE2) * sums for its, sums in parts)
-        total = both[:, HD:]
-        result = both[:, :HD] / total
+        numerator = both[:, :HD]
         slots = ROWS // HALF
-        stats = pack_stats((best * SCALE2 + log2(total)).reshape(slots, HALF, HD))
+        shape = (slots, HALF, HD)
+        best = jnp.broadcast_to(best * SCALE2, numerator.shape)
+        stats = pack_stats(best.reshape(shape), both[:, HD:].reshape(shape))
         empty = jnp.zeros((1, HD), jnp.float32)
         pieces = []
         for slot in range(slots):
-            pieces += [result[slot * HALF : (slot + 1) * HALF], stats[slot : slot + 1], empty]
+            pieces += [numerator[slot * HALF : (slot + 1) * HALF], stats[slot : slot + 1], empty]
         out_ref[pl.ds(trip * slots * MESSAGE, slots * MESSAGE)] = jnp.concatenate(pieces, axis=0).astype(jnp.bfloat16)
 
     trips = q_ref.shape[0] // ROWS
@@ -146,7 +157,7 @@
     part = part_ref[...].astype(jnp.float32)
     starts = range(0, len(served) * MESSAGE, MESSAGE)
     rows = [part[at : at + HALF] for at in starts]
-    sums = unpack_stats([part[at + HALF : at + HALF + 1] for at in starts]).reshape(len(served), HALF, HD)
+    sums = unpack_stats([part[at + HALF : at + HALF + 1] for at in starts]).reshape(len(served), HALF, 2 * HD)
     blocks = []
     for block in range(H // HALF):
         span = slice(block * HALF, (block + 1) * HALF)
@@ -154,12 +165,12 @@
         own_lse = lse_ref[span]
         best = own_lse
         for slot in own:
-            best = jnp.maximum(best, sums[slot])
+            best = jnp.maximum(best, sums[slot, :, :HD])
         total = jnp.exp2(own_lse - best)
         numerator = total * suffix_ref[span]
         for slot in own:
-            factor = jnp.exp2(sums[slot] - best)
-            total = total + factor
+            factor = jnp.exp2(sums[slot, :, :HD] - best)
+            total = total + factor * sums[slot, :, HD:]
             numerator = numerator + factor * rows[slot]
         blocks.append(numerator / total)
     out_ref[0] = jnp.concatenate(blocks, axis=0).astype(jnp.bfloat16)

time: 27.5 us -> 27.5 us (level)
  no operation moved by 1% of the time
where the time goes in v31:
time: 27.5 us; the launch traced here: 27.2 us
  blocking collectives  9.3 us (34%)
  starting transfers between devices  7.62 us (28%)
  waiting for transfers between devices  5.06 us (18%)
  Pallas kernels  3.85 us (14%)
  between operations  0.69 us (3%)
  local copies, waits for them, and re-layouts  0.68 us (2%)
    all_to_all x1, blocking collectives, exchange(): return lax.all_to_all(array, ('grp', 'blk'), 0, 0, tiled=True)  9.3 us
    all_to_all x1, starting transfers between devices, exchange(): return lax.all_to_all(array, ('grp', 'blk'), 0, 0, tiled=True)  7.3 us
    all_to_all x1, waiting for transfers between devices, exchange(): return lax.all_to_all(array, ('grp', 'blk'), 0, 0, tiled=True)  5.05 us
    pallas_call x3, Pallas kernels, call(): pl.pallas_call(kernel, out_shape=outs, in_specs=specs or [VMEM] * len(ope...  2.48 us
    pallas_call x1, Pallas kernels, local(): pl.pallas_call(fan_kernel, out_shape=[half(groups, KVH, chips, SHARE), ha...  1.37 us
    unnamed x2, local copies, waits for them, and re-layouts  0.68 us
  transfers between devices with their start and end apart: 2, of which 1 were waited for; matrix products, arithmetic and copies ran while one was open for 0% of the time, Pallas kernels for 3%

profile of v31, /device:TPU:0, one launch (start us, length us, event | category | flops | bytes accessed | tf_op | source)
XLA Modules:
  0.0 27.2 jit_solution(6304286609548256191)
XLA Ops:
  0.0 1.4 %fan.1 = (bf16[2,4,2,16,128]{4,3,2,1,0:T(8,128)(2,1)}, bf16[4,16,128]{2,1,0:T(8,128)(2,1)S(1)}, bf16[2,1024,128]{2,1,0:T(8,128)(2,1)S(1)}, bf16[2048,128]{1,0:T(8,128)(2,1)S(1)}) custom-call(bf16[4,16,128]{2,1,0:T(8,128)(2,1)} %bitcast.14, bf16[2,1024,128]{2,1,0:T(8,128)(2,1)} %bitcast.12, bf16[2048,128]{1,0:T(8,128)(2,1)} %bitcast.13), custom_call_target="tpu_custom_call" | custom-call | tf_op jit(solution)/shard_map/fan/pallas_call | solution.py:218
  1.4 7.3 %all-to-all-start = ((bf16[32,8,128]{2,1,0:T(8,128)(2,1)}), bf16[32,8,128]{2,1,0:T(8,128)(2,1)S(1)}, u32[]{:S(2)}, u32[]{:S(2)}) async-start(bf16[32,8,128]{2,1,0:T(8,128)(2,1)} %bitcast.3), calls=%async_computation | async-start | bytes 131072 | tf_op jit(solution)/shard_map/all_to_all | solution.py:208
  8.7 0.3 %collective-permute-start = (bf16[2,1024,128]{2,1,0:T(8,128)(2,1)S(1)}, bf16[2,1024,128]{2,1,0:T(8,128)(2,1)S(1)}, u32[]{:S(2)}, u32[]{:S(2)}) collective-permute-start(bf16[2,1024,128]{2,1,0:T(8,128)(2,1)S(1)} %get-tuple-element.20.kv_ref), channel_id=1, source_target_pairs={{0,1},{1,0},{2,3},{3,2},{4,5},{5,4},{6,7},{7,6},{8,9},{9,8},{10,11... | collective-permute-start | bytes 1572872 | tf_op jit(solution)/shard_map/ppermute | solution.py:228
  9.7 0.0 copy-start
  9.7 0.7 %copy-done = bf16[1,2,4,128]{3,2,1,0:T(4,128)(2,1)S(1)} copy-done((bf16[1,2,4,128]{3,2,1,0:T(4,128)(2,1)S(1)}, bf16[1,2,4,128]{3,2,1,0:T(4,128)(2,1)}, u32[]{:S(2)}) %copy-start) | copy-done | bytes 2072
  10.3 0.7 %suffix.1 = (f32[64,128]{1,0:T(8,128)S(1)}, f32[64,128]{1,0:T(8,128)S(1)}) custom-call(s32[1]{0:T(128)S(6)} %copy.6.len_ref, bf16[8,128]{1,0:T(8,128)(2,1)S(1)} %bitcast.11, bf16[4,16,128]{2,1,0:T(8,128)(2,1)S(1)} %get-tuple-element.15.q_ref, bf16[2048,128]{1,0:T(8,128)(2,1)S(1)} %get-tuple-element.16.cache_ref), custom_call_target="tpu_custom_call" | custom-call | flops 20000000000 | bytes 600000 | tf_op jit(solution)/shard_map/suffix/pallas_call | solution.py:180
  11.0 5.1 %all-to-all-done = bf16[32,8,128]{2,1,0:T(8,128)(2,1)S(1)} async-done(((bf16[32,8,128]{2,1,0:T(8,128)(2,1)}), bf16[32,8,128]{2,1,0:T(8,128)(2,1)S(1)}, u32[]{:S(2)}, u32[]{:S(2)}) %all-to-all-start) | async-done | bytes 65568 | tf_op jit(solution)/shard_map/all_to_all | solution.py:208
  16.1 0.0 collective-permute-done.other_ref
  16.1 1.0 %prefix.1 = bf16[320,128]{1,0:T(8,128)(2,1)S(1)} custom-call(bf16[256,128]{1,0:T(8,128)(2,1)S(1)} %bitcast.10, bf16[2,1024,128]{2,1,0:T(8,128)(2,1)S(1)} %get-tuple-element.20.kv_ref, bf16[2,1024,128]{2,1,0:T(8,128)(2,1)S(1)} %collective-permute-done.other_ref), custom_call_target="tpu_custom_call" | custom-call | flops 402653184 | bytes 1600000 | tf_op jit(solution)/shard_map/prefix/pallas_call | solution.py:180
  17.1 9.3 %all_to_all.10 = bf16[32,5,2,128]{3,2,1,0:T(2,128)(2,1)S(1)} all-to-all(bf16[32,5,2,128]{3,2,1,0:T(2,128)(2,1)S(1)} %bitcast.9), channel_id=1, replica_groups=mesh['grp'=2,'blk'=16] {'grp','blk'}, dimensions={0} | all-to-all | bytes 163840 | tf_op jit(solution)/shard_map/all_to_all | solution.py:208
  26.4 0.8 %merge.1 = bf16[1,64,128]{2,1,0:T(8,128)(2,1)} custom-call(bf16[320,128]{1,0:T(8,128)(2,1)S(1)} %bitcast.8, f32[64,128]{1,0:T(8,128)S(1)} %get-tuple-element.21.suffix_ref, f32[64,128]{1,0:T(8,128)S(1)} %get-tuple-element.22.lse_ref), custom_call_target="tpu_custom_call" | custom-call | tf_op jit(solution)/shard_map/merge/pallas_call | solution.py:180
Async XLA Ops:
  1.4 14.7 %all-to-all-start = ((bf16[32,8,128]{2,1,0:T(8,128)(2,1)}), bf16[32,8,128]{2,1,0:T(8,128)(2,1)S(1)}, u32[]{:S(2)}, u32[]{:S(2)}) async-start(bf16[32,8,128]{2,1,0:T(8,128)(2,1)} %bitcast.3), calls=%async_computation | async-start | bytes 131072 | tf_op jit(solution)/shard_map/all_to_all | solution.py:208
  8.7 7.4 %collective-permute-start = (bf16[2,1024,128]{2,1,0:T(8,128)(2,1)S(1)}, bf16[2,1024,128]{2,1,0:T(8,128)(2,1)S(1)}, u32[]{:S(2)}, u32[]{:S(2)}) collective-permute-start(bf16[2,1024,128]{2,1,0:T(8,128)(2,1)S(1)} %get-tuple-element.20.kv_ref), channel_id=1, source_target_pairs={{0,1},{1,0},{2,3},{3,2},{4,5},{5,4},{6,7},{7,6},{8,9},{9,8},{10,11... | collective-permute-start | bytes 1572872 | tf_op jit(solution)/shard_map/ppermute | solution.py:228
  9.7 0.7 %copy-start = (bf16[1,2,4,128]{3,2,1,0:T(4,128)(2,1)S(1)}, bf16[1,2,4,128]{3,2,1,0:T(4,128)(2,1)}, u32[]{:S(2)}) copy-start(bf16[1,2,4,128]{3,2,1,0:T(4,128)(2,1)} %param.8) | copy-start | bytes 6148
